TPU v7x, 32 devices: a whole 2x2x4 slice. The times are simulated.
32 devices in a mesh: cls: 2 (over y), dom: 4 (over x, core), orient: 4 (over z).
Axes of the slice: x: 2, y: 2, z: 4, core: 2. Of those that a mesh axis runs over, the one named last changes fastest.
Arguments:
- references: bfloat16 [2, 8, 4, 32768], P(None, 'cls', None, ('dom', 'orient')), may hold values from -2 to 2
- images: bfloat16 [2, 256, 32768], P(None, ('dom', 'orient')), may hold values from -16 to 16
- orient_lists: int32 [256, 1], P(('dom', 'orient')), may hold values from 0 to 3; in each aligned block of 16 rows (0 to 15, 16 to 31, ...) at most 6 rows name the same one
- shift_ids: int32 [256, 1], P(('dom', 'orient')), may hold values from 0 to 63
- fixed_weights: float32 [256, 1], P(('dom', 'orient')), may hold values from 0.2 to 2
Outputs:
- class_prob: float32 [256, 8], P(('dom', 'orient'), 'cls')
- volume: float32 [2, 8, 4, 32768], P(None, 'cls', 'orient', 'dom')
Inputs may be any that keep to these rules, and one draw needn't show every extreme that they name: `orient_lists`: within the rows of one device (16 particles), no orientation bin is listed by more than 6 particles, a bound that some block reaches.
All inputs are finite; a program needn't handle non-finite values.
Results may differ from a plain program's by a relative error of at most 0.02.
Values may be sent and summed in bfloat16 or wider, within the bound.
No kernel may reach another device: no remote copies, remote signals or barrier semaphores. Data moves between devices by JAX's collectives and lax.ppermute only.
A program may use at most 320 MiB of HBM per device.

v0:
```python
import math

import jax
import jax.numpy as jnp
from jax import lax
from jax.sharding import PartitionSpec as P

IMG = 256
TX = 8
TY = 8


TWO_PI = 2.0 * math.pi


def freq_ids(columns):
    freq_x = (columns % IMG - IMG // 2).astype(jnp.float32)
    freq_y = (columns // IMG).astype(jnp.float32)
    return (freq_x, freq_y)


def offsets(number):
    return (jnp.arange(number, dtype=jnp.int32) - number // 2).astype(jnp.float32)


def local(references, images, orient_lists, shift_ids, fixed_weights):
    particles_here = images.shape[1]
    full_pixels = images.shape[2]
    class_here = references.shape[1]
    orient_here = references.shape[2]
    list_length = orient_lists.shape[1]
    entry_count = particles_here * list_length
    image_re = images[0]
    image_im = images[1]
    piece = lax.all_gather(references, ("dom", "orient"), axis=3, tiled=True)
    band_width = piece.shape[3]
    columns = jnp.arange(band_width, dtype=jnp.int32)
    freq_x, freq_y = freq_ids(columns)
    angle_x = TWO_PI / IMG * (offsets(TX)[:, None] * freq_x[None, :])
    angle_y = TWO_PI / IMG * (offsets(TY)[:, None] * freq_y[None, :])
    cosine_x = jnp.cos(angle_x)
    sine_x = jnp.sin(angle_x)
    cosine_y = jnp.cos(angle_y)
    sine_y = jnp.sin(angle_y)
    band_re = image_re.astype(jnp.float32)
    band_im = image_im.astype(jnp.float32)
    shifted_x_re = (
        (band_re[None] * cosine_x[:, None] - band_im[None] * sine_x[:, None])
        .astype(jnp.bfloat16)
        .reshape(TX * particles_here, band_width)
    )
    shifted_x_im = (
        (band_re[None] * sine_x[:, None] + band_im[None] * cosine_x[:, None])
        .astype(jnp.bfloat16)
        .reshape(TX * particles_here, band_width)
    )
    ref_re = piece[0].reshape(class_here * orient_here, band_width).astype(jnp.float32)
    ref_im = piece[1].reshape(class_here * orient_here, band_width).astype(jnp.float32)
    shifted_ref_re = (
        (ref_re[None] * cosine_y[:, None] + ref_im[None] * sine_y[:, None])
        .astype(jnp.bfloat16)
        .reshape(TY * class_here * orient_here, band_width)
    )
    shifted_ref_im = (
        (ref_im[None] * cosine_y[:, None] - ref_re[None] * sine_y[:, None])
        .astype(jnp.bfloat16)
        .reshape(TY * class_here * orient_here, band_width)
    )
    partial_value = jnp.einsum(
        "aj,bj->ab", shifted_x_re, shifted_ref_re, preferred_element_type=jnp.float32
    )
    partial_value = partial_value + jnp.einsum(
        "aj,bj->ab", shifted_x_im, shifted_ref_im, preferred_element_type=jnp.float32
    )
    logits = partial_value.reshape(TX, particles_here, TY, class_here, orient_here)
    local_top = jnp.max(logits, axis=(0, 2, 3, 4))
    global_top = lax.pmax(local_top, "cls")
    exponent = jnp.exp(logits - global_top[None, :, None, None, None])
    totals = lax.psum(jnp.sum(exponent, axis=(0, 2, 3, 4)), "cls")
    class_prob = jnp.sum(exponent, axis=(0, 2, 4)) / totals[:, None]
    orient_ids = orient_lists.reshape(entry_count)
    shift_index = shift_ids.reshape(entry_count)
    particle_of = jnp.arange(entry_count, dtype=jnp.int32) // list_length
    insert_weight = (
        (fixed_weights[:, :, None] * class_prob[:, None, :])
        .astype(jnp.bfloat16)
        .reshape(entry_count, class_here)
    )
    all_columns = jnp.arange(full_pixels, dtype=jnp.int32)
    freq_x_all, freq_y_all = freq_ids(all_columns)
    orient_range = jnp.arange(orient_here, dtype=jnp.int32)
    band_count = lax.axis_size("dom")
    slot_most = max(2, 3 * entry_count // (2 * orient_here))
    owner_hit = (orient_ids[:, None] == orient_range[None, :]).astype(jnp.int32)
    before = jnp.cumsum(owner_hit, axis=0) - owner_hit
    slot_place = jnp.sum(before * owner_hit, axis=1)
    slot_range = jnp.arange(slot_most, dtype=jnp.int32)
    slot_pick = owner_hit.T[:, None, :] * (
        slot_place[None, None, :] == slot_range[None, :, None]
    ).astype(jnp.int32)
    source = jnp.sum(
        slot_pick * jnp.arange(entry_count, dtype=jnp.int32)[None, None, :], axis=2
    ).reshape(orient_here * slot_most)
    filled = jnp.sum(slot_pick, axis=2).reshape(orient_here * slot_most)
    particle_pick = particle_of[source]
    shift_pick = shift_index[source]
    picked_re = image_re[particle_pick].astype(jnp.float32)
    picked_im = image_im[particle_pick].astype(jnp.float32)
    entry_x = (shift_pick % TX - TX // 2).astype(jnp.float32)
    entry_y = (shift_pick // TX - TY // 2).astype(jnp.float32)
    angle = (
        TWO_PI
        / IMG
        * (entry_x[:, None] * freq_x_all[None, :] + entry_y[:, None] * freq_y_all[None, :])
    )
    cosine = jnp.cos(angle)
    sine = jnp.sin(angle)
    row_re = (picked_re * cosine - picked_im * sine).astype(jnp.bfloat16)
    row_im = (picked_re * sine + picked_im * cosine).astype(jnp.bfloat16)
    row_re, row_im = (row_re, row_im)
    slot_weight = insert_weight[source] * filled[:, None].astype(jnp.bfloat16)
    stacked = jnp.stack([row_re, row_im], 1).reshape(
        orient_here, slot_most, 2, band_count, full_pixels // band_count
    )
    stacked = jnp.transpose(stacked, (3, 0, 1, 2, 4)).reshape(
        band_count * orient_here, slot_most, 2, full_pixels // band_count
    )
    slot_weight = jnp.broadcast_to(
        slot_weight.reshape(1, orient_here, slot_most, class_here),
        (band_count, orient_here, slot_most, class_here),
    ).reshape(band_count * orient_here, slot_most, class_here)
    arrived_rows, arrived_weights = (
        lax.all_to_all(stacked, ("dom", "orient"), split_axis=0, concat_axis=0, tiled=True),
        lax.all_to_all(slot_weight, ("dom", "orient"), split_axis=0, concat_axis=0, tiled=True),
    )
    volume = jnp.einsum(
        "smk,smrj->rkj", arrived_weights, arrived_rows, preferred_element_type=jnp.float32
    )[:, :, None, :]
    return (class_prob, volume)


def solution(mesh):
    in_specs = (
        P(None, "cls", None, ("dom", "orient")),
        P(None, ("dom", "orient"), None),
        P(("dom", "orient"), None),
        P(("dom", "orient"), None),
        P(("dom", "orient"), None),
    )
    out_specs = (P(("dom", "orient"), "cls"), P(None, "cls", "orient", "dom"))
    return jax.shard_map(local, mesh=mesh, in_specs=in_specs, out_specs=out_specs, check_vma=False)
```

profile of v0, /device:TPU:0, one launch (start us, length us, event | category | flops | bytes accessed | tf_op | source)
XLA Modules:
  0.0 216.3 jit_solution(1324730031195048565)
XLA Ops:
  7.2 0.0 copy-start
  7.2 0.0 all-gather.2.cloned.1.call-start
  7.2 0.7 all-gather.2.cloned.1.call-update
  8.0 0.7 fusion.24
  8.7 0.7 fusion.31
  9.4 0.0 copy-start.6
  9.4 3.9 %slice_bitcast_fusion.1 = (bf16[16,32768]{1,0:T(8,128)(2,1)S(1)}, f32[16,32768]{1,0:T(8,128)}, f32[16,32768]{1,0:T(8,128)}, bf16[16,32768]{1,0:T(8,128)(2,1)S(1)}) fusion(bf16[2,16,32768]{2,1,0:T(8,128)(2,1)} %param.6), kind=kLoop, calls=%fused_computation.27 | loop fusion | flops 1048576 | bytes 8388608 | tf_op jit(solution)/shard_map/mul | solution.py:48
  13.3 0.0 copy-done.6
  13.3 0.2 select_reduce_fusion
  13.5 9.1 %fusion.4 = (f32[8,32768]{1,0:T(8,128)}, f32[8,32768]{1,0:T(8,128)}, f32[8,32768]{1,0:T(8,128)}, f32[8,32768]{1,0:T(8,128)}) fusion(f32[32768]{0:T(1024)S(1)} %fusion.10, f32[8]{0:T(128)S(1)} %add_convert_fusion.3, f32[32768]{0:T(1024)S(1)} %fusion.8), kind=kLoop, calls=%fused_computation.22 | loop fusion | flops 1048576 | bytes 4456480 | tf_op jit(solution)/shard_map/cos | solution.py:43
  22.5 0.3 multiply_reduce_fusion
  22.8 0.1 copy.57
  22.9 0.1 reshape.559
  23.0 0.1 copy.60
  23.1 0.7 gather_fusion
  23.8 2.7 %gather_fusion.1 = bf16[24,32768]{1,0:T(8,128)(2,1)} fusion(bf16[16,32768]{1,0:T(8,128)(2,1)S(1)} %get-tuple-element.24, s32[1024]{0:T(1024)S(1)} %pad_clamp_fusion), kind=kCustom, calls=%fused_computation.1 | custom fusion | bytes 3145824 | tf_op jit(solution)/shard_map/gather | solution.py:107
  26.6 5.2 %reshape.565 = f32[4,6,1,4,8192]{4,3,1,0,2:T(4,128)} reshape(bf16[24,32768]{1,0:T(8,128)(2,1)} %gather_fusion.1) | data formatting | bytes 4718592 | tf_op jit(solution)/shard_map/convert_element_type | solution.py:107
  31.8 2.8 %gather_fusion.3 = bf16[24,32768]{1,0:T(8,128)(2,1)} fusion(bf16[16,32768]{1,0:T(8,128)(2,1)S(1)} %get-tuple-element.27, s32[1024]{0:T(1024)S(1)} %pad_clamp_fusion), kind=kCustom, calls=%fused_computation.3 | custom fusion | bytes 3145824 | tf_op jit(solution)/shard_map/gather | solution.py:108
  34.6 0.0 copy-start.3
  34.6 5.3 %reshape.566 = f32[4,6,1,4,8192]{4,3,1,0,2:T(4,128)} reshape(bf16[24,32768]{1,0:T(8,128)(2,1)} %gather_fusion.3) | data formatting | bytes 4718592 | tf_op jit(solution)/shard_map/convert_element_type | solution.py:108
  39.9 0.0 copy-done
  39.9 0.7 gather_fusion.2
  40.6 0.1 gather.25
  40.7 0.2 fusion.12
  40.9 0.0 copy-done.3
  40.9 26.7 %subtract_convert_fusion.2 = (bf16[4,6,1,4,8192]{4,3,1,0,2:T(4,128)(2,1)}, bf16[4,6,1,4,8192]{4,3,1,0,2:T(4,128)(2,1)}) fusion(f32[4,6,1,4,8192]{4,3,1,0,2:T(4,128)} %reshape.566, f32[4,6,1,4,8192]{4,3,1,0,2:T(4,128)S(1)} %copy-done.3, f32[4,8192]{1,0:T(4,128)S(1)} %get-tuple-element.43, f32[4,6]{1,0:T(4,128)S(1)} %get-tuple-element.35, ...), kind=kLoop, calls=%fused_computation.13 | loop fusion | flops 9437184 | bytes 9699520 | tf_op jit(solution)/shard_map/convert_element_type | solution.py:118
  67.6 0.0 all-gather.2.cloned.1.call-done
  67.6 3.8 %slice_convert_fusion.1 = (f32[1,4,4,32768]{3,2,1,0:T(4,128)}, f32[1,4,4,32768]{3,2,1,0:T(4,128)}) fusion(bf16[2,4,4,32768]{3,2,1,0:T(4,128)(2,1)} %all-gather.2.cloned.1.call-done), kind=kLoop, calls=%fused_computation.19 | loop fusion | flops 1048576 | bytes 6291456 | tf_op jit(solution)/shard_map/convert_element_type | solution.py:57
  71.4 2.0 reshape.563
  73.4 3.0 %reshape.564 = f32[16,32768]{1,0:T(8,128)} reshape(f32[1,4,4,32768]{3,2,1,0:T(4,128)} %get-tuple-element.29) | data formatting | bytes 4194304 | tf_op jit(solution)/shard_map/convert_element_type | solution.py:58
  76.4 14.4 %subtract_convert_fusion = (bf16[8,16,32768]{2,1,0:T(8,128)(2,1)}, bf16[8,16,32768]{2,1,0:T(8,128)(2,1)S(1)}, bf16[8,16,32768]{2,1,0:T(8,128)(2,1)S(1)}, bf16[8,16,32768]{2,1,0:T(8,128)(2,1)}) fusion(f32[8,32768]{1,0:T(8,128)} %get-tuple-element.31, f32[16,32768]{1,0:T(8,128)} %reshape.564, f32[8,32768]{1,0:T(8,128)} %get-tuple-element.30, ...), kind=kLoop, calls=%fused_computation.5 | loop fusion | flops 67108864 | bytes 46137344 | tf_op jit(solution)/shard_map/convert_element_type | solution.py:66
  90.7 0.0 copy-start.2
  90.7 2.3 %fusion.38 = f32[128,128]{0,1:T(8,128)S(1)} fusion(bf16[128,32768]{1,0:T(8,128)(2,1)S(1)} %bitcast.48, bf16[128,32768]{1,0:T(8,128)(2,1)S(1)} %bitcast.47), kind=kOutput, calls=%fused_computation.91 | convolution fusion | flops 1073741824 | bytes 16842752 | tf_op jit(solution)/shard_map/aj,bj->ab/dot_general | solution.py:69
  93.1 1.0 copy-done.2
  94.1 0.0 copy-start.7
  94.1 6.2 %fusion.37 = (f32[128]{0:T(128)S(1)}, f32[128,128]{0,1:T(8,128)S(1)}) fusion(f32[128,128]{0,1:T(8,128)S(1)} %fusion.38, bf16[128,32768]{1,0:T(8,128)(2,1)} %bitcast.50, bf16[128,32768]{1,0:T(8,128)(2,1)S(1)} %bitcast.49), kind=kOutput, calls=%fused_computation.90 | convolution fusion | flops 1073774464 | bytes 16908800 | tf_op jit(solution)/shard_map/aj,bj->ab/dot_general | solution.py:72
  100.3 0.1 reduce_max.14
  100.4 5.9 %pmax.7 = f32[16]{0:T(128)S(1)} all-reduce(f32[16]{0:T(128)S(1)} %reduce_max.18), channel_id=1, replica_groups=mesh['cls'=2,'dom'=4,'orient'=4] {'cls'}, use_global_device_ids=true, to_apply=%region_2.3 | all-reduce | flops 16 | bytes 128 | tf_op jit(solution)/shard_map/pmax | solution.py:77
  106.2 0.1 sub.119
  106.3 1.0 reshape.558
  107.3 0.1 reduce_sum.54
  107.5 4.9 %psum.7 = f32[16]{0:T(128)S(1)} all-reduce(f32[16]{0:T(128)S(1)} %reduce_sum.55), channel_id=1, replica_groups=mesh['cls'=2,'dom'=4,'orient'=4] {'cls'}, use_global_device_ids=true, to_apply=%region_6.7 | all-reduce | flops 16 | bytes 128 | tf_op jit(solution)/shard_map/psum | solution.py:79
  112.4 1.2 exponential_reduce_fusion
  113.5 0.1 copy.56
  113.6 0.0 copy-done.7
  113.6 0.1 multiply_convert_fusion
  113.7 0.6 gather_fusion.4
  114.3 0.1 copy.59
  114.4 0.1 gather.28
  114.5 0.6 broadcast_in_dim.4.clone
  115.1 6.4 %all-to-all-start.1 = ((bf16[16,6,4]{1,2,0:T(4,128)(2,1)}), bf16[16,6,4]{1,2,0:T(4,128)(2,1)S(1)}, u32[]{:S(2)}, u32[]{:S(2)}) async-start(bf16[16,6,4]{1,2,0:T(4,128)(2,1)} %bitcast.14), calls=%async_computation.1 | async-start | bytes 32768 | tf_op jit(solution)/shard_map/all_to_all | solution.py:134
  121.5 0.0 copy-done.4
  121.5 0.0 copy-done.5
  121.6 2.2 %maximum_bitcast_fusion = bf16[4,4,6,2,8192]{4,0,2,1,3:T(4,128)(2,1)S(1)} fusion(bf16[4,6,1,4,8192]{4,3,1,0,2:T(4,128)(2,1)S(1)} %copy-done.5, bf16[4,6,1,4,8192]{4,3,1,0,2:T(4,128)(2,1)S(1)} %copy-done.4), kind=kLoop, calls=%fused_computation.10 | loop fusion | flops 1572864 | bytes 6291456 | tf_op jit(solution)/shard_map/transpose | solution.py:125
  123.8 4.9 %copy.58 = bf16[4,4,6,2,8192]{4,3,2,1,0:T(2,128)(2,1)} copy(bf16[4,4,6,2,8192]{4,0,2,1,3:T(4,128)(2,1)S(1)} %maximum_bitcast_fusion) | data formatting | bytes 6291456 | tf_op jit(solution)/shard_map/transpose | solution.py:125
  128.7 0.0 all-to-all-done.1
  128.7 6.0 %all-to-all-start = ((bf16[16,6,2,8192]{3,2,1,0:T(2,128)(2,1)}), bf16[16,6,2,8192]{3,2,1,0:T(2,128)(2,1)S(1)}, u32[]{:S(2)}, u32[]{:S(2)}) async-start(bf16[16,6,2,8192]{3,2,1,0:T(2,128)(2,1)} %bitcast.12), calls=%async_computation | async-start | bytes 6291456 | tf_op jit(solution)/shard_map/all_to_all | solution.py:133
  134.8 0.0 copy-start.1
  134.8 0.7 copy.65
  135.4 0.1 copy.64
  135.5 71.1 %all-to-all-done = bf16[16,6,2,8192]{3,2,1,0:T(2,128)(2,1)S(1)} async-done(((bf16[16,6,2,8192]{3,2,1,0:T(2,128)(2,1)}), bf16[16,6,2,8192]{3,2,1,0:T(2,128)(2,1)S(1)}, u32[]{:S(2)}, u32[]{:S(2)}) %all-to-all-start) | async-done | bytes 3145760 | tf_op jit(solution)/shard_map/all_to_all | solution.py:133
  206.7 1.8 convolution_bitcast_fusion
  208.4 1.0 copy.66
  209.4 0.0 copy-done.1
  (21 shorter events, 0.2 us)
Async XLA Ops:
  7.2 32.7 %copy-start = (s32[16,1]{0,1:T(1,128)S(1)}, s32[16,1]{0,1:T(1,128)}, u32[]{:S(2)}) copy-start(s32[16,1]{0,1:T(1,128)} %param.8) | copy-start | bytes 196
  7.2 60.4 %all-gather.2.cloned.1.call-start = ((), (), s32[]{:S(2)}) async-start(), calls=%async_computation.2 | async-start | bytes 2228224 | tf_op jit(solution)/shard_map/all_gather | solution.py:35
  9.4 3.9 %copy-start.6 = (s32[16,1]{0,1:T(1,128)S(1)}, s32[16,1]{0,1:T(1,128)}, u32[]{:S(2)}) copy-start(s32[16,1]{0,1:T(1,128)} %param.7) | copy-start | bytes 196
  34.6 6.4 %copy-start.3 = (f32[4,6,1,4,8192]{4,3,1,0,2:T(4,128)S(1)}, f32[4,6,1,4,8192]{4,3,1,0,2:T(4,128)}, u32[]{:S(2)}) copy-start(f32[4,6,1,4,8192]{4,3,1,0,2:T(4,128)} %reshape.565) | copy-start | bytes 9437188
  90.7 3.4 %copy-start.2 = (bf16[8,16,32768]{2,1,0:T(8,128)(2,1)S(1)}, bf16[8,16,32768]{2,1,0:T(8,128)(2,1)}, u32[]{:S(2)}) copy-start(bf16[8,16,32768]{2,1,0:T(8,128)(2,1)} %get-tuple-element.20) | copy-start | bytes 25165828
  94.1 19.5 %copy-start.7 = (f32[16,1]{0,1:T(1,128)S(1)}, f32[16,1]{0,1:T(1,128)}, u32[]{:S(2)}) copy-start(f32[16,1]{0,1:T(1,128)} %param.9) | copy-start | bytes 196
  94.1 27.4 %copy-start.4 = (bf16[4,6,1,4,8192]{4,3,1,0,2:T(4,128)(2,1)S(1)}, bf16[4,6,1,4,8192]{4,3,1,0,2:T(4,128)(2,1)}, u32[]{:S(2)}) copy-start(bf16[4,6,1,4,8192]{4,3,1,0,2:T(4,128)(2,1)} %get-tuple-element.18) | copy-start | bytes 4718596
  94.1 27.4 %copy-start.5 = (bf16[4,6,1,4,8192]{4,3,1,0,2:T(4,128)(2,1)S(1)}, bf16[4,6,1,4,8192]{4,3,1,0,2:T(4,128)(2,1)}, u32[]{:S(2)}) copy-start(bf16[4,6,1,4,8192]{4,3,1,0,2:T(4,128)(2,1)} %get-tuple-element.19) | copy-start | bytes 4718596
  115.1 13.6 %all-to-all-start.1 = ((bf16[16,6,4]{1,2,0:T(4,128)(2,1)}), bf16[16,6,4]{1,2,0:T(4,128)(2,1)S(1)}, u32[]{:S(2)}, u32[]{:S(2)}) async-start(bf16[16,6,4]{1,2,0:T(4,128)(2,1)} %bitcast.14), calls=%async_computation.1 | async-start | bytes 32768 | tf_op jit(solution)/shard_map/all_to_all | solution.py:134
  128.7 77.9 %all-to-all-start = ((bf16[16,6,2,8192]{3,2,1,0:T(2,128)(2,1)}), bf16[16,6,2,8192]{3,2,1,0:T(2,128)(2,1)S(1)}, u32[]{:S(2)}, u32[]{:S(2)}) async-start(bf16[16,6,2,8192]{3,2,1,0:T(2,128)(2,1)} %bitcast.12), calls=%async_computation | async-start | bytes 6291456 | tf_op jit(solution)/shard_map/all_to_all | solution.py:133
  134.8 74.7 %copy-start.1 = (s32[16,1]{0,1:T(1,128)S(1)}, s32[16,1]{0,1:T(1,128)}, u32[]{:S(2)}) copy-start(s32[16,1]{0,1:T(1,128)} %param.8) | copy-start | bytes 196
Sparse Core Ops, SparseCore 0:
  10.2 44.1 all-gather.1
where the time goes:
time: 217 us; the launch traced here: 216 us
  waiting for transfers between devices  71.8 us (33%)
  other arithmetic  63.5 us (29%)
  local copies, waits for them, and re-layouts  33.2 us (15%)
  between operations  14.2 us (7%)
  starting transfers between devices  12.5 us (6%)
  blocking collectives  10.8 us (5%)
  matrix products  10.3 us (5%)
    all_to_all x1, waiting for transfers between devices, local(): lax.all_to_all(stacked, ('dom', 'orient'), split_axis=0, concat_axis=0, t...  71.1 us
    convert_element_type x1, other arithmetic, local(): row_re = (picked_re * cosine - picked_im * sine).astype(jnp.bfloat16)  26.7 us
    convert_element_type x1, other arithmetic, local(): shifted_ref_im = (ref_im[None] * cosine_y[:, None] - ref_re[None] * sine_...  14.4 us
    cos x1, other arithmetic, local(): cosine_y = jnp.cos(angle_y)  9.06 us
    all_to_all x1, starting transfers between devices, local(): lax.all_to_all(slot_weight, ('dom', 'orient'), split_axis=0, concat_axis=...  6.41 us
    dot_general x1, matrix products, local(): jnp.einsum('aj,bj->ab', shifted_x_im, shifted_ref_im, preferred_element_t...  6.16 us
    all_to_all x1, starting transfers between devices, local(): lax.all_to_all(stacked, ('dom', 'orient'), split_axis=0, concat_axis=0, t...  6 us
    pmax x1, blocking collectives, local(): global_top = lax.pmax(local_top, 'cls')  5.86 us
  transfers between devices with their start and end apart: 3, of which 1 were waited for; matrix products, arithmetic and copies ran while one was open for 31% of the time, Pallas kernels for 0%

commit v1 on v0

v1 whole, which is shorter than its diff:
```python
import functools
import math

import jax
import jax.numpy as jnp
import numpy as np
from jax import lax
from jax.experimental import pallas as pl
from jax.experimental.pallas import tpu as pltpu
from jax.sharding import PartitionSpec as P

IMG = 256
TX = 8
TY = 8
HALF = TX // 2
LANES = 128
BF = jnp.bfloat16
F32 = jnp.float32


def trig_tables():
    steps = np.arange(1, HALF + 1)
    angle_x = 2.0 * math.pi / IMG * steps[:, None] * (np.arange(IMG) - IMG // 2)[None, :]
    angle_y = 2.0 * math.pi / IMG * np.arange(IMG // 2)[:, None] * steps[None, :]
    table_x = np.concatenate([np.cos(angle_x), np.sin(angle_x)], 0).astype(np.float32)
    table_y = np.concatenate([np.cos(angle_y), np.sin(angle_y)], 1).astype(np.float32)
    return table_x, table_y.reshape(-1)


def xor_pairs(size, step):
    return [(i, i ^ step) for i in range(size)]


def bands_kernel(ids, images, *rest):
    outs, sems = rest[:-1], rest[-1]
    width = outs[0].shape[2]
    copies = []
    for place, out in enumerate(outs):
        band = ids[0] ^ (place + 1)
        start = pl.multiple_of(band * width, width)
        copies.append(
            pltpu.make_async_copy(images.at[:, :, pl.ds(start, width)], out, sems.at[place])
        )
    for copy in copies:
        copy.start()
    for copy in copies:
        copy.wait()


def image_bands(ids, images, dom):
    parts, rows, pixels = images.shape
    width = pixels // dom
    return pl.pallas_call(
        bands_kernel,
        out_shape=[jax.ShapeDtypeStruct((parts, rows, width), images.dtype)] * (dom - 1),
        in_specs=[pl.BlockSpec(memory_space=pltpu.SMEM), pl.BlockSpec(memory_space=pl.ANY)],
        out_specs=[pl.BlockSpec(memory_space=pl.ANY)] * (dom - 1),
        scratch_shapes=[pltpu.SemaphoreType.DMA((dom - 1,))],
        name="image_bands",
    )(ids, images)


def logits_kernel(groups, ids, table_y, table_x, refs, *rest):
    images, outs = rest[:groups], rest[groups : 2 * groups]
    left, right = rest[2 * groups :]
    step = pl.program_id(0)
    chunk = refs.shape[3]
    rows = images[0].shape[1]
    group_rows = TX * rows
    names = refs.shape[1] * refs.shape[2]
    lines = chunk // IMG
    line_base = (ids[0] * pl.num_programs(0) + step) * lines
    for line in range(lines):
        cols = slice(line * IMG, (line + 1) * IMG)
        cols_im = slice(chunk + line * IMG, chunk + (line + 1) * IMG)
        base = (line_base + line) * TY
        ref_re = refs[0, :, :, cols].astype(F32).reshape(names, IMG)
        ref_im = refs[1, :, :, cols].astype(F32).reshape(names, IMG)

        def put_ref(b, re, im):
            right[b * names : (b + 1) * names, cols] = re.astype(BF)
            right[b * names : (b + 1) * names, cols_im] = im.astype(BF)

        put_ref(TY // 2, ref_re, ref_im)
        for t in range(1, HALF + 1):
            cosine = table_y[base + t - 1]
            sine = table_y[base + HALF + t - 1]
            re_c, im_s = ref_re * cosine, ref_im * sine
            im_c, re_s = ref_im * cosine, ref_re * sine
            put_ref(TY // 2 - t, re_c - im_s, im_c + re_s)
            if t < HALF:
                put_ref(TY // 2 + t, re_c + im_s, im_c - re_s)
        for g in range(groups):
            re = images[g][0, :, cols].astype(F32)
            im = images[g][1, :, cols].astype(F32)

            def put(a, re, im):
                top = g * group_rows + a * rows
                left[top : top + rows, cols] = re.astype(BF)
                left[top : top + rows, cols_im] = im.astype(BF)

            put(TX // 2, re, im)
            for t in range(1, HALF + 1):
                cosine = table_x[t - 1 : t, :]
                sine = table_x[HALF + t - 1 : HALF + t, :]
                re_c, im_s = re * cosine, im * sine
                re_s, im_c = re * sine, im * cosine
                put(TX // 2 - t, re_c + im_s, im_c - re_s)
                if t < HALF:
                    put(TX // 2 + t, re_c - im_s, re_s + im_c)
    value = lax.dot_general(
        left[...], right[...], (((1,), (1,)), ((), ())), preferred_element_type=F32
    )

    @pl.when(step == 0)
    def _():
        for g in range(groups):
            outs[g][...] = value[g * group_rows : (g + 1) * group_rows]

    @pl.when(step > 0)
    def _():
        for g in range(groups):
            outs[g][...] += value[g * group_rows : (g + 1) * group_rows]


def chunk_of(width):
    return min(width, 4 * IMG)


def partial_logits(ids, table_x, table_y, refs, own, others):
    parts, classes, orients, width = refs.shape
    chunk = chunk_of(width)
    count = width // chunk
    arrays = ([own] if own is not None else []) + list(others)
    groups = len(arrays)
    rows = arrays[0].shape[1]
    names = classes * orients
    specs = []
    for array in arrays:
        if array is own:
            specs.append(
                pl.BlockSpec((parts, rows, chunk), lambda i, s: (0, 0, s[0] * count + i))
            )
        else:
            specs.append(pl.BlockSpec((parts, rows, chunk), lambda i, s: (0, 0, i)))
    out_shape = (TX * rows, TY * names)
    return pl.pallas_call(
        functools.partial(logits_kernel, groups),
        out_shape=[jax.ShapeDtypeStruct(out_shape, F32)] * groups,
        grid_spec=pltpu.PrefetchScalarGridSpec(
            num_scalar_prefetch=1,
            grid=(count,),
            in_specs=[
                pl.BlockSpec(memory_space=pltpu.SMEM),
                pl.BlockSpec((TX, IMG), lambda i, s: (0, 0)),
                pl.BlockSpec((parts, classes, orients, chunk), lambda i, s: (0, 0, 0, i)),
            ]
            + specs,
            out_specs=[pl.BlockSpec(out_shape, lambda i, s: (0, 0))] * groups,
            scratch_shapes=[
                pltpu.VMEM((groups * TX * rows, 2 * chunk), BF),
                pltpu.VMEM((TY * names, 2 * chunk), BF),
            ],
        ),
        compiler_params=pltpu.CompilerParams(vmem_limit_bytes=32 * 1024 * 1024),
        cost_estimate=pl.CostEstimate(
            flops=2 * groups * TX * rows * TY * names * 2 * width,
            bytes_accessed=2 * 2 * width * (groups * rows + names),
            transcendentals=0,
        ),
        name="partial_logits",
    )(ids, table_y, table_x, refs, *arrays)


def stats_kernel(swap, classes, orients, here, there, out):
    groups, group_rows, lanes = here.shape
    rows = group_rows // TX
    lane = lax.broadcasted_iota(jnp.int32, (rows, lanes), 1)
    class_of = (lane // orients) % classes
    out_lane = lax.broadcasted_iota(jnp.int32, (rows, LANES), 1)
    for g in range(groups):
        logits = here[g] + there[g ^ swap]
        pieces = [logits[a * rows : (a + 1) * rows] for a in range(TX)]
        top = functools.reduce(jnp.maximum, pieces)
        top = jnp.max(top, axis=1, keepdims=True)
        sums = sum(jnp.exp(piece - top) for piece in pieces)
        line = jnp.where(out_lane == 0, top, 0.0)
        for k in range(classes):
            part = jnp.sum(jnp.where(class_of == k, sums, 0.0), axis=1, keepdims=True)
            line = jnp.where(out_lane == k + 1, part, line)
        out[g * rows : (g + 1) * rows, :] = line


def logit_stats(here, there, swap, classes, orients):
    groups, group_rows, lanes = here.shape
    return pl.pallas_call(
        functools.partial(stats_kernel, swap, classes, orients),
        out_shape=jax.ShapeDtypeStruct((groups * group_rows // TX, LANES), F32),
        cost_estimate=pl.CostEstimate(
            flops=4 * here.size, bytes_accessed=8 * here.size, transcendentals=here.size
        ),
        name="logit_stats",
    )(here, there)


def rows_kernel(groups, ids, table_y, table_x, *rest):
    metas, images = rest[:groups], rest[groups : 2 * groups]
    out, phase_c, phase_s = rest[2 * groups :]
    step = pl.program_id(0)
    chunk = out.shape[2]
    rows = images[0].shape[1]
    lines = chunk // IMG
    line_base = (ids[0] * pl.num_programs(0) + step) * lines

    def offsets(g):
        shift = metas[g][:, 1:2].astype(jnp.int32)
        move_x = shift % TX - TX // 2
        move_y = shift // TX - TY // 2
        return move_x, move_y

    @pl.when(step == 0)
    def _():
        for g in range(groups):
            move = jnp.broadcast_to(offsets(g)[0], (rows, IMG))
            cosine = jnp.ones((rows, IMG), F32)
            sine = jnp.zeros((rows, IMG), F32)
            for t in range(1, HALF + 1):
                hit = jnp.abs(move) == t
                cosine = jnp.where(hit, table_x[t - 1 : t, :], cosine)
                sine = jnp.where(hit, table_x[HALF + t - 1 : HALF + t, :], sine)
            phase_c[g * rows : (g + 1) * rows, :] = cosine
            phase_s[g * rows : (g + 1) * rows, :] = jnp.where(move < 0, -sine, sine)

    for g in range(groups):
        own = slice(g * rows, (g + 1) * rows)
        move = jnp.broadcast_to(offsets(g)[1], (rows, LANES))
        hits = [jnp.abs(move) == t for t in range(1, HALF + 1)]
        sign = jnp.where(move < 0, -1.0, 1.0)
        for line in range(lines):
            base = (line_base + line) * TY
            cos_y = jnp.ones((rows, LANES), F32)
            sin_y = jnp.zeros((rows, LANES), F32)
            for t in range(1, HALF + 1):
                cos_y = jnp.where(hits[t - 1], table_y[base + t - 1], cos_y)
                sin_y = jnp.where(hits[t - 1], table_y[base + HALF + t - 1], sin_y)
            sin_y = sin_y * sign
            for part in range(IMG // LANES):
                across = slice(part * LANES, (part + 1) * LANES)
                cols = slice(line * IMG + part * LANES, line * IMG + (part + 1) * LANES)
                cos_x, sin_x = phase_c[own, across], phase_s[own, across]
                cosine = cos_x * cos_y - sin_x * sin_y
                sine = sin_x * cos_y + cos_x * sin_y
                re = images[g][0, :, cols].astype(F32)
                im = images[g][1, :, cols].astype(F32)
                out[0, own, cols] = (re * cosine - im * sine).astype(BF)
                out[1, own, cols] = (re * sine + im * cosine).astype(BF)


def aligned_rows(ids, table_x, table_y, metas, own, others, dom):
    parts, rows, pixels = own.shape
    width = pixels // dom
    chunk = chunk_of(width)
    count = width // chunk
    groups = len(metas)
    return pl.pallas_call(
        functools.partial(rows_kernel, groups),
        out_shape=jax.ShapeDtypeStruct((parts, groups * rows, width), BF),
        grid_spec=pltpu.PrefetchScalarGridSpec(
            num_scalar_prefetch=1,
            grid=(count,),
            in_specs=[
                pl.BlockSpec(memory_space=pltpu.SMEM),
                pl.BlockSpec((TX, IMG), lambda i, s: (0, 0)),
            ]
            + [pl.BlockSpec((rows, LANES), lambda i, s: (0, 0))] * groups
            + [pl.BlockSpec((parts, rows, chunk), lambda i, s: (0, 0, s[0] * count + i))]
            + [pl.BlockSpec((parts, rows, chunk), lambda i, s: (0, 0, i))] * (groups - 1),
            out_specs=pl.BlockSpec((parts, groups * rows, chunk), lambda i, s: (0, 0, i)),
            scratch_shapes=[
                pltpu.VMEM((groups * rows, IMG), F32),
                pltpu.VMEM((groups * rows, IMG), F32),
            ],
        ),
        compiler_params=pltpu.CompilerParams(vmem_limit_bytes=32 * 1024 * 1024),
        cost_estimate=pl.CostEstimate(
            flops=20 * groups * rows * width,
            bytes_accessed=8 * groups * rows * width,
            transcendentals=0,
        ),
        name="aligned_rows",
    )(ids, table_y, table_x, *metas, own, *others)


def volume_kernel(groups, orients, classes, ids, *rest):
    stats, metas = rest[:4], rest[4 : 4 + groups]
    aligned = rest[4 + groups]
    prob, outs, mix = rest[5 + groups], rest[6 + groups : -1], rest[-1]
    step = pl.program_id(0)
    rows = metas[0].shape[0]

    @pl.when(step == 0)
    def _():
        lane = lax.broadcasted_iota(jnp.int32, (rows, LANES), 1)
        pieces = []
        for g in range(groups):
            near, far = (stats[0], stats[2]) if g % 2 == 0 else (stats[1], stats[3])
            place = g // 2
            near = near[place * rows : (place + 1) * rows, :]
            far = far[place * rows : (place + 1) * rows, :]
            top = jnp.maximum(near[:, 0:1], far[:, 0:1])
            near_scale = jnp.exp(near[:, 0:1] - top)
            far_scale = jnp.exp(far[:, 0:1] - top)
            held = (lane >= 1) & (lane <= classes)
            both = jnp.where(held, near * near_scale + far * far_scale, 0.0)
            totals = jnp.sum(both, axis=1, keepdims=True)
            spread = jnp.zeros((rows, LANES), F32)
            for k in range(classes):
                spread = jnp.where(lane % classes == k, near[:, k + 1 : k + 2], spread)
            class_prob = spread * near_scale / totals
            if g == 0:
                prob[...] = class_prob
            weight = (metas[g][:, 2:3] * class_prob).astype(BF).astype(F32)
            bin_of = metas[g][:, 0:1].astype(jnp.int32) ^ ids[1]
            pieces.append(jnp.where(lane // classes == bin_of, weight, 0.0))
        mixing = jnp.concatenate(pieces, axis=0)
        mix[...] = jnp.transpose(mixing)[: orients * classes].astype(BF)

    for part in range(2):
        value = jnp.dot(mix[...], aligned[part], preferred_element_type=F32)
        for o in range(orients):
            outs[o][part] = value[o * classes : (o + 1) * classes].astype(outs[o].dtype)


def volume_terms(ids, stats, metas, aligned, orients, classes):
    parts, entries, width = aligned.shape
    groups = len(metas)
    rows = entries // groups
    chunk = chunk_of(width)
    count = width // chunk
    out_shape = (parts, classes, width)
    fixed = lambda i, s: (0, 0)
    return pl.pallas_call(
        functools.partial(volume_kernel, groups, orients, classes),
        out_shape=[jax.ShapeDtypeStruct((rows, LANES), F32)]
        + [
            jax.ShapeDtypeStruct(out_shape, F32 if o == 0 else BF)
            for o in range(orients)
        ],
        grid_spec=pltpu.PrefetchScalarGridSpec(
            num_scalar_prefetch=1,
            grid=(count,),
            in_specs=[pl.BlockSpec(stats[0].shape, fixed)] * 4
            + [pl.BlockSpec((rows, LANES), fixed)] * groups
            + [pl.BlockSpec((parts, entries, chunk), lambda i, s: (0, 0, i))],
            out_specs=[pl.BlockSpec((rows, LANES), fixed)]
            + [pl.BlockSpec((parts, classes, chunk), lambda i, s: (0, 0, i))] * orients,
            scratch_shapes=[pltpu.VMEM((orients * classes, entries), BF)],
        ),
        cost_estimate=pl.CostEstimate(
            flops=4 * orients * classes * entries * width,
            bytes_accessed=4 * entries * width + 4 * orients * classes * width,
            transcendentals=0,
        ),
        name="volume_terms",
    )(ids, *stats, *metas, aligned)


def local(dom, orient, cls, references, images, orient_lists, shift_ids, fixed_weights):
    classes, orients = references.shape[1], references.shape[2]
    table_x, table_y = (jnp.asarray(t) for t in trig_tables())
    ids = jnp.stack([lax.axis_index("dom"), lax.axis_index("orient")]).astype(jnp.int32)
    rows = images.shape[1]

    def swap_dom(array, step):
        return lax.ppermute(array, "dom", xor_pairs(dom, step))

    refs = lax.all_gather(references, "orient", axis=3, tiled=True)
    bands = image_bands(ids, images, dom)
    others = [swap_dom(band, step + 1) for step, band in enumerate(bands)]
    meta = jnp.concatenate(
        [orient_lists.astype(F32), shift_ids.astype(F32), fixed_weights], axis=1
    )
    meta = jnp.pad(meta, ((0, 0), (0, LANES - meta.shape[1])))
    metas = [meta] + [swap_dom(meta, step) for step in range(1, dom)]

    near = partial_logits(ids, table_x, table_y, refs, images, others[:1])
    far = partial_logits(ids, table_x, table_y, refs, None, others[1:])
    partial = list(near) + list(far)
    kept = [partial[s] + swap_dom(partial[s ^ 1], 1) for s in range(0, dom, 2)]
    here = jnp.stack(kept)
    step = 2
    there, swap = jnp.zeros_like(here), 0
    while step < dom:
        there, swap = swap_dom(here, step), step // 2
        if step * 2 < dom:
            order = np.arange(dom // 2) ^ swap
            here = here + jnp.stack([there[i] for i in order])
        step *= 2
    stats = logit_stats(here, there, swap, classes, orients)

    pairs = [(i, i ^ dom) for i in range(cls * dom)]
    cross = [(i, i ^ dom ^ 1) for i in range(cls * dom)]
    stats_all = [
        stats,
        swap_dom(stats, 1),
        lax.ppermute(stats, ("cls", "dom"), pairs),
        lax.ppermute(stats, ("cls", "dom"), cross),
    ]
    aligned = aligned_rows(ids, table_x, table_y, metas, images, others, dom)
    prob, *terms = volume_terms(ids, stats_all, metas, aligned, orients, classes)
    volume = terms[0]
    for o in range(1, orients):
        volume = volume + lax.ppermute(terms[o], "orient", xor_pairs(orient, o)).astype(F32)
    return prob[:, :classes], volume[:, :, None, :]


def solution(mesh):
    in_specs = (
        P(None, "cls", None, ("dom", "orient")),
        P(None, ("dom", "orient"), None),
        P(("dom", "orient"), None),
        P(("dom", "orient"), None),
        P(("dom", "orient"), None),
    )
    out_specs = (P(("dom", "orient"), "cls"), P(None, "cls", "orient", "dom"))
    body = functools.partial(local, mesh.shape["dom"], mesh.shape["orient"], mesh.shape["cls"])
    return jax.shard_map(body, mesh=mesh, in_specs=in_specs, out_specs=out_specs, check_vma=False)
```

time: 217 us -> 130 us (0.60)
  Pallas kernels: 0 us -> 73.5 us
  other arithmetic: 63.5 us -> 1.7 us
  waiting for transfers between devices: 71.8 us -> 16.7 us
  local copies, waits for them, and re-layouts: 33.2 us -> 6.69 us
  between operations: 14.2 us -> 0.9 us
  matrix products: 10.3 us -> 0 us
  blocking collectives: 10.8 us -> 16.8 us
    pallas_call x0 -> x6, Pallas kernels: none -> 73.5 us  [the longest x1 49.6 us: image_bands(): pl.pallas_call(bands_kernel, out_shape=[jax.ShapeDtypeStruct((parts, rows...]
    all_to_all x2 -> x0, waiting for transfers between devices: 71.1 us -> none  [the longest x1 71.1 us: local(): lax.all_to_all(stacked, ('dom', 'orient'), split_axis=0, concat_axis=0, t...]
    convert_element_type x13 -> x2, other arithmetic: 46.6 us -> 0.01 us  [the longest x1 0.01 us: local(): orient_lists.astype(F32)]
    all_gather x0 -> x1, blocking collectives: none -> 16.8 us  [local(): refs = lax.all_gather(references, 'orient', axis=3, tiled=True)]
    ppermute x0 -> x15, waiting for transfers between devices: none -> 16.7 us  [the longest x3 8.48 us: local(): lax.ppermute(terms[o], 'orient', xor_pairs(orient, o)).astype(F32)]
    convert_element_type x4 -> x0, local copies, waits for them, and re-layouts: 15.5 us -> none  [the longest x1 5.33 us: local(): picked_im = image_im[particle_pick].astype(jnp.float32)]
    ppermute x0 -> x15, starting transfers between devices: none -> 13.1 us  [the longest x10 6.87 us: swap_dom(): return lax.ppermute(array, 'dom', xor_pairs(dom, step))]
    all_to_all x2 -> x0, starting transfers between devices: 12.4 us -> none  [the longest x1 6.41 us: local(): lax.all_to_all(slot_weight, ('dom', 'orient'), split_axis=0, concat_axis=...]
  transfers between devices with their start and end apart: 3 -> 15, of which waited for: 1 -> 6; matrix products, arithmetic and copies ran while one was open for 31% -> 1% of each run, Pallas kernels for 0% -> 13%
where the time goes in v1:
time: 130 us; the launch traced here: 129 us
  Pallas kernels  73.5 us (57%)
  blocking collectives  16.8 us (13%)
  waiting for transfers between devices  16.7 us (13%)
  starting transfers between devices  13.1 us (10%)
  local copies, waits for them, and re-layouts  6.69 us (5%)
  other arithmetic  1.7 us (1%)
    pallas_call x1, Pallas kernels, image_bands(): pl.pallas_call(bands_kernel, out_shape=[jax.ShapeDtypeStruct((parts, rows...  49.6 us
    all_gather x1, blocking collectives, local(): refs = lax.all_gather(references, 'orient', axis=3, tiled=True)  16.8 us
    pallas_call x2, Pallas kernels, partial_logits(): pl.pallas_call(functools.partial(logits_kernel, groups), out_shape=[jax.S...  10.8 us
    ppermute x3, waiting for transfers between devices, local(): lax.ppermute(terms[o], 'orient', xor_pairs(orient, o)).astype(F32)  8.48 us
    ppermute x10, waiting for transfers between devices, swap_dom(): return lax.ppermute(array, 'dom', xor_pairs(dom, step))  8.24 us
    pallas_call x1, Pallas kernels, volume_terms(): pl.pallas_call(functools.partial(volume_kernel, groups, orients, classes)...  6.91 us
    ppermute x10, starting transfers between devices, swap_dom(): return lax.ppermute(array, 'dom', xor_pairs(dom, step))  6.87 us
    unnamed x40, local copies, waits for them, and re-layouts  6.6 us
  transfers between devices with their start and end apart: 15, of which 6 were waited for; matrix products, arithmetic and copies ran while one was open for 1% of the time, Pallas kernels for 13%

profile of v1, /device:TPU:0, one launch (start us, length us, event | category | flops | bytes accessed | tf_op | source)
XLA Modules:
  0.0 129.3 jit_solution(521624243430585328)
XLA Ops:
  0.6 0.0 copy-start.10
  0.6 0.0 copy-start.8
  0.7 0.0 copy-start
  0.7 0.6 pad_add_fusion.ids
  1.3 49.6 %image_bands.1 = (bf16[2,16,8192]{2,1,0:T(8,128)(2,1)}, bf16[2,16,8192]{2,1,0:T(8,128)(2,1)}, bf16[2,16,8192]{2,1,0:T(8,128)(2,1)}) custom-call(s32[2]{0:T(128)} %pad_add_fusion.ids, bf16[2,16,32768]{2,1,0:T(8,128)(2,1)} %rest_4_.1), custom_call_target="tpu_custom_call" | custom-call | tf_op jit(solution)/shard_map/image_bands/pallas_call | solution.py:53
  50.8 0.5 collective-permute-start
  51.4 2.6 %collective-permute-start.2 = (bf16[2,16,8192]{2,1,0:T(8,128)(2,1)}, bf16[2,16,8192]{2,1,0:T(8,128)(2,1)S(1)}, u32[]{:S(2)}, u32[]{:S(2)}) collective-permute-start(bf16[2,16,8192]{2,1,0:T(8,128)(2,1)} %get-tuple-element.17), channel_id=1, source_target_pairs={{0,8},{4,12},{8,0},{12,4},{1,9},{5,13},{9,1},{13,5},{2,10},{6,14},... | collective-permute-start | bytes 1572872 | tf_op jit(solution)/shard_map/ppermute | solution.py:375
  53.9 0.1 collective-permute-start.3
  54.0 16.8 %all_gather.3.refs = bf16[2,4,4,8192]{3,2,1,0:T(4,128)(2,1)S(1)} all-gather(bf16[2,4,4,2048]{3,2,1,0:T(4,128)(2,1)} %param.7), channel_id=1, replica_groups=mesh['cls'=2,'dom'=4,'orient'=4] {'orient'}, dimensions={3}, use_global_device_ids=true | all-gather | bytes 655360 | tf_op jit(solution)/shard_map/all_gather | solution.py:377
  70.8 0.0 collective-permute-done.rest_1_.rest_5_
  70.8 0.0 copy-done.10
  70.8 0.0 copy-done.8
  70.8 0.0 copy-done
  70.8 0.0 copy-done.9
  70.8 5.5 %partial_logits.2 = (f32[128,128]{1,0:T(8,128)S(1)}, f32[128,128]{1,0:T(8,128)S(1)}) custom-call(s32[2]{0:T(128)S(1)} %copy-done.9, f32[1024]{0:T(1024)S(1)} %copy-done.10, f32[8,256]{1,0:T(8,128)S(1)} %copy-done.8, bf16[2,4,4,8192]{3,2,1,0:T(4,128)(2,1)S(1)} %all_gather.3.refs, bf16[2,16,32768]{2,1,0:T(8,128)(2,1)S(1)} %copy-done, ...), custom_call_target="tpu_custom_call" | custom-call | flops 1073741824 | bytes 1572864 | tf_op jit(solution)/shard_map/partial_logits/pallas_call | solution.py:147
  76.3 0.0 copy-start.17
  76.3 0.0 copy-start.18
  76.3 0.0 copy-start.16
  76.3 0.1 collective-permute-start.1
  76.4 0.0 collective-permute-done.2.rest_0_.rest_6_
  76.4 1.2 collective-permute-done.3.rest_1_.rest_7_
  77.6 5.4 %partial_logits.3 = (f32[128,128]{1,0:T(8,128)S(1)}, f32[128,128]{1,0:T(8,128)S(1)}) custom-call(s32[2]{0:T(128)S(1)} %copy-done.9, f32[1024]{0:T(1024)S(1)} %copy-done.10, f32[8,256]{1,0:T(8,128)S(1)} %copy-done.8, bf16[2,4,4,8192]{3,2,1,0:T(4,128)(2,1)S(1)} %all_gather.3.refs, bf16[2,16,8192]{2,1,0:T(8,128)(2,1)S(1)} %collective-permute-done.2.rest_0_.rest_6_, ...), custom_call_target="tpu_custom_call" | custom-call | flops 1073741824 | bytes 1572864 | tf_op jit(solution)/shard_map/partial_logits/pallas_call | solution.py:147
  83.0 0.2 collective-permute-start.4
  83.2 0.0 collective-permute-done.1
  83.2 1.1 collective-permute-done.4
  84.3 0.0 copy-done.2
  84.4 0.0 copy-start.11
  84.4 1.6 %collective-permute-start.5 = (f32[2,128,128]{2,1,0:T(8,128)S(1)}, f32[2,128,128]{2,1,0:T(8,128)S(1)}, u32[]{:S(2)}, u32[]{:S(2)}) collective-permute-start(f32[2,128,128]{2,1,0:T(8,128)S(1)} %pad_maximum_fusion.here), channel_id=1, source_target_pairs={{0,8},{4,12},{8,0},{12,4},{1,9},{5,13},{9,1},{13,5},{2,10},{6,14},... | collective-permute-start | bytes 393224 | tf_op jit(solution)/shard_map/ppermute | solution.py:375
  86.0 0.0 copy-done.17
  86.0 0.0 copy-done.18
  86.0 0.0 copy-done.16
  86.1 0.1 copy.14
  86.2 0.0 collective-permute-start.11
  86.2 3.9 %collective-permute-done.5.there = f32[2,128,128]{2,1,0:T(8,128)S(1)} collective-permute-done((f32[2,128,128]{2,1,0:T(8,128)S(1)}, f32[2,128,128]{2,1,0:T(8,128)S(1)}, u32[]{:S(2)}, u32[]{:S(2)}) %collective-permute-start.5) | collective-permute-done | bytes 131104 | tf_op jit(solution)/shard_map/ppermute | solution.py:375
  90.1 0.0 copy-done.11
  90.1 0.6 copy-done.12
  90.7 1.8 %logit_stats.1.rest_0_ = f32[32,128]{1,0:T(8,128)} custom-call(f32[2,128,128]{2,1,0:T(8,128)} %copy-done.11, f32[2,128,128]{2,1,0:T(8,128)} %copy-done.12), custom_call_target="tpu_custom_call" | custom-call | flops 131072 | bytes 262144 | tf_op jit(solution)/shard_map/logit_stats/pallas_call | solution.py:196
  92.5 0.7 collective-permute-start.8
  93.2 1.1 collective-permute-start.7
  94.3 0.1 collective-permute-start.6
  94.4 1.7 %collective-permute-start.10 = (f32[16,128]{1,0:T(8,128)S(1)}, f32[16,128]{1,0:T(8,128)S(1)}, u32[]{:S(2)}, u32[]{:S(2)}) collective-permute-start(f32[16,128]{1,0:T(8,128)S(1)} %pad.4.rest_0_.rest_4_), channel_id=1, source_target_pairs={{0,8},{4,12},{8,0},{12,4},{1,9},{5,13},{9,1},{13,5},{2,10},{6,14},... | collective-permute-start | bytes 24584 | tf_op jit(solution)/shard_map/ppermute | solution.py:375
  96.1 0.0 collective-permute-done.11.rest_3_.rest_7_
  96.1 0.0 collective-permute-start.9
  96.1 2.0 %collective-permute-done.10.rest_2_.rest_6_ = f32[16,128]{1,0:T(8,128)S(1)} collective-permute-done((f32[16,128]{1,0:T(8,128)S(1)}, f32[16,128]{1,0:T(8,128)S(1)}, u32[]{:S(2)}, u32[]{:S(2)}) %collective-permute-start.10) | collective-permute-done | bytes 8224 | tf_op jit(solution)/shard_map/ppermute | solution.py:375
  98.1 0.0 collective-permute-done.9.rest_1_.rest_5_
  98.1 1.0 copy-done.3
  99.1 4.4 %aligned_rows.1.rest_8_ = bf16[2,64,8192]{2,1,0:T(8,128)(2,1)S(1)} custom-call(s32[2]{0:T(128)S(1)} %copy-done.9, f32[1024]{0:T(1024)S(1)} %copy-done.10, f32[8,256]{1,0:T(8,128)S(1)} %copy-done.8, f32[16,128]{1,0:T(8,128)S(1)} %pad.4.rest_0_.rest_4_, f32[16,128]{1,0:T(8,128)S(1)} %collective-permute-done.9.rest_1_.rest_5_, ...), custom_call_target="tpu_custom_call" | custom-call | flops 10485760 | bytes 4194304 | tf_op jit(solution)/shard_map/aligned_rows/pallas_call | solution.py:265
  103.5 1.3 %copy-done.1 = bf16[2,64,8192]{2,1,0:T(8,128)(2,1)} copy-done((bf16[2,64,8192]{2,1,0:T(8,128)(2,1)}, bf16[2,64,8192]{2,1,0:T(8,128)(2,1)S(1)}, u32[]{:S(2)}) %copy-start.1) | copy-done | bytes 2097176
  104.9 0.0 collective-permute-done.8.rest_3_
  104.9 0.0 collective-permute-done.7.rest_2_
  104.9 0.0 collective-permute-done.6.rest_1_
  104.9 0.6 copy-done.13
  105.5 0.0 copy-done.14
  105.5 0.6 copy-done.15
  106.1 6.9 %volume_terms.1 = (f32[16,128]{1,0:T(8,128)}, f32[2,4,8192]{2,1,0:T(4,128)}, bf16[2,4,8192]{2,1,0:T(4,128)(2,1)}, bf16[2,4,8192]{2,1,0:T(4,128)(2,1)}, bf16[2,4,8192]{2,1,0:T(4,128)(2,1)}) custom-call(s32[2]{0:T(128)} %pad_add_fusion.ids, f32[32,128]{1,0:T(8,128)} %logit_stats.1.rest_0_, f32[32,128]{1,0:T(8,128)} %copy-done.15, f32[32,128]{1,0:T(8,128)} %copy-done.14, ...), custom_call_target="tpu_custom_call" | custom-call | flops 33554432 | bytes 2621440 | tf_op jit(solution)/shard_map/volume_terms/pallas_call | solution.py:342
  113.0 1.8 %collective-permute-start.12 = (bf16[2,4,8192]{2,1,0:T(4,128)(2,1)}, bf16[2,4,8192]{2,1,0:T(4,128)(2,1)S(1)}, u32[]{:S(2)}, u32[]{:S(2)}) collective-permute-start(bf16[2,4,8192]{2,1,0:T(4,128)(2,1)} %get-tuple-element.23), channel_id=1, source_target_pairs={{0,1},{1,0},{2,3},{3,2},{4,5},{5,4},{6,7},{7,6},{8,9},{9,8},{10,11... | collective-permute-start | bytes 393224 | tf_op jit(solution)/shard_map/ppermute | solution.py:413
  114.8 2.6 %collective-permute-start.13 = (bf16[2,4,8192]{2,1,0:T(4,128)(2,1)}, bf16[2,4,8192]{2,1,0:T(4,128)(2,1)S(1)}, u32[]{:S(2)}, u32[]{:S(2)}) collective-permute-start(bf16[2,4,8192]{2,1,0:T(4,128)(2,1)} %get-tuple-element.24), channel_id=1, source_target_pairs={{0,2},{1,3},{2,0},{3,1},{4,6},{5,7},{6,4},{7,5},{8,10},{9,11},{10,... | collective-permute-start | bytes 393224 | tf_op jit(solution)/shard_map/ppermute | solution.py:413
  117.4 0.1 collective-permute-start.14
  117.4 1.3 %copy.15 = f32[16,4]{0,1:T(4,128)} copy(f32[16,4]{1,0:T(8,128)} %bitcast.9) | data formatting | bytes 512
  118.8 0.9 collective-permute-done.12
  119.6 7.6 %collective-permute-done.13 = bf16[2,4,8192]{2,1,0:T(4,128)(2,1)S(1)} collective-permute-done((bf16[2,4,8192]{2,1,0:T(4,128)(2,1)}, bf16[2,4,8192]{2,1,0:T(4,128)(2,1)S(1)}, u32[]{:S(2)}, u32[]{:S(2)}) %collective-permute-start.13) | collective-permute-done | bytes 131104 | tf_op jit(solution)/shard_map/ppermute | solution.py:413
  127.3 0.0 collective-permute-done.14
  127.3 1.1 add_bitcast_fusion
  128.3 1.0 copy.16
  (23 shorter events, 0.1 us)
Async XLA Ops:
  0.6 70.2 %copy-start.10 = (f32[1024]{0:T(1024)S(1)}, f32[1024]{0:T(1024)}, u32[]{:S(2)}) copy-start(f32[1024]{0:T(1024)} %constant.15.clone.table_y) | copy-start | bytes 12292
  0.6 70.1 %copy-start.8 = (f32[8,256]{1,0:T(8,128)S(1)}, f32[8,256]{1,0:T(8,128)}, u32[]{:S(2)}) copy-start(f32[8,256]{1,0:T(8,128)} %constant.14.clone.table_x) | copy-start | bytes 24580
  0.7 70.1 %copy-start = (bf16[2,16,32768]{2,1,0:T(8,128)(2,1)S(1)}, bf16[2,16,32768]{2,1,0:T(8,128)(2,1)}, u32[]{:S(2)}) copy-start(bf16[2,16,32768]{2,1,0:T(8,128)(2,1)} %rest_4_.1) | copy-start | bytes 6291460
  1.3 69.5 %copy-start.9 = (s32[2]{0:T(128)S(1)}, s32[2]{0:T(128)}, u32[]{:S(2)}) copy-start(s32[2]{0:T(128)} %pad_add_fusion.ids) | copy-start | bytes 28
  50.8 19.9 %collective-permute-start = (bf16[2,16,8192]{2,1,0:T(8,128)(2,1)}, bf16[2,16,8192]{2,1,0:T(8,128)(2,1)S(1)}, u32[]{:S(2)}, u32[]{:S(2)}) collective-permute-start(bf16[2,16,8192]{2,1,0:T(8,128)(2,1)} %get-tuple-element.14), channel_id=1, source_target_pairs={{0,4},{4,0},{8,12},{12,8},{1,5},{5,1},{9,13},{13,9},{2,6},{6,2},{1... | collective-permute-start | bytes 1572872 | tf_op jit(solution)/shard_map/ppermute | solution.py:375
  51.4 25.0 %collective-permute-start.2 = (bf16[2,16,8192]{2,1,0:T(8,128)(2,1)}, bf16[2,16,8192]{2,1,0:T(8,128)(2,1)S(1)}, u32[]{:S(2)}, u32[]{:S(2)}) collective-permute-start(bf16[2,16,8192]{2,1,0:T(8,128)(2,1)} %get-tuple-element.17), channel_id=1, source_target_pairs={{0,8},{4,12},{8,0},{12,4},{1,9},{5,13},{9,1},{13,5},{2,10},{6,14},... | collective-permute-start | bytes 1572872 | tf_op jit(solution)/shard_map/ppermute | solution.py:375
  53.9 23.7 %collective-permute-start.3 = (bf16[2,16,8192]{2,1,0:T(8,128)(2,1)}, bf16[2,16,8192]{2,1,0:T(8,128)(2,1)S(1)}, u32[]{:S(2)}, u32[]{:S(2)}) collective-permute-start(bf16[2,16,8192]{2,1,0:T(8,128)(2,1)} %get-tuple-element.18), channel_id=1, source_target_pairs={{0,12},{4,8},{8,4},{12,0},{1,13},{5,9},{9,5},{13,1},{2,14},{6,10},... | collective-permute-start | bytes 1572872 | tf_op jit(solution)/shard_map/ppermute | solution.py:375
  76.3 9.7 %copy-start.17 = (s32[16,1]{0,1:T(1,128)S(1)}, s32[16,1]{0,1:T(1,128)}, u32[]{:S(2)}) copy-start(s32[16,1]{0,1:T(1,128)} %param.9) | copy-start | bytes 196
  76.3 9.7 %copy-start.18 = (s32[16,1]{0,1:T(1,128)S(1)}, s32[16,1]{0,1:T(1,128)}, u32[]{:S(2)}) copy-start(s32[16,1]{0,1:T(1,128)} %param.10) | copy-start | bytes 196
  76.3 9.7 %copy-start.16 = (f32[16,1]{0,1:T(1,128)S(1)}, f32[16,1]{0,1:T(1,128)}, u32[]{:S(2)}) copy-start(f32[16,1]{0,1:T(1,128)} %param.11) | copy-start | bytes 196
  76.3 6.9 %collective-permute-start.1 = (f32[128,128]{1,0:T(8,128)S(1)}, f32[128,128]{1,0:T(8,128)S(1)}, u32[]{:S(2)}, u32[]{:S(2)}) collective-permute-start(f32[128,128]{1,0:T(8,128)S(1)} %get-tuple-element.16), channel_id=1, source_target_pairs={{0,4},{4,0},{8,12},{12,8},{1,5},{5,1},{9,13},{13,9},{2,6},{6,2},{1... | collective-permute-start | bytes 196616 | tf_op jit(solution)/shard_map/ppermute | solution.py:375
  77.6 6.7 %copy-start.2 = (bf16[2,16,8192]{2,1,0:T(8,128)(2,1)}, bf16[2,16,8192]{2,1,0:T(8,128)(2,1)S(1)}, u32[]{:S(2)}) copy-start(bf16[2,16,8192]{2,1,0:T(8,128)(2,1)S(1)} %collective-permute-done.3.rest_1_.rest_7_) | copy-start | bytes 1572868
  83.0 1.3 %collective-permute-start.4 = (f32[128,128]{1,0:T(8,128)S(1)}, f32[128,128]{1,0:T(8,128)S(1)}, u32[]{:S(2)}, u32[]{:S(2)}) collective-permute-start(f32[128,128]{1,0:T(8,128)S(1)} %get-tuple-element.20), channel_id=1, source_target_pairs={{0,4},{4,0},{8,12},{12,8},{1,5},{5,1},{9,13},{13,9},{2,6},{6,2},{1... | collective-permute-start | bytes 196616 | tf_op jit(solution)/shard_map/ppermute | solution.py:375
  84.4 5.7 %copy-start.11 = (f32[2,128,128]{2,1,0:T(8,128)}, f32[2,128,128]{2,1,0:T(8,128)S(1)}, u32[]{:S(2)}) copy-start(f32[2,128,128]{2,1,0:T(8,128)S(1)} %pad_maximum_fusion.here) | copy-start | bytes 393220
  84.4 5.7 %collective-permute-start.5 = (f32[2,128,128]{2,1,0:T(8,128)S(1)}, f32[2,128,128]{2,1,0:T(8,128)S(1)}, u32[]{:S(2)}, u32[]{:S(2)}) collective-permute-start(f32[2,128,128]{2,1,0:T(8,128)S(1)} %pad_maximum_fusion.here), channel_id=1, source_target_pairs={{0,8},{4,12},{8,0},{12,4},{1,9},{5,13},{9,1},{13,5},{2,10},{6,14},... | collective-permute-start | bytes 393224 | tf_op jit(solution)/shard_map/ppermute | solution.py:375
  86.2 17.3 %copy-start.4 = (f32[16,128]{1,0:T(8,128)}, f32[16,128]{1,0:T(8,128)S(1)}, u32[]{:S(2)}) copy-start(f32[16,128]{1,0:T(8,128)S(1)} %pad.4.rest_0_.rest_4_) | copy-start | bytes 24580
  86.2 9.9 %collective-permute-start.11 = (f32[16,128]{1,0:T(8,128)S(1)}, f32[16,128]{1,0:T(8,128)S(1)}, u32[]{:S(2)}, u32[]{:S(2)}) collective-permute-start(f32[16,128]{1,0:T(8,128)S(1)} %pad.4.rest_0_.rest_4_), channel_id=1, source_target_pairs={{0,12},{4,8},{8,4},{12,0},{1,13},{5,9},{9,5},{13,1},{2,14},{6,10},... | collective-permute-start | bytes 24584 | tf_op jit(solution)/shard_map/ppermute | solution.py:375
  90.1 0.6 copy-start.12
  92.5 12.4 %collective-permute-start.8 = (f32[32,128]{1,0:T(8,128)}, f32[32,128]{1,0:T(8,128)S(1)}, u32[]{:S(2)}, u32[]{:S(2)}) collective-permute-start(f32[32,128]{1,0:T(8,128)} %logit_stats.1.rest_0_), channel_id=1, source_target_pairs={{0,20},{4,16},{8,28},{12,24},{16,4},{20,0},{24,12},{28,8},{1,21},{... | collective-permute-start | bytes 49160 | tf_op jit(solution)/shard_map/ppermute | solution.py:407
  93.2 11.7 %collective-permute-start.7 = (f32[32,128]{1,0:T(8,128)}, f32[32,128]{1,0:T(8,128)S(1)}, u32[]{:S(2)}, u32[]{:S(2)}) collective-permute-start(f32[32,128]{1,0:T(8,128)} %logit_stats.1.rest_0_), channel_id=1, source_target_pairs={{0,16},{4,20},{8,24},{12,28},{16,0},{20,4},{24,8},{28,12},{1,17},{... | collective-permute-start | bytes 49160 | tf_op jit(solution)/shard_map/ppermute | solution.py:406
  94.3 10.6 %collective-permute-start.6 = (f32[32,128]{1,0:T(8,128)}, f32[32,128]{1,0:T(8,128)S(1)}, u32[]{:S(2)}, u32[]{:S(2)}) collective-permute-start(f32[32,128]{1,0:T(8,128)} %logit_stats.1.rest_0_), channel_id=1, source_target_pairs={{0,4},{4,0},{8,12},{12,8},{1,5},{5,1},{9,13},{13,9},{2,6},{6,2},{1... | collective-permute-start | bytes 49160 | tf_op jit(solution)/shard_map/ppermute | solution.py:375
  94.4 3.7 %collective-permute-start.10 = (f32[16,128]{1,0:T(8,128)S(1)}, f32[16,128]{1,0:T(8,128)S(1)}, u32[]{:S(2)}, u32[]{:S(2)}) collective-permute-start(f32[16,128]{1,0:T(8,128)S(1)} %pad.4.rest_0_.rest_4_), channel_id=1, source_target_pairs={{0,8},{4,12},{8,0},{12,4},{1,9},{5,13},{9,1},{13,5},{2,10},{6,14},... | collective-permute-start | bytes 24584 | tf_op jit(solution)/shard_map/ppermute | solution.py:375
  96.1 7.4 %copy-start.5 = (f32[16,128]{1,0:T(8,128)}, f32[16,128]{1,0:T(8,128)S(1)}, u32[]{:S(2)}) copy-start(f32[16,128]{1,0:T(8,128)S(1)} %collective-permute-done.11.rest_3_.rest_7_) | copy-start | bytes 24580
  96.1 2.0 %collective-permute-start.9 = (f32[16,128]{1,0:T(8,128)S(1)}, f32[16,128]{1,0:T(8,128)S(1)}, u32[]{:S(2)}, u32[]{:S(2)}) collective-permute-start(f32[16,128]{1,0:T(8,128)S(1)} %pad.4.rest_0_.rest_4_), channel_id=1, source_target_pairs={{0,4},{4,0},{8,12},{12,8},{1,5},{5,1},{9,13},{13,9},{2,6},{6,2},{1... | collective-permute-start | bytes 24584 | tf_op jit(solution)/shard_map/ppermute | solution.py:375
  98.1 5.4 %copy-start.6 = (f32[16,128]{1,0:T(8,128)}, f32[16,128]{1,0:T(8,128)S(1)}, u32[]{:S(2)}) copy-start(f32[16,128]{1,0:T(8,128)S(1)} %collective-permute-done.10.rest_2_.rest_6_) | copy-start | bytes 24580
  98.1 1.0 copy-start.3
  99.1 4.4 %copy-start.7 = (f32[16,128]{1,0:T(8,128)}, f32[16,128]{1,0:T(8,128)S(1)}, u32[]{:S(2)}) copy-start(f32[16,128]{1,0:T(8,128)S(1)} %collective-permute-done.9.rest_1_.rest_5_) | copy-start | bytes 24580
  103.5 1.4 %copy-start.1 = (bf16[2,64,8192]{2,1,0:T(8,128)(2,1)}, bf16[2,64,8192]{2,1,0:T(8,128)(2,1)S(1)}, u32[]{:S(2)}) copy-start(bf16[2,64,8192]{2,1,0:T(8,128)(2,1)S(1)} %aligned_rows.1.rest_8_) | copy-start | bytes 6291460
  104.9 0.6 copy-start.13
  104.9 0.6 copy-start.14
  105.5 0.6 copy-start.15
  113.0 6.7 %collective-permute-start.12 = (bf16[2,4,8192]{2,1,0:T(4,128)(2,1)}, bf16[2,4,8192]{2,1,0:T(4,128)(2,1)S(1)}, u32[]{:S(2)}, u32[]{:S(2)}) collective-permute-start(bf16[2,4,8192]{2,1,0:T(4,128)(2,1)} %get-tuple-element.23), channel_id=1, source_target_pairs={{0,1},{1,0},{2,3},{3,2},{4,5},{5,4},{6,7},{7,6},{8,9},{9,8},{10,11... | collective-permute-start | bytes 393224 | tf_op jit(solution)/shard_map/ppermute | solution.py:413
  114.8 12.5 %collective-permute-start.13 = (bf16[2,4,8192]{2,1,0:T(4,128)(2,1)}, bf16[2,4,8192]{2,1,0:T(4,128)(2,1)S(1)}, u32[]{:S(2)}, u32[]{:S(2)}) collective-permute-start(bf16[2,4,8192]{2,1,0:T(4,128)(2,1)} %get-tuple-element.24), channel_id=1, source_target_pairs={{0,2},{1,3},{2,0},{3,1},{4,6},{5,7},{6,4},{7,5},{8,10},{9,11},{10,... | collective-permute-start | bytes 393224 | tf_op jit(solution)/shard_map/ppermute | solution.py:413
  117.4 9.9 %collective-permute-start.14 = (bf16[2,4,8192]{2,1,0:T(4,128)(2,1)}, bf16[2,4,8192]{2,1,0:T(4,128)(2,1)S(1)}, u32[]{:S(2)}, u32[]{:S(2)}) collective-permute-start(bf16[2,4,8192]{2,1,0:T(4,128)(2,1)} %get-tuple-element.25), channel_id=1, source_target_pairs={{0,3},{1,2},{2,1},{3,0},{4,7},{5,6},{6,5},{7,4},{8,11},{9,10},{10,... | collective-permute-start | bytes 393224 | tf_op jit(solution)/shard_map/ppermute | solution.py:413

commit v2 on v1

--- a/solution.py
+++ b/solution.py
@@ -14,6 +14,7 @@
 TY = 8
 HALF = TX // 2
 LANES = 128
+VMEM_BYTES = 24 * 1024 * 1024
 BF = jnp.bfloat16
 F32 = jnp.float32
 
@@ -27,59 +28,83 @@
     return table_x, table_y.reshape(-1)
 
 
+def chunk_of(width):
+    return min(width, 8 * IMG)
+
+
 def xor_pairs(size, step):
     return [(i, i ^ step) for i in range(size)]
 
 
-def bands_kernel(ids, images, *rest):
-    outs, sems = rest[:-1], rest[-1]
-    width = outs[0].shape[2]
-    copies = []
-    for place, out in enumerate(outs):
-        band = ids[0] ^ (place + 1)
-        start = pl.multiple_of(band * width, width)
-        copies.append(
-            pltpu.make_async_copy(images.at[:, :, pl.ds(start, width)], out, sems.at[place])
-        )
-    for copy in copies:
-        copy.start()
-    for copy in copies:
-        copy.wait()
+def bands_kernel(ids, *refs):
+    half = len(refs) // 2
+    for source, target in zip(refs[:half], refs[half:]):
+        target[...] = source[...]
 
 
 def image_bands(ids, images, dom):
     parts, rows, pixels = images.shape
     width = pixels // dom
+    chunk = min(width, 16 * IMG)
+    count = width // chunk
+
+    def spec(step):
+        return pl.BlockSpec(
+            (parts, rows, chunk), lambda i, s: (0, 0, (s[0] ^ step) * count + i)
+        )
+
     return pl.pallas_call(
         bands_kernel,
         out_shape=[jax.ShapeDtypeStruct((parts, rows, width), images.dtype)] * (dom - 1),
-        in_specs=[pl.BlockSpec(memory_space=pltpu.SMEM), pl.BlockSpec(memory_space=pl.ANY)],
-        out_specs=[pl.BlockSpec(memory_space=pl.ANY)] * (dom - 1),
-        scratch_shapes=[pltpu.SemaphoreType.DMA((dom - 1,))],
+        grid_spec=pltpu.PrefetchScalarGridSpec(
+            num_scalar_prefetch=1,
+            grid=(count,),
+            in_specs=[spec(step) for step in range(1, dom)],
+            out_specs=[pl.BlockSpec((parts, rows, chunk), lambda i, s: (0, 0, i))] * (dom - 1),
+        ),
+        compiler_params=pltpu.CompilerParams(vmem_limit_bytes=VMEM_BYTES),
+        cost_estimate=pl.CostEstimate(
+            flops=0, bytes_accessed=4 * parts * rows * (pixels - width), transcendentals=0
+        ),
         name="image_bands",
-    )(ids, images)
-
-
-def logits_kernel(groups, ids, table_y, table_x, refs, *rest):
+    )(ids, *([images] * (dom - 1)))
+
+
+def logits_kernel(groups, orients, span, ids, table_y, table_x, *rest):
+    shards, rest = rest[:orients], rest[orients:]
     images, outs = rest[:groups], rest[groups : 2 * groups]
-    left, right = rest[2 * groups :]
+    refs, buffers = rest[2 * groups], rest[2 * groups + 1 :]
     step = pl.program_id(0)
     chunk = refs.shape[3]
     rows = images[0].shape[1]
     group_rows = TX * rows
     names = refs.shape[1] * refs.shape[2]
     lines = chunk // IMG
-    line_base = (ids[0] * pl.num_programs(0) + step) * lines
+    line_base = (ids[0] * orients + (ids[1] ^ step)) * lines
+    for place, shard in enumerate(shards):
+
+        @pl.when(step == place)
+        def _():
+            refs[...] = shard[...]
+
+    @pl.when(step == 0)
+    def _():
+        for out in outs:
+            out[...] = jnp.zeros_like(out)
+
     for line in range(lines):
+        left, right = buffers[2 * (line // span % 2) : 2 * (line // span % 2) + 2]
         cols = slice(line * IMG, (line + 1) * IMG)
-        cols_im = slice(chunk + line * IMG, chunk + (line + 1) * IMG)
+        place = line % span
+        to_re = slice(2 * place * IMG, (2 * place + 1) * IMG)
+        to_im = slice((2 * place + 1) * IMG, (2 * place + 2) * IMG)
         base = (line_base + line) * TY
         ref_re = refs[0, :, :, cols].astype(F32).reshape(names, IMG)
         ref_im = refs[1, :, :, cols].astype(F32).reshape(names, IMG)
 
         def put_ref(b, re, im):
-            right[b * names : (b + 1) * names, cols] = re.astype(BF)
-            right[b * names : (b + 1) * names, cols_im] = im.astype(BF)
+            right[b * names : (b + 1) * names, to_re] = re.astype(BF)
+            right[b * names : (b + 1) * names, to_im] = im.astype(BF)
 
         put_ref(TY // 2, ref_re, ref_im)
         for t in range(1, HALF + 1):
@@ -96,8 +121,8 @@
 
             def put(a, re, im):
                 top = g * group_rows + a * rows
-                left[top : top + rows, cols] = re.astype(BF)
-                left[top : top + rows, cols_im] = im.astype(BF)
+                left[top : top + rows, to_re] = re.astype(BF)
+                left[top : top + rows, to_im] = im.astype(BF)
 
             put(TX // 2, re, im)
             for t in range(1, HALF + 1):
@@ -108,44 +133,36 @@
                 put(TX // 2 - t, re_c + im_s, im_c - re_s)
                 if t < HALF:
                     put(TX // 2 + t, re_c - im_s, re_s + im_c)
-    value = lax.dot_general(
-        left[...], right[...], (((1,), (1,)), ((), ())), preferred_element_type=F32
-    )
-
-    @pl.when(step == 0)
-    def _():
-        for g in range(groups):
-            outs[g][...] = value[g * group_rows : (g + 1) * group_rows]
-
-    @pl.when(step > 0)
-    def _():
-        for g in range(groups):
-            outs[g][...] += value[g * group_rows : (g + 1) * group_rows]
-
-
-def chunk_of(width):
-    return min(width, 4 * IMG)
-
-
-def partial_logits(ids, table_x, table_y, refs, own, others):
-    parts, classes, orients, width = refs.shape
-    chunk = chunk_of(width)
-    count = width // chunk
+        if place == span - 1:
+            value = lax.dot_general(
+                left[...], right[...], (((1,), (1,)), ((), ())), preferred_element_type=F32
+            )
+            for g in range(groups):
+                outs[g][...] += value[g * group_rows : (g + 1) * group_rows]
+
+
+def partial_logits(ids, table_x, table_y, shards, own, others):
+    parts, classes, orients, chunk = shards[0].shape
     arrays = ([own] if own is not None else []) + list(others)
     groups = len(arrays)
     rows = arrays[0].shape[1]
     names = classes * orients
+    count = len(shards)
+    lines = chunk // IMG
+    span = 2 if lines % 4 == 0 else 1
     specs = []
     for array in arrays:
         if array is own:
             specs.append(
-                pl.BlockSpec((parts, rows, chunk), lambda i, s: (0, 0, s[0] * count + i))
+                pl.BlockSpec(
+                    (parts, rows, chunk), lambda i, s: (0, 0, s[0] * count + (s[1] ^ i))
+                )
             )
         else:
-            specs.append(pl.BlockSpec((parts, rows, chunk), lambda i, s: (0, 0, i)))
+            specs.append(pl.BlockSpec((parts, rows, chunk), lambda i, s: (0, 0, s[1] ^ i)))
     out_shape = (TX * rows, TY * names)
     return pl.pallas_call(
-        functools.partial(logits_kernel, groups),
+        functools.partial(logits_kernel, groups, count, span),
         out_shape=[jax.ShapeDtypeStruct(out_shape, F32)] * groups,
         grid_spec=pltpu.PrefetchScalarGridSpec(
             num_scalar_prefetch=1,
@@ -153,23 +170,25 @@
             in_specs=[
                 pl.BlockSpec(memory_space=pltpu.SMEM),
                 pl.BlockSpec((TX, IMG), lambda i, s: (0, 0)),
-                pl.BlockSpec((parts, classes, orients, chunk), lambda i, s: (0, 0, 0, i)),
             ]
+            + [pl.BlockSpec(shards[0].shape, lambda i, s: (0, 0, 0, 0))] * count
             + specs,
             out_specs=[pl.BlockSpec(out_shape, lambda i, s: (0, 0))] * groups,
-            scratch_shapes=[
-                pltpu.VMEM((groups * TX * rows, 2 * chunk), BF),
-                pltpu.VMEM((TY * names, 2 * chunk), BF),
-            ],
-        ),
-        compiler_params=pltpu.CompilerParams(vmem_limit_bytes=32 * 1024 * 1024),
+            scratch_shapes=[pltpu.VMEM(shards[0].shape, BF)]
+            + [
+                pltpu.VMEM((groups * TX * rows, 2 * span * IMG), BF),
+                pltpu.VMEM((TY * names, 2 * span * IMG), BF),
+            ]
+            * 2,
+        ),
+        compiler_params=pltpu.CompilerParams(vmem_limit_bytes=VMEM_BYTES),
         cost_estimate=pl.CostEstimate(
-            flops=2 * groups * TX * rows * TY * names * 2 * width,
-            bytes_accessed=2 * 2 * width * (groups * rows + names),
+            flops=4 * groups * TX * rows * TY * names * count * chunk,
+            bytes_accessed=4 * count * chunk * (groups * rows + names),
             transcendentals=0,
         ),
         name="partial_logits",
-    )(ids, table_y, table_x, refs, *arrays)
+    )(ids, table_y, table_x, *shards, *arrays)
 
 
 def stats_kernel(swap, classes, orients, here, there, out):
@@ -196,6 +215,7 @@
     return pl.pallas_call(
         functools.partial(stats_kernel, swap, classes, orients),
         out_shape=jax.ShapeDtypeStruct((groups * group_rows // TX, LANES), F32),
+        compiler_params=pltpu.CompilerParams(vmem_limit_bytes=VMEM_BYTES),
         cost_estimate=pl.CostEstimate(
             flops=4 * here.size, bytes_accessed=8 * here.size, transcendentals=here.size
         ),
@@ -256,12 +276,20 @@
                 out[1, own, cols] = (re * sine + im * cosine).astype(BF)
 
 
-def aligned_rows(ids, table_x, table_y, metas, own, others, dom):
-    parts, rows, pixels = own.shape
-    width = pixels // dom
+def aligned_rows(ids, table_x, table_y, metas, own, others, width):
+    arrays = ([own] if own is not None else []) + list(others)
+    parts, rows = arrays[0].shape[:2]
     chunk = chunk_of(width)
     count = width // chunk
     groups = len(metas)
+    specs = []
+    for array in arrays:
+        if array is own:
+            specs.append(
+                pl.BlockSpec((parts, rows, chunk), lambda i, s: (0, 0, s[0] * count + i))
+            )
+        else:
+            specs.append(pl.BlockSpec((parts, rows, chunk), lambda i, s: (0, 0, i)))
     return pl.pallas_call(
         functools.partial(rows_kernel, groups),
         out_shape=jax.ShapeDtypeStruct((parts, groups * rows, width), BF),
@@ -273,28 +301,27 @@
                 pl.BlockSpec((TX, IMG), lambda i, s: (0, 0)),
             ]
             + [pl.BlockSpec((rows, LANES), lambda i, s: (0, 0))] * groups
-            + [pl.BlockSpec((parts, rows, chunk), lambda i, s: (0, 0, s[0] * count + i))]
-            + [pl.BlockSpec((parts, rows, chunk), lambda i, s: (0, 0, i))] * (groups - 1),
+            + specs,
             out_specs=pl.BlockSpec((parts, groups * rows, chunk), lambda i, s: (0, 0, i)),
             scratch_shapes=[
                 pltpu.VMEM((groups * rows, IMG), F32),
                 pltpu.VMEM((groups * rows, IMG), F32),
             ],
         ),
-        compiler_params=pltpu.CompilerParams(vmem_limit_bytes=32 * 1024 * 1024),
+        compiler_params=pltpu.CompilerParams(vmem_limit_bytes=VMEM_BYTES),
         cost_estimate=pl.CostEstimate(
             flops=20 * groups * rows * width,
             bytes_accessed=8 * groups * rows * width,
             transcendentals=0,
         ),
         name="aligned_rows",
-    )(ids, table_y, table_x, *metas, own, *others)
+    )(ids, table_y, table_x, *metas, *arrays)
 
 
 def volume_kernel(groups, orients, classes, ids, *rest):
     stats, metas = rest[:4], rest[4 : 4 + groups]
-    aligned = rest[4 + groups]
-    prob, outs, mix = rest[5 + groups], rest[6 + groups : -1], rest[-1]
+    near, far = rest[4 + groups], rest[5 + groups]
+    prob, outs, mixes = rest[6 + groups], rest[7 + groups : -2], rest[-2:]
     step = pl.program_id(0)
     rows = metas[0].shape[0]
 
@@ -303,38 +330,41 @@
         lane = lax.broadcasted_iota(jnp.int32, (rows, LANES), 1)
         pieces = []
         for g in range(groups):
-            near, far = (stats[0], stats[2]) if g % 2 == 0 else (stats[1], stats[3])
+            mine, other = (stats[0], stats[2]) if g % 2 == 0 else (stats[1], stats[3])
             place = g // 2
-            near = near[place * rows : (place + 1) * rows, :]
-            far = far[place * rows : (place + 1) * rows, :]
-            top = jnp.maximum(near[:, 0:1], far[:, 0:1])
-            near_scale = jnp.exp(near[:, 0:1] - top)
-            far_scale = jnp.exp(far[:, 0:1] - top)
+            mine = mine[place * rows : (place + 1) * rows, :]
+            other = other[place * rows : (place + 1) * rows, :]
+            top = jnp.maximum(mine[:, 0:1], other[:, 0:1])
+            mine_scale = jnp.exp(mine[:, 0:1] - top)
+            other_scale = jnp.exp(other[:, 0:1] - top)
             held = (lane >= 1) & (lane <= classes)
-            both = jnp.where(held, near * near_scale + far * far_scale, 0.0)
+            both = jnp.where(held, mine * mine_scale + other * other_scale, 0.0)
             totals = jnp.sum(both, axis=1, keepdims=True)
             spread = jnp.zeros((rows, LANES), F32)
             for k in range(classes):
-                spread = jnp.where(lane % classes == k, near[:, k + 1 : k + 2], spread)
-            class_prob = spread * near_scale / totals
+                spread = jnp.where(lane % classes == k, mine[:, k + 1 : k + 2], spread)
+            class_prob = spread * mine_scale / totals
             if g == 0:
                 prob[...] = class_prob
             weight = (metas[g][:, 2:3] * class_prob).astype(BF).astype(F32)
             bin_of = metas[g][:, 0:1].astype(jnp.int32) ^ ids[1]
             pieces.append(jnp.where(lane // classes == bin_of, weight, 0.0))
-        mixing = jnp.concatenate(pieces, axis=0)
-        mix[...] = jnp.transpose(mixing)[: orients * classes].astype(BF)
+        for mix, held in zip(mixes, (pieces[:2], pieces[2:])):
+            mixing = jnp.concatenate(held, axis=0)
+            mix[...] = jnp.transpose(mixing)[: orients * classes].astype(BF)
 
     for part in range(2):
-        value = jnp.dot(mix[...], aligned[part], preferred_element_type=F32)
+        value = jnp.dot(mixes[0][...], near[part], preferred_element_type=F32)
+        value += jnp.dot(mixes[1][...], far[part], preferred_element_type=F32)
         for o in range(orients):
             outs[o][part] = value[o * classes : (o + 1) * classes].astype(outs[o].dtype)
 
 
-def volume_terms(ids, stats, metas, aligned, orients, classes):
-    parts, entries, width = aligned.shape
+def volume_terms(ids, stats, metas, near, far, orients, classes):
+    parts, entries, width = near.shape
+    rest = far.shape[1]
     groups = len(metas)
-    rows = entries // groups
+    rows = metas[0].shape[0]
     chunk = chunk_of(width)
     count = width // chunk
     out_shape = (parts, classes, width)
@@ -351,18 +381,45 @@
             grid=(count,),
             in_specs=[pl.BlockSpec(stats[0].shape, fixed)] * 4
             + [pl.BlockSpec((rows, LANES), fixed)] * groups
-            + [pl.BlockSpec((parts, entries, chunk), lambda i, s: (0, 0, i))],
+            + [
+                pl.BlockSpec((parts, entries, chunk), lambda i, s: (0, 0, i)),
+                pl.BlockSpec((parts, rest, chunk), lambda i, s: (0, 0, i)),
+            ],
             out_specs=[pl.BlockSpec((rows, LANES), fixed)]
             + [pl.BlockSpec((parts, classes, chunk), lambda i, s: (0, 0, i))] * orients,
-            scratch_shapes=[pltpu.VMEM((orients * classes, entries), BF)],
-        ),
+            scratch_shapes=[
+                pltpu.VMEM((orients * classes, entries), BF),
+                pltpu.VMEM((orients * classes, rest), BF),
+            ],
+        ),
+        compiler_params=pltpu.CompilerParams(vmem_limit_bytes=VMEM_BYTES),
         cost_estimate=pl.CostEstimate(
-            flops=4 * orients * classes * entries * width,
-            bytes_accessed=4 * entries * width + 4 * orients * classes * width,
+            flops=4 * orients * classes * (entries + rest) * width,
+            bytes_accessed=4 * (entries + rest) * width + 4 * orients * classes * width,
             transcendentals=0,
         ),
         name="volume_terms",
-    )(ids, *stats, *metas, aligned)
+    )(ids, *stats, *metas, near, far)
+
+
+def total_kernel(first, *rest):
+    out = rest[-1]
+    total = first[...]
+    for term in rest[:-1]:
+        total = total + term[...].astype(F32)
+    for part in range(out.shape[0]):
+        for k in range(out.shape[1]):
+            out[part, k] = total[part, k : k + 1]
+
+
+def total_volume(terms):
+    parts, classes, width = terms[0].shape
+    return pl.pallas_call(
+        total_kernel,
+        out_shape=jax.ShapeDtypeStruct((parts, classes, 1, width), F32),
+        compiler_params=pltpu.CompilerParams(vmem_limit_bytes=VMEM_BYTES),
+        name="total_volume",
+    )(*terms)
 
 
 def local(dom, orient, cls, references, images, orient_lists, shift_ids, fixed_weights):
@@ -374,17 +431,23 @@
     def swap_dom(array, step):
         return lax.ppermute(array, "dom", xor_pairs(dom, step))
 
-    refs = lax.all_gather(references, "orient", axis=3, tiled=True)
+    def swap_orient(array, step):
+        return lax.ppermute(array, "orient", xor_pairs(orient, step))
+
     bands = image_bands(ids, images, dom)
     others = [swap_dom(band, step + 1) for step, band in enumerate(bands)]
+    shards = [references] + [swap_orient(references, step) for step in range(1, orient)]
     meta = jnp.concatenate(
         [orient_lists.astype(F32), shift_ids.astype(F32), fixed_weights], axis=1
     )
     meta = jnp.pad(meta, ((0, 0), (0, LANES - meta.shape[1])))
     metas = [meta] + [swap_dom(meta, step) for step in range(1, dom)]
 
-    near = partial_logits(ids, table_x, table_y, refs, images, others[:1])
-    far = partial_logits(ids, table_x, table_y, refs, None, others[1:])
+    width = images.shape[2] // dom
+    aligned_near = aligned_rows(ids, table_x, table_y, metas[:2], images, others[:1], width)
+    shards[-1], aligned_near = lax.optimization_barrier((shards[-1], aligned_near))
+    near = partial_logits(ids, table_x, table_y, shards, images, others[:1])
+    far = partial_logits(ids, table_x, table_y, shards, None, others[1:])
     partial = list(near) + list(far)
     kept = [partial[s] + swap_dom(partial[s ^ 1], 1) for s in range(0, dom, 2)]
     here = jnp.stack(kept)
@@ -396,6 +459,8 @@
             order = np.arange(dom // 2) ^ swap
             here = here + jnp.stack([there[i] for i in order])
         step *= 2
+    aligned_far = aligned_rows(ids, table_x, table_y, metas[2:], None, others[1:], width)
+    there, aligned_far = lax.optimization_barrier((there, aligned_far))
     stats = logit_stats(here, there, swap, classes, orients)
 
     pairs = [(i, i ^ dom) for i in range(cls * dom)]
@@ -406,12 +471,11 @@
         lax.ppermute(stats, ("cls", "dom"), pairs),
         lax.ppermute(stats, ("cls", "dom"), cross),
     ]
-    aligned = aligned_rows(ids, table_x, table_y, metas, images, others, dom)
-    prob, *terms = volume_terms(ids, stats_all, metas, aligned, orients, classes)
-    volume = terms[0]
-    for o in range(1, orients):
-        volume = volume + lax.ppermute(terms[o], "orient", xor_pairs(orient, o)).astype(F32)
-    return prob[:, :classes], volume[:, :, None, :]
+    prob, *terms = volume_terms(
+        ids, stats_all, metas, aligned_near, aligned_far, orients, classes
+    )
+    terms = [terms[0]] + [swap_orient(terms[o], o) for o in range(1, orients)]
+    return prob[:, :classes], total_volume(terms)
 
 
 def solution(mesh):

time: 130 us -> 68.6 us (0.53)
  Pallas kernels: 73.5 us -> 21 us
  blocking collectives: 16.8 us -> 0 us
  waiting for transfers between devices: 16.7 us -> 25.9 us
  starting transfers between devices: 13.1 us -> 18.2 us
  local copies, waits for them, and re-layouts: 6.69 us -> 2.37 us
  other arithmetic: 1.7 us -> 0.12 us
    pallas_call x1, Pallas kernels: 49.6 us -> 1.96 us  [image_bands(): pl.pallas_call(bands_kernel, out_shape=[jax.ShapeDtypeStruct((parts, rows...]
    all_gather x1 -> x0, blocking collectives: 16.8 us -> none  [local(): refs = lax.all_gather(references, 'orient', axis=3, tiled=True)]
    ppermute x3 -> x6, waiting for transfers between devices: 8.48 us -> 15.8 us  [swap_orient(): return lax.ppermute(array, 'orient', xor_pairs(orient, step))]
    ppermute x3 -> x6, starting transfers between devices: 4.45 us -> 9.9 us  [swap_orient(): return lax.ppermute(array, 'orient', xor_pairs(orient, step))]
    pallas_call x1, Pallas kernels: 6.91 us -> 2.13 us  [volume_terms(): pl.pallas_call(functools.partial(volume_kernel, groups, orients, classes)...]
    unnamed x40 -> x17, local copies, waits for them, and re-layouts: 6.6 us -> 2.27 us
    ppermute x1, waiting for transfers between devices: 0.01 us -> 1.96 us  [local(): lax.ppermute(stats, ('cls', 'dom'), pairs)]
    pallas_call x1 -> x2, Pallas kernels: 4.37 us -> 6.3 us  [aligned_rows(): pl.pallas_call(functools.partial(rows_kernel, groups), out_shape=jax.Shap...]
  transfers between devices with their start and end apart: 15 -> 18, of which waited for: 6 -> 9; matrix products, arithmetic and copies ran while one was open for 1% -> 1% of each run, Pallas kernels for 13% -> 23%
where the time goes in v2:
time: 68.6 us; the launch traced here: 68.4 us
  waiting for transfers between devices  25.9 us (38%)
  Pallas kernels  21 us (31%)
  starting transfers between devices  18.2 us (27%)
  local copies, waits for them, and re-layouts  2.37 us (3%)
  between operations  0.8 us (1%)
    ppermute x6, waiting for transfers between devices, swap_orient(): return lax.ppermute(array, 'orient', xor_pairs(orient, step))  15.8 us
    ppermute x6, starting transfers between devices, swap_orient(): return lax.ppermute(array, 'orient', xor_pairs(orient, step))  9.9 us
    pallas_call x2, Pallas kernels, partial_logits(): pl.pallas_call(functools.partial(logits_kernel, groups, count, span), out...  9.64 us
    ppermute x10, waiting for transfers between devices, swap_dom(): return lax.ppermute(array, 'dom', xor_pairs(dom, step))  7.05 us
    ppermute x10, starting transfers between devices, swap_dom(): return lax.ppermute(array, 'dom', xor_pairs(dom, step))  6.5 us
    pallas_call x2, Pallas kernels, aligned_rows(): pl.pallas_call(functools.partial(rows_kernel, groups), out_shape=jax.Shap...  6.3 us
    unnamed x17, local copies, waits for them, and re-layouts  2.27 us
    pallas_call x1, Pallas kernels, volume_terms(): pl.pallas_call(functools.partial(volume_kernel, groups, orients, classes)...  2.13 us
  transfers between devices with their start and end apart: 18, of which 9 were waited for; matrix products, arithmetic and copies ran while one was open for 1% of the time, Pallas kernels for 23%

profile of v2, /device:TPU:0, one launch (start us, length us, event | category | flops | bytes accessed | tf_op | source)
XLA Modules:
  0.0 68.4 jit_solution(15064470192341048699)
XLA Ops:
  0.6 0.1 pad_add_fusion.ids
  0.7 0.0 copy-start
  0.7 1.6 %copy-done = bf16[2,16,32768]{2,1,0:T(8,128)(2,1)S(1)} copy-done((bf16[2,16,32768]{2,1,0:T(8,128)(2,1)S(1)}, bf16[2,16,32768]{2,1,0:T(8,128)(2,1)}, u32[]{:S(2)}) %copy-start) | copy-done | bytes 2097176
  2.3 0.0 copy-start.6
  2.3 0.0 copy-start.7
  2.3 0.0 copy-start.5
  2.3 0.0 copy-start.4
  2.3 0.0 copy-start.1
  2.3 0.0 copy-start.2
  2.3 0.0 copy-start.3
  2.3 2.0 %image_bands.1 = (bf16[2,16,8192]{2,1,0:T(8,128)(2,1)}, bf16[2,16,8192]{2,1,0:T(8,128)(2,1)}, bf16[2,16,8192]{2,1,0:T(8,128)(2,1)}) custom-call(s32[2]{0:T(128)S(1)} %pad_add_fusion.ids, bf16[2,16,32768]{2,1,0:T(8,128)(2,1)S(1)} %copy-done, bf16[2,16,32768]{2,1,0:T(8,128)(2,1)S(1)} %copy-done, bf16[2,16,32768]{2,1,0:T(8,128)(2,1)S(1)} %copy-done), custom_call_target="tpu_custom_call" | custom-call | bytes 3145728 | tf_op jit(solution)/shard_map/image_bands/pallas_call | solution.py:56
  4.3 0.5 collective-permute-start.4
  4.8 2.5 %collective-permute-start.6 = (bf16[2,16,8192]{2,1,0:T(8,128)(2,1)}, bf16[2,16,8192]{2,1,0:T(8,128)(2,1)S(1)}, u32[]{:S(2)}, u32[]{:S(2)}) collective-permute-start(bf16[2,16,8192]{2,1,0:T(8,128)(2,1)} %get-tuple-element.22), channel_id=1, source_target_pairs={{0,8},{4,12},{8,0},{12,4},{1,9},{5,13},{9,1},{13,5},{2,10},{6,14},... | collective-permute-start | bytes 1572872 | tf_op jit(solution)/shard_map/ppermute | solution.py:432
  7.2 0.1 collective-permute-start.7
  7.4 0.0 copy-done.6
  7.4 0.0 copy-done.7
  7.4 0.0 copy-done.5
  7.4 0.1 copy.13
  7.5 0.1 collective-permute-start.3
  7.6 0.0 copy-done.4
  7.6 4.0 %collective-permute-start.2 = (bf16[2,4,4,2048]{3,2,1,0:T(4,128)(2,1)S(1)}, bf16[2,4,4,2048]{3,2,1,0:T(4,128)(2,1)S(1)}, u32[]{:S(2)}, u32[]{:S(2)}) collective-permute-start(bf16[2,4,4,2048]{3,2,1,0:T(4,128)(2,1)S(1)} %copy-done.4), channel_id=1, source_target_pairs={{0,3},{1,2},{2,1},{3,0},{4,7},{5,6},{6,5},{7,4},{8,11},{9,10},{10,... | collective-permute-start | bytes 393224 | tf_op jit(solution)/shard_map/ppermute | solution.py:435
  11.6 0.0 collective-permute-done.3.rest_1_.rest_5_
  11.6 0.0 collective-permute-start
  11.6 0.0 collective-permute-done.4.rest_3_.rest_5_
  11.6 1.4 %collective-permute-start.1 = (bf16[2,4,4,2048]{3,2,1,0:T(4,128)(2,1)S(1)}, bf16[2,4,4,2048]{3,2,1,0:T(4,128)(2,1)S(1)}, u32[]{:S(2)}, u32[]{:S(2)}) collective-permute-start(bf16[2,4,4,2048]{3,2,1,0:T(4,128)(2,1)S(1)} %copy-done.4), channel_id=1, source_target_pairs={{0,2},{1,3},{2,0},{3,1},{4,6},{5,7},{6,4},{7,5},{8,10},{9,11},{10,... | collective-permute-start | bytes 393224 | tf_op jit(solution)/shard_map/ppermute | solution.py:435
  13.1 0.0 copy-done.1
  13.1 0.0 copy-done.2
  13.1 0.0 copy-done.3
  13.1 3.6 %aligned_rows.2.rest_8_ = bf16[2,32,8192]{2,1,0:T(8,128)(2,1)S(1)} custom-call(s32[2]{0:T(128)S(1)} %pad_add_fusion.ids, f32[1024]{0:T(1024)S(1)} %copy-done.3, f32[8,256]{1,0:T(8,128)S(1)} %copy-done.2, f32[16,128]{1,0:T(8,128)S(1)} %pad.4.rest_0_.rest_4_, f32[16,128]{1,0:T(8,128)S(1)} %collective-permute-done.3.rest_1_.rest_5_, ...), custom_call_target="tpu_custom_call" | custom-call | flops 5242880 | bytes 2097152 | tf_op jit(solution)/shard_map/aligned_rows/pallas_call | solution.py:293
  16.7 0.0 collective-permute-done.2.rest_3_
  16.7 2.7 %collective-permute-done.rest_1_ = bf16[2,4,4,2048]{3,2,1,0:T(4,128)(2,1)S(1)} collective-permute-done((bf16[2,4,4,2048]{3,2,1,0:T(4,128)(2,1)S(1)}, bf16[2,4,4,2048]{3,2,1,0:T(4,128)(2,1)S(1)}, u32[]{:S(2)}, u32[]{:S(2)}) %collective-permute-start) | collective-permute-done | bytes 131104 | tf_op jit(solution)/shard_map/ppermute | solution.py:435
  19.4 3.7 %collective-permute-done.1.rest_2_ = bf16[2,4,4,2048]{3,2,1,0:T(4,128)(2,1)S(1)} collective-permute-done((bf16[2,4,4,2048]{3,2,1,0:T(4,128)(2,1)S(1)}, bf16[2,4,4,2048]{3,2,1,0:T(4,128)(2,1)S(1)}, u32[]{:S(2)}, u32[]{:S(2)}) %collective-permute-start.1) | collective-permute-done | bytes 131104 | tf_op jit(solution)/shard_map/ppermute | solution.py:435
  23.1 5.0 %partial_logits.2 = (f32[128,128]{1,0:T(8,128)S(1)}, f32[128,128]{1,0:T(8,128)S(1)}) custom-call(s32[2]{0:T(128)S(1)} %pad_add_fusion.ids, f32[1024]{0:T(1024)S(1)} %copy-done.3, f32[8,256]{1,0:T(8,128)S(1)} %copy-done.2, bf16[2,4,4,2048]{3,2,1,0:T(4,128)(2,1)S(1)} %copy-done.4, bf16[2,4,4,2048]{3,2,1,0:T(4,128)(2,1)S(1)} %collective-permute-done.rest_1_, ...), custom_call_target="tpu_custom_call" | custom-call | flops 1073741824 | bytes 1572864 | tf_op jit(solution)/shard_map/partial_logits/pallas_call | solution.py:164
  28.1 0.1 collective-permute-start.5
  28.2 0.0 collective-permute-done.6.rest_4_.rest_2_
  28.2 2.9 %collective-permute-done.7.rest_5_.rest_3_ = bf16[2,16,8192]{2,1,0:T(8,128)(2,1)S(1)} collective-permute-done((bf16[2,16,8192]{2,1,0:T(8,128)(2,1)}, bf16[2,16,8192]{2,1,0:T(8,128)(2,1)S(1)}, u32[]{:S(2)}, u32[]{:S(2)}) %collective-permute-start.7) | collective-permute-done | bytes 524320 | tf_op jit(solution)/shard_map/ppermute | solution.py:432
  31.1 4.6 %partial_logits.3 = (f32[128,128]{1,0:T(8,128)S(1)}, f32[128,128]{1,0:T(8,128)S(1)}) custom-call(s32[2]{0:T(128)S(1)} %pad_add_fusion.ids, f32[1024]{0:T(1024)S(1)} %copy-done.3, f32[8,256]{1,0:T(8,128)S(1)} %copy-done.2, bf16[2,4,4,2048]{3,2,1,0:T(4,128)(2,1)S(1)} %copy-done.4, bf16[2,4,4,2048]{3,2,1,0:T(4,128)(2,1)S(1)} %collective-permute-done.rest_1_, ...), custom_call_target="tpu_custom_call" | custom-call | flops 1073741824 | bytes 1572864 | tf_op jit(solution)/shard_map/partial_logits/pallas_call | solution.py:164
  35.7 0.2 collective-permute-start.8
  35.9 0.0 collective-permute-done.5
  35.9 1.1 %collective-permute-done.8 = f32[128,128]{1,0:T(8,128)S(1)} collective-permute-done((f32[128,128]{1,0:T(8,128)S(1)}, f32[128,128]{1,0:T(8,128)S(1)}, u32[]{:S(2)}, u32[]{:S(2)}) %collective-permute-start.8) | collective-permute-done | bytes 65568 | tf_op jit(solution)/shard_map/ppermute | solution.py:432
  37.1 1.6 %collective-permute-start.9 = (f32[2,128,128]{2,1,0:T(8,128)S(1)}, f32[2,128,128]{2,1,0:T(8,128)S(1)}, u32[]{:S(2)}, u32[]{:S(2)}) collective-permute-start(f32[2,128,128]{2,1,0:T(8,128)S(1)} %pad_maximum_fusion.here), channel_id=1, source_target_pairs={{0,8},{4,12},{8,0},{12,4},{1,9},{5,13},{9,1},{13,5},{2,10},{6,14},... | collective-permute-start | bytes 393224 | tf_op jit(solution)/shard_map/ppermute | solution.py:432
  38.7 0.5 collective-permute-start.10
  39.2 0.8 %collective-permute-start.11 = (f32[16,128]{1,0:T(8,128)S(1)}, f32[16,128]{1,0:T(8,128)S(1)}, u32[]{:S(2)}, u32[]{:S(2)}) collective-permute-start(f32[16,128]{1,0:T(8,128)S(1)} %pad.4.rest_0_.rest_4_), channel_id=1, source_target_pairs={{0,12},{4,8},{8,4},{12,0},{1,13},{5,9},{9,5},{13,1},{2,14},{6,10},... | collective-permute-start | bytes 24584 | tf_op jit(solution)/shard_map/ppermute | solution.py:432
  40.0 3.0 %collective-permute-done.10.rest_0_.rest_6_ = f32[16,128]{1,0:T(8,128)S(1)} collective-permute-done((f32[16,128]{1,0:T(8,128)S(1)}, f32[16,128]{1,0:T(8,128)S(1)}, u32[]{:S(2)}, u32[]{:S(2)}) %collective-permute-start.10) | collective-permute-done | bytes 8224 | tf_op jit(solution)/shard_map/ppermute | solution.py:432
  43.0 0.0 collective-permute-done.11.rest_1_.rest_7_
  43.0 2.7 %aligned_rows.3.rest_9_ = bf16[2,32,8192]{2,1,0:T(8,128)(2,1)S(1)} custom-call(s32[2]{0:T(128)S(1)} %pad_add_fusion.ids, f32[1024]{0:T(1024)S(1)} %copy-done.3, f32[8,256]{1,0:T(8,128)S(1)} %copy-done.2, f32[16,128]{1,0:T(8,128)S(1)} %collective-permute-done.10.rest_0_.rest_6_, f32[16,128]{1,0:T(8,128)S(1)} %collective-permute-done.11.rest_1_.rest_7_, ...), custom_call_target="tpu_custom_call" | custom-call | flops 5242880 | bytes 2097152 | tf_op jit(solution)/shard_map/aligned_rows/pallas_call | solution.py:293
  45.7 0.0 collective-permute-done.9.there
  45.7 0.2 logit_stats.1.rest_0_
  45.9 0.2 collective-permute-start.12
  46.1 1.6 %collective-permute-start.13 = (f32[32,128]{1,0:T(8,128)S(1)}, f32[32,128]{1,0:T(8,128)S(1)}, u32[]{:S(2)}, u32[]{:S(2)}) collective-permute-start(f32[32,128]{1,0:T(8,128)S(1)} %logit_stats.1.rest_0_), channel_id=1, source_target_pairs={{0,16},{4,20},{8,24},{12,28},{16,0},{20,4},{24,8},{28,12},{1,17},{... | collective-permute-start | bytes 49160 | tf_op jit(solution)/shard_map/ppermute | solution.py:471
  47.7 0.2 collective-permute-start.14
  47.9 0.0 collective-permute-done.12.rest_1_
  47.9 2.0 %collective-permute-done.13.rest_2_ = f32[32,128]{1,0:T(8,128)S(1)} collective-permute-done((f32[32,128]{1,0:T(8,128)S(1)}, f32[32,128]{1,0:T(8,128)S(1)}, u32[]{:S(2)}, u32[]{:S(2)}) %collective-permute-start.13) | collective-permute-done | bytes 16416 | tf_op jit(solution)/shard_map/ppermute | solution.py:471
  49.9 1.0 %collective-permute-done.14.rest_3_ = f32[32,128]{1,0:T(8,128)S(1)} collective-permute-done((f32[32,128]{1,0:T(8,128)S(1)}, f32[32,128]{1,0:T(8,128)S(1)}, u32[]{:S(2)}, u32[]{:S(2)}) %collective-permute-start.14) | collective-permute-done | bytes 16416 | tf_op jit(solution)/shard_map/ppermute | solution.py:472
  50.9 2.1 %volume_terms.1 = (f32[16,128]{1,0:T(8,128)S(1)}, f32[2,4,8192]{2,1,0:T(4,128)S(1)}, bf16[2,4,8192]{2,1,0:T(4,128)(2,1)S(1)}, bf16[2,4,8192]{2,1,0:T(4,128)(2,1)S(1)}, bf16[2,4,8192]{2,1,0:T(4,128)(2,1)S(1)}) custom-call(s32[2]{0:T(128)S(1)} %pad_add_fusion.ids, f32[32,128]{1,0:T(8,128)S(1)} %logit_stats.1.rest_0_, ...), custom_call_target="tpu_custom_call" | custom-call | flops 33554432 | bytes 2621440 | tf_op jit(solution)/shard_map/volume_terms/pallas_call | solution.py:372
  53.0 1.6 %collective-permute-start.15 = (bf16[2,4,8192]{2,1,0:T(4,128)(2,1)S(1)}, bf16[2,4,8192]{2,1,0:T(4,128)(2,1)S(1)}, u32[]{:S(2)}, u32[]{:S(2)}) collective-permute-start(bf16[2,4,8192]{2,1,0:T(4,128)(2,1)S(1)} %get-tuple-element.31), channel_id=1, source_target_pairs={{0,1},{1,0},{2,3},{3,2},{4,5},{5,4},{6,7},{7,6},{8,9},{9,8},{10,11... | collective-permute-start | bytes 393224 | tf_op jit(solution)/shard_map/ppermute | solution.py:435
  54.7 2.6 %collective-permute-start.16 = (bf16[2,4,8192]{2,1,0:T(4,128)(2,1)S(1)}, bf16[2,4,8192]{2,1,0:T(4,128)(2,1)S(1)}, u32[]{:S(2)}, u32[]{:S(2)}) collective-permute-start(bf16[2,4,8192]{2,1,0:T(4,128)(2,1)S(1)} %get-tuple-element.32), channel_id=1, source_target_pairs={{0,2},{1,3},{2,0},{3,1},{4,6},{5,7},{6,4},{7,5},{8,10},{9,11},{10,... | collective-permute-start | bytes 393224 | tf_op jit(solution)/shard_map/ppermute | solution.py:435
  57.3 0.2 collective-permute-start.17
  57.5 0.7 copy.14
  58.1 2.5 %collective-permute-done.15.rest_0_ = bf16[2,4,8192]{2,1,0:T(4,128)(2,1)S(1)} collective-permute-done((bf16[2,4,8192]{2,1,0:T(4,128)(2,1)S(1)}, bf16[2,4,8192]{2,1,0:T(4,128)(2,1)S(1)}, u32[]{:S(2)}, u32[]{:S(2)}) %collective-permute-start.15) | collective-permute-done | bytes 131104 | tf_op jit(solution)/shard_map/ppermute | solution.py:435
  60.6 7.0 %collective-permute-done.16.rest_1_ = bf16[2,4,8192]{2,1,0:T(4,128)(2,1)S(1)} collective-permute-done((bf16[2,4,8192]{2,1,0:T(4,128)(2,1)S(1)}, bf16[2,4,8192]{2,1,0:T(4,128)(2,1)S(1)}, u32[]{:S(2)}, u32[]{:S(2)}) %collective-permute-start.16) | collective-permute-done | bytes 131104 | tf_op jit(solution)/shard_map/ppermute | solution.py:435
  67.6 0.0 collective-permute-done.17.rest_2_
  67.6 0.8 %total_volume.1 = f32[2,4,1,8192]{3,2,1,0:T(1,128)} custom-call(f32[2,4,8192]{2,1,0:T(4,128)S(1)} %get-tuple-element.30.first, bf16[2,4,8192]{2,1,0:T(4,128)(2,1)S(1)} %collective-permute-done.15.rest_0_, bf16[2,4,8192]{2,1,0:T(4,128)(2,1)S(1)} %collective-permute-done.16.rest_1_, bf16[2,4,8192]{2,1,0:T(4,128)(2,1)S(1)} %collective-permute-done.17.rest_2_), custom_call_target="tpu_custom_call" | custom-call | tf_op jit(solution)/shard_map/total_volume/pallas_call | solution.py:417
  (7 shorter events, 0.1 us)
Async XLA Ops:
  0.7 1.6 %copy-start = (bf16[2,16,32768]{2,1,0:T(8,128)(2,1)S(1)}, bf16[2,16,32768]{2,1,0:T(8,128)(2,1)}, u32[]{:S(2)}) copy-start(bf16[2,16,32768]{2,1,0:T(8,128)(2,1)} %rest_4_.1) | copy-start | bytes 6291460
  2.3 5.1 %copy-start.6 = (s32[16,1]{0,1:T(1,128)S(1)}, s32[16,1]{0,1:T(1,128)}, u32[]{:S(2)}) copy-start(s32[16,1]{0,1:T(1,128)} %param.9) | copy-start | bytes 196
  2.3 5.1 %copy-start.7 = (s32[16,1]{0,1:T(1,128)S(1)}, s32[16,1]{0,1:T(1,128)}, u32[]{:S(2)}) copy-start(s32[16,1]{0,1:T(1,128)} %param.10) | copy-start | bytes 196
  2.3 5.1 %copy-start.5 = (f32[16,1]{0,1:T(1,128)S(1)}, f32[16,1]{0,1:T(1,128)}, u32[]{:S(2)}) copy-start(f32[16,1]{0,1:T(1,128)} %param.11) | copy-start | bytes 196
  2.3 5.3 %copy-start.4 = (bf16[2,4,4,2048]{3,2,1,0:T(4,128)(2,1)S(1)}, bf16[2,4,4,2048]{3,2,1,0:T(4,128)(2,1)}, u32[]{:S(2)}) copy-start(bf16[2,4,4,2048]{3,2,1,0:T(4,128)(2,1)} %rest_0_.3) | copy-start | bytes 393220
  2.3 10.8 %copy-start.1 = (bf16[2,16,32768]{2,1,0:T(8,128)(2,1)S(1)}, bf16[2,16,32768]{2,1,0:T(8,128)(2,1)}, u32[]{:S(2)}) copy-start(bf16[2,16,32768]{2,1,0:T(8,128)(2,1)} %rest_4_.1) | copy-start | bytes 6291460
  2.3 10.8 %copy-start.2 = (f32[8,256]{1,0:T(8,128)S(1)}, f32[8,256]{1,0:T(8,128)}, u32[]{:S(2)}) copy-start(f32[8,256]{1,0:T(8,128)} %constant.14.clone.table_x) | copy-start | bytes 24580
  2.3 10.8 %copy-start.3 = (f32[1024]{0:T(1024)S(1)}, f32[1024]{0:T(1024)}, u32[]{:S(2)}) copy-start(f32[1024]{0:T(1024)} %constant.15.clone.table_y) | copy-start | bytes 12292
  4.3 7.3 %collective-permute-start.4 = (bf16[2,16,8192]{2,1,0:T(8,128)(2,1)}, bf16[2,16,8192]{2,1,0:T(8,128)(2,1)}, u32[]{:S(2)}, u32[]{:S(2)}) collective-permute-start(bf16[2,16,8192]{2,1,0:T(8,128)(2,1)} %get-tuple-element.18), channel_id=1, source_target_pairs={{0,4},{4,0},{8,12},{12,8},{1,5},{5,1},{9,13},{13,9},{2,6},{6,2},{1... | collective-permute-start | bytes 1572872 | tf_op jit(solution)/shard_map/ppermute | solution.py:432
  4.8 23.4 %collective-permute-start.6 = (bf16[2,16,8192]{2,1,0:T(8,128)(2,1)}, bf16[2,16,8192]{2,1,0:T(8,128)(2,1)S(1)}, u32[]{:S(2)}, u32[]{:S(2)}) collective-permute-start(bf16[2,16,8192]{2,1,0:T(8,128)(2,1)} %get-tuple-element.22), channel_id=1, source_target_pairs={{0,8},{4,12},{8,0},{12,4},{1,9},{5,13},{9,1},{13,5},{2,10},{6,14},... | collective-permute-start | bytes 1572872 | tf_op jit(solution)/shard_map/ppermute | solution.py:432
  7.2 23.9 %collective-permute-start.7 = (bf16[2,16,8192]{2,1,0:T(8,128)(2,1)}, bf16[2,16,8192]{2,1,0:T(8,128)(2,1)S(1)}, u32[]{:S(2)}, u32[]{:S(2)}) collective-permute-start(bf16[2,16,8192]{2,1,0:T(8,128)(2,1)} %get-tuple-element.23), channel_id=1, source_target_pairs={{0,12},{4,8},{8,4},{12,0},{1,13},{5,9},{9,5},{13,1},{2,14},{6,10},... | collective-permute-start | bytes 1572872 | tf_op jit(solution)/shard_map/ppermute | solution.py:432
  7.5 4.1 %collective-permute-start.3 = (f32[16,128]{1,0:T(8,128)S(1)}, f32[16,128]{1,0:T(8,128)S(1)}, u32[]{:S(2)}, u32[]{:S(2)}) collective-permute-start(f32[16,128]{1,0:T(8,128)S(1)} %pad.4.rest_0_.rest_4_), channel_id=1, source_target_pairs={{0,4},{4,0},{8,12},{12,8},{1,5},{5,1},{9,13},{13,9},{2,6},{6,2},{1... | collective-permute-start | bytes 24584 | tf_op jit(solution)/shard_map/ppermute | solution.py:432
  7.6 9.1 %collective-permute-start.2 = (bf16[2,4,4,2048]{3,2,1,0:T(4,128)(2,1)S(1)}, bf16[2,4,4,2048]{3,2,1,0:T(4,128)(2,1)S(1)}, u32[]{:S(2)}, u32[]{:S(2)}) collective-permute-start(bf16[2,4,4,2048]{3,2,1,0:T(4,128)(2,1)S(1)} %copy-done.4), channel_id=1, source_target_pairs={{0,3},{1,2},{2,1},{3,0},{4,7},{5,6},{6,5},{7,4},{8,11},{9,10},{10,... | collective-permute-start | bytes 393224 | tf_op jit(solution)/shard_map/ppermute | solution.py:435
  11.6 7.8 %collective-permute-start = (bf16[2,4,4,2048]{3,2,1,0:T(4,128)(2,1)S(1)}, bf16[2,4,4,2048]{3,2,1,0:T(4,128)(2,1)S(1)}, u32[]{:S(2)}, u32[]{:S(2)}) collective-permute-start(bf16[2,4,4,2048]{3,2,1,0:T(4,128)(2,1)S(1)} %copy-done.4), channel_id=1, source_target_pairs={{0,1},{1,0},{2,3},{3,2},{4,5},{5,4},{6,7},{7,6},{8,9},{9,8},{10,11... | collective-permute-start | bytes 393224 | tf_op jit(solution)/shard_map/ppermute | solution.py:435
  11.6 11.5 %collective-permute-start.1 = (bf16[2,4,4,2048]{3,2,1,0:T(4,128)(2,1)S(1)}, bf16[2,4,4,2048]{3,2,1,0:T(4,128)(2,1)S(1)}, u32[]{:S(2)}, u32[]{:S(2)}) collective-permute-start(bf16[2,4,4,2048]{3,2,1,0:T(4,128)(2,1)S(1)} %copy-done.4), channel_id=1, source_target_pairs={{0,2},{1,3},{2,0},{3,1},{4,6},{5,7},{6,4},{7,5},{8,10},{9,11},{10,... | collective-permute-start | bytes 393224 | tf_op jit(solution)/shard_map/ppermute | solution.py:435
  28.1 7.8 %collective-permute-start.5 = (f32[128,128]{1,0:T(8,128)S(1)}, f32[128,128]{1,0:T(8,128)S(1)}, u32[]{:S(2)}, u32[]{:S(2)}) collective-permute-start(f32[128,128]{1,0:T(8,128)S(1)} %get-tuple-element.21), channel_id=1, source_target_pairs={{0,4},{4,0},{8,12},{12,8},{1,5},{5,1},{9,13},{13,9},{2,6},{6,2},{1... | collective-permute-start | bytes 196616 | tf_op jit(solution)/shard_map/ppermute | solution.py:432
  35.7 1.3 %collective-permute-start.8 = (f32[128,128]{1,0:T(8,128)S(1)}, f32[128,128]{1,0:T(8,128)S(1)}, u32[]{:S(2)}, u32[]{:S(2)}) collective-permute-start(f32[128,128]{1,0:T(8,128)S(1)} %get-tuple-element.25), channel_id=1, source_target_pairs={{0,4},{4,0},{8,12},{12,8},{1,5},{5,1},{9,13},{13,9},{2,6},{6,2},{1... | collective-permute-start | bytes 196616 | tf_op jit(solution)/shard_map/ppermute | solution.py:432
  37.1 8.6 %collective-permute-start.9 = (f32[2,128,128]{2,1,0:T(8,128)S(1)}, f32[2,128,128]{2,1,0:T(8,128)S(1)}, u32[]{:S(2)}, u32[]{:S(2)}) collective-permute-start(f32[2,128,128]{2,1,0:T(8,128)S(1)} %pad_maximum_fusion.here), channel_id=1, source_target_pairs={{0,8},{4,12},{8,0},{12,4},{1,9},{5,13},{9,1},{13,5},{2,10},{6,14},... | collective-permute-start | bytes 393224 | tf_op jit(solution)/shard_map/ppermute | solution.py:432
  38.7 4.3 %collective-permute-start.10 = (f32[16,128]{1,0:T(8,128)S(1)}, f32[16,128]{1,0:T(8,128)S(1)}, u32[]{:S(2)}, u32[]{:S(2)}) collective-permute-start(f32[16,128]{1,0:T(8,128)S(1)} %pad.4.rest_0_.rest_4_), channel_id=1, source_target_pairs={{0,8},{4,12},{8,0},{12,4},{1,9},{5,13},{9,1},{13,5},{2,10},{6,14},... | collective-permute-start | bytes 24584 | tf_op jit(solution)/shard_map/ppermute | solution.py:432
  39.2 3.8 %collective-permute-start.11 = (f32[16,128]{1,0:T(8,128)S(1)}, f32[16,128]{1,0:T(8,128)S(1)}, u32[]{:S(2)}, u32[]{:S(2)}) collective-permute-start(f32[16,128]{1,0:T(8,128)S(1)} %pad.4.rest_0_.rest_4_), channel_id=1, source_target_pairs={{0,12},{4,8},{8,4},{12,0},{1,13},{5,9},{9,5},{13,1},{2,14},{6,10},... | collective-permute-start | bytes 24584 | tf_op jit(solution)/shard_map/ppermute | solution.py:432
  45.9 2.0 %collective-permute-start.12 = (f32[32,128]{1,0:T(8,128)S(1)}, f32[32,128]{1,0:T(8,128)S(1)}, u32[]{:S(2)}, u32[]{:S(2)}) collective-permute-start(f32[32,128]{1,0:T(8,128)S(1)} %logit_stats.1.rest_0_), channel_id=1, source_target_pairs={{0,4},{4,0},{8,12},{12,8},{1,5},{5,1},{9,13},{13,9},{2,6},{6,2},{1... | collective-permute-start | bytes 49160 | tf_op jit(solution)/shard_map/ppermute | solution.py:432
  46.1 3.7 %collective-permute-start.13 = (f32[32,128]{1,0:T(8,128)S(1)}, f32[32,128]{1,0:T(8,128)S(1)}, u32[]{:S(2)}, u32[]{:S(2)}) collective-permute-start(f32[32,128]{1,0:T(8,128)S(1)} %logit_stats.1.rest_0_), channel_id=1, source_target_pairs={{0,16},{4,20},{8,24},{12,28},{16,0},{20,4},{24,8},{28,12},{1,17},{... | collective-permute-start | bytes 49160 | tf_op jit(solution)/shard_map/ppermute | solution.py:471
  47.7 3.2 %collective-permute-start.14 = (f32[32,128]{1,0:T(8,128)S(1)}, f32[32,128]{1,0:T(8,128)S(1)}, u32[]{:S(2)}, u32[]{:S(2)}) collective-permute-start(f32[32,128]{1,0:T(8,128)S(1)} %logit_stats.1.rest_0_), channel_id=1, source_target_pairs={{0,20},{4,16},{8,28},{12,24},{16,4},{20,0},{24,12},{28,8},{1,21},{... | collective-permute-start | bytes 49160 | tf_op jit(solution)/shard_map/ppermute | solution.py:472
  53.0 7.6 %collective-permute-start.15 = (bf16[2,4,8192]{2,1,0:T(4,128)(2,1)S(1)}, bf16[2,4,8192]{2,1,0:T(4,128)(2,1)S(1)}, u32[]{:S(2)}, u32[]{:S(2)}) collective-permute-start(bf16[2,4,8192]{2,1,0:T(4,128)(2,1)S(1)} %get-tuple-element.31), channel_id=1, source_target_pairs={{0,1},{1,0},{2,3},{3,2},{4,5},{5,4},{6,7},{7,6},{8,9},{9,8},{10,11... | collective-permute-start | bytes 393224 | tf_op jit(solution)/shard_map/ppermute | solution.py:435
  54.7 12.9 %collective-permute-start.16 = (bf16[2,4,8192]{2,1,0:T(4,128)(2,1)S(1)}, bf16[2,4,8192]{2,1,0:T(4,128)(2,1)S(1)}, u32[]{:S(2)}, u32[]{:S(2)}) collective-permute-start(bf16[2,4,8192]{2,1,0:T(4,128)(2,1)S(1)} %get-tuple-element.32), channel_id=1, source_target_pairs={{0,2},{1,3},{2,0},{3,1},{4,6},{5,7},{6,4},{7,5},{8,10},{9,11},{10,... | collective-permute-start | bytes 393224 | tf_op jit(solution)/shard_map/ppermute | solution.py:435
  57.3 10.3 %collective-permute-start.17 = (bf16[2,4,8192]{2,1,0:T(4,128)(2,1)S(1)}, bf16[2,4,8192]{2,1,0:T(4,128)(2,1)S(1)}, u32[]{:S(2)}, u32[]{:S(2)}) collective-permute-start(bf16[2,4,8192]{2,1,0:T(4,128)(2,1)S(1)} %get-tuple-element.33), channel_id=1, source_target_pairs={{0,3},{1,2},{2,1},{3,0},{4,7},{5,6},{6,5},{7,4},{8,11},{9,10},{10,... | collective-permute-start | bytes 393224 | tf_op jit(solution)/shard_map/ppermute | solution.py:435

commit v3 on v2

--- a/solution.py
+++ b/solution.py
@@ -36,44 +36,115 @@
     return [(i, i ^ step) for i in range(size)]
 
 
-def bands_kernel(ids, *refs):
-    half = len(refs) // 2
-    for source, target in zip(refs[:half], refs[half:]):
-        target[...] = source[...]
-
-
-def image_bands(ids, images, dom):
+def column_of(line):
+    size = line.shape[1]
+    rows = lax.broadcasted_iota(jnp.int32, (size, size), 0)
+    cols = lax.broadcasted_iota(jnp.int32, (size, size), 1)
+    return jnp.sum(jnp.where(rows == cols, line, 0.0), axis=1, keepdims=True)
+
+
+def bands_kernel(steps, ids, images, references, *rest):
+    lists, rest = rest[:3], rest[3:]
+    outs, meta, shard = rest[: len(steps)], rest[len(steps)], rest[len(steps) + 1]
+    lines, sems, meta_sems, line_sems, shard_sem = rest[len(steps) + 2 :]
+    width = outs[0].shape[2] - LANES
+    copies = [pltpu.make_async_copy(references, shard, shard_sem)]
+    for place, (step, out) in enumerate(zip(steps, outs)):
+        start = pl.multiple_of((ids[0] ^ step) * width, width)
+        for part in range(out.shape[0]):
+            copies.append(
+                pltpu.make_async_copy(
+                    images.at[part, :, pl.ds(start, width)],
+                    out.at[part, :, pl.ds(0, width)],
+                    sems.at[place, part],
+                )
+            )
+    line_copies = [
+        pltpu.make_async_copy(source, lines[place], line_sems.at[place])
+        for place, source in enumerate(lists)
+    ]
+    for copy in line_copies + copies:
+        copy.start()
+    for copy in line_copies:
+        copy.wait()
+    lane = lax.broadcasted_iota(jnp.int32, meta.shape[1:], 1)
+    fixed = column_of(lines[2][...])
+    high = fixed.astype(BF).astype(F32)
+    middle = (fixed - high).astype(BF).astype(F32)
+    values = [column_of(lines[0][...].astype(F32)), column_of(lines[1][...].astype(F32))]
+    table = jnp.zeros(meta.shape[1:], F32)
+    for place, value in enumerate(values + [high, middle, fixed - high - middle]):
+        table = jnp.where(lane == place, value, table)
+    meta[0] = table.astype(BF)
+    meta[1] = jnp.zeros(meta.shape[1:], BF)
+    meta_copies = [
+        pltpu.make_async_copy(meta, out.at[:, :, pl.ds(width, LANES)], meta_sems.at[place])
+        for place, out in enumerate(outs)
+    ]
+    for copy in meta_copies:
+        copy.start()
+    for copy in copies + meta_copies:
+        copy.wait()
+
+
+def image_bands(ids, orient_lists, shift_ids, fixed_weights, images, references, dom):
     parts, rows, pixels = images.shape
     width = pixels // dom
-    chunk = min(width, 16 * IMG)
-    count = width // chunk
-
-    def spec(step):
-        return pl.BlockSpec(
-            (parts, rows, chunk), lambda i, s: (0, 0, (s[0] ^ step) * count + i)
-        )
-
-    return pl.pallas_call(
-        bands_kernel,
-        out_shape=[jax.ShapeDtypeStruct((parts, rows, width), images.dtype)] * (dom - 1),
-        grid_spec=pltpu.PrefetchScalarGridSpec(
-            num_scalar_prefetch=1,
-            grid=(count,),
-            in_specs=[spec(step) for step in range(1, dom)],
-            out_specs=[pl.BlockSpec((parts, rows, chunk), lambda i, s: (0, 0, i))] * (dom - 1),
-        ),
+    steps = list(range(1, dom))
+    sources = [images, references] + [
+        array.reshape(1, rows) for array in (orient_lists, shift_ids, fixed_weights)
+    ]
+    sources = [pltpu.with_memory_space_constraint(array, pltpu.HBM) for array in sources]
+    *bands, meta, shard = pl.pallas_call(
+        functools.partial(bands_kernel, steps),
+        out_shape=[pltpu.VMEM((parts, rows, width + LANES), images.dtype)] * len(steps)
+        + [
+            jax.ShapeDtypeStruct((parts, rows, LANES), BF),
+            pltpu.VMEM(references.shape, references.dtype),
+        ],
+        in_specs=[pl.BlockSpec(memory_space=pltpu.SMEM)]
+        + [pl.BlockSpec(memory_space=pl.ANY)] * len(sources),
+        out_specs=[pl.BlockSpec(memory_space=pl.ANY)] * len(steps)
+        + [pl.BlockSpec(memory_space=pltpu.VMEM), pl.BlockSpec(memory_space=pl.ANY)],
+        scratch_shapes=[
+            [pltpu.VMEM((1, rows), array.dtype) for array in sources[2:]],
+            pltpu.SemaphoreType.DMA((len(steps), parts)),
+            pltpu.SemaphoreType.DMA((len(steps),)),
+            pltpu.SemaphoreType.DMA((3,)),
+            pltpu.SemaphoreType.DMA,
+        ],
         compiler_params=pltpu.CompilerParams(vmem_limit_bytes=VMEM_BYTES),
         cost_estimate=pl.CostEstimate(
             flops=0, bytes_accessed=4 * parts * rows * (pixels - width), transcendentals=0
         ),
         name="image_bands",
-    )(ids, *([images] * (dom - 1)))
+    )(ids, *sources)
+    return bands, meta, shard
+
+
+def image_specs(groups, own, chunk, column, base):
+    parts, rows = own.shape[:2]
+    block = (parts, rows, chunk)
+    return [
+        pl.BlockSpec(block, lambda i, s: (0, 0, base(s) + column(i, s)))
+        if image is own
+        else pl.BlockSpec(block, lambda i, s: (0, 0, column(i, s)))
+        for image, _ in groups
+    ]
+
+
+def table_specs(groups):
+    specs = []
+    for _, table in groups:
+        last = table.shape[2] // LANES - 1
+        specs.append(pl.BlockSpec((1, table.shape[1], LANES), lambda i, s, last=last: (0, 0, last)))
+    return specs
 
 
 def logits_kernel(groups, orients, span, ids, table_y, table_x, *rest):
     shards, rest = rest[:orients], rest[orients:]
-    images, outs = rest[:groups], rest[groups : 2 * groups]
-    refs, buffers = rest[2 * groups], rest[2 * groups + 1 :]
+    images, rest = rest[:groups], rest[groups:]
+    outs, refs, buffers = rest[:groups], rest[groups], rest[groups + 1 :]
     step = pl.program_id(0)
     chunk = refs.shape[3]
     rows = images[0].shape[1]
@@ -141,25 +212,16 @@
                 outs[g][...] += value[g * group_rows : (g + 1) * group_rows]
 
 
-def partial_logits(ids, table_x, table_y, shards, own, others):
+def partial_logits(ids, table_x, table_y, shards, own, picked):
     parts, classes, orients, chunk = shards[0].shape
-    arrays = ([own] if own is not None else []) + list(others)
-    groups = len(arrays)
-    rows = arrays[0].shape[1]
+    groups = len(picked)
+    rows = own.shape[1]
     names = classes * orients
     count = len(shards)
     lines = chunk // IMG
     span = 2 if lines % 4 == 0 else 1
-    specs = []
-    for array in arrays:
-        if array is own:
-            specs.append(
-                pl.BlockSpec(
-                    (parts, rows, chunk), lambda i, s: (0, 0, s[0] * count + (s[1] ^ i))
-                )
-            )
-        else:
-            specs.append(pl.BlockSpec((parts, rows, chunk), lambda i, s: (0, 0, s[1] ^ i)))
+    specs = image_specs(picked, own, chunk, lambda i, s: s[1] ^ i, lambda s: s[0] * count)
+    arrays = [image for image, _ in picked]
     out_shape = (TX * rows, TY * names)
     return pl.pallas_call(
         functools.partial(logits_kernel, groups, count, span),
@@ -228,12 +290,12 @@
     out, phase_c, phase_s = rest[2 * groups :]
     step = pl.program_id(0)
     chunk = out.shape[2]
-    rows = images[0].shape[1]
+    rows = metas[0].shape[1]
     lines = chunk // IMG
     line_base = (ids[0] * pl.num_programs(0) + step) * lines
 
     def offsets(g):
-        shift = metas[g][:, 1:2].astype(jnp.int32)
+        shift = metas[g][0].astype(F32)[:, 1:2].astype(jnp.int32)
         move_x = shift % TX - TX // 2
         move_y = shift // TX - TY // 2
         return move_x, move_y
@@ -276,20 +338,13 @@
                 out[1, own, cols] = (re * sine + im * cosine).astype(BF)
 
 
-def aligned_rows(ids, table_x, table_y, metas, own, others, width):
-    arrays = ([own] if own is not None else []) + list(others)
-    parts, rows = arrays[0].shape[:2]
+def aligned_rows(ids, table_x, table_y, own, picked, width):
+    parts, rows = own.shape[:2]
     chunk = chunk_of(width)
     count = width // chunk
-    groups = len(metas)
-    specs = []
-    for array in arrays:
-        if array is own:
-            specs.append(
-                pl.BlockSpec((parts, rows, chunk), lambda i, s: (0, 0, s[0] * count + i))
-            )
-        else:
-            specs.append(pl.BlockSpec((parts, rows, chunk), lambda i, s: (0, 0, i)))
+    groups = len(picked)
+    specs = image_specs(picked, own, chunk, lambda i, s: i, lambda s: s[0] * count)
+    arrays = [table for _, table in picked] + [image for image, _ in picked]
     return pl.pallas_call(
         functools.partial(rows_kernel, groups),
         out_shape=jax.ShapeDtypeStruct((parts, groups * rows, width), BF),
@@ -300,7 +355,7 @@
                 pl.BlockSpec(memory_space=pltpu.SMEM),
                 pl.BlockSpec((TX, IMG), lambda i, s: (0, 0)),
             ]
-            + [pl.BlockSpec((rows, LANES), lambda i, s: (0, 0))] * groups
+            + table_specs(picked)
             + specs,
             out_specs=pl.BlockSpec((parts, groups * rows, chunk), lambda i, s: (0, 0, i)),
             scratch_shapes=[
@@ -315,7 +370,7 @@
             transcendentals=0,
         ),
         name="aligned_rows",
-    )(ids, table_y, table_x, *metas, *arrays)
+    )(ids, table_y, table_x, *arrays)
 
 
 def volume_kernel(groups, orients, classes, ids, *rest):
@@ -323,7 +378,7 @@
     near, far = rest[4 + groups], rest[5 + groups]
     prob, outs, mixes = rest[6 + groups], rest[7 + groups : -2], rest[-2:]
     step = pl.program_id(0)
-    rows = metas[0].shape[0]
+    rows = metas[0].shape[1]
 
     @pl.when(step == 0)
     def _():
@@ -346,8 +401,10 @@
             class_prob = spread * mine_scale / totals
             if g == 0:
                 prob[...] = class_prob
-            weight = (metas[g][:, 2:3] * class_prob).astype(BF).astype(F32)
-            bin_of = metas[g][:, 0:1].astype(jnp.int32) ^ ids[1]
+            table = metas[g][0].astype(F32)
+            fixed = table[:, 2:3] + table[:, 3:4] + table[:, 4:5]
+            weight = (fixed * class_prob).astype(BF).astype(F32)
+            bin_of = table[:, 0:1].astype(jnp.int32) ^ ids[1]
             pieces.append(jnp.where(lane // classes == bin_of, weight, 0.0))
         for mix, held in zip(mixes, (pieces[:2], pieces[2:])):
             mixing = jnp.concatenate(held, axis=0)
@@ -360,17 +417,16 @@
             outs[o][part] = value[o * classes : (o + 1) * classes].astype(outs[o].dtype)
 
 
-def volume_terms(ids, stats, metas, near, far, orients, classes):
+def volume_terms(ids, stats, groups, near, far, orients, classes):
     parts, entries, width = near.shape
     rest = far.shape[1]
-    groups = len(metas)
-    rows = metas[0].shape[0]
+    rows = groups[0][0].shape[1]
     chunk = chunk_of(width)
     count = width // chunk
     out_shape = (parts, classes, width)
     fixed = lambda i, s: (0, 0)
     return pl.pallas_call(
-        functools.partial(volume_kernel, groups, orients, classes),
+        functools.partial(volume_kernel, len(groups), orients, classes),
         out_shape=[jax.ShapeDtypeStruct((rows, LANES), F32)]
         + [
             jax.ShapeDtypeStruct(out_shape, F32 if o == 0 else BF)
@@ -380,7 +436,7 @@
             num_scalar_prefetch=1,
             grid=(count,),
             in_specs=[pl.BlockSpec(stats[0].shape, fixed)] * 4
-            + [pl.BlockSpec((rows, LANES), fixed)] * groups
+            + table_specs(groups)
             + [
                 pl.BlockSpec((parts, entries, chunk), lambda i, s: (0, 0, i)),
                 pl.BlockSpec((parts, rest, chunk), lambda i, s: (0, 0, i)),
@@ -399,7 +455,7 @@
             transcendentals=0,
         ),
         name="volume_terms",
-    )(ids, *stats, *metas, near, far)
+    )(ids, *stats, *[table for _, table in groups], near, far)
 
 
 def total_kernel(first, *rest):
@@ -425,8 +481,8 @@
 def local(dom, orient, cls, references, images, orient_lists, shift_ids, fixed_weights):
     classes, orients = references.shape[1], references.shape[2]
     table_x, table_y = (jnp.asarray(t) for t in trig_tables())
-    ids = jnp.stack([lax.axis_index("dom"), lax.axis_index("orient")]).astype(jnp.int32)
-    rows = images.shape[1]
+    ids = jnp.stack([lax.axis_index(name) for name in ("dom", "orient", "cls")])
+    ids = ids.astype(jnp.int32)
 
     def swap_dom(array, step):
         return lax.ppermute(array, "dom", xor_pairs(dom, step))
@@ -434,21 +490,23 @@
     def swap_orient(array, step):
         return lax.ppermute(array, "orient", xor_pairs(orient, step))
 
-    bands = image_bands(ids, images, dom)
-    others = [swap_dom(band, step + 1) for step, band in enumerate(bands)]
-    shards = [references] + [swap_orient(references, step) for step in range(1, orient)]
-    meta = jnp.concatenate(
-        [orient_lists.astype(F32), shift_ids.astype(F32), fixed_weights], axis=1
+    bands, meta, shard = image_bands(
+        ids, orient_lists, shift_ids, fixed_weights, images, references, dom
     )
-    meta = jnp.pad(meta, ((0, 0), (0, LANES - meta.shape[1])))
-    metas = [meta] + [swap_dom(meta, step) for step in range(1, dom)]
+    arrived = {step: swap_dom(bands[step - 1], step) for step in [1, *range(dom - 1, 1, -1)]}
+    shards = [shard] + [swap_orient(shard, step) for step in range(1, orient)]
+    groups = [(images, meta)] + [(arrived[step], arrived[step]) for step in range(1, dom)]
+
+    def logits_of(picked):
+        return partial_logits(ids, table_x, table_y, shards, images, picked)
 
     width = images.shape[2] // dom
-    aligned_near = aligned_rows(ids, table_x, table_y, metas[:2], images, others[:1], width)
-    shards[-1], aligned_near = lax.optimization_barrier((shards[-1], aligned_near))
-    near = partial_logits(ids, table_x, table_y, shards, images, others[:1])
-    far = partial_logits(ids, table_x, table_y, shards, None, others[1:])
-    partial = list(near) + list(far)
+    aligned_near = aligned_rows(ids, table_x, table_y, images, groups[:2], width)
+    *shards, aligned_near = lax.optimization_barrier((*shards, aligned_near))
+    partial = [None] * dom
+    partial[0:2] = logits_of(groups[:2])
+    partial[3::2] = logits_of(groups[3::2])
+    partial[2::2] = logits_of(groups[2::2])
     kept = [partial[s] + swap_dom(partial[s ^ 1], 1) for s in range(0, dom, 2)]
     here = jnp.stack(kept)
     step = 2
@@ -459,7 +517,7 @@
             order = np.arange(dom // 2) ^ swap
             here = here + jnp.stack([there[i] for i in order])
         step *= 2
-    aligned_far = aligned_rows(ids, table_x, table_y, metas[2:], None, others[1:], width)
+    aligned_far = aligned_rows(ids, table_x, table_y, images, groups[2:], width)
     there, aligned_far = lax.optimization_barrier((there, aligned_far))
     stats = logit_stats(here, there, swap, classes, orients)
 
@@ -472,9 +530,9 @@
         lax.ppermute(stats, ("cls", "dom"), cross),
     ]
     prob, *terms = volume_terms(
-        ids, stats_all, metas, aligned_near, aligned_far, orients, classes
+        ids, stats_all, groups, aligned_near, aligned_far, orients, classes
     )
-    terms = [terms[0]] + [swap_orient(terms[o], o) for o in range(1, orients)]
+    terms = [terms[0]] + [swap_orient(terms[o], o) for o in range(orients - 1, 0, -1)]
     return prob[:, :classes], total_volume(terms)
 
 

time: 68.6 us -> 62.9 us (0.917)
  waiting for transfers between devices: 25.9 us -> 20.1 us
  Pallas kernels: 21 us -> 24.4 us
  local copies, waits for them, and re-layouts: 2.37 us -> 0.67 us
  starting transfers between devices: 18.2 us -> 16.7 us
    ppermute x10 -> x7, waiting for transfers between devices: 7.05 us -> 0.86 us  [swap_dom(): return lax.ppermute(array, 'dom', xor_pairs(dom, step))]
    pallas_call x2 -> x3, Pallas kernels: 9.64 us -> 13 us  [partial_logits(): pl.pallas_call(functools.partial(logits_kernel, groups, count, span), out...]
    unnamed x17 -> x7, local copies, waits for them, and re-layouts: 2.27 us -> 0.67 us
    ppermute x6, waiting for transfers between devices: 15.8 us -> 16.6 us  [swap_orient(): return lax.ppermute(array, 'orient', xor_pairs(orient, step))]
    ppermute x6, starting transfers between devices: 9.9 us -> 9.11 us  [swap_orient(): return lax.ppermute(array, 'orient', xor_pairs(orient, step))]
    ppermute x10 -> x7, starting transfers between devices: 6.5 us -> 5.97 us  [swap_dom(): return lax.ppermute(array, 'dom', xor_pairs(dom, step))]
  transfers between devices with their start and end apart: 18 -> 15, of which waited for: 9 -> 6; matrix products, arithmetic and copies ran while one was open for 1% -> 1% of each run, Pallas kernels for 23% -> 30%
where the time goes in v3:
time: 62.9 us; the launch traced here: 62.7 us
  Pallas kernels  24.4 us (39%)
  waiting for transfers between devices  20.1 us (32%)
  starting transfers between devices  16.7 us (27%)
  between operations  0.81 us (1%)
  local copies, waits for them, and re-layouts  0.67 us (1%)
    ppermute x6, waiting for transfers between devices, swap_orient(): return lax.ppermute(array, 'orient', xor_pairs(orient, step))  16.6 us
    pallas_call x3, Pallas kernels, partial_logits(): pl.pallas_call(functools.partial(logits_kernel, groups, count, span), out...  13 us
    ppermute x6, starting transfers between devices, swap_orient(): return lax.ppermute(array, 'orient', xor_pairs(orient, step))  9.11 us
    pallas_call x2, Pallas kernels, aligned_rows(): pl.pallas_call(functools.partial(rows_kernel, groups), out_shape=jax.Shap...  6.03 us
    ppermute x7, starting transfers between devices, swap_dom(): return lax.ppermute(array, 'dom', xor_pairs(dom, step))  5.97 us
    pallas_call x1, Pallas kernels, volume_terms(): pl.pallas_call(functools.partial(volume_kernel, len(groups), orients, cla...  2.3 us
    pallas_call x1, Pallas kernels, image_bands(): pl.pallas_call(functools.partial(bands_kernel, steps), out_shape=[pltpu.V...  2.1 us
    ppermute x1, waiting for transfers between devices, local(): lax.ppermute(stats, ('cls', 'dom'), pairs)  1.6 us
  transfers between devices with their start and end apart: 15, of which 6 were waited for; matrix products, arithmetic and copies ran while one was open for 1% of the time, Pallas kernels for 30%

profile of v3, /device:TPU:0, one launch (start us, length us, event | category | flops | bytes accessed | tf_op | source)
XLA Modules:
  0.0 62.7 jit_solution(11214317485622827638)
XLA Ops:
  0.6 0.0 copy-start.1
  0.6 0.0 copy-start.2
  0.7 0.0 copy-start
  0.7 0.1 pad_add_fusion.ids
  0.7 2.1 %image_bands.1 = (bf16[2,16,8320]{2,1,0:T(8,128)(2,1)S(1)}, bf16[2,16,8320]{2,1,0:T(8,128)(2,1)S(1)}, bf16[2,16,8320]{2,1,0:T(8,128)(2,1)S(1)}, bf16[2,16,128]{2...) custom-call(s32[3]{0:T(128)S(1)} %pad_add_fusion.ids, bf16[2,16,32768]{2,1,0:T(8,128)(2,1)} %rest_4_.1, ...), custom_call_target="tpu_custom_call" | custom-call | bytes 3145728 | tf_op jit(solution)/shard_map/image_bands/pallas_call | solution.py:98
  2.9 0.5 collective-permute-start.3
  3.4 2.6 %collective-permute-start.6 = (bf16[2,16,8320]{2,1,0:T(8,128)(2,1)S(1)}, bf16[2,16,8320]{2,1,0:T(8,128)(2,1)S(1)}, u32[]{:S(2)}, u32[]{:S(2)}) collective-permute-start(bf16[2,16,8320]{2,1,0:T(8,128)(2,1)S(1)} %get-tuple-element.31), channel_id=1, source_target_pairs={{0,12},{4,8},{8,4},{12,0},{1,13},{5,9},{9,5},{13,1},{2,14},{6,10},... | collective-permute-start | bytes 1597448 | tf_op jit(solution)/shard_map/ppermute | solution.py:488
  6.0 0.0 collective-permute-start.5
  6.0 2.1 %collective-permute-start = (bf16[2,4,4,2048]{3,2,1,0:T(4,128)(2,1)S(1)}, bf16[2,4,4,2048]{3,2,1,0:T(4,128)(2,1)S(1)}, u32[]{:S(2)}, u32[]{:S(2)}) collective-permute-start(bf16[2,4,4,2048]{3,2,1,0:T(4,128)(2,1)S(1)} %get-tuple-element.24.rest_0_), channel_id=1, source_target_pairs={{0,1},{1,0},{2,3},{3,2},{4,5},{5,4},{6,7},{7,6},{8,9},{9,8},{10,11... | collective-permute-start | bytes 393224 | tf_op jit(solution)/shard_map/ppermute | solution.py:491
  8.1 2.6 %collective-permute-start.1 = (bf16[2,4,4,2048]{3,2,1,0:T(4,128)(2,1)S(1)}, bf16[2,4,4,2048]{3,2,1,0:T(4,128)(2,1)S(1)}, u32[]{:S(2)}, u32[]{:S(2)}) collective-permute-start(bf16[2,4,4,2048]{3,2,1,0:T(4,128)(2,1)S(1)} %get-tuple-element.24.rest_0_), channel_id=1, source_target_pairs={{0,2},{1,3},{2,0},{3,1},{4,6},{5,7},{6,4},{7,5},{8,10},{9,11},{10,... | collective-permute-start | bytes 393224 | tf_op jit(solution)/shard_map/ppermute | solution.py:491
  10.7 0.0 collective-permute-done.3.rest_1_.rest_3_.rest_5_
  10.7 0.0 collective-permute-start.2
  10.7 0.0 copy-done.1
  10.7 0.0 copy-done.2
  10.7 0.0 copy-done
  10.7 2.9 %aligned_rows.2.rest_8_ = bf16[2,32,8192]{2,1,0:T(8,128)(2,1)S(1)} custom-call(s32[3]{0:T(128)S(1)} %pad_add_fusion.ids, f32[1024]{0:T(1024)S(1)} %copy-done.2, f32[8,256]{1,0:T(8,128)S(1)} %copy-done.1, bf16[2,16,128]{2,1,0:T(8,128)(2,1)S(1)} %get-tuple-element.22.rest_0_.rest_4_, bf16[2,16,8320]{2,1,0:T(8,128)(2,1)S(1)} %collective-permute-done.3.rest_1_.rest_3_.rest_5_, ...), custom_call_target="tpu_custom_call" | custom-call | flops 5242880 | bytes 2097152 | tf_op jit(solution)/shard_map/aligned_rows/pallas_call | solution.py:348
  13.7 0.0 collective-permute-done.rest_1_
  13.7 7.3 %collective-permute-done.1.rest_2_ = bf16[2,4,4,2048]{3,2,1,0:T(4,128)(2,1)S(1)} collective-permute-done((bf16[2,4,4,2048]{3,2,1,0:T(4,128)(2,1)S(1)}, bf16[2,4,4,2048]{3,2,1,0:T(4,128)(2,1)S(1)}, u32[]{:S(2)}, u32[]{:S(2)}) %collective-permute-start.1) | collective-permute-done | bytes 131104 | tf_op jit(solution)/shard_map/ppermute | solution.py:491
  21.0 0.0 collective-permute-done.2.rest_3_
  21.0 4.8 %partial_logits.3 = (f32[128,128]{1,0:T(8,128)S(1)}, f32[128,128]{1,0:T(8,128)S(1)}) custom-call(s32[3]{0:T(128)S(1)} %pad_add_fusion.ids, f32[1024]{0:T(1024)S(1)} %copy-done.2, f32[8,256]{1,0:T(8,128)S(1)} %copy-done.1, bf16[2,4,4,2048]{3,2,1,0:T(4,128)(2,1)S(1)} %get-tuple-element.24.rest_0_, bf16[2,4,4,2048]{3,2,1,0:T(4,128)(2,1)S(1)} %collective-permute-done.rest_1_, ...), custom_call_target="tpu_custom_call" | custom-call | flops 1073741824 | bytes 1572864 | tf_op jit(solution)/shard_map/partial_logits/pallas_call | solution.py:226
  25.8 0.1 collective-permute-start.4
  25.9 0.0 collective-permute-done.6.rest_4_.rest_1_.rest_3_.rest_7_
  25.9 4.1 %partial_logits.5 = f32[128,128]{1,0:T(8,128)S(1)} custom-call(s32[3]{0:T(128)S(1)} %pad_add_fusion.ids, f32[1024]{0:T(1024)S(1)} %copy-done.2, f32[8,256]{1,0:T(8,128)S(1)} %copy-done.1, bf16[2,4,4,2048]{3,2,1,0:T(4,128)(2,1)S(1)} %get-tuple-element.24.rest_0_, bf16[2,4,4,2048]{3,2,1,0:T(4,128)(2,1)S(1)} %collective-permute-done.rest_1_, ...), custom_call_target="tpu_custom_call" | custom-call | flops 536870912 | bytes 1048576 | tf_op jit(solution)/shard_map/partial_logits/pallas_call | solution.py:226
  30.0 0.6 collective-permute-start.7
  30.6 0.0 collective-permute-done.5.rest_4_.rest_0_.rest_2_.rest_6_
  30.6 4.1 %partial_logits.4 = f32[128,128]{1,0:T(8,128)S(1)} custom-call(s32[3]{0:T(128)S(1)} %pad_add_fusion.ids, f32[1024]{0:T(1024)S(1)} %copy-done.2, f32[8,256]{1,0:T(8,128)S(1)} %copy-done.1, bf16[2,4,4,2048]{3,2,1,0:T(4,128)(2,1)S(1)} %get-tuple-element.24.rest_0_, bf16[2,4,4,2048]{3,2,1,0:T(4,128)(2,1)S(1)} %collective-permute-done.rest_1_, ...), custom_call_target="tpu_custom_call" | custom-call | flops 536870912 | bytes 1048576 | tf_op jit(solution)/shard_map/partial_logits/pallas_call | solution.py:226
  34.6 0.0 collective-permute-done.4
  34.7 0.0 collective-permute-done.7
  34.7 1.6 %collective-permute-start.8 = (f32[2,128,128]{2,1,0:T(8,128)S(1)}, f32[2,128,128]{2,1,0:T(8,128)S(1)}, u32[]{:S(2)}, u32[]{:S(2)}) collective-permute-start(f32[2,128,128]{2,1,0:T(8,128)S(1)} %pad_maximum_fusion.here), channel_id=1, source_target_pairs={{0,8},{4,12},{8,0},{12,4},{1,9},{5,13},{9,1},{13,5},{2,10},{6,14},... | collective-permute-start | bytes 393224 | tf_op jit(solution)/shard_map/ppermute | solution.py:488
  36.3 3.1 %aligned_rows.3.rest_9_ = bf16[2,32,8192]{2,1,0:T(8,128)(2,1)S(1)} custom-call(s32[3]{0:T(128)S(1)} %pad_add_fusion.ids, f32[1024]{0:T(1024)S(1)} %copy-done.2, f32[8,256]{1,0:T(8,128)S(1)} %copy-done.1, bf16[2,16,8320]{2,1,0:T(8,128)(2,1)S(1)} %collective-permute-done.5.rest_4_.rest_0_.rest_2_.rest_6_, ...), custom_call_target="tpu_custom_call" | custom-call | flops 5242880 | bytes 2097152 | tf_op jit(solution)/shard_map/aligned_rows/pallas_call | solution.py:348
  39.4 0.8 %collective-permute-done.8.there = f32[2,128,128]{2,1,0:T(8,128)S(1)} collective-permute-done((f32[2,128,128]{2,1,0:T(8,128)S(1)}, f32[2,128,128]{2,1,0:T(8,128)S(1)}, u32[]{:S(2)}, u32[]{:S(2)}) %collective-permute-start.8) | collective-permute-done | bytes 131104 | tf_op jit(solution)/shard_map/ppermute | solution.py:488
  40.2 0.2 logit_stats.1.rest_0_
  40.4 1.6 %collective-permute-start.10 = (f32[32,128]{1,0:T(8,128)S(1)}, f32[32,128]{1,0:T(8,128)S(1)}, u32[]{:S(2)}, u32[]{:S(2)}) collective-permute-start(f32[32,128]{1,0:T(8,128)S(1)} %logit_stats.1.rest_0_), channel_id=1, source_target_pairs={{0,16},{4,20},{8,24},{12,28},{16,0},{20,4},{24,8},{28,12},{1,17},{... | collective-permute-start | bytes 49160 | tf_op jit(solution)/shard_map/ppermute | solution.py:529
  42.0 0.0 collective-permute-start.11
  42.0 0.6 collective-permute-start.9
  42.6 1.6 %collective-permute-done.10.rest_2_ = f32[32,128]{1,0:T(8,128)S(1)} collective-permute-done((f32[32,128]{1,0:T(8,128)S(1)}, f32[32,128]{1,0:T(8,128)S(1)}, u32[]{:S(2)}, u32[]{:S(2)}) %collective-permute-start.10) | collective-permute-done | bytes 16416 | tf_op jit(solution)/shard_map/ppermute | solution.py:529
  44.2 1.0 %collective-permute-done.11.rest_3_ = f32[32,128]{1,0:T(8,128)S(1)} collective-permute-done((f32[32,128]{1,0:T(8,128)S(1)}, f32[32,128]{1,0:T(8,128)S(1)}, u32[]{:S(2)}, u32[]{:S(2)}) %collective-permute-start.11) | collective-permute-done | bytes 16416 | tf_op jit(solution)/shard_map/ppermute | solution.py:530
  45.2 0.0 collective-permute-done.9.rest_1_
  45.2 2.3 %volume_terms.1 = (f32[16,128]{1,0:T(8,128)S(1)}, f32[2,4,8192]{2,1,0:T(4,128)S(1)}, bf16[2,4,8192]{2,1,0:T(4,128)(2,1)S(1)}, bf16[2,4,8192]{2,1,0:T(4,128)(2,1)S(1)}, bf16[2,4,8192]{2,1,0:T(4,128)(2,1)S(1)}) custom-call(s32[3]{0:T(128)S(1)} %pad_add_fusion.ids, f32[32,128]{1,0:T(8,128)S(1)} %logit_stats.1.rest_0_, ...), custom_call_target="tpu_custom_call" | custom-call | flops 33554432 | bytes 2621440 | tf_op jit(solution)/shard_map/volume_terms/pallas_call | solution.py:428
  47.5 2.9 %collective-permute-start.12 = (bf16[2,4,8192]{2,1,0:T(4,128)(2,1)S(1)}, bf16[2,4,8192]{2,1,0:T(4,128)(2,1)S(1)}, u32[]{:S(2)}, u32[]{:S(2)}) collective-permute-start(bf16[2,4,8192]{2,1,0:T(4,128)(2,1)S(1)} %get-tuple-element.37), channel_id=1, source_target_pairs={{0,3},{1,2},{2,1},{3,0},{4,7},{5,6},{6,5},{7,4},{8,11},{9,10},{10,... | collective-permute-start | bytes 393224 | tf_op jit(solution)/shard_map/ppermute | solution.py:491
  50.4 0.6 collective-permute-start.13
  51.0 1.0 %collective-permute-start.14 = (bf16[2,4,8192]{2,1,0:T(4,128)(2,1)S(1)}, bf16[2,4,8192]{2,1,0:T(4,128)(2,1)S(1)}, u32[]{:S(2)}, u32[]{:S(2)}) collective-permute-start(bf16[2,4,8192]{2,1,0:T(4,128)(2,1)S(1)} %get-tuple-element.39), channel_id=1, source_target_pairs={{0,1},{1,0},{2,3},{3,2},{4,5},{5,4},{6,7},{7,6},{8,9},{9,8},{10,11... | collective-permute-start | bytes 393224 | tf_op jit(solution)/shard_map/ppermute | solution.py:491
  51.9 0.7 %copy.9 = f32[16,4]{0,1:T(4,128)} copy(f32[16,4]{1,0:T(8,128)S(1)} %bitcast.11) | data formatting | bytes 512
  52.6 3.2 %collective-permute-done.12.rest_0_ = bf16[2,4,8192]{2,1,0:T(4,128)(2,1)S(1)} collective-permute-done((bf16[2,4,8192]{2,1,0:T(4,128)(2,1)S(1)}, bf16[2,4,8192]{2,1,0:T(4,128)(2,1)S(1)}, u32[]{:S(2)}, u32[]{:S(2)}) %collective-permute-start.12) | collective-permute-done | bytes 131104 | tf_op jit(solution)/shard_map/ppermute | solution.py:491
  55.8 6.2 %collective-permute-done.13.rest_1_ = bf16[2,4,8192]{2,1,0:T(4,128)(2,1)S(1)} collective-permute-done((bf16[2,4,8192]{2,1,0:T(4,128)(2,1)S(1)}, bf16[2,4,8192]{2,1,0:T(4,128)(2,1)S(1)}, u32[]{:S(2)}, u32[]{:S(2)}) %collective-permute-start.13) | collective-permute-done | bytes 131104 | tf_op jit(solution)/shard_map/ppermute | solution.py:491
  61.9 0.0 collective-permute-done.14.rest_2_
  61.9 0.8 %total_volume.1 = f32[2,4,1,8192]{3,2,1,0:T(1,128)} custom-call(f32[2,4,8192]{2,1,0:T(4,128)S(1)} %get-tuple-element.36.first, bf16[2,4,8192]{2,1,0:T(4,128)(2,1)S(1)} %collective-permute-done.12.rest_0_, bf16[2,4,8192]{2,1,0:T(4,128)(2,1)S(1)} %collective-permute-done.13.rest_1_, bf16[2,4,8192]{2,1,0:T(4,128)(2,1)S(1)} %collective-permute-done.14.rest_2_), custom_call_target="tpu_custom_call" | custom-call | tf_op jit(solution)/shard_map/total_volume/pallas_call | solution.py:473
  (3 shorter events, 0.0 us)
Async XLA Ops:
  0.6 10.1 %copy-start.1 = (f32[8,256]{1,0:T(8,128)S(1)}, f32[8,256]{1,0:T(8,128)}, u32[]{:S(2)}) copy-start(f32[8,256]{1,0:T(8,128)} %constant.17.clone.table_x) | copy-start | bytes 24580
  0.6 10.1 %copy-start.2 = (f32[1024]{0:T(1024)S(1)}, f32[1024]{0:T(1024)}, u32[]{:S(2)}) copy-start(f32[1024]{0:T(1024)} %constant.18.clone.table_y) | copy-start | bytes 12292
  0.7 10.1 %copy-start = (bf16[2,16,32768]{2,1,0:T(8,128)(2,1)S(1)}, bf16[2,16,32768]{2,1,0:T(8,128)(2,1)}, u32[]{:S(2)}) copy-start(bf16[2,16,32768]{2,1,0:T(8,128)(2,1)} %rest_4_.1) | copy-start | bytes 6291460
  2.9 7.8 %collective-permute-start.3 = (bf16[2,16,8320]{2,1,0:T(8,128)(2,1)S(1)}, bf16[2,16,8320]{2,1,0:T(8,128)(2,1)S(1)}, u32[]{:S(2)}, u32[]{:S(2)}) collective-permute-start(bf16[2,16,8320]{2,1,0:T(8,128)(2,1)S(1)} %get-tuple-element.23), channel_id=1, source_target_pairs={{0,4},{4,0},{8,12},{12,8},{1,5},{5,1},{9,13},{13,9},{2,6},{6,2},{1... | collective-permute-start | bytes 1597448 | tf_op jit(solution)/shard_map/ppermute | solution.py:488
  3.4 22.5 %collective-permute-start.6 = (bf16[2,16,8320]{2,1,0:T(8,128)(2,1)S(1)}, bf16[2,16,8320]{2,1,0:T(8,128)(2,1)S(1)}, u32[]{:S(2)}, u32[]{:S(2)}) collective-permute-start(bf16[2,16,8320]{2,1,0:T(8,128)(2,1)S(1)} %get-tuple-element.31), channel_id=1, source_target_pairs={{0,12},{4,8},{8,4},{12,0},{1,13},{5,9},{9,5},{13,1},{2,14},{6,10},... | collective-permute-start | bytes 1597448 | tf_op jit(solution)/shard_map/ppermute | solution.py:488
  6.0 24.6 %collective-permute-start.5 = (bf16[2,16,8320]{2,1,0:T(8,128)(2,1)S(1)}, bf16[2,16,8320]{2,1,0:T(8,128)(2,1)S(1)}, u32[]{:S(2)}, u32[]{:S(2)}) collective-permute-start(bf16[2,16,8320]{2,1,0:T(8,128)(2,1)S(1)} %get-tuple-element.30), channel_id=1, source_target_pairs={{0,8},{4,12},{8,0},{12,4},{1,9},{5,13},{9,1},{13,5},{2,10},{6,14},... | collective-permute-start | bytes 1597448 | tf_op jit(solution)/shard_map/ppermute | solution.py:488
  6.0 7.7 %collective-permute-start = (bf16[2,4,4,2048]{3,2,1,0:T(4,128)(2,1)S(1)}, bf16[2,4,4,2048]{3,2,1,0:T(4,128)(2,1)S(1)}, u32[]{:S(2)}, u32[]{:S(2)}) collective-permute-start(bf16[2,4,4,2048]{3,2,1,0:T(4,128)(2,1)S(1)} %get-tuple-element.24.rest_0_), channel_id=1, source_target_pairs={{0,1},{1,0},{2,3},{3,2},{4,5},{5,4},{6,7},{7,6},{8,9},{9,8},{10,11... | collective-permute-start | bytes 393224 | tf_op jit(solution)/shard_map/ppermute | solution.py:491
  8.1 12.9 %collective-permute-start.1 = (bf16[2,4,4,2048]{3,2,1,0:T(4,128)(2,1)S(1)}, bf16[2,4,4,2048]{3,2,1,0:T(4,128)(2,1)S(1)}, u32[]{:S(2)}, u32[]{:S(2)}) collective-permute-start(bf16[2,4,4,2048]{3,2,1,0:T(4,128)(2,1)S(1)} %get-tuple-element.24.rest_0_), channel_id=1, source_target_pairs={{0,2},{1,3},{2,0},{3,1},{4,6},{5,7},{6,4},{7,5},{8,10},{9,11},{10,... | collective-permute-start | bytes 393224 | tf_op jit(solution)/shard_map/ppermute | solution.py:491
  10.7 10.3 %collective-permute-start.2 = (bf16[2,4,4,2048]{3,2,1,0:T(4,128)(2,1)S(1)}, bf16[2,4,4,2048]{3,2,1,0:T(4,128)(2,1)S(1)}, u32[]{:S(2)}, u32[]{:S(2)}) collective-permute-start(bf16[2,4,4,2048]{3,2,1,0:T(4,128)(2,1)S(1)} %get-tuple-element.24.rest_0_), channel_id=1, source_target_pairs={{0,3},{1,2},{2,1},{3,0},{4,7},{5,6},{6,5},{7,4},{8,11},{9,10},{10,... | collective-permute-start | bytes 393224 | tf_op jit(solution)/shard_map/ppermute | solution.py:491
  25.8 8.8 %collective-permute-start.4 = (f32[128,128]{1,0:T(8,128)S(1)}, f32[128,128]{1,0:T(8,128)S(1)}, u32[]{:S(2)}, u32[]{:S(2)}) collective-permute-start(f32[128,128]{1,0:T(8,128)S(1)} %get-tuple-element.29), channel_id=1, source_target_pairs={{0,4},{4,0},{8,12},{12,8},{1,5},{5,1},{9,13},{13,9},{2,6},{6,2},{1... | collective-permute-start | bytes 196616 | tf_op jit(solution)/shard_map/ppermute | solution.py:488
  30.0 4.7 %collective-permute-start.7 = (f32[128,128]{1,0:T(8,128)S(1)}, f32[128,128]{1,0:T(8,128)S(1)}, u32[]{:S(2)}, u32[]{:S(2)}) collective-permute-start(f32[128,128]{1,0:T(8,128)S(1)} %partial_logits.5), channel_id=1, source_target_pairs={{0,4},{4,0},{8,12},{12,8},{1,5},{5,1},{9,13},{13,9},{2,6},{6,2},{1... | collective-permute-start | bytes 196616 | tf_op jit(solution)/shard_map/ppermute | solution.py:488
  34.7 5.5 %collective-permute-start.8 = (f32[2,128,128]{2,1,0:T(8,128)S(1)}, f32[2,128,128]{2,1,0:T(8,128)S(1)}, u32[]{:S(2)}, u32[]{:S(2)}) collective-permute-start(f32[2,128,128]{2,1,0:T(8,128)S(1)} %pad_maximum_fusion.here), channel_id=1, source_target_pairs={{0,8},{4,12},{8,0},{12,4},{1,9},{5,13},{9,1},{13,5},{2,10},{6,14},... | collective-permute-start | bytes 393224 | tf_op jit(solution)/shard_map/ppermute | solution.py:488
  40.4 3.8 %collective-permute-start.10 = (f32[32,128]{1,0:T(8,128)S(1)}, f32[32,128]{1,0:T(8,128)S(1)}, u32[]{:S(2)}, u32[]{:S(2)}) collective-permute-start(f32[32,128]{1,0:T(8,128)S(1)} %logit_stats.1.rest_0_), channel_id=1, source_target_pairs={{0,16},{4,20},{8,24},{12,28},{16,0},{20,4},{24,8},{28,12},{1,17},{... | collective-permute-start | bytes 49160 | tf_op jit(solution)/shard_map/ppermute | solution.py:529
  42.0 3.2 %collective-permute-start.11 = (f32[32,128]{1,0:T(8,128)S(1)}, f32[32,128]{1,0:T(8,128)S(1)}, u32[]{:S(2)}, u32[]{:S(2)}) collective-permute-start(f32[32,128]{1,0:T(8,128)S(1)} %logit_stats.1.rest_0_), channel_id=1, source_target_pairs={{0,20},{4,16},{8,28},{12,24},{16,4},{20,0},{24,12},{28,8},{1,21},{... | collective-permute-start | bytes 49160 | tf_op jit(solution)/shard_map/ppermute | solution.py:530
  42.0 3.2 %collective-permute-start.9 = (f32[32,128]{1,0:T(8,128)S(1)}, f32[32,128]{1,0:T(8,128)S(1)}, u32[]{:S(2)}, u32[]{:S(2)}) collective-permute-start(f32[32,128]{1,0:T(8,128)S(1)} %logit_stats.1.rest_0_), channel_id=1, source_target_pairs={{0,4},{4,0},{8,12},{12,8},{1,5},{5,1},{9,13},{13,9},{2,6},{6,2},{1... | collective-permute-start | bytes 49160 | tf_op jit(solution)/shard_map/ppermute | solution.py:488
  47.5 8.3 %collective-permute-start.12 = (bf16[2,4,8192]{2,1,0:T(4,128)(2,1)S(1)}, bf16[2,4,8192]{2,1,0:T(4,128)(2,1)S(1)}, u32[]{:S(2)}, u32[]{:S(2)}) collective-permute-start(bf16[2,4,8192]{2,1,0:T(4,128)(2,1)S(1)} %get-tuple-element.37), channel_id=1, source_target_pairs={{0,3},{1,2},{2,1},{3,0},{4,7},{5,6},{6,5},{7,4},{8,11},{9,10},{10,... | collective-permute-start | bytes 393224 | tf_op jit(solution)/shard_map/ppermute | solution.py:491
  50.4 11.6 %collective-permute-start.13 = (bf16[2,4,8192]{2,1,0:T(4,128)(2,1)S(1)}, bf16[2,4,8192]{2,1,0:T(4,128)(2,1)S(1)}, u32[]{:S(2)}, u32[]{:S(2)}) collective-permute-start(bf16[2,4,8192]{2,1,0:T(4,128)(2,1)S(1)} %get-tuple-element.38), channel_id=1, source_target_pairs={{0,2},{1,3},{2,0},{3,1},{4,6},{5,7},{6,4},{7,5},{8,10},{9,11},{10,... | collective-permute-start | bytes 393224 | tf_op jit(solution)/shard_map/ppermute | solution.py:491
  51.0 11.0 %collective-permute-start.14 = (bf16[2,4,8192]{2,1,0:T(4,128)(2,1)S(1)}, bf16[2,4,8192]{2,1,0:T(4,128)(2,1)S(1)}, u32[]{:S(2)}, u32[]{:S(2)}) collective-permute-start(bf16[2,4,8192]{2,1,0:T(4,128)(2,1)S(1)} %get-tuple-element.39), channel_id=1, source_target_pairs={{0,1},{1,0},{2,3},{3,2},{4,5},{5,4},{6,7},{7,6},{8,9},{9,8},{10,11... | collective-permute-start | bytes 393224 | tf_op jit(solution)/shard_map/ppermute | solution.py:491

commit v4 on v3

v4 whole, which is shorter than its diff:
```python
import functools
import math

import jax
import jax.numpy as jnp
import numpy as np
from jax import lax
from jax.experimental import pallas as pl
from jax.experimental.pallas import tpu as pltpu
from jax.sharding import PartitionSpec as P

IMG = 256
TX = 8
TY = 8
HALF = TX // 2
LANES = 128
SUBLANES = 8
VMEM_BYTES = 24 * 1024 * 1024
VMEM_SPEC = pl.BlockSpec(memory_space=pltpu.VMEM)
SMEM_SPEC = pl.BlockSpec(memory_space=pltpu.SMEM)
BF = jnp.bfloat16
F32 = jnp.float32


def trig_tables():
    steps = np.arange(1, HALF + 1)
    angle_x = 2.0 * math.pi / IMG * steps[:, None] * (np.arange(IMG) - IMG // 2)[None, :]
    angle_y = 2.0 * math.pi / IMG * np.arange(IMG // 2)[:, None] * steps[None, :]
    table_x = np.concatenate([np.cos(angle_x), np.sin(angle_x)], 0).astype(np.float32)
    table_y = np.concatenate([np.cos(angle_y), np.sin(angle_y)], 1).astype(np.float32)
    return table_x, table_y.reshape(-1)


def xor_pairs(size, step):
    return [(i, i ^ step) for i in range(size)]


def column_of(line):
    size = line.shape[1]
    rows = lax.broadcasted_iota(jnp.int32, (size, size), 0)
    cols = lax.broadcasted_iota(jnp.int32, (size, size), 1)
    return jnp.sum(jnp.where(rows == cols, line, 0.0), axis=1, keepdims=True)


def bands_kernel(steps, ids, images, references, *rest):
    lists, rest = rest[:3], rest[3:]
    outs, meta, shard = rest[: len(steps)], rest[len(steps)], rest[len(steps) + 1]
    lines, sems, meta_sems, line_sems, shard_sem = rest[len(steps) + 2 :]
    width = outs[0].shape[2] - LANES
    copies = [pltpu.make_async_copy(references, shard, shard_sem)]
    for place, (step, out) in enumerate(zip(steps, outs)):
        start = pl.multiple_of((ids[0] ^ step) * width, width)
        for part in range(out.shape[0]):
            copies.append(
                pltpu.make_async_copy(
                    images.at[part, :, pl.ds(start, width)],
                    out.at[part, :, pl.ds(0, width)],
                    sems.at[place, part],
                )
            )
    line_copies = [
        pltpu.make_async_copy(source, lines[place], line_sems.at[place])
        for place, source in enumerate(lists)
    ]
    for copy in line_copies + copies:
        copy.start()
    for copy in line_copies:
        copy.wait()
    lane = lax.broadcasted_iota(jnp.int32, meta.shape[1:], 1)
    fixed = column_of(lines[2][...])
    high = fixed.astype(BF).astype(F32)
    middle = (fixed - high).astype(BF).astype(F32)
    values = [column_of(lines[0][...].astype(F32)), column_of(lines[1][...].astype(F32))]
    table = jnp.zeros(meta.shape[1:], F32)
    for place, value in enumerate(values + [high, middle, fixed - high - middle]):
        table = jnp.where(lane == place, value, table)
    meta[0] = table.astype(BF)
    meta[1] = jnp.zeros(meta.shape[1:], BF)
    meta_copies = [
        pltpu.make_async_copy(meta, out.at[:, :, pl.ds(width, LANES)], meta_sems.at[place])
        for place, out in enumerate(outs)
    ]
    for copy in meta_copies:
        copy.start()
    for copy in copies + meta_copies:
        copy.wait()


def image_bands(ids, orient_lists, shift_ids, fixed_weights, images, references, dom):
    parts, rows, pixels = images.shape
    width = pixels // dom
    steps = list(range(1, dom))
    sources = [images, references] + [
        array.reshape(1, rows) for array in (orient_lists, shift_ids, fixed_weights)
    ]
    sources = [pltpu.with_memory_space_constraint(array, pltpu.HBM) for array in sources]
    *bands, meta, shard = pl.pallas_call(
        functools.partial(bands_kernel, steps),
        out_shape=[pltpu.VMEM((parts, rows, width + LANES), images.dtype)] * len(steps)
        + [
            jax.ShapeDtypeStruct((parts, rows, LANES), BF),
            pltpu.VMEM(references.shape, references.dtype),
        ],
        in_specs=[pl.BlockSpec(memory_space=pltpu.SMEM)]
        + [pl.BlockSpec(memory_space=pl.ANY)] * len(sources),
        out_specs=[pl.BlockSpec(memory_space=pl.ANY)] * len(steps)
        + [pl.BlockSpec(memory_space=pltpu.VMEM), pl.BlockSpec(memory_space=pl.ANY)],
        scratch_shapes=[
            [pltpu.VMEM((1, rows), array.dtype) for array in sources[2:]],
            pltpu.SemaphoreType.DMA((len(steps), parts)),
            pltpu.SemaphoreType.DMA((len(steps),)),
            pltpu.SemaphoreType.DMA((3,)),
            pltpu.SemaphoreType.DMA,
        ],
        compiler_params=pltpu.CompilerParams(vmem_limit_bytes=VMEM_BYTES),
        cost_estimate=pl.CostEstimate(
            flops=0, bytes_accessed=4 * parts * rows * (pixels - width), transcendentals=0
        ),
        name="image_bands",
    )(ids, *sources)
    return bands, meta, shard


def own_kernel(ids, images, band, sems):
    width = band.shape[2]
    start = pl.multiple_of(ids[0] * width, width)
    copies = [
        pltpu.make_async_copy(images.at[part, :, pl.ds(start, width)], band.at[part], sems.at[part])
        for part in range(band.shape[0])
    ]
    for copy in copies:
        copy.start()
    for copy in copies:
        copy.wait()


def own_band(ids, images, dom):
    parts, rows, pixels = images.shape
    shape = (parts, rows, pixels // dom)
    return pl.pallas_call(
        own_kernel,
        out_shape=pltpu.VMEM(shape, images.dtype),
        in_specs=[pl.BlockSpec(memory_space=pltpu.SMEM), pl.BlockSpec(memory_space=pl.ANY)],
        out_specs=pl.BlockSpec(memory_space=pl.ANY),
        scratch_shapes=[pltpu.SemaphoreType.DMA((parts,))],
        compiler_params=pltpu.CompilerParams(vmem_limit_bytes=VMEM_BYTES),
        name="own_band",
    )(ids, pltpu.with_memory_space_constraint(images, pltpu.HBM))


def in_vmem(arrays):
    placed = [pltpu.with_memory_space_constraint(array, pltpu.VMEM) for array in arrays]
    return placed, [VMEM_SPEC] * len(placed)


def logits_kernel(groups, orients, ids, table_y, table_x, *rest):
    shards, rest = rest[:orients], rest[orients:]
    images, rest = rest[:groups], rest[groups:]
    outs, (refs, left, right) = rest[:groups], rest[groups:]
    chunk = shards[0].shape[3]
    rows = images[0].shape[1]
    group_rows = TX * rows
    names = refs.shape[1]
    lines = chunk // IMG
    per_class = shards[0].shape[2]
    for place, shard in enumerate(shards):
        cols = slice(place * chunk, (place + 1) * chunk)
        for part in range(2):
            for k in range(shard.shape[1]):
                refs[part, k * per_class : (k + 1) * per_class, cols] = shard[part, k]
    for out in outs:
        out[...] = jnp.zeros_like(out)

    def add_shard(step, carry):
        column = ids[1] ^ step
        line_base = (ids[0] * orients + column) * lines
        for line in range(lines):
            to_re = slice(2 * line * IMG, (2 * line + 1) * IMG)
            to_im = slice((2 * line + 1) * IMG, (2 * line + 2) * IMG)
            base = (line_base + line) * TY
            ref_cols = pl.ds(pl.multiple_of(step * chunk + line * IMG, IMG), IMG)
            ref_re = refs[0, :, ref_cols].astype(F32)
            ref_im = refs[1, :, ref_cols].astype(F32)

            def put_ref(b, re, im):
                right[b * names : (b + 1) * names, to_re] = re.astype(BF)
                right[b * names : (b + 1) * names, to_im] = im.astype(BF)

            put_ref(TY // 2, ref_re, ref_im)
            for t in range(1, HALF + 1):
                cosine = table_y[base + t - 1]
                sine = table_y[base + HALF + t - 1]
                re_c, im_s = ref_re * cosine, ref_im * sine
                im_c, re_s = ref_im * cosine, ref_re * sine
                put_ref(TY // 2 - t, re_c - im_s, im_c + re_s)
                if t < HALF:
                    put_ref(TY // 2 + t, re_c + im_s, im_c - re_s)
            for g in range(groups):
                cols = pl.ds(pl.multiple_of(column * chunk + line * IMG, IMG), IMG)
                re = images[g][0, :, cols].astype(F32)
                im = images[g][1, :, cols].astype(F32)

                def put(a, re, im):
                    top = g * group_rows + a * rows
                    left[top : top + rows, to_re] = re.astype(BF)
                    left[top : top + rows, to_im] = im.astype(BF)

                put(TX // 2, re, im)
                for t in range(1, HALF + 1):
                    cosine = table_x[t - 1 : t, :]
                    sine = table_x[HALF + t - 1 : HALF + t, :]
                    re_c, im_s = re * cosine, im * sine
                    re_s, im_c = re * sine, im * cosine
                    put(TX // 2 - t, re_c + im_s, im_c - re_s)
                    if t < HALF:
                        put(TX // 2 + t, re_c - im_s, re_s + im_c)
        value = lax.dot_general(
            left[...], right[...], (((1,), (1,)), ((), ())), preferred_element_type=F32
        )
        for g in range(groups):
            outs[g][...] += value[g * group_rows : (g + 1) * group_rows]
        return carry

    lax.fori_loop(0, orients, add_shard, 0)


def partial_logits(ids, table_x, table_y, shards, picked):
    parts, classes, orients, chunk = shards[0].shape
    groups = len(picked)
    rows = picked[0][0].shape[1]
    names = classes * orients
    count = len(shards)
    out_shape = (TX * rows, TY * names)
    arrays, specs = in_vmem([table_x, *shards, *(image for image, _ in picked)])
    return pl.pallas_call(
        functools.partial(logits_kernel, groups, count),
        out_shape=[pltpu.VMEM(out_shape, F32)] * groups,
        in_specs=[SMEM_SPEC] * 2 + specs,
        out_specs=[VMEM_SPEC] * groups,
        scratch_shapes=[
            pltpu.VMEM((parts, names, count * chunk), BF),
            pltpu.VMEM((groups * TX * rows, 2 * chunk), BF),
            pltpu.VMEM((TY * names, 2 * chunk), BF),
        ],
        compiler_params=pltpu.CompilerParams(vmem_limit_bytes=VMEM_BYTES),
        cost_estimate=pl.CostEstimate(
            flops=4 * groups * TX * rows * TY * names * count * chunk,
            bytes_accessed=4 * count * chunk * (groups * rows + names),
            transcendentals=0,
        ),
        name="partial_logits",
    )(ids, table_y, *arrays)


def stats_kernel(swap, classes, orients, here, there, out):
    groups, group_rows, lanes = here.shape
    rows = group_rows // TX
    lane = lax.broadcasted_iota(jnp.int32, (rows, lanes), 1)
    class_of = (lane // orients) % classes
    out_lane = lax.broadcasted_iota(jnp.int32, (rows, LANES), 1)
    for g in range(groups):
        logits = here[g] + there[g ^ swap]
        pieces = [logits[a * rows : (a + 1) * rows] for a in range(TX)]
        top = functools.reduce(jnp.maximum, pieces)
        top = jnp.max(top, axis=1, keepdims=True)
        sums = sum(jnp.exp(piece - top) for piece in pieces)
        line = jnp.where(out_lane == 0, top, 0.0)
        for k in range(classes):
            part = jnp.sum(jnp.where(class_of == k, sums, 0.0), axis=1, keepdims=True)
            line = jnp.where(out_lane == k + 1, part, line)
        out[g * rows : (g + 1) * rows, :] = line


def logit_stats(here, there, swap, classes, orients):
    groups, group_rows, lanes = here.shape
    arrays, specs = in_vmem([here, there])
    return pl.pallas_call(
        functools.partial(stats_kernel, swap, classes, orients),
        out_shape=pltpu.VMEM((groups * group_rows // TX, LANES), F32),
        in_specs=specs,
        out_specs=VMEM_SPEC,
        compiler_params=pltpu.CompilerParams(vmem_limit_bytes=VMEM_BYTES),
        cost_estimate=pl.CostEstimate(
            flops=4 * here.size, bytes_accessed=8 * here.size, transcendentals=here.size
        ),
        name="logit_stats",
    )(*arrays)


def rows_kernel(groups, ids, table_y, table_x, *rest):
    metas, images = rest[:groups], rest[groups : 2 * groups]
    out = rest[2 * groups]
    rows = metas[0].shape[1]
    width = out.shape[2]
    lines = width // IMG
    line_base = ids[0] * lines
    for g in range(groups):
        own = slice(g * rows, (g + 1) * rows)
        last = metas[g].shape[2] - LANES
        shift = metas[g][0, :, last:].astype(F32)[:, 1:2].astype(jnp.int32)
        move_x = jnp.broadcast_to(shift % TX - TX // 2, (rows, IMG))
        move_y = jnp.broadcast_to(shift // TX - TY // 2, (rows, LANES))
        phase_c = jnp.ones((rows, IMG), F32)
        phase_s = jnp.zeros((rows, IMG), F32)
        for t in range(1, HALF + 1):
            hit = jnp.abs(move_x) == t
            phase_c = jnp.where(hit, table_x[t - 1 : t, :], phase_c)
            phase_s = jnp.where(hit, table_x[HALF + t - 1 : HALF + t, :], phase_s)
        phase_s = jnp.where(move_x < 0, -phase_s, phase_s)
        hits = [jnp.abs(move_y) == t for t in range(1, HALF + 1)]
        sign = jnp.where(move_y < 0, -1.0, 1.0)

        def add_line(line, carry):
            base = (line_base + line) * TY
            cos_y = jnp.ones((rows, LANES), F32)
            sin_y = jnp.zeros((rows, LANES), F32)
            for t in range(1, HALF + 1):
                cos_y = jnp.where(hits[t - 1], table_y[base + t - 1], cos_y)
                sin_y = jnp.where(hits[t - 1], table_y[base + HALF + t - 1], sin_y)
            sin_y = sin_y * sign
            for part in range(IMG // LANES):
                across = slice(part * LANES, (part + 1) * LANES)
                start = pl.multiple_of(line * IMG + part * LANES, LANES)
                cols = pl.ds(start, LANES)
                cos_x, sin_x = phase_c[:, across], phase_s[:, across]
                cosine = cos_x * cos_y - sin_x * sin_y
                sine = sin_x * cos_y + cos_x * sin_y
                re = images[g][0, :, cols].astype(F32)
                im = images[g][1, :, cols].astype(F32)
                out[0, own, cols] = (re * cosine - im * sine).astype(BF)
                out[1, own, cols] = (re * sine + im * cosine).astype(BF)
            return carry

        lax.fori_loop(0, lines, add_line, 0, unroll=min(lines, 4))


def aligned_rows(ids, table_x, table_y, picked, width):
    parts, rows = picked[0][0].shape[:2]
    groups = len(picked)
    arrays, specs = in_vmem(
        [table_x] + [table for _, table in picked] + [image for image, _ in picked]
    )
    return pl.pallas_call(
        functools.partial(rows_kernel, groups),
        out_shape=pltpu.VMEM((parts, groups * rows, width), BF),
        in_specs=[SMEM_SPEC] * 2 + specs,
        out_specs=VMEM_SPEC,
        compiler_params=pltpu.CompilerParams(vmem_limit_bytes=VMEM_BYTES),
        cost_estimate=pl.CostEstimate(
            flops=20 * groups * rows * width,
            bytes_accessed=8 * groups * rows * width,
            transcendentals=0,
        ),
        name="aligned_rows",
    )(ids, table_y, *arrays)


def volume_kernel(groups, orients, classes, ids, *rest):
    stats, metas = rest[:4], rest[4 : 4 + groups]
    near, far = rest[4 + groups], rest[5 + groups]
    prob, outs = rest[6 + groups], rest[7 + groups :]
    rows = metas[0].shape[1]
    width = near.shape[2]
    chunk = min(width, 8 * IMG)
    lane = lax.broadcasted_iota(jnp.int32, (rows, LANES), 1)
    pieces = []
    for g in range(groups):
        mine, other = (stats[0], stats[2]) if g % 2 == 0 else (stats[1], stats[3])
        place = g // 2
        mine = mine[place * rows : (place + 1) * rows, :]
        other = other[place * rows : (place + 1) * rows, :]
        top = jnp.maximum(mine[:, 0:1], other[:, 0:1])
        mine_scale = jnp.exp(mine[:, 0:1] - top)
        other_scale = jnp.exp(other[:, 0:1] - top)
        held = (lane >= 1) & (lane <= classes)
        both = jnp.where(held, mine * mine_scale + other * other_scale, 0.0)
        totals = jnp.sum(both, axis=1, keepdims=True)
        spread = jnp.zeros((rows, LANES), F32)
        for k in range(classes):
            spread = jnp.where(lane % SUBLANES == k, mine[:, k + 1 : k + 2], spread)
        class_prob = spread * mine_scale / totals
        if g == 0:
            prob[...] = class_prob
        last = metas[g].shape[2] - LANES
        table = metas[g][0, :, last:].astype(F32)
        fixed = table[:, 2:3] + table[:, 3:4] + table[:, 4:5]
        weight = (fixed * class_prob).astype(BF).astype(F32)
        bin_of = table[:, 0:1].astype(jnp.int32) ^ ids[1]
        pieces.append(jnp.where(lane // SUBLANES == bin_of, weight, 0.0))
    mixes = []
    for held in (pieces[:2], pieces[2:]):
        mixing = jnp.transpose(jnp.concatenate(held, axis=0))
        mixes.append(mixing[: orients * SUBLANES].astype(BF))
    for part in range(2):
        for column in range(0, width, chunk):
            cols = slice(column, column + chunk)
            value = jnp.dot(mixes[0], near[part, :, cols], preferred_element_type=F32)
            value += jnp.dot(mixes[1], far[part, :, cols], preferred_element_type=F32)
            for o in range(orients):
                term = value[o * SUBLANES : o * SUBLANES + classes]
                outs[o][part, :, cols] = term.astype(outs[o].dtype)


def volume_terms(ids, stats, groups, near, far, orients, classes):
    parts, entries, width = near.shape
    rest = far.shape[1]
    rows = groups[0][0].shape[1]
    out_shape = (parts, classes, width)
    arrays, specs = in_vmem([*stats, *(table for _, table in groups), near, far])
    return pl.pallas_call(
        functools.partial(volume_kernel, len(groups), orients, classes),
        out_shape=[jax.ShapeDtypeStruct((rows, LANES), F32)]
        + [pltpu.VMEM(out_shape, F32 if o == 0 else BF) for o in range(orients)],
        in_specs=[SMEM_SPEC] + specs,
        out_specs=[VMEM_SPEC] * (1 + orients),
        compiler_params=pltpu.CompilerParams(vmem_limit_bytes=VMEM_BYTES),
        cost_estimate=pl.CostEstimate(
            flops=4 * orients * classes * (entries + rest) * width,
            bytes_accessed=4 * (entries + rest) * width + 4 * orients * classes * width,
            transcendentals=0,
        ),
        name="volume_terms",
    )(ids, *arrays)


def total_kernel(first, *rest):
    out = rest[-1]
    total = first[...]
    for term in rest[:-1]:
        total = total + term[...].astype(F32)
    for part in range(out.shape[0]):
        for k in range(out.shape[1]):
            out[part, k] = total[part, k : k + 1]


def total_volume(terms):
    parts, classes, width = terms[0].shape
    arrays, specs = in_vmem(terms)
    return pl.pallas_call(
        total_kernel,
        out_shape=jax.ShapeDtypeStruct((parts, classes, 1, width), F32),
        in_specs=specs,
        compiler_params=pltpu.CompilerParams(vmem_limit_bytes=VMEM_BYTES),
        name="total_volume",
    )(*arrays)


def local(dom, orient, cls, references, images, orient_lists, shift_ids, fixed_weights):
    classes, orients = references.shape[1], references.shape[2]
    table_x, table_y = (jnp.asarray(t) for t in trig_tables())
    ids = jnp.stack([lax.axis_index(name) for name in ("dom", "orient", "cls")])
    ids = ids.astype(jnp.int32)

    def swap_dom(array, step):
        return lax.ppermute(array, "dom", xor_pairs(dom, step))

    def swap_orient(array, step):
        return lax.ppermute(array, "orient", xor_pairs(orient, step))

    bands, meta, shard = image_bands(
        ids, orient_lists, shift_ids, fixed_weights, images, references, dom
    )
    arrived = {step: swap_dom(bands[step - 1], step) for step in [1, *range(dom - 1, 1, -1)]}
    shards = [shard] + [swap_orient(shard, step) for step in range(1, orient)]
    groups = [(own_band(ids, images, dom), meta)] + [(arrived[step], arrived[step]) for step in range(1, dom)]

    def logits_of(picked):
        return partial_logits(ids, table_x, table_y, shards, picked)

    width = images.shape[2] // dom
    aligned_near = aligned_rows(ids, table_x, table_y, groups[:2], width)
    *shards, aligned_near = lax.optimization_barrier((*shards, aligned_near))
    partial = [None] * dom
    partial[0:2] = logits_of(groups[:2])
    partial[3::2] = logits_of(groups[3::2])
    partial[2::2] = logits_of(groups[2::2])
    kept = [partial[s] + swap_dom(partial[s ^ 1], 1) for s in range(0, dom, 2)]
    here = jnp.stack(kept)
    step = 2
    there, swap = jnp.zeros_like(here), 0
    while step < dom:
        there, swap = swap_dom(here, step), step // 2
        if step * 2 < dom:
            order = np.arange(dom // 2) ^ swap
            here = here + jnp.stack([there[i] for i in order])
        step *= 2
    aligned_far = aligned_rows(ids, table_x, table_y, groups[2:], width)
    there, aligned_far = lax.optimization_barrier((there, aligned_far))
    stats = logit_stats(here, there, swap, classes, orients)

    pairs = [(i, i ^ dom) for i in range(cls * dom)]
    cross = [(i, i ^ dom ^ 1) for i in range(cls * dom)]
    stats_all = [
        stats,
        swap_dom(stats, 1),
        lax.ppermute(stats, ("cls", "dom"), pairs),
        lax.ppermute(stats, ("cls", "dom"), cross),
    ]
    prob, *terms = volume_terms(
        ids, stats_all, groups, aligned_near, aligned_far, orients, classes
    )
    terms = [terms[0]] + [swap_orient(terms[o], o) for o in range(orients - 1, 0, -1)]
    return prob[:, :classes], total_volume(terms)


def solution(mesh):
    in_specs = (
        P(None, "cls", None, ("dom", "orient")),
        P(None, ("dom", "orient"), None),
        P(("dom", "orient"), None),
        P(("dom", "orient"), None),
        P(("dom", "orient"), None),
    )
    out_specs = (P(("dom", "orient"), "cls"), P(None, "cls", "orient", "dom"))
    body = functools.partial(local, mesh.shape["dom"], mesh.shape["orient"], mesh.shape["cls"])
    return jax.shard_map(body, mesh=mesh, in_specs=in_specs, out_specs=out_specs, check_vma=False)
```

time: 62.9 us -> 60.1 us (0.955)
  Pallas kernels: 24.4 us -> 20.1 us
  waiting for transfers between devices: 20.1 us -> 21.4 us
    pallas_call x5 -> x6, Pallas kernels: 19 us -> 15.4 us  [the longest x3 10.4 us: partial_logits(): pl.pallas_call(functools.partial(logits_kernel, groups, count), out_shape...]
    ppermute x7, waiting for transfers between devices: 0.86 us -> 3.02 us  [swap_dom(): return lax.ppermute(array, 'dom', xor_pairs(dom, step))]
    ppermute x6, waiting for transfers between devices: 16.6 us -> 15.9 us  [swap_orient(): return lax.ppermute(array, 'orient', xor_pairs(orient, step))]
    pallas_call x1, Pallas kernels: 2.3 us -> 1.57 us  [volume_terms(): pl.pallas_call(functools.partial(volume_kernel, len(groups), orients, cla...]
  transfers between devices with their start and end apart: 15 -> 15, of which waited for: 6 -> 7; matrix products, arithmetic and copies ran while one was open for 1% -> 1% of each run, Pallas kernels for 30% -> 26%
where the time goes in v4:
time: 60.1 us; the launch traced here: 59.9 us
  waiting for transfers between devices  21.4 us (36%)
  Pallas kernels  20.1 us (33%)
  starting transfers between devices  16.9 us (28%)
  between operations  0.79 us (1%)
  local copies, waits for them, and re-layouts  0.66 us (1%)
    ppermute x6, waiting for transfers between devices, swap_orient(): return lax.ppermute(array, 'orient', xor_pairs(orient, step))  15.9 us
    pallas_call x3, Pallas kernels, partial_logits(): pl.pallas_call(functools.partial(logits_kernel, groups, count), out_shape...  10.4 us
    ppermute x6, starting transfers between devices, swap_orient(): return lax.ppermute(array, 'orient', xor_pairs(orient, step))  9.11 us
    ppermute x7, starting transfers between devices, swap_dom(): return lax.ppermute(array, 'dom', xor_pairs(dom, step))  6.26 us
    pallas_call x2, Pallas kernels, aligned_rows(): pl.pallas_call(functools.partial(rows_kernel, groups), out_shape=pltpu.VM...  3.46 us
    ppermute x7, waiting for transfers between devices, swap_dom(): return lax.ppermute(array, 'dom', xor_pairs(dom, step))  3.02 us
    pallas_call x1, Pallas kernels, image_bands(): pl.pallas_call(functools.partial(bands_kernel, steps), out_shape=[pltpu.V...  2.1 us
    ppermute x1, waiting for transfers between devices, local(): lax.ppermute(stats, ('cls', 'dom'), pairs)  1.6 us
  transfers between devices with their start and end apart: 15, of which 7 were waited for; matrix products, arithmetic and copies ran while one was open for 1% of the time, Pallas kernels for 26%

profile of v4, /device:TPU:0, one launch (start us, length us, event | category | flops | bytes accessed | tf_op | source)
XLA Modules:
  0.0 59.9 jit_solution(3548665715166774125)
XLA Ops:
  0.6 0.1 pad_add_fusion.ids
  0.7 0.0 copy-start
  0.7 0.0 copy-start.1
  0.7 2.1 %image_bands.1 = (bf16[2,16,8320]{2,1,0:T(8,128)(2,1)S(1)}, bf16[2,16,8320]{2,1,0:T(8,128)(2,1)S(1)}, bf16[2,16,8320]{2,1,0:T(8,128)(2,1)S(1)}, bf16[2,16,128]{2...) custom-call(s32[3]{0:T(128)S(1)} %pad_add_fusion.ids, bf16[2,16,32768]{2,1,0:T(8,128)(2,1)} %images.3, ...), custom_call_target="tpu_custom_call" | custom-call | bytes 3145728 | tf_op jit(solution)/shard_map/image_bands/pallas_call | solution.py:97
  2.8 0.5 collective-permute-start.3
  3.3 2.6 %collective-permute-start.6 = (bf16[2,16,8320]{2,1,0:T(8,128)(2,1)S(1)}, bf16[2,16,8320]{2,1,0:T(8,128)(2,1)S(1)}, u32[]{:S(2)}, u32[]{:S(2)}) collective-permute-start(bf16[2,16,8320]{2,1,0:T(8,128)(2,1)S(1)} %get-tuple-element.31), channel_id=1, source_target_pairs={{0,12},{4,8},{8,4},{12,0},{1,13},{5,9},{9,5},{13,1},{2,14},{6,10},... | collective-permute-start | bytes 1597448 | tf_op jit(solution)/shard_map/ppermute | solution.py:455
  6.0 0.0 collective-permute-start.5
  6.0 2.1 %collective-permute-start = (bf16[2,4,4,2048]{3,2,1,0:T(4,128)(2,1)S(1)}, bf16[2,4,4,2048]{3,2,1,0:T(4,128)(2,1)S(1)}, u32[]{:S(2)}, u32[]{:S(2)}) collective-permute-start(bf16[2,4,4,2048]{3,2,1,0:T(4,128)(2,1)S(1)} %get-tuple-element.24.rest_0_), channel_id=1, source_target_pairs={{0,1},{1,0},{2,3},{3,2},{4,5},{5,4},{6,7},{7,6},{8,9},{9,8},{10,11... | collective-permute-start | bytes 393224 | tf_op jit(solution)/shard_map/ppermute | solution.py:458
  8.1 2.6 %collective-permute-start.1 = (bf16[2,4,4,2048]{3,2,1,0:T(4,128)(2,1)S(1)}, bf16[2,4,4,2048]{3,2,1,0:T(4,128)(2,1)S(1)}, u32[]{:S(2)}, u32[]{:S(2)}) collective-permute-start(bf16[2,4,4,2048]{3,2,1,0:T(4,128)(2,1)S(1)} %get-tuple-element.24.rest_0_), channel_id=1, source_target_pairs={{0,2},{1,3},{2,0},{3,1},{4,6},{5,7},{6,4},{7,5},{8,10},{9,11},{10,... | collective-permute-start | bytes 393224 | tf_op jit(solution)/shard_map/ppermute | solution.py:458
  10.7 0.0 collective-permute-done.3.rest_1_.rest_3_.rest_5_
  10.7 0.0 collective-permute-start.2
  10.7 1.6 %own_band.1.rest_2_.rest_4_ = bf16[2,16,8192]{2,1,0:T(8,128)(2,1)S(1)} custom-call(s32[3]{0:T(128)S(1)} %pad_add_fusion.ids, bf16[2,16,32768]{2,1,0:T(8,128)(2,1)} %images.3), custom_call_target="tpu_custom_call" | custom-call | tf_op jit(solution)/shard_map/own_band/pallas_call | solution.py:140
  12.3 0.0 copy-done
  12.3 0.0 copy-done.1
  12.3 1.7 %aligned_rows.2.rest_8_ = bf16[2,32,8192]{2,1,0:T(8,128)(2,1)S(1)} custom-call(s32[3]{0:T(128)S(1)} %pad_add_fusion.ids, f32[1024]{0:T(1024)S(1)} %copy-done.1, f32[8,256]{1,0:T(8,128)S(1)} %copy-done, bf16[2,16,128]{2,1,0:T(8,128)(2,1)S(1)} %get-tuple-element.22.rest_0_.rest_4_, bf16[2,16,8320]{2,1,0:T(8,128)(2,1)S(1)} %collective-permute-done.3.rest_1_.rest_3_.rest_5_, ...), custom_call_target="tpu_custom_call" | custom-call | flops 5242880 | bytes 2097152 | tf_op jit(solution)/shard_map/aligned_rows/pallas_call | solution.py:343
  14.0 0.0 collective-permute-done.rest_1_
  14.0 6.9 %collective-permute-done.1.rest_2_ = bf16[2,4,4,2048]{3,2,1,0:T(4,128)(2,1)S(1)} collective-permute-done((bf16[2,4,4,2048]{3,2,1,0:T(4,128)(2,1)S(1)}, bf16[2,4,4,2048]{3,2,1,0:T(4,128)(2,1)S(1)}, u32[]{:S(2)}, u32[]{:S(2)}) %collective-permute-start.1) | collective-permute-done | bytes 131104 | tf_op jit(solution)/shard_map/ppermute | solution.py:458
  20.9 0.0 collective-permute-done.2.rest_3_
  20.9 4.0 %partial_logits.3 = (f32[128,128]{1,0:T(8,128)S(1)}, f32[128,128]{1,0:T(8,128)S(1)}) custom-call(s32[3]{0:T(128)S(1)} %pad_add_fusion.ids, f32[1024]{0:T(1024)S(1)} %copy-done.1, f32[8,256]{1,0:T(8,128)S(1)} %copy-done, bf16[2,4,4,2048]{3,2,1,0:T(4,128)(2,1)S(1)} %get-tuple-element.24.rest_0_, bf16[2,4,4,2048]{3,2,1,0:T(4,128)(2,1)S(1)} %collective-permute-done.rest_1_, ...), custom_call_target="tpu_custom_call" | custom-call | flops 1073741824 | bytes 1572864 | tf_op jit(solution)/shard_map/partial_logits/pallas_call | solution.py:235
  25.0 0.1 collective-permute-start.4
  25.1 0.0 collective-permute-done.6.rest_4_.rest_1_.rest_3_.rest_7_
  25.1 3.2 %partial_logits.5 = f32[128,128]{1,0:T(8,128)S(1)} custom-call(s32[3]{0:T(128)S(1)} %pad_add_fusion.ids, f32[1024]{0:T(1024)S(1)} %copy-done.1, f32[8,256]{1,0:T(8,128)S(1)} %copy-done, bf16[2,4,4,2048]{3,2,1,0:T(4,128)(2,1)S(1)} %get-tuple-element.24.rest_0_, bf16[2,4,4,2048]{3,2,1,0:T(4,128)(2,1)S(1)} %collective-permute-done.rest_1_, ...), custom_call_target="tpu_custom_call" | custom-call | flops 536870912 | bytes 1048576 | tf_op jit(solution)/shard_map/partial_logits/pallas_call | solution.py:235
  28.3 0.6 collective-permute-start.7
  28.8 1.2 %collective-permute-done.5.rest_4_.rest_0_.rest_2_.rest_6_ = bf16[2,16,8320]{2,1,0:T(8,128)(2,1)S(1)} collective-permute-done((bf16[2,16,8320]{2,1,0:T(8,128)(2,1)S(1)}, bf16[2,16,8320]{2,1,0:T(8,128)(2,1)S(1)}, u32[]{:S(2)}, u32[]{:S(2)}) %collective-permute-start.5) | collective-permute-done | bytes 532512 | tf_op jit(solution)/shard_map/ppermute | solution.py:455
  30.0 3.2 %partial_logits.4 = f32[128,128]{1,0:T(8,128)S(1)} custom-call(s32[3]{0:T(128)S(1)} %pad_add_fusion.ids, f32[1024]{0:T(1024)S(1)} %copy-done.1, f32[8,256]{1,0:T(8,128)S(1)} %copy-done, bf16[2,4,4,2048]{3,2,1,0:T(4,128)(2,1)S(1)} %get-tuple-element.24.rest_0_, bf16[2,4,4,2048]{3,2,1,0:T(4,128)(2,1)S(1)} %collective-permute-done.rest_1_, ...), custom_call_target="tpu_custom_call" | custom-call | flops 536870912 | bytes 1048576 | tf_op jit(solution)/shard_map/partial_logits/pallas_call | solution.py:235
  33.2 0.0 collective-permute-done.4
  33.2 0.0 collective-permute-done.7
  33.3 1.8 %collective-permute-start.8 = (f32[2,128,128]{2,1,0:T(8,128)S(1)}, f32[2,128,128]{2,1,0:T(8,128)S(1)}, u32[]{:S(2)}, u32[]{:S(2)}) collective-permute-start(f32[2,128,128]{2,1,0:T(8,128)S(1)} %pad_maximum_fusion.here), channel_id=1, source_target_pairs={{0,8},{4,12},{8,0},{12,4},{1,9},{5,13},{9,1},{13,5},{2,10},{6,14},... | collective-permute-start | bytes 393224 | tf_op jit(solution)/shard_map/ppermute | solution.py:455
  35.0 1.7 %aligned_rows.3.rest_9_ = bf16[2,32,8192]{2,1,0:T(8,128)(2,1)S(1)} custom-call(s32[3]{0:T(128)S(1)} %pad_add_fusion.ids, f32[1024]{0:T(1024)S(1)} %copy-done.1, f32[8,256]{1,0:T(8,128)S(1)} %copy-done, bf16[2,16,8320]{2,1,0:T(8,128)(2,1)S(1)} %collective-permute-done.5.rest_4_.rest_0_.rest_2_.rest_6_, ...), custom_call_target="tpu_custom_call" | custom-call | flops 5242880 | bytes 2097152 | tf_op jit(solution)/shard_map/aligned_rows/pallas_call | solution.py:343
  36.8 1.8 %collective-permute-done.8.there = f32[2,128,128]{2,1,0:T(8,128)S(1)} collective-permute-done((f32[2,128,128]{2,1,0:T(8,128)S(1)}, f32[2,128,128]{2,1,0:T(8,128)S(1)}, u32[]{:S(2)}, u32[]{:S(2)}) %collective-permute-start.8) | collective-permute-done | bytes 131104 | tf_op jit(solution)/shard_map/ppermute | solution.py:455
  38.6 0.2 logit_stats.1.rest_0_
  38.8 1.5 %collective-permute-start.10 = (f32[32,128]{1,0:T(8,128)S(1)}, f32[32,128]{1,0:T(8,128)S(1)}, u32[]{:S(2)}, u32[]{:S(2)}) collective-permute-start(f32[32,128]{1,0:T(8,128)S(1)} %logit_stats.1.rest_0_), channel_id=1, source_target_pairs={{0,16},{4,20},{8,24},{12,28},{16,0},{20,4},{24,8},{28,12},{1,17},{... | collective-permute-start | bytes 49160 | tf_op jit(solution)/shard_map/ppermute | solution.py:496
  40.3 0.0 collective-permute-start.11
  40.3 0.7 %collective-permute-start.9 = (f32[32,128]{1,0:T(8,128)S(1)}, f32[32,128]{1,0:T(8,128)S(1)}, u32[]{:S(2)}, u32[]{:S(2)}) collective-permute-start(f32[32,128]{1,0:T(8,128)S(1)} %logit_stats.1.rest_0_), channel_id=1, source_target_pairs={{0,4},{4,0},{8,12},{12,8},{1,5},{5,1},{9,13},{13,9},{2,6},{6,2},{1... | collective-permute-start | bytes 49160 | tf_op jit(solution)/shard_map/ppermute | solution.py:455
  41.0 1.6 %collective-permute-done.10.rest_2_ = f32[32,128]{1,0:T(8,128)S(1)} collective-permute-done((f32[32,128]{1,0:T(8,128)S(1)}, f32[32,128]{1,0:T(8,128)S(1)}, u32[]{:S(2)}, u32[]{:S(2)}) %collective-permute-start.10) | collective-permute-done | bytes 16416 | tf_op jit(solution)/shard_map/ppermute | solution.py:496
  42.6 0.9 %collective-permute-done.11.rest_3_ = f32[32,128]{1,0:T(8,128)S(1)} collective-permute-done((f32[32,128]{1,0:T(8,128)S(1)}, f32[32,128]{1,0:T(8,128)S(1)}, u32[]{:S(2)}, u32[]{:S(2)}) %collective-permute-start.11) | collective-permute-done | bytes 16416 | tf_op jit(solution)/shard_map/ppermute | solution.py:497
  43.5 0.0 collective-permute-done.9.rest_1_
  43.5 1.6 %volume_terms.1 = (f32[16,128]{1,0:T(8,128)S(1)}, f32[2,4,8192]{2,1,0:T(4,128)S(1)}, bf16[2,4,8192]{2,1,0:T(4,128)(2,1)S(1)}, bf16[2,4,8192]{2,1,0:T(4,128)(2,1)S(1)}, bf16[2,4,8192]{2,1,0:T(4,128)(2,1)S(1)}) custom-call(s32[3]{0:T(128)S(1)} %pad_add_fusion.ids, f32[32,128]{1,0:T(8,128)S(1)} %logit_stats.1.rest_0_, ...), custom_call_target="tpu_custom_call" | custom-call | flops 33554432 | bytes 2621440 | tf_op jit(solution)/shard_map/volume_terms/pallas_call | solution.py:410
  45.0 3.7 %collective-permute-start.12 = (bf16[2,4,8192]{2,1,0:T(4,128)(2,1)S(1)}, bf16[2,4,8192]{2,1,0:T(4,128)(2,1)S(1)}, u32[]{:S(2)}, u32[]{:S(2)}) collective-permute-start(bf16[2,4,8192]{2,1,0:T(4,128)(2,1)S(1)} %get-tuple-element.37), channel_id=1, source_target_pairs={{0,3},{1,2},{2,1},{3,0},{4,7},{5,6},{6,5},{7,4},{8,11},{9,10},{10,... | collective-permute-start | bytes 393224 | tf_op jit(solution)/shard_map/ppermute | solution.py:458
  48.7 0.0 collective-permute-start.13
  48.7 0.8 %collective-permute-start.14 = (bf16[2,4,8192]{2,1,0:T(4,128)(2,1)S(1)}, bf16[2,4,8192]{2,1,0:T(4,128)(2,1)S(1)}, u32[]{:S(2)}, u32[]{:S(2)}) collective-permute-start(bf16[2,4,8192]{2,1,0:T(4,128)(2,1)S(1)} %get-tuple-element.39), channel_id=1, source_target_pairs={{0,1},{1,0},{2,3},{3,2},{4,5},{5,4},{6,7},{7,6},{8,9},{9,8},{10,11... | collective-permute-start | bytes 393224 | tf_op jit(solution)/shard_map/ppermute | solution.py:458
  49.5 0.7 %copy.9 = f32[16,4]{0,1:T(4,128)} copy(f32[16,4]{1,0:T(8,128)S(1)} %bitcast.11) | data formatting | bytes 512
  50.2 3.2 %collective-permute-done.12.rest_0_ = bf16[2,4,8192]{2,1,0:T(4,128)(2,1)S(1)} collective-permute-done((bf16[2,4,8192]{2,1,0:T(4,128)(2,1)S(1)}, bf16[2,4,8192]{2,1,0:T(4,128)(2,1)S(1)}, u32[]{:S(2)}, u32[]{:S(2)}) %collective-permute-start.12) | collective-permute-done | bytes 131104 | tf_op jit(solution)/shard_map/ppermute | solution.py:458
  53.3 5.8 %collective-permute-done.13.rest_1_ = bf16[2,4,8192]{2,1,0:T(4,128)(2,1)S(1)} collective-permute-done((bf16[2,4,8192]{2,1,0:T(4,128)(2,1)S(1)}, bf16[2,4,8192]{2,1,0:T(4,128)(2,1)S(1)}, u32[]{:S(2)}, u32[]{:S(2)}) %collective-permute-start.13) | collective-permute-done | bytes 131104 | tf_op jit(solution)/shard_map/ppermute | solution.py:458
  59.1 0.0 collective-permute-done.14.rest_2_
  59.1 0.8 %total_volume.1 = f32[2,4,1,8192]{3,2,1,0:T(1,128)} custom-call(f32[2,4,8192]{2,1,0:T(4,128)S(1)} %get-tuple-element.36.first, bf16[2,4,8192]{2,1,0:T(4,128)(2,1)S(1)} %collective-permute-done.12.rest_0_, bf16[2,4,8192]{2,1,0:T(4,128)(2,1)S(1)} %collective-permute-done.13.rest_1_, bf16[2,4,8192]{2,1,0:T(4,128)(2,1)S(1)} %collective-permute-done.14.rest_2_), custom_call_target="tpu_custom_call" | custom-call | tf_op jit(solution)/shard_map/total_volume/pallas_call | solution.py:439
  (3 shorter events, 0.0 us)
Async XLA Ops:
  0.7 11.6 %copy-start = (f32[8,256]{1,0:T(8,128)S(1)}, f32[8,256]{1,0:T(8,128)}, u32[]{:S(2)}) copy-start(f32[8,256]{1,0:T(8,128)} %constant.17.clone.table_x) | copy-start | bytes 24580
  0.7 11.6 %copy-start.1 = (f32[1024]{0:T(1024)S(1)}, f32[1024]{0:T(1024)}, u32[]{:S(2)}) copy-start(f32[1024]{0:T(1024)} %constant.18.clone.table_y) | copy-start | bytes 12292
  2.8 7.8 %collective-permute-start.3 = (bf16[2,16,8320]{2,1,0:T(8,128)(2,1)S(1)}, bf16[2,16,8320]{2,1,0:T(8,128)(2,1)S(1)}, u32[]{:S(2)}, u32[]{:S(2)}) collective-permute-start(bf16[2,16,8320]{2,1,0:T(8,128)(2,1)S(1)} %get-tuple-element.23), channel_id=1, source_target_pairs={{0,4},{4,0},{8,12},{12,8},{1,5},{5,1},{9,13},{13,9},{2,6},{6,2},{1... | collective-permute-start | bytes 1597448 | tf_op jit(solution)/shard_map/ppermute | solution.py:455
  3.3 21.7 %collective-permute-start.6 = (bf16[2,16,8320]{2,1,0:T(8,128)(2,1)S(1)}, bf16[2,16,8320]{2,1,0:T(8,128)(2,1)S(1)}, u32[]{:S(2)}, u32[]{:S(2)}) collective-permute-start(bf16[2,16,8320]{2,1,0:T(8,128)(2,1)S(1)} %get-tuple-element.31), channel_id=1, source_target_pairs={{0,12},{4,8},{8,4},{12,0},{1,13},{5,9},{9,5},{13,1},{2,14},{6,10},... | collective-permute-start | bytes 1597448 | tf_op jit(solution)/shard_map/ppermute | solution.py:455
  6.0 24.1 %collective-permute-start.5 = (bf16[2,16,8320]{2,1,0:T(8,128)(2,1)S(1)}, bf16[2,16,8320]{2,1,0:T(8,128)(2,1)S(1)}, u32[]{:S(2)}, u32[]{:S(2)}) collective-permute-start(bf16[2,16,8320]{2,1,0:T(8,128)(2,1)S(1)} %get-tuple-element.30), channel_id=1, source_target_pairs={{0,8},{4,12},{8,0},{12,4},{1,9},{5,13},{9,1},{13,5},{2,10},{6,14},... | collective-permute-start | bytes 1597448 | tf_op jit(solution)/shard_map/ppermute | solution.py:455
  6.0 8.0 %collective-permute-start = (bf16[2,4,4,2048]{3,2,1,0:T(4,128)(2,1)S(1)}, bf16[2,4,4,2048]{3,2,1,0:T(4,128)(2,1)S(1)}, u32[]{:S(2)}, u32[]{:S(2)}) collective-permute-start(bf16[2,4,4,2048]{3,2,1,0:T(4,128)(2,1)S(1)} %get-tuple-element.24.rest_0_), channel_id=1, source_target_pairs={{0,1},{1,0},{2,3},{3,2},{4,5},{5,4},{6,7},{7,6},{8,9},{9,8},{10,11... | collective-permute-start | bytes 393224 | tf_op jit(solution)/shard_map/ppermute | solution.py:458
  8.1 12.9 %collective-permute-start.1 = (bf16[2,4,4,2048]{3,2,1,0:T(4,128)(2,1)S(1)}, bf16[2,4,4,2048]{3,2,1,0:T(4,128)(2,1)S(1)}, u32[]{:S(2)}, u32[]{:S(2)}) collective-permute-start(bf16[2,4,4,2048]{3,2,1,0:T(4,128)(2,1)S(1)} %get-tuple-element.24.rest_0_), channel_id=1, source_target_pairs={{0,2},{1,3},{2,0},{3,1},{4,6},{5,7},{6,4},{7,5},{8,10},{9,11},{10,... | collective-permute-start | bytes 393224 | tf_op jit(solution)/shard_map/ppermute | solution.py:458
  10.7 10.3 %collective-permute-start.2 = (bf16[2,4,4,2048]{3,2,1,0:T(4,128)(2,1)S(1)}, bf16[2,4,4,2048]{3,2,1,0:T(4,128)(2,1)S(1)}, u32[]{:S(2)}, u32[]{:S(2)}) collective-permute-start(bf16[2,4,4,2048]{3,2,1,0:T(4,128)(2,1)S(1)} %get-tuple-element.24.rest_0_), channel_id=1, source_target_pairs={{0,3},{1,2},{2,1},{3,0},{4,7},{5,6},{6,5},{7,4},{8,11},{9,10},{10,... | collective-permute-start | bytes 393224 | tf_op jit(solution)/shard_map/ppermute | solution.py:458
  25.0 8.2 %collective-permute-start.4 = (f32[128,128]{1,0:T(8,128)S(1)}, f32[128,128]{1,0:T(8,128)S(1)}, u32[]{:S(2)}, u32[]{:S(2)}) collective-permute-start(f32[128,128]{1,0:T(8,128)S(1)} %get-tuple-element.29), channel_id=1, source_target_pairs={{0,4},{4,0},{8,12},{12,8},{1,5},{5,1},{9,13},{13,9},{2,6},{6,2},{1... | collective-permute-start | bytes 196616 | tf_op jit(solution)/shard_map/ppermute | solution.py:455
  28.3 5.0 %collective-permute-start.7 = (f32[128,128]{1,0:T(8,128)S(1)}, f32[128,128]{1,0:T(8,128)S(1)}, u32[]{:S(2)}, u32[]{:S(2)}) collective-permute-start(f32[128,128]{1,0:T(8,128)S(1)} %partial_logits.5), channel_id=1, source_target_pairs={{0,4},{4,0},{8,12},{12,8},{1,5},{5,1},{9,13},{13,9},{2,6},{6,2},{1... | collective-permute-start | bytes 196616 | tf_op jit(solution)/shard_map/ppermute | solution.py:455
  33.3 5.3 %collective-permute-start.8 = (f32[2,128,128]{2,1,0:T(8,128)S(1)}, f32[2,128,128]{2,1,0:T(8,128)S(1)}, u32[]{:S(2)}, u32[]{:S(2)}) collective-permute-start(f32[2,128,128]{2,1,0:T(8,128)S(1)} %pad_maximum_fusion.here), channel_id=1, source_target_pairs={{0,8},{4,12},{8,0},{12,4},{1,9},{5,13},{9,1},{13,5},{2,10},{6,14},... | collective-permute-start | bytes 393224 | tf_op jit(solution)/shard_map/ppermute | solution.py:455
  38.8 3.8 %collective-permute-start.10 = (f32[32,128]{1,0:T(8,128)S(1)}, f32[32,128]{1,0:T(8,128)S(1)}, u32[]{:S(2)}, u32[]{:S(2)}) collective-permute-start(f32[32,128]{1,0:T(8,128)S(1)} %logit_stats.1.rest_0_), channel_id=1, source_target_pairs={{0,16},{4,20},{8,24},{12,28},{16,0},{20,4},{24,8},{28,12},{1,17},{... | collective-permute-start | bytes 49160 | tf_op jit(solution)/shard_map/ppermute | solution.py:496
  40.3 3.2 %collective-permute-start.11 = (f32[32,128]{1,0:T(8,128)S(1)}, f32[32,128]{1,0:T(8,128)S(1)}, u32[]{:S(2)}, u32[]{:S(2)}) collective-permute-start(f32[32,128]{1,0:T(8,128)S(1)} %logit_stats.1.rest_0_), channel_id=1, source_target_pairs={{0,20},{4,16},{8,28},{12,24},{16,4},{20,0},{24,12},{28,8},{1,21},{... | collective-permute-start | bytes 49160 | tf_op jit(solution)/shard_map/ppermute | solution.py:497
  40.3 3.2 %collective-permute-start.9 = (f32[32,128]{1,0:T(8,128)S(1)}, f32[32,128]{1,0:T(8,128)S(1)}, u32[]{:S(2)}, u32[]{:S(2)}) collective-permute-start(f32[32,128]{1,0:T(8,128)S(1)} %logit_stats.1.rest_0_), channel_id=1, source_target_pairs={{0,4},{4,0},{8,12},{12,8},{1,5},{5,1},{9,13},{13,9},{2,6},{6,2},{1... | collective-permute-start | bytes 49160 | tf_op jit(solution)/shard_map/ppermute | solution.py:455
  45.0 8.3 %collective-permute-start.12 = (bf16[2,4,8192]{2,1,0:T(4,128)(2,1)S(1)}, bf16[2,4,8192]{2,1,0:T(4,128)(2,1)S(1)}, u32[]{:S(2)}, u32[]{:S(2)}) collective-permute-start(bf16[2,4,8192]{2,1,0:T(4,128)(2,1)S(1)} %get-tuple-element.37), channel_id=1, source_target_pairs={{0,3},{1,2},{2,1},{3,0},{4,7},{5,6},{6,5},{7,4},{8,11},{9,10},{10,... | collective-permute-start | bytes 393224 | tf_op jit(solution)/shard_map/ppermute | solution.py:458
  48.7 10.4 %collective-permute-start.13 = (bf16[2,4,8192]{2,1,0:T(4,128)(2,1)S(1)}, bf16[2,4,8192]{2,1,0:T(4,128)(2,1)S(1)}, u32[]{:S(2)}, u32[]{:S(2)}) collective-permute-start(bf16[2,4,8192]{2,1,0:T(4,128)(2,1)S(1)} %get-tuple-element.38), channel_id=1, source_target_pairs={{0,2},{1,3},{2,0},{3,1},{4,6},{5,7},{6,4},{7,5},{8,10},{9,11},{10,... | collective-permute-start | bytes 393224 | tf_op jit(solution)/shard_map/ppermute | solution.py:458
  48.7 10.4 %collective-permute-start.14 = (bf16[2,4,8192]{2,1,0:T(4,128)(2,1)S(1)}, bf16[2,4,8192]{2,1,0:T(4,128)(2,1)S(1)}, u32[]{:S(2)}, u32[]{:S(2)}) collective-permute-start(bf16[2,4,8192]{2,1,0:T(4,128)(2,1)S(1)} %get-tuple-element.39), channel_id=1, source_target_pairs={{0,1},{1,0},{2,3},{3,2},{4,5},{5,4},{6,7},{7,6},{8,9},{9,8},{10,11... | collective-permute-start | bytes 393224 | tf_op jit(solution)/shard_map/ppermute | solution.py:458

commit v5 on v4

--- a/solution.py
+++ b/solution.py
@@ -15,6 +15,9 @@
 HALF = TX // 2
 LANES = 128
 SUBLANES = 8
+SHARED = 2
+EARLY = 2
+FLOPS_OF_MICRO = 1_000_000_000
 VMEM_BYTES = 24 * 1024 * 1024
 VMEM_SPEC = pl.BlockSpec(memory_space=pltpu.VMEM)
 SMEM_SPEC = pl.BlockSpec(memory_space=pltpu.SMEM)
@@ -46,10 +49,13 @@
     lists, rest = rest[:3], rest[3:]
     outs, meta, shard = rest[: len(steps)], rest[len(steps)], rest[len(steps) + 1]
     lines, sems, meta_sems, line_sems, shard_sem = rest[len(steps) + 2 :]
-    width = outs[0].shape[2] - LANES
     copies = [pltpu.make_async_copy(references, shard, shard_sem)]
     for place, (step, out) in enumerate(zip(steps, outs)):
-        start = pl.multiple_of((ids[0] ^ step) * width, width)
+        width = out.shape[2] - LANES
+        start = (ids[0] ^ step) * width
+        if step == SHARED:
+            start = 2 * start + ids[2] * width
+        start = pl.multiple_of(start, width)
         for part in range(out.shape[0]):
             copies.append(
                 pltpu.make_async_copy(
@@ -77,7 +83,9 @@
     meta[0] = table.astype(BF)
     meta[1] = jnp.zeros(meta.shape[1:], BF)
     meta_copies = [
-        pltpu.make_async_copy(meta, out.at[:, :, pl.ds(width, LANES)], meta_sems.at[place])
+        pltpu.make_async_copy(
+            meta, out.at[:, :, pl.ds(out.shape[2] - LANES, LANES)], meta_sems.at[place]
+        )
         for place, out in enumerate(outs)
     ]
     for copy in meta_copies:
@@ -96,7 +104,10 @@
     sources = [pltpu.with_memory_space_constraint(array, pltpu.HBM) for array in sources]
     *bands, meta, shard = pl.pallas_call(
         functools.partial(bands_kernel, steps),
-        out_shape=[pltpu.VMEM((parts, rows, width + LANES), images.dtype)] * len(steps)
+        out_shape=[
+            pltpu.VMEM((parts, rows, width // (1 + (step == SHARED)) + LANES), images.dtype)
+            for step in steps
+        ]
         + [
             jax.ShapeDtypeStruct((parts, rows, LANES), BF),
             pltpu.VMEM(references.shape, references.dtype),
@@ -153,12 +164,40 @@
     return placed, [VMEM_SPEC] * len(placed)
 
 
-def logits_kernel(groups, orients, ids, table_y, table_x, *rest):
-    shards, rest = rest[:orients], rest[orients:]
-    images, rest = rest[:groups], rest[groups:]
+def flat(groups):
+    return [image for images, _ in groups for image in images]
+
+
+def sizes_of(groups):
+    return [len(images) for images, _ in groups]
+
+
+def by_group(sizes, refs):
+    images, at = [], 0
+    for size in sizes:
+        images.append(refs[at : at + size])
+        at += size
+    return images, refs[at:]
+
+
+def load(images, ids, part, start, size):
+    if len(images) == 1:
+        return images[0][part, :, pl.ds(pl.multiple_of(start, size), size)].astype(F32)
+    half = images[0].shape[2] - LANES
+    side = start // half
+    cols = pl.ds(pl.multiple_of(start - side * half, size), size)
+    mine, other = (image[part, :, cols].astype(F32) for image in images)
+    return jnp.where(side == ids[2], mine, other)
+
+
+def logits_kernel(sizes, orients, steps, sums, ids, table_y, table_x, *rest):
+    groups, count = len(sizes), len(steps)
+    shards, rest = rest[:count], rest[count:]
+    images, rest = by_group(sizes, rest)
+    before, rest = rest[: groups * sums], rest[groups * sums :]
     outs, (refs, left, right) = rest[:groups], rest[groups:]
     chunk = shards[0].shape[3]
-    rows = images[0].shape[1]
+    rows = images[0][0].shape[1]
     group_rows = TX * rows
     names = refs.shape[1]
     lines = chunk // IMG
@@ -168,11 +207,11 @@
         for part in range(2):
             for k in range(shard.shape[1]):
                 refs[part, k * per_class : (k + 1) * per_class, cols] = shard[part, k]
-    for out in outs:
-        out[...] = jnp.zeros_like(out)
+    for g, out in enumerate(outs):
+        out[...] = before[g][...] if sums else jnp.zeros_like(out)
 
     def add_shard(step, carry):
-        column = ids[1] ^ step
+        column = ids[1] ^ (step + steps[0])
         line_base = (ids[0] * orients + column) * lines
         for line in range(lines):
             to_re = slice(2 * line * IMG, (2 * line + 1) * IMG)
@@ -196,9 +235,9 @@
                 if t < HALF:
                     put_ref(TY // 2 + t, re_c + im_s, im_c - re_s)
             for g in range(groups):
-                cols = pl.ds(pl.multiple_of(column * chunk + line * IMG, IMG), IMG)
-                re = images[g][0, :, cols].astype(F32)
-                im = images[g][1, :, cols].astype(F32)
+                start = column * chunk + line * IMG
+                re = load(images[g], ids, 0, start, IMG)
+                im = load(images[g], ids, 1, start, IMG)
 
                 def put(a, re, im):
                     top = g * group_rows + a * rows
@@ -221,19 +260,22 @@
             outs[g][...] += value[g * group_rows : (g + 1) * group_rows]
         return carry
 
-    lax.fori_loop(0, orients, add_shard, 0)
-
-
-def partial_logits(ids, table_x, table_y, shards, picked):
+    lax.fori_loop(0, count, add_shard, 0)
+
+
+def partial_logits(ids, table_x, table_y, shards, picked, steps, before, micros):
     parts, classes, orients, chunk = shards[0].shape
     groups = len(picked)
-    rows = picked[0][0].shape[1]
+    rows = picked[0][0][0].shape[1]
     names = classes * orients
-    count = len(shards)
+    count = len(steps)
     out_shape = (TX * rows, TY * names)
-    arrays, specs = in_vmem([table_x, *shards, *(image for image, _ in picked)])
+    used = [shards[step] for step in steps]
+    arrays, specs = in_vmem([table_x, *used, *flat(picked), *before])
     return pl.pallas_call(
-        functools.partial(logits_kernel, groups, count),
+        functools.partial(
+            logits_kernel, sizes_of(picked), len(shards), steps, len(before) > 0
+        ),
         out_shape=[pltpu.VMEM(out_shape, F32)] * groups,
         in_specs=[SMEM_SPEC] * 2 + specs,
         out_specs=[VMEM_SPEC] * groups,
@@ -244,8 +286,8 @@
         ],
         compiler_params=pltpu.CompilerParams(vmem_limit_bytes=VMEM_BYTES),
         cost_estimate=pl.CostEstimate(
-            flops=4 * groups * TX * rows * TY * names * count * chunk,
-            bytes_accessed=4 * count * chunk * (groups * rows + names),
+            flops=micros * FLOPS_OF_MICRO,
+            bytes_accessed=0,
             transcendentals=0,
         ),
         name="partial_logits",
@@ -287,9 +329,10 @@
     )(*arrays)
 
 
-def rows_kernel(groups, ids, table_y, table_x, *rest):
-    metas, images = rest[:groups], rest[groups : 2 * groups]
-    out = rest[2 * groups]
+def rows_kernel(sizes, ids, table_y, table_x, *rest):
+    groups = len(sizes)
+    metas = rest[:groups]
+    images, (out,) = by_group(sizes, rest[groups:])
     rows = metas[0].shape[1]
     width = out.shape[2]
     lines = width // IMG
@@ -325,8 +368,8 @@
                 cos_x, sin_x = phase_c[:, across], phase_s[:, across]
                 cosine = cos_x * cos_y - sin_x * sin_y
                 sine = sin_x * cos_y + cos_x * sin_y
-                re = images[g][0, :, cols].astype(F32)
-                im = images[g][1, :, cols].astype(F32)
+                re = load(images[g], ids, 0, start, LANES)
+                im = load(images[g], ids, 1, start, LANES)
                 out[0, own, cols] = (re * cosine - im * sine).astype(BF)
                 out[1, own, cols] = (re * sine + im * cosine).astype(BF)
             return carry
@@ -335,20 +378,18 @@
 
 
 def aligned_rows(ids, table_x, table_y, picked, width):
-    parts, rows = picked[0][0].shape[:2]
+    parts, rows = picked[0][0][0].shape[:2]
     groups = len(picked)
-    arrays, specs = in_vmem(
-        [table_x] + [table for _, table in picked] + [image for image, _ in picked]
-    )
+    arrays, specs = in_vmem([table_x] + [table for _, table in picked] + flat(picked))
     return pl.pallas_call(
-        functools.partial(rows_kernel, groups),
+        functools.partial(rows_kernel, sizes_of(picked)),
         out_shape=pltpu.VMEM((parts, groups * rows, width), BF),
         in_specs=[SMEM_SPEC] * 2 + specs,
         out_specs=VMEM_SPEC,
         compiler_params=pltpu.CompilerParams(vmem_limit_bytes=VMEM_BYTES),
         cost_estimate=pl.CostEstimate(
-            flops=20 * groups * rows * width,
-            bytes_accessed=8 * groups * rows * width,
+            flops=0,
+            bytes_accessed=0,
             transcendentals=0,
         ),
         name="aligned_rows",
@@ -404,7 +445,7 @@
 def volume_terms(ids, stats, groups, near, far, orients, classes):
     parts, entries, width = near.shape
     rest = far.shape[1]
-    rows = groups[0][0].shape[1]
+    rows = groups[0][1].shape[1]
     out_shape = (parts, classes, width)
     arrays, specs = in_vmem([*stats, *(table for _, table in groups), near, far])
     return pl.pallas_call(
@@ -461,19 +502,24 @@
         ids, orient_lists, shift_ids, fixed_weights, images, references, dom
     )
     arrived = {step: swap_dom(bands[step - 1], step) for step in [1, *range(dom - 1, 1, -1)]}
+    shard, arrived[1] = lax.optimization_barrier((shard, arrived[1]))
     shards = [shard] + [swap_orient(shard, step) for step in range(1, orient)]
-    groups = [(own_band(ids, images, dom), meta)] + [(arrived[step], arrived[step]) for step in range(1, dom)]
-
-    def logits_of(picked):
-        return partial_logits(ids, table_x, table_y, shards, picked)
+    half = arrived[SHARED]
+    groups = [([own_band(ids, images, dom)], meta)]
+    groups += [([arrived[step]], arrived[step]) for step in range(1, dom)]
+    groups[SHARED] = ([half, lax.ppermute(half, "cls", xor_pairs(cls, 1))], half)
+
+    def logits_of(picked, steps, before, micros):
+        return partial_logits(ids, table_x, table_y, shards, picked, steps, before, micros)
 
     width = images.shape[2] // dom
     aligned_near = aligned_rows(ids, table_x, table_y, groups[:2], width)
-    *shards, aligned_near = lax.optimization_barrier((*shards, aligned_near))
+    shards[1], aligned_near = lax.optimization_barrier((shards[1], aligned_near))
     partial = [None] * dom
-    partial[0:2] = logits_of(groups[:2])
-    partial[3::2] = logits_of(groups[3::2])
-    partial[2::2] = logits_of(groups[2::2])
+    every = range(orient)
+    first = logits_of(groups[:2], every[:EARLY], [], 0)
+    partial[0:2] = logits_of(groups[:2], every[EARLY:], first, 20)
+    partial[2:] = logits_of(groups[2:], every, [], 3)
     kept = [partial[s] + swap_dom(partial[s ^ 1], 1) for s in range(0, dom, 2)]
     here = jnp.stack(kept)
     step = 2

time: 60.1 us -> 57.9 us (0.963)
  waiting for transfers between devices: 21.4 us -> 19 us
  starting transfers between devices: 16.9 us -> 18.6 us
  Pallas kernels: 20.1 us -> 18.6 us
    ppermute x6, waiting for transfers between devices: 15.9 us -> 11.2 us  [swap_orient(): return lax.ppermute(array, 'orient', xor_pairs(orient, step))]
    ppermute x0 -> x1, starting transfers between devices: none -> 1.79 us  [local(): lax.ppermute(half, 'cls', xor_pairs(cls, 1))]
    ppermute x7, waiting for transfers between devices: 3.02 us -> 4.75 us  [swap_dom(): return lax.ppermute(array, 'dom', xor_pairs(dom, step))]
    pallas_call x5, Pallas kernels: 13.8 us -> 12.4 us  [the longest x3 8.64 us: partial_logits(): pl.pallas_call(functools.partial(logits_kernel, sizes_of(picked), len(sha...]
  transfers between devices with their start and end apart: 15 -> 16, of which waited for: 7 -> 9; matrix products, arithmetic and copies ran while one was open for 1% -> 1% of each run, Pallas kernels for 26% -> 24%
where the time goes in v5:
time: 57.9 us; the launch traced here: 57.7 us
  waiting for transfers between devices  19 us (33%)
  Pallas kernels  18.6 us (32%)
  starting transfers between devices  18.6 us (32%)
  between operations  0.76 us (1%)
  local copies, waits for them, and re-layouts  0.66 us (1%)
    ppermute x6, waiting for transfers between devices, swap_orient(): return lax.ppermute(array, 'orient', xor_pairs(orient, step))  11.2 us
    ppermute x6, starting transfers between devices, swap_orient(): return lax.ppermute(array, 'orient', xor_pairs(orient, step))  8.97 us
    pallas_call x3, Pallas kernels, partial_logits(): pl.pallas_call(functools.partial(logits_kernel, sizes_of(picked), len(sha...  8.64 us
    ppermute x7, starting transfers between devices, swap_dom(): return lax.ppermute(array, 'dom', xor_pairs(dom, step))  5.73 us
    ppermute x7, waiting for transfers between devices, swap_dom(): return lax.ppermute(array, 'dom', xor_pairs(dom, step))  4.75 us
    pallas_call x2, Pallas kernels, aligned_rows(): pl.pallas_call(functools.partial(rows_kernel, sizes_of(picked)), out_shap...  3.81 us
    ppermute x1, starting transfers between devices, local(): lax.ppermute(stats, ('cls', 'dom'), pairs)  2.03 us
    pallas_call x1, Pallas kernels, image_bands(): pl.pallas_call(functools.partial(bands_kernel, steps), out_shape=[pltpu.V...  2.02 us
  transfers between devices with their start and end apart: 16, of which 9 were waited for; matrix products, arithmetic and copies ran while one was open for 1% of the time, Pallas kernels for 24%

profile of v5, /device:TPU:0, one launch (start us, length us, event | category | flops | bytes accessed | tf_op | source)
XLA Modules:
  0.0 57.7 jit_solution(10403375283849798016)
XLA Ops:
  0.6 0.1 pad_add_fusion.ids
  0.7 0.0 copy-start
  0.7 0.0 copy-start.1
  0.7 2.0 %image_bands.1 = (bf16[2,16,8320]{2,1,0:T(8,128)(2,1)S(1)}, bf16[2,16,4224]{2,1,0:T(8,128)(2,1)S(1)}, bf16[2,16,8320]{2,1,0:T(8,128)(2,1)S(1)}, bf16[2,16,128]{2...) custom-call(s32[3]{0:T(128)S(1)} %pad_add_fusion.ids, bf16[2,16,32768]{2,1,0:T(8,128)(2,1)} %images.3, ...), custom_call_target="tpu_custom_call" | custom-call | bytes 3145728 | tf_op jit(solution)/shard_map/image_bands/pallas_call | solution.py:105
  2.7 0.5 collective-permute-start
  3.3 2.6 %collective-permute-start.5 = (bf16[2,16,4224]{2,1,0:T(8,128)(2,1)S(1)}, bf16[2,16,4224]{2,1,0:T(8,128)(2,1)S(1)}, u32[]{:S(2)}, u32[]{:S(2)}) collective-permute-start(bf16[2,16,4224]{2,1,0:T(8,128)(2,1)S(1)} %get-tuple-element.34), channel_id=1, source_target_pairs={{0,8},{4,12},{8,0},{12,4},{1,9},{5,13},{9,1},{13,5},{2,10},{6,14},... | collective-permute-start | bytes 811016 | tf_op jit(solution)/shard_map/ppermute | solution.py:496
  5.8 0.0 collective-permute-done.rest_1_.rest_3_.rest_5_
  5.8 1.9 %collective-permute-start.3 = (bf16[2,4,4,2048]{3,2,1,0:T(4,128)(2,1)S(1)}, bf16[2,4,4,2048]{3,2,1,0:T(4,128)(2,1)S(1)}, u32[]{:S(2)}, u32[]{:S(2)}) collective-permute-start(bf16[2,4,4,2048]{3,2,1,0:T(4,128)(2,1)S(1)} %get-tuple-element.26.rest_0_), channel_id=1, source_target_pairs={{0,1},{1,0},{2,3},{3,2},{4,5},{5,4},{6,7},{7,6},{8,9},{9,8},{10,11... | collective-permute-start | bytes 393224 | tf_op jit(solution)/shard_map/ppermute | solution.py:499
  7.8 2.6 %collective-permute-start.1 = (bf16[2,4,4,2048]{3,2,1,0:T(4,128)(2,1)S(1)}, bf16[2,4,4,2048]{3,2,1,0:T(4,128)(2,1)S(1)}, u32[]{:S(2)}, u32[]{:S(2)}) collective-permute-start(bf16[2,4,4,2048]{3,2,1,0:T(4,128)(2,1)S(1)} %get-tuple-element.26.rest_0_), channel_id=1, source_target_pairs={{0,2},{1,3},{2,0},{3,1},{4,6},{5,7},{6,4},{7,5},{8,10},{9,11},{10,... | collective-permute-start | bytes 393224 | tf_op jit(solution)/shard_map/ppermute | solution.py:499
  10.3 0.0 collective-permute-start.2
  10.3 0.7 %collective-permute-start.7 = (bf16[2,16,8320]{2,1,0:T(8,128)(2,1)S(1)}, bf16[2,16,8320]{2,1,0:T(8,128)(2,1)S(1)}, u32[]{:S(2)}, u32[]{:S(2)}) collective-permute-start(bf16[2,16,8320]{2,1,0:T(8,128)(2,1)S(1)} %get-tuple-element.35), channel_id=1, source_target_pairs={{0,12},{4,8},{8,4},{12,0},{1,13},{5,9},{9,5},{13,1},{2,14},{6,10},... | collective-permute-start | bytes 1597448 | tf_op jit(solution)/shard_map/ppermute | solution.py:496
  11.0 1.6 %own_band.1.rest_2_ = bf16[2,16,8192]{2,1,0:T(8,128)(2,1)S(1)} custom-call(s32[3]{0:T(128)S(1)} %pad_add_fusion.ids, bf16[2,16,32768]{2,1,0:T(8,128)(2,1)} %images.3), custom_call_target="tpu_custom_call" | custom-call | tf_op jit(solution)/shard_map/own_band/pallas_call | solution.py:151
  12.6 0.3 collective-permute-done.5.rest_4_.rest_0_.rest_2_.rest_6_
  12.9 1.8 %collective-permute-start.6 = (bf16[2,16,4224]{2,1,0:T(8,128)(2,1)S(1)}, bf16[2,16,4224]{2,1,0:T(8,128)(2,1)S(1)}, u32[]{:S(2)}, u32[]{:S(2)}) collective-permute-start(bf16[2,16,4224]{2,1,0:T(8,128)(2,1)S(1)} %collective-permute-done.5.rest_4_.rest_0_.rest_2_.rest_6_), channel_id=1, source_target_pairs={{0,16},{16,0},{1,17},{17,1},{2,18},{18,2},{3,19},{19,3},{4,20},{20... | collective-permute-start | bytes 811016 | tf_op jit(solution)/shard_map/ppermute | solution.py:510
  14.7 0.0 copy-done
  14.7 0.0 copy-done.1
  14.7 1.7 %aligned_rows.2.rest_8_ = bf16[2,32,8192]{2,1,0:T(8,128)(2,1)S(1)} custom-call(s32[3]{0:T(128)S(1)} %pad_add_fusion.ids, f32[1024]{0:T(1024)S(1)} %copy-done.1, f32[8,256]{1,0:T(8,128)S(1)} %copy-done, bf16[2,16,128]{2,1,0:T(8,128)(2,1)S(1)} %get-tuple-element.28.rest_0_.rest_4_, bf16[2,16,8320]{2,1,0:T(8,128)(2,1)S(1)} %collective-permute-done.rest_1_.rest_3_.rest_5_, ...), custom_call_target="tpu_custom_call" | custom-call | tf_op jit(solution)/shard_map/aligned_rows/pallas_call | solution.py:384
  16.4 0.0 collective-permute-done.3.rest_1_
  16.4 2.3 %partial_logits.3 = (f32[128,128]{1,0:T(8,128)S(1)}, f32[128,128]{1,0:T(8,128)S(1)}) custom-call(s32[3]{0:T(128)S(1)} %pad_add_fusion.ids, f32[1024]{0:T(1024)S(1)} %copy-done.1, f32[8,256]{1,0:T(8,128)S(1)} %copy-done, bf16[2,4,4,2048]{3,2,1,0:T(4,128)(2,1)S(1)} %get-tuple-element.26.rest_0_, bf16[2,4,4,2048]{3,2,1,0:T(4,128)(2,1)S(1)} %collective-permute-done.3.rest_1_, ...), custom_call_target="tpu_custom_call" | custom-call | tf_op jit(solution)/shard_map/partial_logits/pallas_call | solution.py:275
  18.8 1.9 %collective-permute-done.1.rest_0_.rest_2_ = bf16[2,4,4,2048]{3,2,1,0:T(4,128)(2,1)S(1)} collective-permute-done((bf16[2,4,4,2048]{3,2,1,0:T(4,128)(2,1)S(1)}, bf16[2,4,4,2048]{3,2,1,0:T(4,128)(2,1)S(1)}, u32[]{:S(2)}, u32[]{:S(2)}) %collective-permute-start.1) | collective-permute-done | bytes 131104 | tf_op jit(solution)/shard_map/ppermute | solution.py:499
  20.7 0.0 collective-permute-done.2.rest_1_.rest_3_
  20.7 2.3 %partial_logits.4 = (f32[128,128]{1,0:T(8,128)S(1)}, f32[128,128]{1,0:T(8,128)S(1)}) custom-call(s32[3]{0:T(128)S(1)} %pad_add_fusion.ids, f32[1024]{0:T(1024)S(1)} %copy-done.1, f32[8,256]{1,0:T(8,128)S(1)} %copy-done, bf16[2,4,4,2048]{3,2,1,0:T(4,128)(2,1)S(1)} %collective-permute-done.1.rest_0_.rest_2_, ...), custom_call_target="tpu_custom_call" | custom-call | flops 20000000000 | tf_op jit(solution)/shard_map/partial_logits/pallas_call | solution.py:275
  23.0 0.1 collective-permute-start.4
  23.0 1.4 %collective-permute-done.7.rest_6_.rest_1_.rest_4_.rest_7_ = bf16[2,16,8320]{2,1,0:T(8,128)(2,1)S(1)} collective-permute-done((bf16[2,16,8320]{2,1,0:T(8,128)(2,1)S(1)}, bf16[2,16,8320]{2,1,0:T(8,128)(2,1)S(1)}, u32[]{:S(2)}, u32[]{:S(2)}) %collective-permute-start.7) | collective-permute-done | bytes 532512 | tf_op jit(solution)/shard_map/ppermute | solution.py:496
  24.5 0.0 collective-permute-done.6.rest_5_.rest_3_
  24.5 4.0 %partial_logits.5 = (f32[128,128]{1,0:T(8,128)S(1)}, f32[128,128]{1,0:T(8,128)S(1)}) custom-call(s32[3]{0:T(128)S(1)} %pad_add_fusion.ids, f32[1024]{0:T(1024)S(1)} %copy-done.1, f32[8,256]{1,0:T(8,128)S(1)} %copy-done, bf16[2,4,4,2048]{3,2,1,0:T(4,128)(2,1)S(1)} %get-tuple-element.26.rest_0_, bf16[2,4,4,2048]{3,2,1,0:T(4,128)(2,1)S(1)} %collective-permute-done.3.rest_1_, ...), custom_call_target="tpu_custom_call" | custom-call | flops 3000000000 | tf_op jit(solution)/shard_map/partial_logits/pallas_call | solution.py:275
  28.5 0.2 collective-permute-start.8
  28.7 0.0 collective-permute-done.4
  28.7 1.1 %collective-permute-done.8 = f32[128,128]{1,0:T(8,128)S(1)} collective-permute-done((f32[128,128]{1,0:T(8,128)S(1)}, f32[128,128]{1,0:T(8,128)S(1)}, u32[]{:S(2)}, u32[]{:S(2)}) %collective-permute-start.8) | collective-permute-done | bytes 65568 | tf_op jit(solution)/shard_map/ppermute | solution.py:496
  29.9 1.7 %collective-permute-start.9 = (f32[2,128,128]{2,1,0:T(8,128)S(1)}, f32[2,128,128]{2,1,0:T(8,128)S(1)}, u32[]{:S(2)}, u32[]{:S(2)}) collective-permute-start(f32[2,128,128]{2,1,0:T(8,128)S(1)} %pad_maximum_fusion.here), channel_id=1, source_target_pairs={{0,8},{4,12},{8,0},{12,4},{1,9},{5,13},{9,1},{13,5},{2,10},{6,14},... | collective-permute-start | bytes 393224 | tf_op jit(solution)/shard_map/ppermute | solution.py:496
  31.5 2.1 %aligned_rows.3.rest_9_ = bf16[2,32,8192]{2,1,0:T(8,128)(2,1)S(1)} custom-call(s32[3]{0:T(128)S(1)} %pad_add_fusion.ids, f32[1024]{0:T(1024)S(1)} %copy-done.1, f32[8,256]{1,0:T(8,128)S(1)} %copy-done, bf16[2,16,4224]{2,1,0:T(8,128)(2,1)S(1)} %collective-permute-done.5.rest_4_.rest_0_.rest_2_.rest_6_, ...), custom_call_target="tpu_custom_call" | custom-call | tf_op jit(solution)/shard_map/aligned_rows/pallas_call | solution.py:384
  33.6 1.9 %collective-permute-done.9.there = f32[2,128,128]{2,1,0:T(8,128)S(1)} collective-permute-done((f32[2,128,128]{2,1,0:T(8,128)S(1)}, f32[2,128,128]{2,1,0:T(8,128)S(1)}, u32[]{:S(2)}, u32[]{:S(2)}) %collective-permute-start.9) | collective-permute-done | bytes 131104 | tf_op jit(solution)/shard_map/ppermute | solution.py:496
  35.5 0.2 logit_stats.1.rest_0_
  35.7 0.1 collective-permute-start.10
  35.8 2.0 %collective-permute-start.11 = (f32[32,128]{1,0:T(8,128)S(1)}, f32[32,128]{1,0:T(8,128)S(1)}, u32[]{:S(2)}, u32[]{:S(2)}) collective-permute-start(f32[32,128]{1,0:T(8,128)S(1)} %logit_stats.1.rest_0_), channel_id=1, source_target_pairs={{0,16},{4,20},{8,24},{12,28},{16,0},{20,4},{24,8},{28,12},{1,17},{... | collective-permute-start | bytes 49160 | tf_op jit(solution)/shard_map/ppermute | solution.py:542
  37.8 0.1 collective-permute-start.12
  37.9 0.0 collective-permute-done.10.rest_1_
  37.9 1.7 %collective-permute-done.11.rest_2_ = f32[32,128]{1,0:T(8,128)S(1)} collective-permute-done((f32[32,128]{1,0:T(8,128)S(1)}, f32[32,128]{1,0:T(8,128)S(1)}, u32[]{:S(2)}, u32[]{:S(2)}) %collective-permute-start.11) | collective-permute-done | bytes 16416 | tf_op jit(solution)/shard_map/ppermute | solution.py:542
  39.6 1.4 %collective-permute-done.12.rest_3_ = f32[32,128]{1,0:T(8,128)S(1)} collective-permute-done((f32[32,128]{1,0:T(8,128)S(1)}, f32[32,128]{1,0:T(8,128)S(1)}, u32[]{:S(2)}, u32[]{:S(2)}) %collective-permute-start.12) | collective-permute-done | bytes 16416 | tf_op jit(solution)/shard_map/ppermute | solution.py:543
  41.0 1.6 %volume_terms.1 = (f32[16,128]{1,0:T(8,128)S(1)}, f32[2,4,8192]{2,1,0:T(4,128)S(1)}, bf16[2,4,8192]{2,1,0:T(4,128)(2,1)S(1)}, bf16[2,4,8192]{2,1,0:T(4,128)(2,1)S(1)}, bf16[2,4,8192]{2,1,0:T(4,128)(2,1)S(1)}) custom-call(s32[3]{0:T(128)S(1)} %pad_add_fusion.ids, f32[32,128]{1,0:T(8,128)S(1)} %logit_stats.1.rest_0_, ...), custom_call_target="tpu_custom_call" | custom-call | flops 33554432 | bytes 2621440 | tf_op jit(solution)/shard_map/volume_terms/pallas_call | solution.py:451
  42.5 3.7 %collective-permute-start.13 = (bf16[2,4,8192]{2,1,0:T(4,128)(2,1)S(1)}, bf16[2,4,8192]{2,1,0:T(4,128)(2,1)S(1)}, u32[]{:S(2)}, u32[]{:S(2)}) collective-permute-start(bf16[2,4,8192]{2,1,0:T(4,128)(2,1)S(1)} %get-tuple-element.43), channel_id=1, source_target_pairs={{0,3},{1,2},{2,1},{3,0},{4,7},{5,6},{6,5},{7,4},{8,11},{9,10},{10,... | collective-permute-start | bytes 393224 | tf_op jit(solution)/shard_map/ppermute | solution.py:499
  46.2 0.0 collective-permute-start.14
  46.2 0.8 %collective-permute-start.15 = (bf16[2,4,8192]{2,1,0:T(4,128)(2,1)S(1)}, bf16[2,4,8192]{2,1,0:T(4,128)(2,1)S(1)}, u32[]{:S(2)}, u32[]{:S(2)}) collective-permute-start(bf16[2,4,8192]{2,1,0:T(4,128)(2,1)S(1)} %get-tuple-element.45), channel_id=1, source_target_pairs={{0,1},{1,0},{2,3},{3,2},{4,5},{5,4},{6,7},{7,6},{8,9},{9,8},{10,11... | collective-permute-start | bytes 393224 | tf_op jit(solution)/shard_map/ppermute | solution.py:499
  47.0 0.7 %copy.9 = f32[16,4]{0,1:T(4,128)} copy(f32[16,4]{1,0:T(8,128)S(1)} %bitcast.11) | data formatting | bytes 512
  47.7 3.2 %collective-permute-done.13.rest_0_ = bf16[2,4,8192]{2,1,0:T(4,128)(2,1)S(1)} collective-permute-done((bf16[2,4,8192]{2,1,0:T(4,128)(2,1)S(1)}, bf16[2,4,8192]{2,1,0:T(4,128)(2,1)S(1)}, u32[]{:S(2)}, u32[]{:S(2)}) %collective-permute-start.13) | collective-permute-done | bytes 131104 | tf_op jit(solution)/shard_map/ppermute | solution.py:499
  50.8 6.1 %collective-permute-done.14.rest_1_ = bf16[2,4,8192]{2,1,0:T(4,128)(2,1)S(1)} collective-permute-done((bf16[2,4,8192]{2,1,0:T(4,128)(2,1)S(1)}, bf16[2,4,8192]{2,1,0:T(4,128)(2,1)S(1)}, u32[]{:S(2)}, u32[]{:S(2)}) %collective-permute-start.14) | collective-permute-done | bytes 131104 | tf_op jit(solution)/shard_map/ppermute | solution.py:499
  56.9 0.0 collective-permute-done.15.rest_2_
  56.9 0.8 %total_volume.1 = f32[2,4,1,8192]{3,2,1,0:T(1,128)} custom-call(f32[2,4,8192]{2,1,0:T(4,128)S(1)} %get-tuple-element.42.first, bf16[2,4,8192]{2,1,0:T(4,128)(2,1)S(1)} %collective-permute-done.13.rest_0_, bf16[2,4,8192]{2,1,0:T(4,128)(2,1)S(1)} %collective-permute-done.14.rest_1_, bf16[2,4,8192]{2,1,0:T(4,128)(2,1)S(1)} %collective-permute-done.15.rest_2_), custom_call_target="tpu_custom_call" | custom-call | tf_op jit(solution)/shard_map/total_volume/pallas_call | solution.py:480
  (3 shorter events, 0.0 us)
Async XLA Ops:
  0.7 14.0 %copy-start = (f32[8,256]{1,0:T(8,128)S(1)}, f32[8,256]{1,0:T(8,128)}, u32[]{:S(2)}) copy-start(f32[8,256]{1,0:T(8,128)} %constant.17.clone.table_x) | copy-start | bytes 24580
  0.7 14.0 %copy-start.1 = (f32[1024]{0:T(1024)S(1)}, f32[1024]{0:T(1024)}, u32[]{:S(2)}) copy-start(f32[1024]{0:T(1024)} %constant.18.clone.table_y) | copy-start | bytes 12292
  2.7 3.1 %collective-permute-start = (bf16[2,16,8320]{2,1,0:T(8,128)(2,1)S(1)}, bf16[2,16,8320]{2,1,0:T(8,128)(2,1)S(1)}, u32[]{:S(2)}, u32[]{:S(2)}) collective-permute-start(bf16[2,16,8320]{2,1,0:T(8,128)(2,1)S(1)} %get-tuple-element.25), channel_id=1, source_target_pairs={{0,4},{4,0},{8,12},{12,8},{1,5},{5,1},{9,13},{13,9},{2,6},{6,2},{1... | collective-permute-start | bytes 1597448 | tf_op jit(solution)/shard_map/ppermute | solution.py:496
  3.3 9.6 %collective-permute-start.5 = (bf16[2,16,4224]{2,1,0:T(8,128)(2,1)S(1)}, bf16[2,16,4224]{2,1,0:T(8,128)(2,1)S(1)}, u32[]{:S(2)}, u32[]{:S(2)}) collective-permute-start(bf16[2,16,4224]{2,1,0:T(8,128)(2,1)S(1)} %get-tuple-element.34), channel_id=1, source_target_pairs={{0,8},{4,12},{8,0},{12,4},{1,9},{5,13},{9,1},{13,5},{2,10},{6,14},... | collective-permute-start | bytes 811016 | tf_op jit(solution)/shard_map/ppermute | solution.py:496
  5.8 10.6 %collective-permute-start.3 = (bf16[2,4,4,2048]{3,2,1,0:T(4,128)(2,1)S(1)}, bf16[2,4,4,2048]{3,2,1,0:T(4,128)(2,1)S(1)}, u32[]{:S(2)}, u32[]{:S(2)}) collective-permute-start(bf16[2,4,4,2048]{3,2,1,0:T(4,128)(2,1)S(1)} %get-tuple-element.26.rest_0_), channel_id=1, source_target_pairs={{0,1},{1,0},{2,3},{3,2},{4,5},{5,4},{6,7},{7,6},{8,9},{9,8},{10,11... | collective-permute-start | bytes 393224 | tf_op jit(solution)/shard_map/ppermute | solution.py:499
  7.8 12.9 %collective-permute-start.1 = (bf16[2,4,4,2048]{3,2,1,0:T(4,128)(2,1)S(1)}, bf16[2,4,4,2048]{3,2,1,0:T(4,128)(2,1)S(1)}, u32[]{:S(2)}, u32[]{:S(2)}) collective-permute-start(bf16[2,4,4,2048]{3,2,1,0:T(4,128)(2,1)S(1)} %get-tuple-element.26.rest_0_), channel_id=1, source_target_pairs={{0,2},{1,3},{2,0},{3,1},{4,6},{5,7},{6,4},{7,5},{8,10},{9,11},{10,... | collective-permute-start | bytes 393224 | tf_op jit(solution)/shard_map/ppermute | solution.py:499
  10.3 10.3 %collective-permute-start.2 = (bf16[2,4,4,2048]{3,2,1,0:T(4,128)(2,1)S(1)}, bf16[2,4,4,2048]{3,2,1,0:T(4,128)(2,1)S(1)}, u32[]{:S(2)}, u32[]{:S(2)}) collective-permute-start(bf16[2,4,4,2048]{3,2,1,0:T(4,128)(2,1)S(1)} %get-tuple-element.26.rest_0_), channel_id=1, source_target_pairs={{0,3},{1,2},{2,1},{3,0},{4,7},{5,6},{6,5},{7,4},{8,11},{9,10},{10,... | collective-permute-start | bytes 393224 | tf_op jit(solution)/shard_map/ppermute | solution.py:499
  10.3 14.1 %collective-permute-start.7 = (bf16[2,16,8320]{2,1,0:T(8,128)(2,1)S(1)}, bf16[2,16,8320]{2,1,0:T(8,128)(2,1)S(1)}, u32[]{:S(2)}, u32[]{:S(2)}) collective-permute-start(bf16[2,16,8320]{2,1,0:T(8,128)(2,1)S(1)} %get-tuple-element.35), channel_id=1, source_target_pairs={{0,12},{4,8},{8,4},{12,0},{1,13},{5,9},{9,5},{13,1},{2,14},{6,10},... | collective-permute-start | bytes 1597448 | tf_op jit(solution)/shard_map/ppermute | solution.py:496
  12.9 11.6 %collective-permute-start.6 = (bf16[2,16,4224]{2,1,0:T(8,128)(2,1)S(1)}, bf16[2,16,4224]{2,1,0:T(8,128)(2,1)S(1)}, u32[]{:S(2)}, u32[]{:S(2)}) collective-permute-start(bf16[2,16,4224]{2,1,0:T(8,128)(2,1)S(1)} %collective-permute-done.5.rest_4_.rest_0_.rest_2_.rest_6_), channel_id=1, source_target_pairs={{0,16},{16,0},{1,17},{17,1},{2,18},{18,2},{3,19},{19,3},{4,20},{20... | collective-permute-start | bytes 811016 | tf_op jit(solution)/shard_map/ppermute | solution.py:510
  23.0 5.8 %collective-permute-start.4 = (f32[128,128]{1,0:T(8,128)S(1)}, f32[128,128]{1,0:T(8,128)S(1)}, u32[]{:S(2)}, u32[]{:S(2)}) collective-permute-start(f32[128,128]{1,0:T(8,128)S(1)} %get-tuple-element.33), channel_id=1, source_target_pairs={{0,4},{4,0},{8,12},{12,8},{1,5},{5,1},{9,13},{13,9},{2,6},{6,2},{1... | collective-permute-start | bytes 196616 | tf_op jit(solution)/shard_map/ppermute | solution.py:496
  28.5 1.3 %collective-permute-start.8 = (f32[128,128]{1,0:T(8,128)S(1)}, f32[128,128]{1,0:T(8,128)S(1)}, u32[]{:S(2)}, u32[]{:S(2)}) collective-permute-start(f32[128,128]{1,0:T(8,128)S(1)} %get-tuple-element.37), channel_id=1, source_target_pairs={{0,4},{4,0},{8,12},{12,8},{1,5},{5,1},{9,13},{13,9},{2,6},{6,2},{1... | collective-permute-start | bytes 196616 | tf_op jit(solution)/shard_map/ppermute | solution.py:496
  29.9 5.6 %collective-permute-start.9 = (f32[2,128,128]{2,1,0:T(8,128)S(1)}, f32[2,128,128]{2,1,0:T(8,128)S(1)}, u32[]{:S(2)}, u32[]{:S(2)}) collective-permute-start(f32[2,128,128]{2,1,0:T(8,128)S(1)} %pad_maximum_fusion.here), channel_id=1, source_target_pairs={{0,8},{4,12},{8,0},{12,4},{1,9},{5,13},{9,1},{13,5},{2,10},{6,14},... | collective-permute-start | bytes 393224 | tf_op jit(solution)/shard_map/ppermute | solution.py:496
  35.7 2.2 %collective-permute-start.10 = (f32[32,128]{1,0:T(8,128)S(1)}, f32[32,128]{1,0:T(8,128)S(1)}, u32[]{:S(2)}, u32[]{:S(2)}) collective-permute-start(f32[32,128]{1,0:T(8,128)S(1)} %logit_stats.1.rest_0_), channel_id=1, source_target_pairs={{0,4},{4,0},{8,12},{12,8},{1,5},{5,1},{9,13},{13,9},{2,6},{6,2},{1... | collective-permute-start | bytes 49160 | tf_op jit(solution)/shard_map/ppermute | solution.py:496
  35.8 3.8 %collective-permute-start.11 = (f32[32,128]{1,0:T(8,128)S(1)}, f32[32,128]{1,0:T(8,128)S(1)}, u32[]{:S(2)}, u32[]{:S(2)}) collective-permute-start(f32[32,128]{1,0:T(8,128)S(1)} %logit_stats.1.rest_0_), channel_id=1, source_target_pairs={{0,16},{4,20},{8,24},{12,28},{16,0},{20,4},{24,8},{28,12},{1,17},{... | collective-permute-start | bytes 49160 | tf_op jit(solution)/shard_map/ppermute | solution.py:542
  37.8 3.2 %collective-permute-start.12 = (f32[32,128]{1,0:T(8,128)S(1)}, f32[32,128]{1,0:T(8,128)S(1)}, u32[]{:S(2)}, u32[]{:S(2)}) collective-permute-start(f32[32,128]{1,0:T(8,128)S(1)} %logit_stats.1.rest_0_), channel_id=1, source_target_pairs={{0,20},{4,16},{8,28},{12,24},{16,4},{20,0},{24,12},{28,8},{1,21},{... | collective-permute-start | bytes 49160 | tf_op jit(solution)/shard_map/ppermute | solution.py:543
  42.5 8.3 %collective-permute-start.13 = (bf16[2,4,8192]{2,1,0:T(4,128)(2,1)S(1)}, bf16[2,4,8192]{2,1,0:T(4,128)(2,1)S(1)}, u32[]{:S(2)}, u32[]{:S(2)}) collective-permute-start(bf16[2,4,8192]{2,1,0:T(4,128)(2,1)S(1)} %get-tuple-element.43), channel_id=1, source_target_pairs={{0,3},{1,2},{2,1},{3,0},{4,7},{5,6},{6,5},{7,4},{8,11},{9,10},{10,... | collective-permute-start | bytes 393224 | tf_op jit(solution)/shard_map/ppermute | solution.py:499
  46.2 10.7 %collective-permute-start.14 = (bf16[2,4,8192]{2,1,0:T(4,128)(2,1)S(1)}, bf16[2,4,8192]{2,1,0:T(4,128)(2,1)S(1)}, u32[]{:S(2)}, u32[]{:S(2)}) collective-permute-start(bf16[2,4,8192]{2,1,0:T(4,128)(2,1)S(1)} %get-tuple-element.44), channel_id=1, source_target_pairs={{0,2},{1,3},{2,0},{3,1},{4,6},{5,7},{6,4},{7,5},{8,10},{9,11},{10,... | collective-permute-start | bytes 393224 | tf_op jit(solution)/shard_map/ppermute | solution.py:499
  46.2 10.7 %collective-permute-start.15 = (bf16[2,4,8192]{2,1,0:T(4,128)(2,1)S(1)}, bf16[2,4,8192]{2,1,0:T(4,128)(2,1)S(1)}, u32[]{:S(2)}, u32[]{:S(2)}) collective-permute-start(bf16[2,4,8192]{2,1,0:T(4,128)(2,1)S(1)} %get-tuple-element.45), channel_id=1, source_target_pairs={{0,1},{1,0},{2,3},{3,2},{4,5},{5,4},{6,7},{7,6},{8,9},{9,8},{10,11... | collective-permute-start | bytes 393224 | tf_op jit(solution)/shard_map/ppermute | solution.py:499

commit v6 on v5

--- a/solution.py
+++ b/solution.py
@@ -34,6 +34,10 @@
     return table_x, table_y.reshape(-1)
 
 
+def device_ids():
+    return [lax.axis_index(name) for name in ("dom", "orient", "cls")]
+
+
 def xor_pairs(size, step):
     return [(i, i ^ step) for i in range(size)]
 
@@ -45,7 +49,8 @@
     return jnp.sum(jnp.where(rows == cols, line, 0.0), axis=1, keepdims=True)
 
 
-def bands_kernel(steps, ids, images, references, *rest):
+def bands_kernel(steps, images, references, *rest):
+    ids = device_ids()
     lists, rest = rest[:3], rest[3:]
     outs, meta, shard = rest[: len(steps)], rest[len(steps)], rest[len(steps) + 1]
     lines, sems, meta_sems, line_sems, shard_sem = rest[len(steps) + 2 :]
@@ -94,7 +99,7 @@
         copy.wait()
 
 
-def image_bands(ids, orient_lists, shift_ids, fixed_weights, images, references, dom):
+def image_bands(orient_lists, shift_ids, fixed_weights, images, references, dom):
     parts, rows, pixels = images.shape
     width = pixels // dom
     steps = list(range(1, dom))
@@ -112,8 +117,7 @@
             jax.ShapeDtypeStruct((parts, rows, LANES), BF),
             pltpu.VMEM(references.shape, references.dtype),
         ],
-        in_specs=[pl.BlockSpec(memory_space=pltpu.SMEM)]
-        + [pl.BlockSpec(memory_space=pl.ANY)] * len(sources),
+        in_specs=[pl.BlockSpec(memory_space=pl.ANY)] * len(sources),
         out_specs=[pl.BlockSpec(memory_space=pl.ANY)] * len(steps)
         + [pl.BlockSpec(memory_space=pltpu.VMEM), pl.BlockSpec(memory_space=pl.ANY)],
         scratch_shapes=[
@@ -128,11 +132,12 @@
             flops=0, bytes_accessed=4 * parts * rows * (pixels - width), transcendentals=0
         ),
         name="image_bands",
-    )(ids, *sources)
+    )(*sources)
     return bands, meta, shard
 
 
-def own_kernel(ids, images, band, sems):
+def own_kernel(images, band, sems):
+    ids = device_ids()
     width = band.shape[2]
     start = pl.multiple_of(ids[0] * width, width)
     copies = [
@@ -145,18 +150,18 @@
         copy.wait()
 
 
-def own_band(ids, images, dom):
+def own_band(images, dom):
     parts, rows, pixels = images.shape
     shape = (parts, rows, pixels // dom)
     return pl.pallas_call(
         own_kernel,
         out_shape=pltpu.VMEM(shape, images.dtype),
-        in_specs=[pl.BlockSpec(memory_space=pltpu.SMEM), pl.BlockSpec(memory_space=pl.ANY)],
+        in_specs=[pl.BlockSpec(memory_space=pl.ANY)],
         out_specs=pl.BlockSpec(memory_space=pl.ANY),
         scratch_shapes=[pltpu.SemaphoreType.DMA((parts,))],
         compiler_params=pltpu.CompilerParams(vmem_limit_bytes=VMEM_BYTES),
         name="own_band",
-    )(ids, pltpu.with_memory_space_constraint(images, pltpu.HBM))
+    )(pltpu.with_memory_space_constraint(images, pltpu.HBM))
 
 
 def in_vmem(arrays):
@@ -190,17 +195,76 @@
     return jnp.where(side == ids[2], mine, other)
 
 
-def logits_kernel(sizes, orients, steps, sums, ids, table_y, table_x, *rest):
+def shift_references(refs, right, step, ids, orients, table_y):
+    names = refs.shape[1]
+    chunk = right.shape[2] // 2
+    lines = chunk // IMG
+    line_base = (ids[0] * orients + (ids[1] ^ step[1])) * lines
+    for line in range(lines):
+        to_re = slice(2 * line * IMG, (2 * line + 1) * IMG)
+        to_im = slice((2 * line + 1) * IMG, (2 * line + 2) * IMG)
+        base = (line_base + line) * TY
+        cols = pl.ds(pl.multiple_of(step[0] * chunk + line * IMG, IMG), IMG)
+        ref_re = refs[0, :, cols].astype(F32)
+        ref_im = refs[1, :, cols].astype(F32)
+
+        def put(b, re, im):
+            right[step[0], b * names : (b + 1) * names, to_re] = re.astype(BF)
+            right[step[0], b * names : (b + 1) * names, to_im] = im.astype(BF)
+
+        put(TY // 2, ref_re, ref_im)
+        for t in range(1, HALF + 1):
+            cosine = table_y[base + t - 1]
+            sine = table_y[base + HALF + t - 1]
+            re_c, im_s = ref_re * cosine, ref_im * sine
+            im_c, re_s = ref_im * cosine, ref_re * sine
+            put(TY // 2 - t, re_c - im_s, im_c + re_s)
+            if t < HALF:
+                put(TY // 2 + t, re_c + im_s, im_c - re_s)
+
+
+def shift_images(images, left, column, ids, table_x):
+    chunk = left.shape[1] // 2
+    rows = images[0][0].shape[1]
+    for line in range(chunk // IMG):
+        to_re = slice(2 * line * IMG, (2 * line + 1) * IMG)
+        to_im = slice((2 * line + 1) * IMG, (2 * line + 2) * IMG)
+        for g, group in enumerate(images):
+            start = column * chunk + line * IMG
+            re = load(group, ids, 0, start, IMG)
+            im = load(group, ids, 1, start, IMG)
+
+            def put(a, re, im):
+                top = (g * TX + a) * rows
+                left[top : top + rows, to_re] = re.astype(BF)
+                left[top : top + rows, to_im] = im.astype(BF)
+
+            put(TX // 2, re, im)
+            for t in range(1, HALF + 1):
+                cosine = table_x[t - 1 : t, :]
+                sine = table_x[HALF + t - 1 : HALF + t, :]
+                re_c, im_s = re * cosine, im * sine
+                re_s, im_c = re * sine, im * cosine
+                put(TX // 2 - t, re_c + im_s, im_c - re_s)
+                if t < HALF:
+                    put(TX // 2 + t, re_c - im_s, re_s + im_c)
+
+
+def add_products(outs, left, right):
+    rows = outs[0].shape[0]
+    value = lax.dot_general(left, right, (((1,), (1,)), ((), ())), preferred_element_type=F32)
+    for g, out in enumerate(outs):
+        out[...] += value[g * rows : (g + 1) * rows]
+
+
+def near_kernel(sizes, orients, steps, sums, table_y, table_x, *rest):
+    ids = device_ids()
     groups, count = len(sizes), len(steps)
     shards, rest = rest[:count], rest[count:]
     images, rest = by_group(sizes, rest)
     before, rest = rest[: groups * sums], rest[groups * sums :]
-    outs, (refs, left, right) = rest[:groups], rest[groups:]
+    outs, (right, refs, left) = rest[:groups], rest[groups:]
     chunk = shards[0].shape[3]
-    rows = images[0][0].shape[1]
-    group_rows = TX * rows
-    names = refs.shape[1]
-    lines = chunk // IMG
     per_class = shards[0].shape[2]
     for place, shard in enumerate(shards):
         cols = slice(place * chunk, (place + 1) * chunk)
@@ -210,60 +274,41 @@
     for g, out in enumerate(outs):
         out[...] = before[g][...] if sums else jnp.zeros_like(out)
 
-    def add_shard(step, carry):
-        column = ids[1] ^ (step + steps[0])
-        line_base = (ids[0] * orients + column) * lines
-        for line in range(lines):
-            to_re = slice(2 * line * IMG, (2 * line + 1) * IMG)
-            to_im = slice((2 * line + 1) * IMG, (2 * line + 2) * IMG)
-            base = (line_base + line) * TY
-            ref_cols = pl.ds(pl.multiple_of(step * chunk + line * IMG, IMG), IMG)
-            ref_re = refs[0, :, ref_cols].astype(F32)
-            ref_im = refs[1, :, ref_cols].astype(F32)
-
-            def put_ref(b, re, im):
-                right[b * names : (b + 1) * names, to_re] = re.astype(BF)
-                right[b * names : (b + 1) * names, to_im] = im.astype(BF)
-
-            put_ref(TY // 2, ref_re, ref_im)
-            for t in range(1, HALF + 1):
-                cosine = table_y[base + t - 1]
-                sine = table_y[base + HALF + t - 1]
-                re_c, im_s = ref_re * cosine, ref_im * sine
-                im_c, re_s = ref_im * cosine, ref_re * sine
-                put_ref(TY // 2 - t, re_c - im_s, im_c + re_s)
-                if t < HALF:
-                    put_ref(TY // 2 + t, re_c + im_s, im_c - re_s)
-            for g in range(groups):
-                start = column * chunk + line * IMG
-                re = load(images[g], ids, 0, start, IMG)
-                im = load(images[g], ids, 1, start, IMG)
-
-                def put(a, re, im):
-                    top = g * group_rows + a * rows
-                    left[top : top + rows, to_re] = re.astype(BF)
-                    left[top : top + rows, to_im] = im.astype(BF)
-
-                put(TX // 2, re, im)
-                for t in range(1, HALF + 1):
-                    cosine = table_x[t - 1 : t, :]
-                    sine = table_x[HALF + t - 1 : HALF + t, :]
-                    re_c, im_s = re * cosine, im * sine
-                    re_s, im_c = re * sine, im * cosine
-                    put(TX // 2 - t, re_c + im_s, im_c - re_s)
-                    if t < HALF:
-                        put(TX // 2 + t, re_c - im_s, re_s + im_c)
-        value = lax.dot_general(
-            left[...], right[...], (((1,), (1,)), ((), ())), preferred_element_type=F32
-        )
-        for g in range(groups):
-            outs[g][...] += value[g * group_rows : (g + 1) * group_rows]
+    def add_shard(place, carry):
+        step = place + steps[0]
+        shift_references(refs, right, (place, step), ids, orients, table_y)
+        shift_images(images, left, ids[1] ^ step, ids, table_x)
+        add_products(outs, left[...], right[place])
         return carry
 
     lax.fori_loop(0, count, add_shard, 0)
 
 
-def partial_logits(ids, table_x, table_y, shards, picked, steps, before, micros):
+def far_kernel(sizes, counts, table_x, *rest):
+    ids = device_ids()
+    groups = len(sizes)
+    rights, rest = rest[: len(counts)], rest[len(counts) :]
+    images, rest = by_group(sizes, rest)
+    outs, left = rest[:groups], rest[groups]
+    for out in outs:
+        out[...] = jnp.zeros_like(out)
+    base = 0
+    for right, count in zip(rights, counts):
+
+        def add_shard(place, carry, base=base, right=right):
+            shift_images(images, left, ids[1] ^ (place + base), ids, table_x)
+            add_products(outs, left[...], right[place])
+            return carry
+
+        lax.fori_loop(0, count, add_shard, 0)
+        base += count
+
+
+def logits_cost(micros):
+    return pl.CostEstimate(flops=micros * FLOPS_OF_MICRO, bytes_accessed=0, transcendentals=0)
+
+
+def near_logits(table_x, table_y, shards, picked, steps, before, micros):
     parts, classes, orients, chunk = shards[0].shape
     groups = len(picked)
     rows = picked[0][0][0].shape[1]
@@ -272,26 +317,41 @@
     out_shape = (TX * rows, TY * names)
     used = [shards[step] for step in steps]
     arrays, specs = in_vmem([table_x, *used, *flat(picked), *before])
-    return pl.pallas_call(
+    *sums, right = pl.pallas_call(
         functools.partial(
-            logits_kernel, sizes_of(picked), len(shards), steps, len(before) > 0
+            near_kernel, sizes_of(picked), len(shards), steps, len(before) > 0
         ),
-        out_shape=[pltpu.VMEM(out_shape, F32)] * groups,
-        in_specs=[SMEM_SPEC] * 2 + specs,
-        out_specs=[VMEM_SPEC] * groups,
+        out_shape=[pltpu.VMEM(out_shape, F32)] * groups
+        + [pltpu.VMEM((count, TY * names, 2 * chunk), BF)],
+        in_specs=[SMEM_SPEC] + specs,
+        out_specs=[VMEM_SPEC] * (groups + 1),
         scratch_shapes=[
             pltpu.VMEM((parts, names, count * chunk), BF),
             pltpu.VMEM((groups * TX * rows, 2 * chunk), BF),
-            pltpu.VMEM((TY * names, 2 * chunk), BF),
         ],
         compiler_params=pltpu.CompilerParams(vmem_limit_bytes=VMEM_BYTES),
-        cost_estimate=pl.CostEstimate(
-            flops=micros * FLOPS_OF_MICRO,
-            bytes_accessed=0,
-            transcendentals=0,
-        ),
-        name="partial_logits",
-    )(ids, table_y, *arrays)
+        cost_estimate=logits_cost(micros),
+        name="near_logits",
+    )(table_y, *arrays)
+    return sums, right
+
+
+def far_logits(table_x, rights, picked, micros):
+    groups = len(picked)
+    rows = picked[0][0][0].shape[1]
+    names, chunk = rights[0].shape[1:]
+    out_shape = (TX * rows, names)
+    arrays, specs = in_vmem([table_x, *rights, *flat(picked)])
+    return pl.pallas_call(
+        functools.partial(far_kernel, sizes_of(picked), [right.shape[0] for right in rights]),
+        out_shape=[pltpu.VMEM(out_shape, F32)] * groups,
+        in_specs=specs,
+        out_specs=[VMEM_SPEC] * groups,
+        scratch_shapes=[pltpu.VMEM((groups * TX * rows, chunk), BF)],
+        compiler_params=pltpu.CompilerParams(vmem_limit_bytes=VMEM_BYTES),
+        cost_estimate=logits_cost(micros),
+        name="far_logits",
+    )(*arrays)
 
 
 def stats_kernel(swap, classes, orients, here, there, out):
@@ -329,7 +389,8 @@
     )(*arrays)
 
 
-def rows_kernel(sizes, ids, table_y, table_x, *rest):
+def rows_kernel(sizes, table_y, table_x, *rest):
+    ids = device_ids()
     groups = len(sizes)
     metas = rest[:groups]
     images, (out,) = by_group(sizes, rest[groups:])
@@ -377,14 +438,14 @@
         lax.fori_loop(0, lines, add_line, 0, unroll=min(lines, 4))
 
 
-def aligned_rows(ids, table_x, table_y, picked, width):
+def aligned_rows(table_x, table_y, picked, width):
     parts, rows = picked[0][0][0].shape[:2]
     groups = len(picked)
     arrays, specs = in_vmem([table_x] + [table for _, table in picked] + flat(picked))
     return pl.pallas_call(
         functools.partial(rows_kernel, sizes_of(picked)),
         out_shape=pltpu.VMEM((parts, groups * rows, width), BF),
-        in_specs=[SMEM_SPEC] * 2 + specs,
+        in_specs=[SMEM_SPEC] + specs,
         out_specs=VMEM_SPEC,
         compiler_params=pltpu.CompilerParams(vmem_limit_bytes=VMEM_BYTES),
         cost_estimate=pl.CostEstimate(
@@ -393,10 +454,11 @@
             transcendentals=0,
         ),
         name="aligned_rows",
-    )(ids, table_y, *arrays)
-
-
-def volume_kernel(groups, orients, classes, ids, *rest):
+    )(table_y, *arrays)
+
+
+def volume_kernel(groups, orients, classes, *rest):
+    ids = device_ids()
     stats, metas = rest[:4], rest[4 : 4 + groups]
     near, far = rest[4 + groups], rest[5 + groups]
     prob, outs = rest[6 + groups], rest[7 + groups :]
@@ -442,7 +504,7 @@
                 outs[o][part, :, cols] = term.astype(outs[o].dtype)
 
 
-def volume_terms(ids, stats, groups, near, far, orients, classes):
+def volume_terms(stats, groups, near, far, orients, classes):
     parts, entries, width = near.shape
     rest = far.shape[1]
     rows = groups[0][1].shape[1]
@@ -450,9 +512,9 @@
     arrays, specs = in_vmem([*stats, *(table for _, table in groups), near, far])
     return pl.pallas_call(
         functools.partial(volume_kernel, len(groups), orients, classes),
-        out_shape=[jax.ShapeDtypeStruct((rows, LANES), F32)]
+        out_shape=[pltpu.VMEM((rows, LANES), F32)]
         + [pltpu.VMEM(out_shape, F32 if o == 0 else BF) for o in range(orients)],
-        in_specs=[SMEM_SPEC] + specs,
+        in_specs=specs,
         out_specs=[VMEM_SPEC] * (1 + orients),
         compiler_params=pltpu.CompilerParams(vmem_limit_bytes=VMEM_BYTES),
         cost_estimate=pl.CostEstimate(
@@ -461,7 +523,7 @@
             transcendentals=0,
         ),
         name="volume_terms",
-    )(ids, *arrays)
+    )(*arrays)
 
 
 def total_kernel(first, *rest):
@@ -489,8 +551,6 @@
 def local(dom, orient, cls, references, images, orient_lists, shift_ids, fixed_weights):
     classes, orients = references.shape[1], references.shape[2]
     table_x, table_y = (jnp.asarray(t) for t in trig_tables())
-    ids = jnp.stack([lax.axis_index(name) for name in ("dom", "orient", "cls")])
-    ids = ids.astype(jnp.int32)
 
     def swap_dom(array, step):
         return lax.ppermute(array, "dom", xor_pairs(dom, step))
@@ -499,28 +559,30 @@
         return lax.ppermute(array, "orient", xor_pairs(orient, step))
 
     bands, meta, shard = image_bands(
-        ids, orient_lists, shift_ids, fixed_weights, images, references, dom
+        orient_lists, shift_ids, fixed_weights, images, references, dom
     )
     arrived = {step: swap_dom(bands[step - 1], step) for step in [1, *range(dom - 1, 1, -1)]}
     shard, arrived[1] = lax.optimization_barrier((shard, arrived[1]))
     shards = [shard] + [swap_orient(shard, step) for step in range(1, orient)]
     half = arrived[SHARED]
-    groups = [([own_band(ids, images, dom)], meta)]
+    groups = [([own_band(images, dom)], meta)]
     groups += [([arrived[step]], arrived[step]) for step in range(1, dom)]
     groups[SHARED] = ([half, lax.ppermute(half, "cls", xor_pairs(cls, 1))], half)
 
-    def logits_of(picked, steps, before, micros):
-        return partial_logits(ids, table_x, table_y, shards, picked, steps, before, micros)
-
     width = images.shape[2] // dom
-    aligned_near = aligned_rows(ids, table_x, table_y, groups[:2], width)
+    aligned_near = aligned_rows(table_x, table_y, groups[:2], width)
     shards[1], aligned_near = lax.optimization_barrier((shards[1], aligned_near))
-    partial = [None] * dom
     every = range(orient)
-    first = logits_of(groups[:2], every[:EARLY], [], 0)
-    partial[0:2] = logits_of(groups[:2], every[EARLY:], first, 20)
-    partial[2:] = logits_of(groups[2:], every, [], 3)
-    kept = [partial[s] + swap_dom(partial[s ^ 1], 1) for s in range(0, dom, 2)]
+    first, right = near_logits(table_x, table_y, shards, groups[:2], every[:EARLY], [], 0)
+    near, right_late = near_logits(
+        table_x, table_y, shards, groups[:2], every[EARLY:], first, 20
+    )
+    swapped = swap_dom(near[1], 1)
+    right_late, swapped = lax.optimization_barrier((right_late, swapped))
+    far = far_logits(table_x, [right, right_late], groups[2:], 6)
+    partial = [*near, *far]
+    kept = [near[0] + swapped]
+    kept += [partial[s] + swap_dom(partial[s ^ 1], 1) for s in range(2, dom, 2)]
     here = jnp.stack(kept)
     step = 2
     there, swap = jnp.zeros_like(here), 0
@@ -530,7 +592,7 @@
             order = np.arange(dom // 2) ^ swap
             here = here + jnp.stack([there[i] for i in order])
         step *= 2
-    aligned_far = aligned_rows(ids, table_x, table_y, groups[2:], width)
+    aligned_far = aligned_rows(table_x, table_y, groups[2:], width)
     there, aligned_far = lax.optimization_barrier((there, aligned_far))
     stats = logit_stats(here, there, swap, classes, orients)
 
@@ -543,9 +605,10 @@
         lax.ppermute(stats, ("cls", "dom"), cross),
     ]
     prob, *terms = volume_terms(
-        ids, stats_all, groups, aligned_near, aligned_far, orients, classes
+        stats_all, groups, aligned_near, aligned_far, orients, classes
     )
-    terms = [terms[0]] + [swap_orient(terms[o], o) for o in range(orients - 1, 0, -1)]
+    order = sorted(range(1, orients), key=lambda place: place != orients // 2)
+    terms = [terms[0]] + [swap_orient(terms[o], o) for o in order]
     return prob[:, :classes], total_volume(terms)
 
 

time: 57.9 us -> 55.4 us (0.957)
  Pallas kernels: 18.6 us -> 16.3 us
    ppermute x6, waiting for transfers between devices: 11.2 us -> 10.2 us  [swap_orient(): return lax.ppermute(array, 'orient', xor_pairs(orient, step))]
    pallas_call x3, Pallas kernels: 8.64 us -> 8 us  [the longest x2 4.74 us: near_logits(): pl.pallas_call(functools.partial(near_kernel, sizes_of(picked), len(shard...]
  transfers between devices with their start and end apart: 16 -> 16, of which waited for: 9 -> 10; matrix products, arithmetic and copies ran while one was open for 1% -> 1% of each run, Pallas kernels for 24% -> 17%
where the time goes in v6:
time: 55.4 us; the launch traced here: 54.9 us
  starting transfers between devices  18.6 us (34%)
  waiting for transfers between devices  18.5 us (33%)
  Pallas kernels  16.3 us (29%)
  between operations  0.77 us (1%)
  local copies, waits for them, and re-layouts  0.66 us (1%)
    ppermute x6, waiting for transfers between devices, swap_orient(): return lax.ppermute(array, 'orient', xor_pairs(orient, step))  10.2 us
    ppermute x6, starting transfers between devices, swap_orient(): return lax.ppermute(array, 'orient', xor_pairs(orient, step))  8.97 us
    ppermute x7, starting transfers between devices, swap_dom(): return lax.ppermute(array, 'dom', xor_pairs(dom, step))  5.74 us
    ppermute x7, waiting for transfers between devices, swap_dom(): return lax.ppermute(array, 'dom', xor_pairs(dom, step))  5.24 us
    pallas_call x2, Pallas kernels, near_logits(): pl.pallas_call(functools.partial(near_kernel, sizes_of(picked), len(shard...  4.74 us
    pallas_call x2, Pallas kernels, aligned_rows(): pl.pallas_call(functools.partial(rows_kernel, sizes_of(picked)), out_shap...  3.79 us
    pallas_call x1, Pallas kernels, far_logits(): pl.pallas_call(functools.partial(far_kernel, sizes_of(picked), [right.sha...  3.26 us
    ppermute x1, starting transfers between devices, local(): lax.ppermute(stats, ('cls', 'dom'), pairs)  2.03 us
  transfers between devices with their start and end apart: 16, of which 10 were waited for; matrix products, arithmetic and copies ran while one was open for 1% of the time, Pallas kernels for 17%

profile of v6, /device:TPU:0, one launch (start us, length us, event | category | flops | bytes accessed | tf_op | source)
XLA Modules:
  0.0 54.9 jit_solution(11752471694842831696)
XLA Ops:
  0.6 0.0 copy-start
  0.6 0.0 copy-start.1
  0.7 1.5 %image_bands.1 = (bf16[2,16,8320]{2,1,0:T(8,128)(2,1)S(1)}, bf16[2,16,4224]{2,1,0:T(8,128)(2,1)S(1)}, bf16[2,16,8320]{2,1,0:T(8,128)(2,1)S(1)}, bf16[2,16,128]{2...) custom-call(bf16[2,16,32768]{2,1,0:T(8,128)(2,1)} %images.3, bf16[2,4,4,2048]{3,2,1,0:T(4,128)(2,1)} %references.1, ...), custom_call_target="tpu_custom_call" | custom-call | bytes 3145728 | tf_op jit(solution)/shard_map/image_bands/pallas_call | solution.py:110
  2.2 0.5 collective-permute-start
  2.7 2.6 %collective-permute-start.5 = (bf16[2,16,4224]{2,1,0:T(8,128)(2,1)S(1)}, bf16[2,16,4224]{2,1,0:T(8,128)(2,1)S(1)}, u32[]{:S(2)}, u32[]{:S(2)}) collective-permute-start(bf16[2,16,4224]{2,1,0:T(8,128)(2,1)S(1)} %get-tuple-element.42), channel_id=1, source_target_pairs={{0,8},{4,12},{8,0},{12,4},{1,9},{5,13},{9,1},{13,5},{2,10},{6,14},... | collective-permute-start | bytes 811016 | tf_op jit(solution)/shard_map/ppermute | solution.py:556
  5.2 0.0 collective-permute-done.rest_1_.rest_3_.rest_5_
  5.2 1.9 %collective-permute-start.3 = (bf16[2,4,4,2048]{3,2,1,0:T(4,128)(2,1)S(1)}, bf16[2,4,4,2048]{3,2,1,0:T(4,128)(2,1)S(1)}, u32[]{:S(2)}, u32[]{:S(2)}) collective-permute-start(bf16[2,4,4,2048]{3,2,1,0:T(4,128)(2,1)S(1)} %get-tuple-element.30.rest_0_), channel_id=1, source_target_pairs={{0,1},{1,0},{2,3},{3,2},{4,5},{5,4},{6,7},{7,6},{8,9},{9,8},{10,11... | collective-permute-start | bytes 393224 | tf_op jit(solution)/shard_map/ppermute | solution.py:559
  7.2 2.6 %collective-permute-start.1 = (bf16[2,4,4,2048]{3,2,1,0:T(4,128)(2,1)S(1)}, bf16[2,4,4,2048]{3,2,1,0:T(4,128)(2,1)S(1)}, u32[]{:S(2)}, u32[]{:S(2)}) collective-permute-start(bf16[2,4,4,2048]{3,2,1,0:T(4,128)(2,1)S(1)} %get-tuple-element.30.rest_0_), channel_id=1, source_target_pairs={{0,2},{1,3},{2,0},{3,1},{4,6},{5,7},{6,4},{7,5},{8,10},{9,11},{10,... | collective-permute-start | bytes 393224 | tf_op jit(solution)/shard_map/ppermute | solution.py:559
  9.8 0.0 collective-permute-start.2
  9.8 0.7 %collective-permute-start.7 = (bf16[2,16,8320]{2,1,0:T(8,128)(2,1)S(1)}, bf16[2,16,8320]{2,1,0:T(8,128)(2,1)S(1)}, u32[]{:S(2)}, u32[]{:S(2)}) collective-permute-start(bf16[2,16,8320]{2,1,0:T(8,128)(2,1)S(1)} %get-tuple-element.43), channel_id=1, source_target_pairs={{0,12},{4,8},{8,4},{12,0},{1,13},{5,9},{9,5},{13,1},{2,14},{6,10},... | collective-permute-start | bytes 1597448 | tf_op jit(solution)/shard_map/ppermute | solution.py:556
  10.4 1.0 %own_band.1.rest_2_ = bf16[2,16,8192]{2,1,0:T(8,128)(2,1)S(1)} custom-call(bf16[2,16,32768]{2,1,0:T(8,128)(2,1)} %images.3), custom_call_target="tpu_custom_call" | custom-call | tf_op jit(solution)/shard_map/own_band/pallas_call | solution.py:156
  11.5 0.8 %collective-permute-done.5.rest_2_.rest_0_.rest_6_ = bf16[2,16,4224]{2,1,0:T(8,128)(2,1)S(1)} collective-permute-done((bf16[2,16,4224]{2,1,0:T(8,128)(2,1)S(1)}, bf16[2,16,4224]{2,1,0:T(8,128)(2,1)S(1)}, u32[]{:S(2)}, u32[]{:S(2)}) %collective-permute-start.5) | collective-permute-done | bytes 270368 | tf_op jit(solution)/shard_map/ppermute | solution.py:556
  12.3 1.8 %collective-permute-start.6 = (bf16[2,16,4224]{2,1,0:T(8,128)(2,1)S(1)}, bf16[2,16,4224]{2,1,0:T(8,128)(2,1)S(1)}, u32[]{:S(2)}, u32[]{:S(2)}) collective-permute-start(bf16[2,16,4224]{2,1,0:T(8,128)(2,1)S(1)} %collective-permute-done.5.rest_2_.rest_0_.rest_6_), channel_id=1, source_target_pairs={{0,16},{16,0},{1,17},{17,1},{2,18},{18,2},{3,19},{19,3},{4,20},{20... | collective-permute-start | bytes 811016 | tf_op jit(solution)/shard_map/ppermute | solution.py:570
  14.1 0.0 copy-done
  14.1 0.0 copy-done.1
  14.1 1.7 %aligned_rows.2.rest_8_ = bf16[2,32,8192]{2,1,0:T(8,128)(2,1)S(1)} custom-call(f32[1024]{0:T(1024)S(1)} %copy-done.1, f32[8,256]{1,0:T(8,128)S(1)} %copy-done, bf16[2,16,128]{2,1,0:T(8,128)(2,1)S(1)} %get-tuple-element.32.rest_0_.rest_4_, bf16[2,16,8320]{2,1,0:T(8,128)(2,1)S(1)} %collective-permute-done.rest_1_.rest_3_.rest_5_, ...), custom_call_target="tpu_custom_call" | custom-call | tf_op jit(solution)/shard_map/aligned_rows/pallas_call | solution.py:445
  15.8 0.0 collective-permute-done.3.rest_1_
  15.8 2.4 %near_logits.2 = (f32[128,128]{1,0:T(8,128)S(1)}, f32[128,128]{1,0:T(8,128)S(1)}, bf16[2,128,4096]{2,1,0:T(8,128)(2,1)S(1)}) custom-call(f32[1024]{0:T(1024)S(1)} %copy-done.1, f32[8,256]{1,0:T(8,128)S(1)} %copy-done, bf16[2,4,4,2048]{3,2,1,0:T(4,128)(2,1)S(1)} %get-tuple-element.30.rest_0_, bf16[2,4,4,2048]{3,2,1,0:T(4,128)(2,1)S(1)} %collective-permute-done.3.rest_1_, ...), custom_call_target="tpu_custom_call" | custom-call | tf_op jit(solution)/shard_map/near_logits/pallas_call | solution.py:320
  18.2 1.8 %collective-permute-done.1.rest_0_ = bf16[2,4,4,2048]{3,2,1,0:T(4,128)(2,1)S(1)} collective-permute-done((bf16[2,4,4,2048]{3,2,1,0:T(4,128)(2,1)S(1)}, bf16[2,4,4,2048]{3,2,1,0:T(4,128)(2,1)S(1)}, u32[]{:S(2)}, u32[]{:S(2)}) %collective-permute-start.1) | collective-permute-done | bytes 131104 | tf_op jit(solution)/shard_map/ppermute | solution.py:559
  20.1 0.0 collective-permute-done.2.rest_1_
  20.1 2.4 %near_logits.3 = (f32[128,128]{1,0:T(8,128)S(1)}, f32[128,128]{1,0:T(8,128)S(1)}, bf16[2,128,4096]{2,1,0:T(8,128)(2,1)S(1)}) custom-call(f32[1024]{0:T(1024)S(1)} %copy-done.1, f32[8,256]{1,0:T(8,128)S(1)} %copy-done, bf16[2,4,4,2048]{3,2,1,0:T(4,128)(2,1)S(1)} %collective-permute-done.1.rest_0_, bf16[2,4,4,2048]{3,2,1,0:T(4,128)(2,1)S(1)} %collective-permute-done.2.rest_1_, ...), custom_call_target="tpu_custom_call" | custom-call | flops 20000000000 | tf_op jit(solution)/shard_map/near_logits/pallas_call | solution.py:320
  22.4 0.1 collective-permute-start.4
  22.5 1.2 %collective-permute-done.4 = f32[128,128]{1,0:T(8,128)S(1)} collective-permute-done((f32[128,128]{1,0:T(8,128)S(1)}, f32[128,128]{1,0:T(8,128)S(1)}, u32[]{:S(2)}, u32[]{:S(2)}) %collective-permute-start.4) | collective-permute-done | bytes 65568 | tf_op jit(solution)/shard_map/ppermute | solution.py:556
  23.7 0.1 collective-permute-done.7.rest_4_.rest_1_.rest_7_
  23.9 0.0 collective-permute-done.6.rest_3_
  23.9 3.3 %far_logits.1 = (f32[128,128]{1,0:T(8,128)S(1)}, f32[128,128]{1,0:T(8,128)S(1)}) custom-call(f32[8,256]{1,0:T(8,128)S(1)} %copy-done, bf16[2,128,4096]{2,1,0:T(8,128)(2,1)S(1)} %get-tuple-element.40.rest_0_, bf16[2,128,4096]{2,1,0:T(8,128)(2,1)S(1)} %get-tuple-element.41.rest_1_, bf16[2,16,4224]{2,1,0:T(8,128)(2,1)S(1)} %collective-permute-done.5.rest_2_.rest_0_.rest_6_, ...), custom_call_target="tpu_custom_call" | custom-call | flops 6000000000 | tf_op jit(solution)/shard_map/far_logits/pallas_call | solution.py:345
  27.2 0.2 collective-permute-start.8
  27.4 1.1 %collective-permute-done.8 = f32[128,128]{1,0:T(8,128)S(1)} collective-permute-done((f32[128,128]{1,0:T(8,128)S(1)}, f32[128,128]{1,0:T(8,128)S(1)}, u32[]{:S(2)}, u32[]{:S(2)}) %collective-permute-start.8) | collective-permute-done | bytes 65568 | tf_op jit(solution)/shard_map/ppermute | solution.py:556
  28.5 1.7 %collective-permute-start.9 = (f32[2,128,128]{2,1,0:T(8,128)S(1)}, f32[2,128,128]{2,1,0:T(8,128)S(1)}, u32[]{:S(2)}, u32[]{:S(2)}) collective-permute-start(f32[2,128,128]{2,1,0:T(8,128)S(1)} %pad_maximum_fusion.here), channel_id=1, source_target_pairs={{0,8},{4,12},{8,0},{12,4},{1,9},{5,13},{9,1},{13,5},{2,10},{6,14},... | collective-permute-start | bytes 393224 | tf_op jit(solution)/shard_map/ppermute | solution.py:556
  30.2 2.1 %aligned_rows.3.rest_9_ = bf16[2,32,8192]{2,1,0:T(8,128)(2,1)S(1)} custom-call(f32[1024]{0:T(1024)S(1)} %copy-done.1, f32[8,256]{1,0:T(8,128)S(1)} %copy-done, bf16[2,16,4224]{2,1,0:T(8,128)(2,1)S(1)} %collective-permute-done.5.rest_2_.rest_0_.rest_6_, bf16[2,16,8320]{2,1,0:T(8,128)(2,1)S(1)} %collective-permute-done.7.rest_4_.rest_1_.rest_7_, ...), custom_call_target="tpu_custom_call" | custom-call | tf_op jit(solution)/shard_map/aligned_rows/pallas_call | solution.py:445
  32.2 1.9 %collective-permute-done.9.there = f32[2,128,128]{2,1,0:T(8,128)S(1)} collective-permute-done((f32[2,128,128]{2,1,0:T(8,128)S(1)}, f32[2,128,128]{2,1,0:T(8,128)S(1)}, u32[]{:S(2)}, u32[]{:S(2)}) %collective-permute-start.9) | collective-permute-done | bytes 131104 | tf_op jit(solution)/shard_map/ppermute | solution.py:556
  34.1 0.2 logit_stats.1.rest_0_
  34.3 0.1 collective-permute-start.10
  34.4 2.0 %collective-permute-start.11 = (f32[32,128]{1,0:T(8,128)S(1)}, f32[32,128]{1,0:T(8,128)S(1)}, u32[]{:S(2)}, u32[]{:S(2)}) collective-permute-start(f32[32,128]{1,0:T(8,128)S(1)} %logit_stats.1.rest_0_), channel_id=1, source_target_pairs={{0,16},{4,20},{8,24},{12,28},{16,0},{20,4},{24,8},{28,12},{1,17},{... | collective-permute-start | bytes 49160 | tf_op jit(solution)/shard_map/ppermute | solution.py:604
  36.5 0.1 collective-permute-start.12
  36.5 0.0 collective-permute-done.10.rest_1_
  36.5 1.7 %collective-permute-done.11.rest_2_ = f32[32,128]{1,0:T(8,128)S(1)} collective-permute-done((f32[32,128]{1,0:T(8,128)S(1)}, f32[32,128]{1,0:T(8,128)S(1)}, u32[]{:S(2)}, u32[]{:S(2)}) %collective-permute-start.11) | collective-permute-done | bytes 16416 | tf_op jit(solution)/shard_map/ppermute | solution.py:604
  38.2 1.4 %collective-permute-done.12.rest_3_ = f32[32,128]{1,0:T(8,128)S(1)} collective-permute-done((f32[32,128]{1,0:T(8,128)S(1)}, f32[32,128]{1,0:T(8,128)S(1)}, u32[]{:S(2)}, u32[]{:S(2)}) %collective-permute-start.12) | collective-permute-done | bytes 16416 | tf_op jit(solution)/shard_map/ppermute | solution.py:605
  39.6 1.0 %volume_terms.1 = (f32[16,128]{1,0:T(8,128)S(1)}, f32[2,4,8192]{2,1,0:T(4,128)S(1)}, bf16[2,4,8192]{2,1,0:T(4,128)(2,1)S(1)}, bf16[2,4,8192]{2,1,0:T(4,128)(2,1)S(1)}, bf16[2,4,8192]{2,1,0:T(4,128)(2,1)S(1)}) custom-call(f32[32,128]{1,0:T(8,128)S(1)} %logit_stats.1.rest_0_, f32[32,128]{1,0:T(8,128)S(1)} %collective-permute-done.10.rest_1_, ...), custom_call_target="tpu_custom_call" | custom-call | flops 33554432 | bytes 2621440 | tf_op jit(solution)/shard_map/volume_terms/pallas_call | solution.py:513
  40.6 2.8 %collective-permute-start.13 = (bf16[2,4,8192]{2,1,0:T(4,128)(2,1)S(1)}, bf16[2,4,8192]{2,1,0:T(4,128)(2,1)S(1)}, u32[]{:S(2)}, u32[]{:S(2)}) collective-permute-start(bf16[2,4,8192]{2,1,0:T(4,128)(2,1)S(1)} %get-tuple-element.51), channel_id=1, source_target_pairs={{0,2},{1,3},{2,0},{3,1},{4,6},{5,7},{6,4},{7,5},{8,10},{9,11},{10,... | collective-permute-start | bytes 393224 | tf_op jit(solution)/shard_map/ppermute | solution.py:559
  43.4 1.4 %collective-permute-start.14 = (bf16[2,4,8192]{2,1,0:T(4,128)(2,1)S(1)}, bf16[2,4,8192]{2,1,0:T(4,128)(2,1)S(1)}, u32[]{:S(2)}, u32[]{:S(2)}) collective-permute-start(bf16[2,4,8192]{2,1,0:T(4,128)(2,1)S(1)} %get-tuple-element.52), channel_id=1, source_target_pairs={{0,1},{1,0},{2,3},{3,2},{4,5},{5,4},{6,7},{7,6},{8,9},{9,8},{10,11... | collective-permute-start | bytes 393224 | tf_op jit(solution)/shard_map/ppermute | solution.py:559
  44.9 0.2 collective-permute-start.15
  45.1 0.7 %copy.9 = f32[16,4]{0,1:T(4,128)} copy(f32[16,4]{1,0:T(8,128)S(1)} %bitcast.8) | data formatting | bytes 512
  45.7 5.3 %collective-permute-done.13.rest_0_ = bf16[2,4,8192]{2,1,0:T(4,128)(2,1)S(1)} collective-permute-done((bf16[2,4,8192]{2,1,0:T(4,128)(2,1)S(1)}, bf16[2,4,8192]{2,1,0:T(4,128)(2,1)S(1)}, u32[]{:S(2)}, u32[]{:S(2)}) %collective-permute-start.13) | collective-permute-done | bytes 131104 | tf_op jit(solution)/shard_map/ppermute | solution.py:559
  51.0 0.0 collective-permute-done.14.rest_1_
  51.0 3.1 %collective-permute-done.15.rest_2_ = bf16[2,4,8192]{2,1,0:T(4,128)(2,1)S(1)} collective-permute-done((bf16[2,4,8192]{2,1,0:T(4,128)(2,1)S(1)}, bf16[2,4,8192]{2,1,0:T(4,128)(2,1)S(1)}, u32[]{:S(2)}, u32[]{:S(2)}) %collective-permute-start.15) | collective-permute-done | bytes 131104 | tf_op jit(solution)/shard_map/ppermute | solution.py:559
  54.1 0.8 %total_volume.1 = f32[2,4,1,8192]{3,2,1,0:T(1,128)} custom-call(f32[2,4,8192]{2,1,0:T(4,128)S(1)} %get-tuple-element.50.first, bf16[2,4,8192]{2,1,0:T(4,128)(2,1)S(1)} %collective-permute-done.13.rest_0_, bf16[2,4,8192]{2,1,0:T(4,128)(2,1)S(1)} %collective-permute-done.14.rest_1_, bf16[2,4,8192]{2,1,0:T(4,128)(2,1)S(1)} %collective-permute-done.15.rest_2_), custom_call_target="tpu_custom_call" | custom-call | tf_op jit(solution)/shard_map/total_volume/pallas_call | solution.py:542
  (3 shorter events, 0.0 us)
Async XLA Ops:
  0.6 13.5 %copy-start = (f32[8,256]{1,0:T(8,128)S(1)}, f32[8,256]{1,0:T(8,128)}, u32[]{:S(2)}) copy-start(f32[8,256]{1,0:T(8,128)} %constant.4.clone.table_x) | copy-start | bytes 24580
  0.6 13.5 %copy-start.1 = (f32[1024]{0:T(1024)S(1)}, f32[1024]{0:T(1024)}, u32[]{:S(2)}) copy-start(f32[1024]{0:T(1024)} %constant.5.clone.table_y) | copy-start | bytes 12292
  2.2 3.1 %collective-permute-start = (bf16[2,16,8320]{2,1,0:T(8,128)(2,1)S(1)}, bf16[2,16,8320]{2,1,0:T(8,128)(2,1)S(1)}, u32[]{:S(2)}, u32[]{:S(2)}) collective-permute-start(bf16[2,16,8320]{2,1,0:T(8,128)(2,1)S(1)} %get-tuple-element.29), channel_id=1, source_target_pairs={{0,4},{4,0},{8,12},{12,8},{1,5},{5,1},{9,13},{13,9},{2,6},{6,2},{1... | collective-permute-start | bytes 1597448 | tf_op jit(solution)/shard_map/ppermute | solution.py:556
  2.7 9.6 %collective-permute-start.5 = (bf16[2,16,4224]{2,1,0:T(8,128)(2,1)S(1)}, bf16[2,16,4224]{2,1,0:T(8,128)(2,1)S(1)}, u32[]{:S(2)}, u32[]{:S(2)}) collective-permute-start(bf16[2,16,4224]{2,1,0:T(8,128)(2,1)S(1)} %get-tuple-element.42), channel_id=1, source_target_pairs={{0,8},{4,12},{8,0},{12,4},{1,9},{5,13},{9,1},{13,5},{2,10},{6,14},... | collective-permute-start | bytes 811016 | tf_op jit(solution)/shard_map/ppermute | solution.py:556
  5.2 10.6 %collective-permute-start.3 = (bf16[2,4,4,2048]{3,2,1,0:T(4,128)(2,1)S(1)}, bf16[2,4,4,2048]{3,2,1,0:T(4,128)(2,1)S(1)}, u32[]{:S(2)}, u32[]{:S(2)}) collective-permute-start(bf16[2,4,4,2048]{3,2,1,0:T(4,128)(2,1)S(1)} %get-tuple-element.30.rest_0_), channel_id=1, source_target_pairs={{0,1},{1,0},{2,3},{3,2},{4,5},{5,4},{6,7},{7,6},{8,9},{9,8},{10,11... | collective-permute-start | bytes 393224 | tf_op jit(solution)/shard_map/ppermute | solution.py:559
  7.2 12.9 %collective-permute-start.1 = (bf16[2,4,4,2048]{3,2,1,0:T(4,128)(2,1)S(1)}, bf16[2,4,4,2048]{3,2,1,0:T(4,128)(2,1)S(1)}, u32[]{:S(2)}, u32[]{:S(2)}) collective-permute-start(bf16[2,4,4,2048]{3,2,1,0:T(4,128)(2,1)S(1)} %get-tuple-element.30.rest_0_), channel_id=1, source_target_pairs={{0,2},{1,3},{2,0},{3,1},{4,6},{5,7},{6,4},{7,5},{8,10},{9,11},{10,... | collective-permute-start | bytes 393224 | tf_op jit(solution)/shard_map/ppermute | solution.py:559
  9.8 10.3 %collective-permute-start.2 = (bf16[2,4,4,2048]{3,2,1,0:T(4,128)(2,1)S(1)}, bf16[2,4,4,2048]{3,2,1,0:T(4,128)(2,1)S(1)}, u32[]{:S(2)}, u32[]{:S(2)}) collective-permute-start(bf16[2,4,4,2048]{3,2,1,0:T(4,128)(2,1)S(1)} %get-tuple-element.30.rest_0_), channel_id=1, source_target_pairs={{0,3},{1,2},{2,1},{3,0},{4,7},{5,6},{6,5},{7,4},{8,11},{9,10},{10,... | collective-permute-start | bytes 393224 | tf_op jit(solution)/shard_map/ppermute | solution.py:559
  9.8 14.1 %collective-permute-start.7 = (bf16[2,16,8320]{2,1,0:T(8,128)(2,1)S(1)}, bf16[2,16,8320]{2,1,0:T(8,128)(2,1)S(1)}, u32[]{:S(2)}, u32[]{:S(2)}) collective-permute-start(bf16[2,16,8320]{2,1,0:T(8,128)(2,1)S(1)} %get-tuple-element.43), channel_id=1, source_target_pairs={{0,12},{4,8},{8,4},{12,0},{1,13},{5,9},{9,5},{13,1},{2,14},{6,10},... | collective-permute-start | bytes 1597448 | tf_op jit(solution)/shard_map/ppermute | solution.py:556
  12.3 11.6 %collective-permute-start.6 = (bf16[2,16,4224]{2,1,0:T(8,128)(2,1)S(1)}, bf16[2,16,4224]{2,1,0:T(8,128)(2,1)S(1)}, u32[]{:S(2)}, u32[]{:S(2)}) collective-permute-start(bf16[2,16,4224]{2,1,0:T(8,128)(2,1)S(1)} %collective-permute-done.5.rest_2_.rest_0_.rest_6_), channel_id=1, source_target_pairs={{0,16},{16,0},{1,17},{17,1},{2,18},{18,2},{3,19},{19,3},{4,20},{20... | collective-permute-start | bytes 811016 | tf_op jit(solution)/shard_map/ppermute | solution.py:570
  22.4 1.3 %collective-permute-start.4 = (f32[128,128]{1,0:T(8,128)S(1)}, f32[128,128]{1,0:T(8,128)S(1)}, u32[]{:S(2)}, u32[]{:S(2)}) collective-permute-start(f32[128,128]{1,0:T(8,128)S(1)} %get-tuple-element.38), channel_id=1, source_target_pairs={{0,4},{4,0},{8,12},{12,8},{1,5},{5,1},{9,13},{13,9},{2,6},{6,2},{1... | collective-permute-start | bytes 196616 | tf_op jit(solution)/shard_map/ppermute | solution.py:556
  27.2 1.3 %collective-permute-start.8 = (f32[128,128]{1,0:T(8,128)S(1)}, f32[128,128]{1,0:T(8,128)S(1)}, u32[]{:S(2)}, u32[]{:S(2)}) collective-permute-start(f32[128,128]{1,0:T(8,128)S(1)} %get-tuple-element.45), channel_id=1, source_target_pairs={{0,4},{4,0},{8,12},{12,8},{1,5},{5,1},{9,13},{13,9},{2,6},{6,2},{1... | collective-permute-start | bytes 196616 | tf_op jit(solution)/shard_map/ppermute | solution.py:556
  28.5 5.6 %collective-permute-start.9 = (f32[2,128,128]{2,1,0:T(8,128)S(1)}, f32[2,128,128]{2,1,0:T(8,128)S(1)}, u32[]{:S(2)}, u32[]{:S(2)}) collective-permute-start(f32[2,128,128]{2,1,0:T(8,128)S(1)} %pad_maximum_fusion.here), channel_id=1, source_target_pairs={{0,8},{4,12},{8,0},{12,4},{1,9},{5,13},{9,1},{13,5},{2,10},{6,14},... | collective-permute-start | bytes 393224 | tf_op jit(solution)/shard_map/ppermute | solution.py:556
  34.3 2.2 %collective-permute-start.10 = (f32[32,128]{1,0:T(8,128)S(1)}, f32[32,128]{1,0:T(8,128)S(1)}, u32[]{:S(2)}, u32[]{:S(2)}) collective-permute-start(f32[32,128]{1,0:T(8,128)S(1)} %logit_stats.1.rest_0_), channel_id=1, source_target_pairs={{0,4},{4,0},{8,12},{12,8},{1,5},{5,1},{9,13},{13,9},{2,6},{6,2},{1... | collective-permute-start | bytes 49160 | tf_op jit(solution)/shard_map/ppermute | solution.py:556
  34.4 3.8 %collective-permute-start.11 = (f32[32,128]{1,0:T(8,128)S(1)}, f32[32,128]{1,0:T(8,128)S(1)}, u32[]{:S(2)}, u32[]{:S(2)}) collective-permute-start(f32[32,128]{1,0:T(8,128)S(1)} %logit_stats.1.rest_0_), channel_id=1, source_target_pairs={{0,16},{4,20},{8,24},{12,28},{16,0},{20,4},{24,8},{28,12},{1,17},{... | collective-permute-start | bytes 49160 | tf_op jit(solution)/shard_map/ppermute | solution.py:604
  36.5 3.2 %collective-permute-start.12 = (f32[32,128]{1,0:T(8,128)S(1)}, f32[32,128]{1,0:T(8,128)S(1)}, u32[]{:S(2)}, u32[]{:S(2)}) collective-permute-start(f32[32,128]{1,0:T(8,128)S(1)} %logit_stats.1.rest_0_), channel_id=1, source_target_pairs={{0,20},{4,16},{8,28},{12,24},{16,4},{20,0},{24,12},{28,8},{1,21},{... | collective-permute-start | bytes 49160 | tf_op jit(solution)/shard_map/ppermute | solution.py:605
  40.6 10.4 %collective-permute-start.13 = (bf16[2,4,8192]{2,1,0:T(4,128)(2,1)S(1)}, bf16[2,4,8192]{2,1,0:T(4,128)(2,1)S(1)}, u32[]{:S(2)}, u32[]{:S(2)}) collective-permute-start(bf16[2,4,8192]{2,1,0:T(4,128)(2,1)S(1)} %get-tuple-element.51), channel_id=1, source_target_pairs={{0,2},{1,3},{2,0},{3,1},{4,6},{5,7},{6,4},{7,5},{8,10},{9,11},{10,... | collective-permute-start | bytes 393224 | tf_op jit(solution)/shard_map/ppermute | solution.py:559
  43.4 7.6 %collective-permute-start.14 = (bf16[2,4,8192]{2,1,0:T(4,128)(2,1)S(1)}, bf16[2,4,8192]{2,1,0:T(4,128)(2,1)S(1)}, u32[]{:S(2)}, u32[]{:S(2)}) collective-permute-start(bf16[2,4,8192]{2,1,0:T(4,128)(2,1)S(1)} %get-tuple-element.52), channel_id=1, source_target_pairs={{0,1},{1,0},{2,3},{3,2},{4,5},{5,4},{6,7},{7,6},{8,9},{9,8},{10,11... | collective-permute-start | bytes 393224 | tf_op jit(solution)/shard_map/ppermute | solution.py:559
  44.9 9.2 %collective-permute-start.15 = (bf16[2,4,8192]{2,1,0:T(4,128)(2,1)S(1)}, bf16[2,4,8192]{2,1,0:T(4,128)(2,1)S(1)}, u32[]{:S(2)}, u32[]{:S(2)}) collective-permute-start(bf16[2,4,8192]{2,1,0:T(4,128)(2,1)S(1)} %get-tuple-element.53), channel_id=1, source_target_pairs={{0,3},{1,2},{2,1},{3,0},{4,7},{5,6},{6,5},{7,4},{8,11},{9,10},{10,... | collective-permute-start | bytes 393224 | tf_op jit(solution)/shard_map/ppermute | solution.py:559

commit v7 on v6

--- a/solution.py
+++ b/solution.py
@@ -354,15 +354,17 @@
     )(*arrays)
 
 
-def stats_kernel(swap, classes, orients, here, there, out):
-    groups, group_rows, lanes = here.shape
-    rows = group_rows // TX
+def stats_kernel(counts, classes, orients, *refs):
+    *logits, out = refs
+    rows, lanes = logits[0].shape[0] // TX, logits[0].shape[1]
     lane = lax.broadcasted_iota(jnp.int32, (rows, lanes), 1)
     class_of = (lane // orients) % classes
     out_lane = lax.broadcasted_iota(jnp.int32, (rows, LANES), 1)
-    for g in range(groups):
-        logits = here[g] + there[g ^ swap]
-        pieces = [logits[a * rows : (a + 1) * rows] for a in range(TX)]
+    packed = jnp.zeros((SUBLANES, LANES), F32)
+    for g, count in enumerate(counts):
+        total = sum(ref[...] for ref in logits[:count])
+        logits = logits[count:]
+        pieces = [total[a * rows : (a + 1) * rows] for a in range(TX)]
         top = functools.reduce(jnp.maximum, pieces)
         top = jnp.max(top, axis=1, keepdims=True)
         sums = sum(jnp.exp(piece - top) for piece in pieces)
@@ -370,21 +372,21 @@
         for k in range(classes):
             part = jnp.sum(jnp.where(class_of == k, sums, 0.0), axis=1, keepdims=True)
             line = jnp.where(out_lane == k + 1, part, line)
-        out[g * rows : (g + 1) * rows, :] = line
-
-
-def logit_stats(here, there, swap, classes, orients):
-    groups, group_rows, lanes = here.shape
-    arrays, specs = in_vmem([here, there])
+        for half in range(rows // SUBLANES):
+            block = line[half * SUBLANES : (half + 1) * SUBLANES]
+            place = (g * (rows // SUBLANES) + half) * SUBLANES
+            packed = packed + pltpu.roll(block, place, 1)
+    out[...] = packed
+
+
+def logit_stats(terms, classes, orients):
+    arrays, specs = in_vmem([array for held in terms for array in held])
     return pl.pallas_call(
-        functools.partial(stats_kernel, swap, classes, orients),
-        out_shape=pltpu.VMEM((groups * group_rows // TX, LANES), F32),
+        functools.partial(stats_kernel, [len(held) for held in terms], classes, orients),
+        out_shape=pltpu.VMEM((SUBLANES, LANES), F32),
         in_specs=specs,
         out_specs=VMEM_SPEC,
         compiler_params=pltpu.CompilerParams(vmem_limit_bytes=VMEM_BYTES),
-        cost_estimate=pl.CostEstimate(
-            flops=4 * here.size, bytes_accessed=8 * here.size, transcendentals=here.size
-        ),
         name="logit_stats",
     )(*arrays)
 
@@ -457,21 +459,28 @@
     )(table_y, *arrays)
 
 
+def unpacked(packed, place, blocks):
+    first = place * blocks * SUBLANES
+    return jnp.concatenate(
+        [pltpu.roll(packed, (LANES - first - i * SUBLANES) % LANES, 1) for i in range(blocks)]
+    )
+
+
 def volume_kernel(groups, orients, classes, *rest):
     ids = device_ids()
-    stats, metas = rest[:4], rest[4 : 4 + groups]
-    near, far = rest[4 + groups], rest[5 + groups]
-    prob, outs = rest[6 + groups], rest[7 + groups :]
+    stats, metas = rest[:2], rest[2 : 2 + groups]
+    near, far = rest[2 + groups], rest[3 + groups]
+    prob, outs = rest[4 + groups], rest[5 + groups :]
     rows = metas[0].shape[1]
     width = near.shape[2]
     chunk = min(width, 8 * IMG)
     lane = lax.broadcasted_iota(jnp.int32, (rows, LANES), 1)
     pieces = []
     for g in range(groups):
-        mine, other = (stats[0], stats[2]) if g % 2 == 0 else (stats[1], stats[3])
-        place = g // 2
-        mine = mine[place * rows : (place + 1) * rows, :]
-        other = other[place * rows : (place + 1) * rows, :]
+        top = g % 2 * SUBLANES
+        mine, other = (
+            unpacked(ref[top : top + SUBLANES, :], g // 2, rows // SUBLANES) for ref in stats
+        )
         top = jnp.maximum(mine[:, 0:1], other[:, 0:1])
         mine_scale = jnp.exp(mine[:, 0:1] - top)
         other_scale = jnp.exp(other[:, 0:1] - top)
@@ -562,8 +571,10 @@
         orient_lists, shift_ids, fixed_weights, images, references, dom
     )
     arrived = {step: swap_dom(bands[step - 1], step) for step in [1, *range(dom - 1, 1, -1)]}
-    shard, arrived[1] = lax.optimization_barrier((shard, arrived[1]))
-    shards = [shard] + [swap_orient(shard, step) for step in range(1, orient)]
+    tied, arrived[1] = lax.optimization_barrier((shard, arrived[1]))
+    shards = [shard] + [
+        swap_orient(tied if step == orient - 1 else shard, step) for step in range(1, orient)
+    ]
     half = arrived[SHARED]
     groups = [([own_band(images, dom)], meta)]
     groups += [([arrived[step]], arrived[step]) for step in range(1, dom)]
@@ -579,31 +590,34 @@
     )
     swapped = swap_dom(near[1], 1)
     right_late, swapped = lax.optimization_barrier((right_late, swapped))
-    far = far_logits(table_x, [right, right_late], groups[2:], 6)
-    partial = [*near, *far]
-    kept = [near[0] + swapped]
-    kept += [partial[s] + swap_dom(partial[s ^ 1], 1) for s in range(2, dom, 2)]
-    here = jnp.stack(kept)
-    step = 2
-    there, swap = jnp.zeros_like(here), 0
-    while step < dom:
-        there, swap = swap_dom(here, step), step // 2
-        if step * 2 < dom:
-            order = np.arange(dom // 2) ^ swap
-            here = here + jnp.stack([there[i] for i in order])
-        step *= 2
+    one_phase = dom == 4
+    if one_phase:
+        crossed = swap_dom(near[0], 2)
+        crossed_over = swap_dom(near[1], 3)
+    far = list(far_logits(table_x, [right, right_late], groups[2:], 6))
+    if one_phase:
+        far[1], crossed, crossed_over = lax.optimization_barrier((far[1], crossed, crossed_over))
+        terms = [
+            [near[0], swapped, swap_dom(far[0], 2), swap_dom(far[1], 3)],
+            [far[0], swap_dom(far[1], 1), crossed, crossed_over],
+        ]
+    else:
+        partial = [*near, *far]
+        here = {s: partial[s] + swap_dom(partial[s ^ 1], 1) for s in range(2, dom, 2)}
+        here[0] = near[0] + swapped
+        step = 2
+        while step < dom:
+            there = {s: swap_dom(here[s ^ step], step) for s in here}
+            step *= 2
+            if step < dom:
+                here = {s: here[s] + there[s] for s in here}
+        terms = [[here[s], there[s]] for s in sorted(here)]
     aligned_far = aligned_rows(table_x, table_y, groups[2:], width)
-    there, aligned_far = lax.optimization_barrier((there, aligned_far))
-    stats = logit_stats(here, there, swap, classes, orients)
-
-    pairs = [(i, i ^ dom) for i in range(cls * dom)]
-    cross = [(i, i ^ dom ^ 1) for i in range(cls * dom)]
-    stats_all = [
-        stats,
-        swap_dom(stats, 1),
-        lax.ppermute(stats, ("cls", "dom"), pairs),
-        lax.ppermute(stats, ("cls", "dom"), cross),
-    ]
+    terms[0][-1], aligned_far = lax.optimization_barrier((terms[0][-1], aligned_far))
+    stats = logit_stats(terms, classes, orients)
+
+    stats = jnp.concatenate([stats, swap_dom(stats, 1)])
+    stats_all = [stats, lax.ppermute(stats, "cls", xor_pairs(cls, 1))]
     prob, *terms = volume_terms(
         stats_all, groups, aligned_near, aligned_far, orients, classes
     )

time: 55.4 us -> 53.6 us (0.968)
  waiting for transfers between devices: 18.5 us -> 14.9 us
  starting transfers between devices: 18.6 us -> 20.6 us
    ppermute x7 -> x10, starting transfers between devices: 5.74 us -> 7.97 us  [swap_dom(): return lax.ppermute(array, 'dom', xor_pairs(dom, step))]
    ppermute x6, waiting for transfers between devices: 10.2 us -> 8.84 us  [swap_orient(): return lax.ppermute(array, 'orient', xor_pairs(orient, step))]
    ppermute x7 -> x10, waiting for transfers between devices: 5.24 us -> 3.93 us  [swap_dom(): return lax.ppermute(array, 'dom', xor_pairs(dom, step))]
    ppermute x2 -> x1, waiting for transfers between devices: 3.09 us -> 2.13 us  [local(): stats_all = [stats, lax.ppermute(stats, 'cls', xor_pairs(cls, 1))]]
    ppermute x2 -> x1, starting transfers between devices: 2.1 us -> 1.52 us  [local(): stats_all = [stats, lax.ppermute(stats, 'cls', xor_pairs(cls, 1))]]
  transfers between devices with their start and end apart: 16 -> 18, of which waited for: 10 -> 8; matrix products, arithmetic and copies ran while one was open for 1% -> 1% of each run, Pallas kernels for 17% -> 24%
where the time goes in v7:
time: 53.6 us; the launch traced here: 53.4 us
  starting transfers between devices  20.6 us (38%)
  Pallas kernels  16.5 us (31%)
  waiting for transfers between devices  14.9 us (28%)
  between operations  0.78 us (1%)
  local copies, waits for them, and re-layouts  0.66 us (1%)
    ppermute x6, starting transfers between devices, swap_orient(): return lax.ppermute(array, 'orient', xor_pairs(orient, step))  9.31 us
    ppermute x6, waiting for transfers between devices, swap_orient(): return lax.ppermute(array, 'orient', xor_pairs(orient, step))  8.84 us
    ppermute x10, starting transfers between devices, swap_dom(): return lax.ppermute(array, 'dom', xor_pairs(dom, step))  7.97 us
    pallas_call x2, Pallas kernels, near_logits(): pl.pallas_call(functools.partial(near_kernel, sizes_of(picked), len(shard...  4.75 us
    ppermute x10, waiting for transfers between devices, swap_dom(): return lax.ppermute(array, 'dom', xor_pairs(dom, step))  3.93 us
    pallas_call x2, Pallas kernels, aligned_rows(): pl.pallas_call(functools.partial(rows_kernel, sizes_of(picked)), out_shap...  3.79 us
    pallas_call x1, Pallas kernels, far_logits(): pl.pallas_call(functools.partial(far_kernel, sizes_of(picked), [right.sha...  3.32 us
    ppermute x1, waiting for transfers between devices, local(): stats_all = [stats, lax.ppermute(stats, 'cls', xor_pairs(cls, 1))]  2.13 us
  transfers between devices with their start and end apart: 18, of which 8 were waited for; matrix products, arithmetic and copies ran while one was open for 1% of the time, Pallas kernels for 24%

profile of v7, /device:TPU:0, one launch (start us, length us, event | category | flops | bytes accessed | tf_op | source)
XLA Modules:
  0.0 53.4 jit_solution(15931984122851693391)
XLA Ops:
  0.6 0.0 copy-start
  0.6 0.0 copy-start.1
  0.7 1.5 %image_bands.1 = (bf16[2,16,8320]{2,1,0:T(8,128)(2,1)S(1)}, bf16[2,16,4224]{2,1,0:T(8,128)(2,1)S(1)}, bf16[2,16,8320]{2,1,0:T(8,128)(2,1)S(1)}, bf16[2,16,128]{2...) custom-call(bf16[2,16,32768]{2,1,0:T(8,128)(2,1)} %images.3, bf16[2,4,4,2048]{3,2,1,0:T(4,128)(2,1)} %references.1, ...), custom_call_target="tpu_custom_call" | custom-call | bytes 3145728 | tf_op jit(solution)/shard_map/image_bands/pallas_call | solution.py:110
  2.2 0.5 collective-permute-start.1
  2.7 2.6 %collective-permute-start.5 = (bf16[2,16,4224]{2,1,0:T(8,128)(2,1)S(1)}, bf16[2,16,4224]{2,1,0:T(8,128)(2,1)S(1)}, u32[]{:S(2)}, u32[]{:S(2)}) collective-permute-start(bf16[2,16,4224]{2,1,0:T(8,128)(2,1)S(1)} %get-tuple-element.45), channel_id=1, source_target_pairs={{0,8},{4,12},{8,0},{12,4},{1,9},{5,13},{9,1},{13,5},{2,10},{6,14},... | collective-permute-start | bytes 811016 | tf_op jit(solution)/shard_map/ppermute | solution.py:565
  5.2 1.6 %collective-permute-start.3 = (bf16[2,4,4,2048]{3,2,1,0:T(4,128)(2,1)S(1)}, bf16[2,4,4,2048]{3,2,1,0:T(4,128)(2,1)S(1)}, u32[]{:S(2)}, u32[]{:S(2)}) collective-permute-start(bf16[2,4,4,2048]{3,2,1,0:T(4,128)(2,1)S(1)} %get-tuple-element.33.rest_0_), channel_id=1, source_target_pairs={{0,1},{1,0},{2,3},{3,2},{4,5},{5,4},{6,7},{7,6},{8,9},{9,8},{10,11... | collective-permute-start | bytes 393224 | tf_op jit(solution)/shard_map/ppermute | solution.py:568
  6.8 2.6 %collective-permute-start = (bf16[2,4,4,2048]{3,2,1,0:T(4,128)(2,1)S(1)}, bf16[2,4,4,2048]{3,2,1,0:T(4,128)(2,1)S(1)}, u32[]{:S(2)}, u32[]{:S(2)}) collective-permute-start(bf16[2,4,4,2048]{3,2,1,0:T(4,128)(2,1)S(1)} %get-tuple-element.33.rest_0_), channel_id=1, source_target_pairs={{0,2},{1,3},{2,0},{3,1},{4,6},{5,7},{6,4},{7,5},{8,10},{9,11},{10,... | collective-permute-start | bytes 393224 | tf_op jit(solution)/shard_map/ppermute | solution.py:568
  9.4 0.0 collective-permute-done.1.rest_1_.rest_3_
  9.4 0.2 collective-permute-start.2
  9.6 0.5 collective-permute-start.7
  10.1 1.0 %own_band.1.rest_2_ = bf16[2,16,8192]{2,1,0:T(8,128)(2,1)S(1)} custom-call(bf16[2,16,32768]{2,1,0:T(8,128)(2,1)} %images.3), custom_call_target="tpu_custom_call" | custom-call | tf_op jit(solution)/shard_map/own_band/pallas_call | solution.py:156
  11.2 1.1 %collective-permute-done.5.rest_2_.rest_0_.rest_4_ = bf16[2,16,4224]{2,1,0:T(8,128)(2,1)S(1)} collective-permute-done((bf16[2,16,4224]{2,1,0:T(8,128)(2,1)S(1)}, bf16[2,16,4224]{2,1,0:T(8,128)(2,1)S(1)}, u32[]{:S(2)}, u32[]{:S(2)}) %collective-permute-start.5) | collective-permute-done | bytes 270368 | tf_op jit(solution)/shard_map/ppermute | solution.py:565
  12.3 1.8 %collective-permute-start.6 = (bf16[2,16,4224]{2,1,0:T(8,128)(2,1)S(1)}, bf16[2,16,4224]{2,1,0:T(8,128)(2,1)S(1)}, u32[]{:S(2)}, u32[]{:S(2)}) collective-permute-start(bf16[2,16,4224]{2,1,0:T(8,128)(2,1)S(1)} %collective-permute-done.5.rest_2_.rest_0_.rest_4_), channel_id=1, source_target_pairs={{0,16},{16,0},{1,17},{17,1},{2,18},{18,2},{3,19},{19,3},{4,20},{20... | collective-permute-start | bytes 811016 | tf_op jit(solution)/shard_map/ppermute | solution.py:581
  14.1 0.0 copy-done
  14.1 0.0 copy-done.1
  14.1 1.7 %aligned_rows.2.rest_6_ = bf16[2,32,8192]{2,1,0:T(8,128)(2,1)S(1)} custom-call(f32[1024]{0:T(1024)S(1)} %copy-done.1, f32[8,256]{1,0:T(8,128)S(1)} %copy-done, bf16[2,16,128]{2,1,0:T(8,128)(2,1)S(1)} %get-tuple-element.35.rest_0_.rest_2_, bf16[2,16,8320]{2,1,0:T(8,128)(2,1)S(1)} %collective-permute-done.1.rest_1_.rest_3_, ...), custom_call_target="tpu_custom_call" | custom-call | tf_op jit(solution)/shard_map/aligned_rows/pallas_call | solution.py:447
  15.8 0.0 collective-permute-done.3.rest_1_
  15.8 2.4 %near_logits.2 = (f32[128,128]{1,0:T(8,128)S(1)}, f32[128,128]{1,0:T(8,128)S(1)}, bf16[2,128,4096]{2,1,0:T(8,128)(2,1)S(1)}) custom-call(f32[1024]{0:T(1024)S(1)} %copy-done.1, f32[8,256]{1,0:T(8,128)S(1)} %copy-done, bf16[2,4,4,2048]{3,2,1,0:T(4,128)(2,1)S(1)} %get-tuple-element.33.rest_0_, bf16[2,4,4,2048]{3,2,1,0:T(4,128)(2,1)S(1)} %collective-permute-done.3.rest_1_, ...), custom_call_target="tpu_custom_call" | custom-call | tf_op jit(solution)/shard_map/near_logits/pallas_call | solution.py:320
  18.2 1.5 %collective-permute-done.rest_0_ = bf16[2,4,4,2048]{3,2,1,0:T(4,128)(2,1)S(1)} collective-permute-done((bf16[2,4,4,2048]{3,2,1,0:T(4,128)(2,1)S(1)}, bf16[2,4,4,2048]{3,2,1,0:T(4,128)(2,1)S(1)}, u32[]{:S(2)}, u32[]{:S(2)}) %collective-permute-start) | collective-permute-done | bytes 131104 | tf_op jit(solution)/shard_map/ppermute | solution.py:568
  19.7 0.0 collective-permute-done.2.rest_1_
  19.7 2.4 %near_logits.3 = (f32[128,128]{1,0:T(8,128)S(1)}, f32[128,128]{1,0:T(8,128)S(1)}, bf16[2,128,4096]{2,1,0:T(8,128)(2,1)S(1)}) custom-call(f32[1024]{0:T(1024)S(1)} %copy-done.1, f32[8,256]{1,0:T(8,128)S(1)} %copy-done, bf16[2,4,4,2048]{3,2,1,0:T(4,128)(2,1)S(1)} %collective-permute-done.rest_0_, bf16[2,4,4,2048]{3,2,1,0:T(4,128)(2,1)S(1)} %collective-permute-done.2.rest_1_, ...), custom_call_target="tpu_custom_call" | custom-call | flops 20000000000 | tf_op jit(solution)/shard_map/near_logits/pallas_call | solution.py:320
  22.1 0.1 collective-permute-start.4
  22.2 0.6 %collective-permute-start.10 = (f32[128,128]{1,0:T(8,128)S(1)}, f32[128,128]{1,0:T(8,128)S(1)}, u32[]{:S(2)}, u32[]{:S(2)}) collective-permute-start(f32[128,128]{1,0:T(8,128)S(1)} %get-tuple-element.41), channel_id=1, source_target_pairs={{0,12},{4,8},{8,4},{12,0},{1,13},{5,9},{9,5},{13,1},{2,14},{6,10},... | collective-permute-start | bytes 196616 | tf_op jit(solution)/shard_map/ppermute | solution.py:565
  22.8 1.5 %collective-permute-start.9 = (f32[128,128]{1,0:T(8,128)S(1)}, f32[128,128]{1,0:T(8,128)S(1)}, u32[]{:S(2)}, u32[]{:S(2)}) collective-permute-start(f32[128,128]{1,0:T(8,128)S(1)} %get-tuple-element.39.refs_0_), channel_id=1, source_target_pairs={{0,8},{4,12},{8,0},{12,4},{1,9},{5,13},{9,1},{13,5},{2,10},{6,14},... | collective-permute-start | bytes 196616 | tf_op jit(solution)/shard_map/ppermute | solution.py:565
  24.3 0.0 collective-permute-done.4.refs_1_
  24.3 0.0 collective-permute-done.7.rest_4_.rest_1_.rest_5_
  24.3 0.0 collective-permute-done.6.rest_3_
  24.3 3.3 %far_logits.1 = (f32[128,128]{1,0:T(8,128)S(1)}, f32[128,128]{1,0:T(8,128)S(1)}) custom-call(f32[8,256]{1,0:T(8,128)S(1)} %copy-done, bf16[2,128,4096]{2,1,0:T(8,128)(2,1)S(1)} %get-tuple-element.43.rest_0_, bf16[2,128,4096]{2,1,0:T(8,128)(2,1)S(1)} %get-tuple-element.44.rest_1_, bf16[2,16,4224]{2,1,0:T(8,128)(2,1)S(1)} %collective-permute-done.5.rest_2_.rest_0_.rest_4_, ...), custom_call_target="tpu_custom_call" | custom-call | flops 6000000000 | tf_op jit(solution)/shard_map/far_logits/pallas_call | solution.py:345
  27.7 0.0 collective-permute-done.10.refs_7_
  27.7 0.4 collective-permute-done.9.refs_6_
  28.0 0.3 collective-permute-start.11
  28.3 0.4 collective-permute-start.12
  28.7 1.5 %collective-permute-start.8 = (f32[128,128]{1,0:T(8,128)S(1)}, f32[128,128]{1,0:T(8,128)S(1)}, u32[]{:S(2)}, u32[]{:S(2)}) collective-permute-start(f32[128,128]{1,0:T(8,128)S(1)} %get-tuple-element.47.refs_4_), channel_id=1, source_target_pairs={{0,8},{4,12},{8,0},{12,4},{1,9},{5,13},{9,1},{13,5},{2,10},{6,14},... | collective-permute-start | bytes 196616 | tf_op jit(solution)/shard_map/ppermute | solution.py:565
  30.2 2.1 %aligned_rows.3.rest_7_ = bf16[2,32,8192]{2,1,0:T(8,128)(2,1)S(1)} custom-call(f32[1024]{0:T(1024)S(1)} %copy-done.1, f32[8,256]{1,0:T(8,128)S(1)} %copy-done, bf16[2,16,4224]{2,1,0:T(8,128)(2,1)S(1)} %collective-permute-done.5.rest_2_.rest_0_.rest_4_, bf16[2,16,8320]{2,1,0:T(8,128)(2,1)S(1)} %collective-permute-done.7.rest_4_.rest_1_.rest_5_, ...), custom_call_target="tpu_custom_call" | custom-call | tf_op jit(solution)/shard_map/aligned_rows/pallas_call | solution.py:447
  32.2 0.0 collective-permute-done.11.refs_3_
  32.3 0.0 collective-permute-done.12.refs_5_
  32.3 1.3 %collective-permute-done.8.refs_2_ = f32[128,128]{1,0:T(8,128)S(1)} collective-permute-done((f32[128,128]{1,0:T(8,128)S(1)}, f32[128,128]{1,0:T(8,128)S(1)}, u32[]{:S(2)}, u32[]{:S(2)}) %collective-permute-start.8) | collective-permute-done | bytes 65568 | tf_op jit(solution)/shard_map/ppermute | solution.py:565
  33.6 0.3 logit_stats.1
  33.8 0.0 collective-permute-start.13
  33.9 1.2 %collective-permute-done.13 = f32[8,128]{1,0:T(8,128)S(1)} collective-permute-done((f32[8,128]{1,0:T(8,128)S(1)}, f32[8,128]{1,0:T(8,128)S(1)}, u32[]{:S(2)}, u32[]{:S(2)}) %collective-permute-start.13) | collective-permute-done | bytes 4128 | tf_op jit(solution)/shard_map/ppermute | solution.py:565
  35.0 1.5 %collective-permute-start.14 = (f32[16,128]{1,0:T(8,128)S(1)}, f32[16,128]{1,0:T(8,128)S(1)}, u32[]{:S(2)}, u32[]{:S(2)}) collective-permute-start(f32[16,128]{1,0:T(8,128)S(1)} %pad_maximum_fusion.rest_0_), channel_id=1, source_target_pairs={{0,16},{16,0},{1,17},{17,1},{2,18},{18,2},{3,19},{19,3},{4,20},{20... | collective-permute-start | bytes 24584 | tf_op jit(solution)/shard_map/ppermute | solution.py:620
  36.5 2.1 %collective-permute-done.14.rest_1_ = f32[16,128]{1,0:T(8,128)S(1)} collective-permute-done((f32[16,128]{1,0:T(8,128)S(1)}, f32[16,128]{1,0:T(8,128)S(1)}, u32[]{:S(2)}, u32[]{:S(2)}) %collective-permute-start.14) | collective-permute-done | bytes 8224 | tf_op jit(solution)/shard_map/ppermute | solution.py:620
  38.7 1.0 %volume_terms.1 = (f32[16,128]{1,0:T(8,128)S(1)}, f32[2,4,8192]{2,1,0:T(4,128)S(1)}, bf16[2,4,8192]{2,1,0:T(4,128)(2,1)S(1)}, bf16[2,4,8192]{2,1,0:T(4,128)(2,1)S(1)}, bf16[2,4,8192]{2,1,0:T(4,128)(2,1)S(1)}) custom-call(f32[16,128]{1,0:T(8,128)S(1)} %pad_maximum_fusion.rest_0_, f32[16,128]{1,0:T(8,128)S(1)} %collective-permute-done.14.rest_1_, ...), custom_call_target="tpu_custom_call" | custom-call | flops 33554432 | bytes 2621440 | tf_op jit(solution)/shard_map/volume_terms/pallas_call | solution.py:522
  39.7 3.4 %collective-permute-start.15 = (bf16[2,4,8192]{2,1,0:T(4,128)(2,1)S(1)}, bf16[2,4,8192]{2,1,0:T(4,128)(2,1)S(1)}, u32[]{:S(2)}, u32[]{:S(2)}) collective-permute-start(bf16[2,4,8192]{2,1,0:T(4,128)(2,1)S(1)} %get-tuple-element.57), channel_id=1, source_target_pairs={{0,2},{1,3},{2,0},{3,1},{4,6},{5,7},{6,4},{7,5},{8,10},{9,11},{10,... | collective-permute-start | bytes 393224 | tf_op jit(solution)/shard_map/ppermute | solution.py:568
  43.1 0.5 collective-permute-start.16
  43.6 1.1 %collective-permute-start.17 = (bf16[2,4,8192]{2,1,0:T(4,128)(2,1)S(1)}, bf16[2,4,8192]{2,1,0:T(4,128)(2,1)S(1)}, u32[]{:S(2)}, u32[]{:S(2)}) collective-permute-start(bf16[2,4,8192]{2,1,0:T(4,128)(2,1)S(1)} %get-tuple-element.59), channel_id=1, source_target_pairs={{0,3},{1,2},{2,1},{3,0},{4,7},{5,6},{6,5},{7,4},{8,11},{9,10},{10,... | collective-permute-start | bytes 393224 | tf_op jit(solution)/shard_map/ppermute | solution.py:568
  44.6 0.7 %copy.9 = f32[16,4]{0,1:T(4,128)} copy(f32[16,4]{1,0:T(8,128)S(1)} %bitcast.4) | data formatting | bytes 512
  45.3 5.9 %collective-permute-done.15.rest_0_ = bf16[2,4,8192]{2,1,0:T(4,128)(2,1)S(1)} collective-permute-done((bf16[2,4,8192]{2,1,0:T(4,128)(2,1)S(1)}, bf16[2,4,8192]{2,1,0:T(4,128)(2,1)S(1)}, u32[]{:S(2)}, u32[]{:S(2)}) %collective-permute-start.15) | collective-permute-done | bytes 131104 | tf_op jit(solution)/shard_map/ppermute | solution.py:568
  51.2 0.0 collective-permute-done.16.rest_1_
  51.2 1.4 %collective-permute-done.17.rest_2_ = bf16[2,4,8192]{2,1,0:T(4,128)(2,1)S(1)} collective-permute-done((bf16[2,4,8192]{2,1,0:T(4,128)(2,1)S(1)}, bf16[2,4,8192]{2,1,0:T(4,128)(2,1)S(1)}, u32[]{:S(2)}, u32[]{:S(2)}) %collective-permute-start.17) | collective-permute-done | bytes 131104 | tf_op jit(solution)/shard_map/ppermute | solution.py:568
  52.6 0.8 %total_volume.1 = f32[2,4,1,8192]{3,2,1,0:T(1,128)} custom-call(f32[2,4,8192]{2,1,0:T(4,128)S(1)} %get-tuple-element.56.first, bf16[2,4,8192]{2,1,0:T(4,128)(2,1)S(1)} %collective-permute-done.15.rest_0_, bf16[2,4,8192]{2,1,0:T(4,128)(2,1)S(1)} %collective-permute-done.16.rest_1_, bf16[2,4,8192]{2,1,0:T(4,128)(2,1)S(1)} %collective-permute-done.17.rest_2_), custom_call_target="tpu_custom_call" | custom-call | tf_op jit(solution)/shard_map/total_volume/pallas_call | solution.py:551
  (1 shorter events, 0.0 us)
Async XLA Ops:
  0.6 13.5 %copy-start = (f32[8,256]{1,0:T(8,128)S(1)}, f32[8,256]{1,0:T(8,128)}, u32[]{:S(2)}) copy-start(f32[8,256]{1,0:T(8,128)} %constant.4.clone.table_x) | copy-start | bytes 24580
  0.6 13.5 %copy-start.1 = (f32[1024]{0:T(1024)S(1)}, f32[1024]{0:T(1024)}, u32[]{:S(2)}) copy-start(f32[1024]{0:T(1024)} %constant.5.clone.table_y) | copy-start | bytes 12292
  2.2 7.3 %collective-permute-start.1 = (bf16[2,16,8320]{2,1,0:T(8,128)(2,1)S(1)}, bf16[2,16,8320]{2,1,0:T(8,128)(2,1)S(1)}, u32[]{:S(2)}, u32[]{:S(2)}) collective-permute-start(bf16[2,16,8320]{2,1,0:T(8,128)(2,1)S(1)} %get-tuple-element.32), channel_id=1, source_target_pairs={{0,4},{4,0},{8,12},{12,8},{1,5},{5,1},{9,13},{13,9},{2,6},{6,2},{1... | collective-permute-start | bytes 1597448 | tf_op jit(solution)/shard_map/ppermute | solution.py:565
  2.7 9.6 %collective-permute-start.5 = (bf16[2,16,4224]{2,1,0:T(8,128)(2,1)S(1)}, bf16[2,16,4224]{2,1,0:T(8,128)(2,1)S(1)}, u32[]{:S(2)}, u32[]{:S(2)}) collective-permute-start(bf16[2,16,4224]{2,1,0:T(8,128)(2,1)S(1)} %get-tuple-element.45), channel_id=1, source_target_pairs={{0,8},{4,12},{8,0},{12,4},{1,9},{5,13},{9,1},{13,5},{2,10},{6,14},... | collective-permute-start | bytes 811016 | tf_op jit(solution)/shard_map/ppermute | solution.py:565
  5.2 10.6 %collective-permute-start.3 = (bf16[2,4,4,2048]{3,2,1,0:T(4,128)(2,1)S(1)}, bf16[2,4,4,2048]{3,2,1,0:T(4,128)(2,1)S(1)}, u32[]{:S(2)}, u32[]{:S(2)}) collective-permute-start(bf16[2,4,4,2048]{3,2,1,0:T(4,128)(2,1)S(1)} %get-tuple-element.33.rest_0_), channel_id=1, source_target_pairs={{0,1},{1,0},{2,3},{3,2},{4,5},{5,4},{6,7},{7,6},{8,9},{9,8},{10,11... | collective-permute-start | bytes 393224 | tf_op jit(solution)/shard_map/ppermute | solution.py:568
  6.8 12.9 %collective-permute-start = (bf16[2,4,4,2048]{3,2,1,0:T(4,128)(2,1)S(1)}, bf16[2,4,4,2048]{3,2,1,0:T(4,128)(2,1)S(1)}, u32[]{:S(2)}, u32[]{:S(2)}) collective-permute-start(bf16[2,4,4,2048]{3,2,1,0:T(4,128)(2,1)S(1)} %get-tuple-element.33.rest_0_), channel_id=1, source_target_pairs={{0,2},{1,3},{2,0},{3,1},{4,6},{5,7},{6,4},{7,5},{8,10},{9,11},{10,... | collective-permute-start | bytes 393224 | tf_op jit(solution)/shard_map/ppermute | solution.py:568
  9.4 10.3 %collective-permute-start.2 = (bf16[2,4,4,2048]{3,2,1,0:T(4,128)(2,1)S(1)}, bf16[2,4,4,2048]{3,2,1,0:T(4,128)(2,1)S(1)}, u32[]{:S(2)}, u32[]{:S(2)}) collective-permute-start(bf16[2,4,4,2048]{3,2,1,0:T(4,128)(2,1)S(1)} %get-tuple-element.33.rest_0_), channel_id=1, source_target_pairs={{0,3},{1,2},{2,1},{3,0},{4,7},{5,6},{6,5},{7,4},{8,11},{9,10},{10,... | collective-permute-start | bytes 393224 | tf_op jit(solution)/shard_map/ppermute | solution.py:568
  9.6 14.7 %collective-permute-start.7 = (bf16[2,16,8320]{2,1,0:T(8,128)(2,1)S(1)}, bf16[2,16,8320]{2,1,0:T(8,128)(2,1)S(1)}, u32[]{:S(2)}, u32[]{:S(2)}) collective-permute-start(bf16[2,16,8320]{2,1,0:T(8,128)(2,1)S(1)} %get-tuple-element.46), channel_id=1, source_target_pairs={{0,12},{4,8},{8,4},{12,0},{1,13},{5,9},{9,5},{13,1},{2,14},{6,10},... | collective-permute-start | bytes 1597448 | tf_op jit(solution)/shard_map/ppermute | solution.py:565
  12.3 12.0 %collective-permute-start.6 = (bf16[2,16,4224]{2,1,0:T(8,128)(2,1)S(1)}, bf16[2,16,4224]{2,1,0:T(8,128)(2,1)S(1)}, u32[]{:S(2)}, u32[]{:S(2)}) collective-permute-start(bf16[2,16,4224]{2,1,0:T(8,128)(2,1)S(1)} %collective-permute-done.5.rest_2_.rest_0_.rest_4_), channel_id=1, source_target_pairs={{0,16},{16,0},{1,17},{17,1},{2,18},{18,2},{3,19},{19,3},{4,20},{20... | collective-permute-start | bytes 811016 | tf_op jit(solution)/shard_map/ppermute | solution.py:581
  22.1 2.2 %collective-permute-start.4 = (f32[128,128]{1,0:T(8,128)S(1)}, f32[128,128]{1,0:T(8,128)S(1)}, u32[]{:S(2)}, u32[]{:S(2)}) collective-permute-start(f32[128,128]{1,0:T(8,128)S(1)} %get-tuple-element.41), channel_id=1, source_target_pairs={{0,4},{4,0},{8,12},{12,8},{1,5},{5,1},{9,13},{13,9},{2,6},{6,2},{1... | collective-permute-start | bytes 196616 | tf_op jit(solution)/shard_map/ppermute | solution.py:565
  22.2 5.5 %collective-permute-start.10 = (f32[128,128]{1,0:T(8,128)S(1)}, f32[128,128]{1,0:T(8,128)S(1)}, u32[]{:S(2)}, u32[]{:S(2)}) collective-permute-start(f32[128,128]{1,0:T(8,128)S(1)} %get-tuple-element.41), channel_id=1, source_target_pairs={{0,12},{4,8},{8,4},{12,0},{1,13},{5,9},{9,5},{13,1},{2,14},{6,10},... | collective-permute-start | bytes 196616 | tf_op jit(solution)/shard_map/ppermute | solution.py:565
  22.8 5.2 %collective-permute-start.9 = (f32[128,128]{1,0:T(8,128)S(1)}, f32[128,128]{1,0:T(8,128)S(1)}, u32[]{:S(2)}, u32[]{:S(2)}) collective-permute-start(f32[128,128]{1,0:T(8,128)S(1)} %get-tuple-element.39.refs_0_), channel_id=1, source_target_pairs={{0,8},{4,12},{8,0},{12,4},{1,9},{5,13},{9,1},{13,5},{2,10},{6,14},... | collective-permute-start | bytes 196616 | tf_op jit(solution)/shard_map/ppermute | solution.py:565
  28.0 4.2 %collective-permute-start.11 = (f32[128,128]{1,0:T(8,128)S(1)}, f32[128,128]{1,0:T(8,128)S(1)}, u32[]{:S(2)}, u32[]{:S(2)}) collective-permute-start(f32[128,128]{1,0:T(8,128)S(1)} %get-tuple-element.49), channel_id=1, source_target_pairs={{0,12},{4,8},{8,4},{12,0},{1,13},{5,9},{9,5},{13,1},{2,14},{6,10},... | collective-permute-start | bytes 196616 | tf_op jit(solution)/shard_map/ppermute | solution.py:565
  28.3 3.9 %collective-permute-start.12 = (f32[128,128]{1,0:T(8,128)S(1)}, f32[128,128]{1,0:T(8,128)S(1)}, u32[]{:S(2)}, u32[]{:S(2)}) collective-permute-start(f32[128,128]{1,0:T(8,128)S(1)} %get-tuple-element.49), channel_id=1, source_target_pairs={{0,4},{4,0},{8,12},{12,8},{1,5},{5,1},{9,13},{13,9},{2,6},{6,2},{1... | collective-permute-start | bytes 196616 | tf_op jit(solution)/shard_map/ppermute | solution.py:565
  28.7 4.9 %collective-permute-start.8 = (f32[128,128]{1,0:T(8,128)S(1)}, f32[128,128]{1,0:T(8,128)S(1)}, u32[]{:S(2)}, u32[]{:S(2)}) collective-permute-start(f32[128,128]{1,0:T(8,128)S(1)} %get-tuple-element.47.refs_4_), channel_id=1, source_target_pairs={{0,8},{4,12},{8,0},{12,4},{1,9},{5,13},{9,1},{13,5},{2,10},{6,14},... | collective-permute-start | bytes 196616 | tf_op jit(solution)/shard_map/ppermute | solution.py:565
  33.8 1.2 %collective-permute-start.13 = (f32[8,128]{1,0:T(8,128)S(1)}, f32[8,128]{1,0:T(8,128)S(1)}, u32[]{:S(2)}, u32[]{:S(2)}) collective-permute-start(f32[8,128]{1,0:T(8,128)S(1)} %logit_stats.1), channel_id=1, source_target_pairs={{0,4},{4,0},{8,12},{12,8},{1,5},{5,1},{9,13},{13,9},{2,6},{6,2},{1... | collective-permute-start | bytes 12296 | tf_op jit(solution)/shard_map/ppermute | solution.py:565
  35.0 3.7 %collective-permute-start.14 = (f32[16,128]{1,0:T(8,128)S(1)}, f32[16,128]{1,0:T(8,128)S(1)}, u32[]{:S(2)}, u32[]{:S(2)}) collective-permute-start(f32[16,128]{1,0:T(8,128)S(1)} %pad_maximum_fusion.rest_0_), channel_id=1, source_target_pairs={{0,16},{16,0},{1,17},{17,1},{2,18},{18,2},{3,19},{19,3},{4,20},{20... | collective-permute-start | bytes 24584 | tf_op jit(solution)/shard_map/ppermute | solution.py:620
  39.7 11.5 %collective-permute-start.15 = (bf16[2,4,8192]{2,1,0:T(4,128)(2,1)S(1)}, bf16[2,4,8192]{2,1,0:T(4,128)(2,1)S(1)}, u32[]{:S(2)}, u32[]{:S(2)}) collective-permute-start(bf16[2,4,8192]{2,1,0:T(4,128)(2,1)S(1)} %get-tuple-element.57), channel_id=1, source_target_pairs={{0,2},{1,3},{2,0},{3,1},{4,6},{5,7},{6,4},{7,5},{8,10},{9,11},{10,... | collective-permute-start | bytes 393224 | tf_op jit(solution)/shard_map/ppermute | solution.py:568
  43.1 8.1 %collective-permute-start.16 = (bf16[2,4,8192]{2,1,0:T(4,128)(2,1)S(1)}, bf16[2,4,8192]{2,1,0:T(4,128)(2,1)S(1)}, u32[]{:S(2)}, u32[]{:S(2)}) collective-permute-start(bf16[2,4,8192]{2,1,0:T(4,128)(2,1)S(1)} %get-tuple-element.58), channel_id=1, source_target_pairs={{0,1},{1,0},{2,3},{3,2},{4,5},{5,4},{6,7},{7,6},{8,9},{9,8},{10,11... | collective-permute-start | bytes 393224 | tf_op jit(solution)/shard_map/ppermute | solution.py:568
  43.6 9.1 %collective-permute-start.17 = (bf16[2,4,8192]{2,1,0:T(4,128)(2,1)S(1)}, bf16[2,4,8192]{2,1,0:T(4,128)(2,1)S(1)}, u32[]{:S(2)}, u32[]{:S(2)}) collective-permute-start(bf16[2,4,8192]{2,1,0:T(4,128)(2,1)S(1)} %get-tuple-element.59), channel_id=1, source_target_pairs={{0,3},{1,2},{2,1},{3,0},{4,7},{5,6},{6,5},{7,4},{8,11},{9,10},{10,... | collective-permute-start | bytes 393224 | tf_op jit(solution)/shard_map/ppermute | solution.py:568

commit v8 on v7

--- a/solution.py
+++ b/solution.py
@@ -16,7 +16,6 @@
 LANES = 128
 SUBLANES = 8
 SHARED = 2
-EARLY = 2
 FLOPS_OF_MICRO = 1_000_000_000
 VMEM_BYTES = 24 * 1024 * 1024
 VMEM_SPEC = pl.BlockSpec(memory_space=pltpu.VMEM)
@@ -275,7 +274,7 @@
         out[...] = before[g][...] if sums else jnp.zeros_like(out)
 
     def add_shard(place, carry):
-        step = place + steps[0]
+        step = 2 * place + steps[0]
         shift_references(refs, right, (place, step), ids, orients, table_y)
         shift_images(images, left, ids[1] ^ step, ids, table_x)
         add_products(outs, left[...], right[place])
@@ -292,16 +291,14 @@
     outs, left = rest[:groups], rest[groups]
     for out in outs:
         out[...] = jnp.zeros_like(out)
-    base = 0
-    for right, count in zip(rights, counts):
-
-        def add_shard(place, carry, base=base, right=right):
-            shift_images(images, left, ids[1] ^ (place + base), ids, table_x)
+    for first, (right, count) in enumerate(zip(rights, counts)):
+
+        def add_shard(place, carry, first=first, right=right):
+            shift_images(images, left, ids[1] ^ (2 * place + first), ids, table_x)
             add_products(outs, left[...], right[place])
             return carry
 
         lax.fori_loop(0, count, add_shard, 0)
-        base += count
 
 
 def logits_cost(micros):
@@ -572,9 +569,9 @@
     )
     arrived = {step: swap_dom(bands[step - 1], step) for step in [1, *range(dom - 1, 1, -1)]}
     tied, arrived[1] = lax.optimization_barrier((shard, arrived[1]))
-    shards = [shard] + [
-        swap_orient(tied if step == orient - 1 else shard, step) for step in range(1, orient)
-    ]
+    shards = [shard] + [None] * (orient - 1)
+    for step in [*range(2, orient, 2), *range(1, orient, 2)]:
+        shards[step] = swap_orient(tied if step == orient - 1 else shard, step)
     half = arrived[SHARED]
     groups = [([own_band(images, dom)], meta)]
     groups += [([arrived[step]], arrived[step]) for step in range(1, dom)]
@@ -582,11 +579,11 @@
 
     width = images.shape[2] // dom
     aligned_near = aligned_rows(table_x, table_y, groups[:2], width)
-    shards[1], aligned_near = lax.optimization_barrier((shards[1], aligned_near))
+    shards[2], aligned_near = lax.optimization_barrier((shards[2], aligned_near))
     every = range(orient)
-    first, right = near_logits(table_x, table_y, shards, groups[:2], every[:EARLY], [], 0)
+    first, right = near_logits(table_x, table_y, shards, groups[:2], every[0::2], [], 0)
     near, right_late = near_logits(
-        table_x, table_y, shards, groups[:2], every[EARLY:], first, 20
+        table_x, table_y, shards, groups[:2], every[1::2], first, 20
     )
     swapped = swap_dom(near[1], 1)
     right_late, swapped = lax.optimization_barrier((right_late, swapped))

time: 53.6 us -> 53.1 us (level)
  waiting for transfers between devices: 14.9 us -> 13.4 us
  starting transfers between devices: 20.6 us -> 21.5 us
    ppermute x6, waiting for transfers between devices: 8.84 us -> 7.32 us  [swap_orient(): return lax.ppermute(array, 'orient', xor_pairs(orient, step))]
    ppermute x10, waiting for transfers between devices: 3.93 us -> 4.49 us  [swap_dom(): return lax.ppermute(array, 'dom', xor_pairs(dom, step))]
  transfers between devices with their start and end apart: 18 -> 18, of which waited for: 8 -> 9; matrix products, arithmetic and copies ran while one was open for 1% -> 1% of each run, Pallas kernels for 24% -> 24%
where the time goes in v8:
time: 53.1 us; the launch traced here: 52.8 us
  starting transfers between devices  21.5 us (40%)
  Pallas kernels  16.5 us (31%)
  waiting for transfers between devices  13.4 us (25%)
  between operations  0.78 us (1%)
  local copies, waits for them, and re-layouts  0.66 us (1%)
    ppermute x6, starting transfers between devices, swap_orient(): return lax.ppermute(array, 'orient', xor_pairs(orient, step))  9.6 us
    ppermute x10, starting transfers between devices, swap_dom(): return lax.ppermute(array, 'dom', xor_pairs(dom, step))  8.03 us
    ppermute x6, waiting for transfers between devices, swap_orient(): return lax.ppermute(array, 'orient', xor_pairs(orient, step))  7.32 us
    pallas_call x2, Pallas kernels, near_logits(): pl.pallas_call(functools.partial(near_kernel, sizes_of(picked), len(shard...  4.76 us
    ppermute x10, waiting for transfers between devices, swap_dom(): return lax.ppermute(array, 'dom', xor_pairs(dom, step))  4.49 us
    pallas_call x2, Pallas kernels, aligned_rows(): pl.pallas_call(functools.partial(rows_kernel, sizes_of(picked)), out_shap...  3.79 us
    pallas_call x1, Pallas kernels, far_logits(): pl.pallas_call(functools.partial(far_kernel, sizes_of(picked), [right.sha...  3.32 us
    ppermute x1, starting transfers between devices, local(): stats_all = [stats, lax.ppermute(stats, 'cls', xor_pairs(cls, 1))]  2.04 us
  transfers between devices with their start and end apart: 18, of which 9 were waited for; matrix products, arithmetic and copies ran while one was open for 1% of the time, Pallas kernels for 24%

profile of v8, /device:TPU:0, one launch (start us, length us, event | category | flops | bytes accessed | tf_op | source)
XLA Modules:
  0.0 52.8 jit_solution(17633858246442720998)
XLA Ops:
  0.6 0.0 copy-start
  0.6 0.0 copy-start.1
  0.7 1.5 %image_bands.1 = (bf16[2,16,8320]{2,1,0:T(8,128)(2,1)S(1)}, bf16[2,16,4224]{2,1,0:T(8,128)(2,1)S(1)}, bf16[2,16,8320]{2,1,0:T(8,128)(2,1)S(1)}, bf16[2,16,128]{2...) custom-call(bf16[2,16,32768]{2,1,0:T(8,128)(2,1)} %images.3, bf16[2,4,4,2048]{3,2,1,0:T(4,128)(2,1)} %references.1, ...), custom_call_target="tpu_custom_call" | custom-call | bytes 3145728 | tf_op jit(solution)/shard_map/image_bands/pallas_call | solution.py:109
  2.2 0.5 collective-permute-start.1
  2.7 2.6 %collective-permute-start.5 = (bf16[2,16,4224]{2,1,0:T(8,128)(2,1)S(1)}, bf16[2,16,4224]{2,1,0:T(8,128)(2,1)S(1)}, u32[]{:S(2)}, u32[]{:S(2)}) collective-permute-start(bf16[2,16,4224]{2,1,0:T(8,128)(2,1)S(1)} %get-tuple-element.45), channel_id=1, source_target_pairs={{0,8},{4,12},{8,0},{12,4},{1,9},{5,13},{9,1},{13,5},{2,10},{6,14},... | collective-permute-start | bytes 811016 | tf_op jit(solution)/shard_map/ppermute | solution.py:562
  5.2 2.6 %collective-permute-start.3 = (bf16[2,4,4,2048]{3,2,1,0:T(4,128)(2,1)S(1)}, bf16[2,4,4,2048]{3,2,1,0:T(4,128)(2,1)S(1)}, u32[]{:S(2)}, u32[]{:S(2)}) collective-permute-start(bf16[2,4,4,2048]{3,2,1,0:T(4,128)(2,1)S(1)} %get-tuple-element.33.rest_0_), channel_id=1, source_target_pairs={{0,2},{1,3},{2,0},{3,1},{4,6},{5,7},{6,4},{7,5},{8,10},{9,11},{10,... | collective-permute-start | bytes 393224 | tf_op jit(solution)/shard_map/ppermute | solution.py:565
  7.8 1.6 %collective-permute-start = (bf16[2,4,4,2048]{3,2,1,0:T(4,128)(2,1)S(1)}, bf16[2,4,4,2048]{3,2,1,0:T(4,128)(2,1)S(1)}, u32[]{:S(2)}, u32[]{:S(2)}) collective-permute-start(bf16[2,4,4,2048]{3,2,1,0:T(4,128)(2,1)S(1)} %get-tuple-element.33.rest_0_), channel_id=1, source_target_pairs={{0,1},{1,0},{2,3},{3,2},{4,5},{5,4},{6,7},{7,6},{8,9},{9,8},{10,11... | collective-permute-start | bytes 393224 | tf_op jit(solution)/shard_map/ppermute | solution.py:565
  9.4 0.0 collective-permute-done.1.rest_1_.rest_3_
  9.4 0.2 collective-permute-start.2
  9.6 0.5 collective-permute-start.7
  10.1 1.0 %own_band.1.rest_2_ = bf16[2,16,8192]{2,1,0:T(8,128)(2,1)S(1)} custom-call(bf16[2,16,32768]{2,1,0:T(8,128)(2,1)} %images.3), custom_call_target="tpu_custom_call" | custom-call | tf_op jit(solution)/shard_map/own_band/pallas_call | solution.py:155
  11.2 1.1 %collective-permute-done.5.rest_2_.rest_0_.rest_4_ = bf16[2,16,4224]{2,1,0:T(8,128)(2,1)S(1)} collective-permute-done((bf16[2,16,4224]{2,1,0:T(8,128)(2,1)S(1)}, bf16[2,16,4224]{2,1,0:T(8,128)(2,1)S(1)}, u32[]{:S(2)}, u32[]{:S(2)}) %collective-permute-start.5) | collective-permute-done | bytes 270368 | tf_op jit(solution)/shard_map/ppermute | solution.py:562
  12.3 1.8 %collective-permute-start.6 = (bf16[2,16,4224]{2,1,0:T(8,128)(2,1)S(1)}, bf16[2,16,4224]{2,1,0:T(8,128)(2,1)S(1)}, u32[]{:S(2)}, u32[]{:S(2)}) collective-permute-start(bf16[2,16,4224]{2,1,0:T(8,128)(2,1)S(1)} %collective-permute-done.5.rest_2_.rest_0_.rest_4_), channel_id=1, source_target_pairs={{0,16},{16,0},{1,17},{17,1},{2,18},{18,2},{3,19},{19,3},{4,20},{20... | collective-permute-start | bytes 811016 | tf_op jit(solution)/shard_map/ppermute | solution.py:578
  14.1 0.0 copy-done
  14.1 0.0 copy-done.1
  14.1 1.7 %aligned_rows.2.rest_6_ = bf16[2,32,8192]{2,1,0:T(8,128)(2,1)S(1)} custom-call(f32[1024]{0:T(1024)S(1)} %copy-done.1, f32[8,256]{1,0:T(8,128)S(1)} %copy-done, bf16[2,16,128]{2,1,0:T(8,128)(2,1)S(1)} %get-tuple-element.35.rest_0_.rest_2_, bf16[2,16,8320]{2,1,0:T(8,128)(2,1)S(1)} %collective-permute-done.1.rest_1_.rest_3_, ...), custom_call_target="tpu_custom_call" | custom-call | tf_op jit(solution)/shard_map/aligned_rows/pallas_call | solution.py:444
  15.8 0.0 collective-permute-done.3.rest_1_
  15.8 2.4 %near_logits.2 = (f32[128,128]{1,0:T(8,128)S(1)}, f32[128,128]{1,0:T(8,128)S(1)}, bf16[2,128,4096]{2,1,0:T(8,128)(2,1)S(1)}) custom-call(f32[1024]{0:T(1024)S(1)} %copy-done.1, f32[8,256]{1,0:T(8,128)S(1)} %copy-done, bf16[2,4,4,2048]{3,2,1,0:T(4,128)(2,1)S(1)} %get-tuple-element.33.rest_0_, bf16[2,4,4,2048]{3,2,1,0:T(4,128)(2,1)S(1)} %collective-permute-done.3.rest_1_, ...), custom_call_target="tpu_custom_call" | custom-call | tf_op jit(solution)/shard_map/near_logits/pallas_call | solution.py:317
  18.2 0.0 collective-permute-done.rest_0_
  18.2 0.2 collective-permute-done.2.rest_1_
  18.5 2.4 %near_logits.3 = (f32[128,128]{1,0:T(8,128)S(1)}, f32[128,128]{1,0:T(8,128)S(1)}, bf16[2,128,4096]{2,1,0:T(8,128)(2,1)S(1)}) custom-call(f32[1024]{0:T(1024)S(1)} %copy-done.1, f32[8,256]{1,0:T(8,128)S(1)} %copy-done, bf16[2,4,4,2048]{3,2,1,0:T(4,128)(2,1)S(1)} %collective-permute-done.rest_0_, bf16[2,4,4,2048]{3,2,1,0:T(4,128)(2,1)S(1)} %collective-permute-done.2.rest_1_, ...), custom_call_target="tpu_custom_call" | custom-call | flops 20000000000 | tf_op jit(solution)/shard_map/near_logits/pallas_call | solution.py:317
  20.9 0.1 collective-permute-start.4
  20.9 1.7 %collective-permute-start.10 = (f32[128,128]{1,0:T(8,128)S(1)}, f32[128,128]{1,0:T(8,128)S(1)}, u32[]{:S(2)}, u32[]{:S(2)}) collective-permute-start(f32[128,128]{1,0:T(8,128)S(1)} %get-tuple-element.41), channel_id=1, source_target_pairs={{0,12},{4,8},{8,4},{12,0},{1,13},{5,9},{9,5},{13,1},{2,14},{6,10},... | collective-permute-start | bytes 196616 | tf_op jit(solution)/shard_map/ppermute | solution.py:562
  22.7 0.4 collective-permute-start.9
  23.1 0.0 collective-permute-done.4.refs_1_
  23.1 0.6 %collective-permute-done.7.rest_4_.rest_1_.rest_5_ = bf16[2,16,8320]{2,1,0:T(8,128)(2,1)S(1)} collective-permute-done((bf16[2,16,8320]{2,1,0:T(8,128)(2,1)S(1)}, bf16[2,16,8320]{2,1,0:T(8,128)(2,1)S(1)}, u32[]{:S(2)}, u32[]{:S(2)}) %collective-permute-start.7) | collective-permute-done | bytes 532512 | tf_op jit(solution)/shard_map/ppermute | solution.py:562
  23.7 0.0 collective-permute-done.6.rest_3_
  23.7 3.3 %far_logits.1 = (f32[128,128]{1,0:T(8,128)S(1)}, f32[128,128]{1,0:T(8,128)S(1)}) custom-call(f32[8,256]{1,0:T(8,128)S(1)} %copy-done, bf16[2,128,4096]{2,1,0:T(8,128)(2,1)S(1)} %get-tuple-element.43.rest_0_, bf16[2,128,4096]{2,1,0:T(8,128)(2,1)S(1)} %get-tuple-element.44.rest_1_, bf16[2,16,4224]{2,1,0:T(8,128)(2,1)S(1)} %collective-permute-done.5.rest_2_.rest_0_.rest_4_, ...), custom_call_target="tpu_custom_call" | custom-call | flops 6000000000 | tf_op jit(solution)/shard_map/far_logits/pallas_call | solution.py:342
  27.1 0.0 collective-permute-done.10.refs_7_
  27.1 0.0 collective-permute-done.9.refs_6_
  27.1 1.2 %collective-permute-start.11 = (f32[128,128]{1,0:T(8,128)S(1)}, f32[128,128]{1,0:T(8,128)S(1)}, u32[]{:S(2)}, u32[]{:S(2)}) collective-permute-start(f32[128,128]{1,0:T(8,128)S(1)} %get-tuple-element.49), channel_id=1, source_target_pairs={{0,12},{4,8},{8,4},{12,0},{1,13},{5,9},{9,5},{13,1},{2,14},{6,10},... | collective-permute-start | bytes 196616 | tf_op jit(solution)/shard_map/ppermute | solution.py:562
  28.3 0.4 collective-permute-start.12
  28.7 0.6 %collective-permute-start.8 = (f32[128,128]{1,0:T(8,128)S(1)}, f32[128,128]{1,0:T(8,128)S(1)}, u32[]{:S(2)}, u32[]{:S(2)}) collective-permute-start(f32[128,128]{1,0:T(8,128)S(1)} %get-tuple-element.47.refs_4_), channel_id=1, source_target_pairs={{0,8},{4,12},{8,0},{12,4},{1,9},{5,13},{9,1},{13,5},{2,10},{6,14},... | collective-permute-start | bytes 196616 | tf_op jit(solution)/shard_map/ppermute | solution.py:562
  29.3 2.1 %aligned_rows.3.rest_7_ = bf16[2,32,8192]{2,1,0:T(8,128)(2,1)S(1)} custom-call(f32[1024]{0:T(1024)S(1)} %copy-done.1, f32[8,256]{1,0:T(8,128)S(1)} %copy-done, bf16[2,16,4224]{2,1,0:T(8,128)(2,1)S(1)} %collective-permute-done.5.rest_2_.rest_0_.rest_4_, bf16[2,16,8320]{2,1,0:T(8,128)(2,1)S(1)} %collective-permute-done.7.rest_4_.rest_1_.rest_5_, ...), custom_call_target="tpu_custom_call" | custom-call | tf_op jit(solution)/shard_map/aligned_rows/pallas_call | solution.py:444
  31.4 0.2 collective-permute-done.11.refs_3_
  31.5 0.0 collective-permute-done.12.refs_5_
  31.5 1.4 %collective-permute-done.8.refs_2_ = f32[128,128]{1,0:T(8,128)S(1)} collective-permute-done((f32[128,128]{1,0:T(8,128)S(1)}, f32[128,128]{1,0:T(8,128)S(1)}, u32[]{:S(2)}, u32[]{:S(2)}) %collective-permute-start.8) | collective-permute-done | bytes 65568 | tf_op jit(solution)/shard_map/ppermute | solution.py:562
  32.9 0.3 logit_stats.1
  33.2 0.0 collective-permute-start.13
  33.2 1.2 %collective-permute-done.13 = f32[8,128]{1,0:T(8,128)S(1)} collective-permute-done((f32[8,128]{1,0:T(8,128)S(1)}, f32[8,128]{1,0:T(8,128)S(1)}, u32[]{:S(2)}, u32[]{:S(2)}) %collective-permute-start.13) | collective-permute-done | bytes 4128 | tf_op jit(solution)/shard_map/ppermute | solution.py:562
  34.4 2.0 %collective-permute-start.14 = (f32[16,128]{1,0:T(8,128)S(1)}, f32[16,128]{1,0:T(8,128)S(1)}, u32[]{:S(2)}, u32[]{:S(2)}) collective-permute-start(f32[16,128]{1,0:T(8,128)S(1)} %pad_maximum_fusion.rest_0_), channel_id=1, source_target_pairs={{0,16},{16,0},{1,17},{17,1},{2,18},{18,2},{3,19},{19,3},{4,20},{20... | collective-permute-start | bytes 24584 | tf_op jit(solution)/shard_map/ppermute | solution.py:617
  36.4 1.6 %collective-permute-done.14.rest_1_ = f32[16,128]{1,0:T(8,128)S(1)} collective-permute-done((f32[16,128]{1,0:T(8,128)S(1)}, f32[16,128]{1,0:T(8,128)S(1)}, u32[]{:S(2)}, u32[]{:S(2)}) %collective-permute-start.14) | collective-permute-done | bytes 8224 | tf_op jit(solution)/shard_map/ppermute | solution.py:617
  38.1 1.0 %volume_terms.1 = (f32[16,128]{1,0:T(8,128)S(1)}, f32[2,4,8192]{2,1,0:T(4,128)S(1)}, bf16[2,4,8192]{2,1,0:T(4,128)(2,1)S(1)}, bf16[2,4,8192]{2,1,0:T(4,128)(2,1)S(1)}, bf16[2,4,8192]{2,1,0:T(4,128)(2,1)S(1)}) custom-call(f32[16,128]{1,0:T(8,128)S(1)} %pad_maximum_fusion.rest_0_, f32[16,128]{1,0:T(8,128)S(1)} %collective-permute-done.14.rest_1_, ...), custom_call_target="tpu_custom_call" | custom-call | flops 33554432 | bytes 2621440 | tf_op jit(solution)/shard_map/volume_terms/pallas_call | solution.py:519
  39.1 3.7 %collective-permute-start.15 = (bf16[2,4,8192]{2,1,0:T(4,128)(2,1)S(1)}, bf16[2,4,8192]{2,1,0:T(4,128)(2,1)S(1)}, u32[]{:S(2)}, u32[]{:S(2)}) collective-permute-start(bf16[2,4,8192]{2,1,0:T(4,128)(2,1)S(1)} %get-tuple-element.57), channel_id=1, source_target_pairs={{0,2},{1,3},{2,0},{3,1},{4,6},{5,7},{6,4},{7,5},{8,10},{9,11},{10,... | collective-permute-start | bytes 393224 | tf_op jit(solution)/shard_map/ppermute | solution.py:565
  42.8 0.8 %collective-permute-start.16 = (bf16[2,4,8192]{2,1,0:T(4,128)(2,1)S(1)}, bf16[2,4,8192]{2,1,0:T(4,128)(2,1)S(1)}, u32[]{:S(2)}, u32[]{:S(2)}) collective-permute-start(bf16[2,4,8192]{2,1,0:T(4,128)(2,1)S(1)} %get-tuple-element.58), channel_id=1, source_target_pairs={{0,1},{1,0},{2,3},{3,2},{4,5},{5,4},{6,7},{7,6},{8,9},{9,8},{10,11... | collective-permute-start | bytes 393224 | tf_op jit(solution)/shard_map/ppermute | solution.py:565
  43.6 0.7 %collective-permute-start.17 = (bf16[2,4,8192]{2,1,0:T(4,128)(2,1)S(1)}, bf16[2,4,8192]{2,1,0:T(4,128)(2,1)S(1)}, u32[]{:S(2)}, u32[]{:S(2)}) collective-permute-start(bf16[2,4,8192]{2,1,0:T(4,128)(2,1)S(1)} %get-tuple-element.59), channel_id=1, source_target_pairs={{0,3},{1,2},{2,1},{3,0},{4,7},{5,6},{6,5},{7,4},{8,11},{9,10},{10,... | collective-permute-start | bytes 393224 | tf_op jit(solution)/shard_map/ppermute | solution.py:565
  44.3 0.7 %copy.9 = f32[16,4]{0,1:T(4,128)} copy(f32[16,4]{1,0:T(8,128)S(1)} %bitcast.4) | data formatting | bytes 512
  44.9 6.7 %collective-permute-done.15.rest_0_ = bf16[2,4,8192]{2,1,0:T(4,128)(2,1)S(1)} collective-permute-done((bf16[2,4,8192]{2,1,0:T(4,128)(2,1)S(1)}, bf16[2,4,8192]{2,1,0:T(4,128)(2,1)S(1)}, u32[]{:S(2)}, u32[]{:S(2)}) %collective-permute-start.15) | collective-permute-done | bytes 131104 | tf_op jit(solution)/shard_map/ppermute | solution.py:565
  51.7 0.4 collective-permute-done.16.rest_1_
  52.0 0.0 collective-permute-done.17.rest_2_
  52.0 0.8 %total_volume.1 = f32[2,4,1,8192]{3,2,1,0:T(1,128)} custom-call(f32[2,4,8192]{2,1,0:T(4,128)S(1)} %get-tuple-element.56.first, bf16[2,4,8192]{2,1,0:T(4,128)(2,1)S(1)} %collective-permute-done.15.rest_0_, bf16[2,4,8192]{2,1,0:T(4,128)(2,1)S(1)} %collective-permute-done.16.rest_1_, bf16[2,4,8192]{2,1,0:T(4,128)(2,1)S(1)} %collective-permute-done.17.rest_2_), custom_call_target="tpu_custom_call" | custom-call | tf_op jit(solution)/shard_map/total_volume/pallas_call | solution.py:548
  (1 shorter events, 0.0 us)
Async XLA Ops:
  0.6 13.5 %copy-start = (f32[8,256]{1,0:T(8,128)S(1)}, f32[8,256]{1,0:T(8,128)}, u32[]{:S(2)}) copy-start(f32[8,256]{1,0:T(8,128)} %constant.4.clone.table_x) | copy-start | bytes 24580
  0.6 13.5 %copy-start.1 = (f32[1024]{0:T(1024)S(1)}, f32[1024]{0:T(1024)}, u32[]{:S(2)}) copy-start(f32[1024]{0:T(1024)} %constant.5.clone.table_y) | copy-start | bytes 12292
  2.2 7.3 %collective-permute-start.1 = (bf16[2,16,8320]{2,1,0:T(8,128)(2,1)S(1)}, bf16[2,16,8320]{2,1,0:T(8,128)(2,1)S(1)}, u32[]{:S(2)}, u32[]{:S(2)}) collective-permute-start(bf16[2,16,8320]{2,1,0:T(8,128)(2,1)S(1)} %get-tuple-element.32), channel_id=1, source_target_pairs={{0,4},{4,0},{8,12},{12,8},{1,5},{5,1},{9,13},{13,9},{2,6},{6,2},{1... | collective-permute-start | bytes 1597448 | tf_op jit(solution)/shard_map/ppermute | solution.py:562
  2.7 9.6 %collective-permute-start.5 = (bf16[2,16,4224]{2,1,0:T(8,128)(2,1)S(1)}, bf16[2,16,4224]{2,1,0:T(8,128)(2,1)S(1)}, u32[]{:S(2)}, u32[]{:S(2)}) collective-permute-start(bf16[2,16,4224]{2,1,0:T(8,128)(2,1)S(1)} %get-tuple-element.45), channel_id=1, source_target_pairs={{0,8},{4,12},{8,0},{12,4},{1,9},{5,13},{9,1},{13,5},{2,10},{6,14},... | collective-permute-start | bytes 811016 | tf_op jit(solution)/shard_map/ppermute | solution.py:562
  5.2 10.6 %collective-permute-start.3 = (bf16[2,4,4,2048]{3,2,1,0:T(4,128)(2,1)S(1)}, bf16[2,4,4,2048]{3,2,1,0:T(4,128)(2,1)S(1)}, u32[]{:S(2)}, u32[]{:S(2)}) collective-permute-start(bf16[2,4,4,2048]{3,2,1,0:T(4,128)(2,1)S(1)} %get-tuple-element.33.rest_0_), channel_id=1, source_target_pairs={{0,2},{1,3},{2,0},{3,1},{4,6},{5,7},{6,4},{7,5},{8,10},{9,11},{10,... | collective-permute-start | bytes 393224 | tf_op jit(solution)/shard_map/ppermute | solution.py:565
  7.8 10.4 %collective-permute-start = (bf16[2,4,4,2048]{3,2,1,0:T(4,128)(2,1)S(1)}, bf16[2,4,4,2048]{3,2,1,0:T(4,128)(2,1)S(1)}, u32[]{:S(2)}, u32[]{:S(2)}) collective-permute-start(bf16[2,4,4,2048]{3,2,1,0:T(4,128)(2,1)S(1)} %get-tuple-element.33.rest_0_), channel_id=1, source_target_pairs={{0,1},{1,0},{2,3},{3,2},{4,5},{5,4},{6,7},{7,6},{8,9},{9,8},{10,11... | collective-permute-start | bytes 393224 | tf_op jit(solution)/shard_map/ppermute | solution.py:565
  9.4 9.1 %collective-permute-start.2 = (bf16[2,4,4,2048]{3,2,1,0:T(4,128)(2,1)S(1)}, bf16[2,4,4,2048]{3,2,1,0:T(4,128)(2,1)S(1)}, u32[]{:S(2)}, u32[]{:S(2)}) collective-permute-start(bf16[2,4,4,2048]{3,2,1,0:T(4,128)(2,1)S(1)} %get-tuple-element.33.rest_0_), channel_id=1, source_target_pairs={{0,3},{1,2},{2,1},{3,0},{4,7},{5,6},{6,5},{7,4},{8,11},{9,10},{10,... | collective-permute-start | bytes 393224 | tf_op jit(solution)/shard_map/ppermute | solution.py:565
  9.6 14.1 %collective-permute-start.7 = (bf16[2,16,8320]{2,1,0:T(8,128)(2,1)S(1)}, bf16[2,16,8320]{2,1,0:T(8,128)(2,1)S(1)}, u32[]{:S(2)}, u32[]{:S(2)}) collective-permute-start(bf16[2,16,8320]{2,1,0:T(8,128)(2,1)S(1)} %get-tuple-element.46), channel_id=1, source_target_pairs={{0,12},{4,8},{8,4},{12,0},{1,13},{5,9},{9,5},{13,1},{2,14},{6,10},... | collective-permute-start | bytes 1597448 | tf_op jit(solution)/shard_map/ppermute | solution.py:562
  12.3 11.4 %collective-permute-start.6 = (bf16[2,16,4224]{2,1,0:T(8,128)(2,1)S(1)}, bf16[2,16,4224]{2,1,0:T(8,128)(2,1)S(1)}, u32[]{:S(2)}, u32[]{:S(2)}) collective-permute-start(bf16[2,16,4224]{2,1,0:T(8,128)(2,1)S(1)} %collective-permute-done.5.rest_2_.rest_0_.rest_4_), channel_id=1, source_target_pairs={{0,16},{16,0},{1,17},{17,1},{2,18},{18,2},{3,19},{19,3},{4,20},{20... | collective-permute-start | bytes 811016 | tf_op jit(solution)/shard_map/ppermute | solution.py:578
  20.9 2.2 %collective-permute-start.4 = (f32[128,128]{1,0:T(8,128)S(1)}, f32[128,128]{1,0:T(8,128)S(1)}, u32[]{:S(2)}, u32[]{:S(2)}) collective-permute-start(f32[128,128]{1,0:T(8,128)S(1)} %get-tuple-element.41), channel_id=1, source_target_pairs={{0,4},{4,0},{8,12},{12,8},{1,5},{5,1},{9,13},{13,9},{2,6},{6,2},{1... | collective-permute-start | bytes 196616 | tf_op jit(solution)/shard_map/ppermute | solution.py:562
  20.9 6.1 %collective-permute-start.10 = (f32[128,128]{1,0:T(8,128)S(1)}, f32[128,128]{1,0:T(8,128)S(1)}, u32[]{:S(2)}, u32[]{:S(2)}) collective-permute-start(f32[128,128]{1,0:T(8,128)S(1)} %get-tuple-element.41), channel_id=1, source_target_pairs={{0,12},{4,8},{8,4},{12,0},{1,13},{5,9},{9,5},{13,1},{2,14},{6,10},... | collective-permute-start | bytes 196616 | tf_op jit(solution)/shard_map/ppermute | solution.py:562
  22.7 4.4 %collective-permute-start.9 = (f32[128,128]{1,0:T(8,128)S(1)}, f32[128,128]{1,0:T(8,128)S(1)}, u32[]{:S(2)}, u32[]{:S(2)}) collective-permute-start(f32[128,128]{1,0:T(8,128)S(1)} %get-tuple-element.39.refs_0_), channel_id=1, source_target_pairs={{0,8},{4,12},{8,0},{12,4},{1,9},{5,13},{9,1},{13,5},{2,10},{6,14},... | collective-permute-start | bytes 196616 | tf_op jit(solution)/shard_map/ppermute | solution.py:562
  27.1 4.4 %collective-permute-start.11 = (f32[128,128]{1,0:T(8,128)S(1)}, f32[128,128]{1,0:T(8,128)S(1)}, u32[]{:S(2)}, u32[]{:S(2)}) collective-permute-start(f32[128,128]{1,0:T(8,128)S(1)} %get-tuple-element.49), channel_id=1, source_target_pairs={{0,12},{4,8},{8,4},{12,0},{1,13},{5,9},{9,5},{13,1},{2,14},{6,10},... | collective-permute-start | bytes 196616 | tf_op jit(solution)/shard_map/ppermute | solution.py:562
  28.3 3.2 %collective-permute-start.12 = (f32[128,128]{1,0:T(8,128)S(1)}, f32[128,128]{1,0:T(8,128)S(1)}, u32[]{:S(2)}, u32[]{:S(2)}) collective-permute-start(f32[128,128]{1,0:T(8,128)S(1)} %get-tuple-element.49), channel_id=1, source_target_pairs={{0,4},{4,0},{8,12},{12,8},{1,5},{5,1},{9,13},{13,9},{2,6},{6,2},{1... | collective-permute-start | bytes 196616 | tf_op jit(solution)/shard_map/ppermute | solution.py:562
  28.7 4.3 %collective-permute-start.8 = (f32[128,128]{1,0:T(8,128)S(1)}, f32[128,128]{1,0:T(8,128)S(1)}, u32[]{:S(2)}, u32[]{:S(2)}) collective-permute-start(f32[128,128]{1,0:T(8,128)S(1)} %get-tuple-element.47.refs_4_), channel_id=1, source_target_pairs={{0,8},{4,12},{8,0},{12,4},{1,9},{5,13},{9,1},{13,5},{2,10},{6,14},... | collective-permute-start | bytes 196616 | tf_op jit(solution)/shard_map/ppermute | solution.py:562
  33.2 1.2 %collective-permute-start.13 = (f32[8,128]{1,0:T(8,128)S(1)}, f32[8,128]{1,0:T(8,128)S(1)}, u32[]{:S(2)}, u32[]{:S(2)}) collective-permute-start(f32[8,128]{1,0:T(8,128)S(1)} %logit_stats.1), channel_id=1, source_target_pairs={{0,4},{4,0},{8,12},{12,8},{1,5},{5,1},{9,13},{13,9},{2,6},{6,2},{1... | collective-permute-start | bytes 12296 | tf_op jit(solution)/shard_map/ppermute | solution.py:562
  34.4 3.7 %collective-permute-start.14 = (f32[16,128]{1,0:T(8,128)S(1)}, f32[16,128]{1,0:T(8,128)S(1)}, u32[]{:S(2)}, u32[]{:S(2)}) collective-permute-start(f32[16,128]{1,0:T(8,128)S(1)} %pad_maximum_fusion.rest_0_), channel_id=1, source_target_pairs={{0,16},{16,0},{1,17},{17,1},{2,18},{18,2},{3,19},{19,3},{4,20},{20... | collective-permute-start | bytes 24584 | tf_op jit(solution)/shard_map/ppermute | solution.py:617
  39.1 12.6 %collective-permute-start.15 = (bf16[2,4,8192]{2,1,0:T(4,128)(2,1)S(1)}, bf16[2,4,8192]{2,1,0:T(4,128)(2,1)S(1)}, u32[]{:S(2)}, u32[]{:S(2)}) collective-permute-start(bf16[2,4,8192]{2,1,0:T(4,128)(2,1)S(1)} %get-tuple-element.57), channel_id=1, source_target_pairs={{0,2},{1,3},{2,0},{3,1},{4,6},{5,7},{6,4},{7,5},{8,10},{9,11},{10,... | collective-permute-start | bytes 393224 | tf_op jit(solution)/shard_map/ppermute | solution.py:565
  42.8 9.3 %collective-permute-start.16 = (bf16[2,4,8192]{2,1,0:T(4,128)(2,1)S(1)}, bf16[2,4,8192]{2,1,0:T(4,128)(2,1)S(1)}, u32[]{:S(2)}, u32[]{:S(2)}) collective-permute-start(bf16[2,4,8192]{2,1,0:T(4,128)(2,1)S(1)} %get-tuple-element.58), channel_id=1, source_target_pairs={{0,1},{1,0},{2,3},{3,2},{4,5},{5,4},{6,7},{7,6},{8,9},{9,8},{10,11... | collective-permute-start | bytes 393224 | tf_op jit(solution)/shard_map/ppermute | solution.py:565
  43.6 8.5 %collective-permute-start.17 = (bf16[2,4,8192]{2,1,0:T(4,128)(2,1)S(1)}, bf16[2,4,8192]{2,1,0:T(4,128)(2,1)S(1)}, u32[]{:S(2)}, u32[]{:S(2)}) collective-permute-start(bf16[2,4,8192]{2,1,0:T(4,128)(2,1)S(1)} %get-tuple-element.59), channel_id=1, source_target_pairs={{0,3},{1,2},{2,1},{3,0},{4,7},{5,6},{6,5},{7,4},{8,11},{9,10},{10,... | collective-permute-start | bytes 393224 | tf_op jit(solution)/shard_map/ppermute | solution.py:565

commit v9 on v8

--- a/solution.py
+++ b/solution.py
@@ -203,7 +203,7 @@
         to_re = slice(2 * line * IMG, (2 * line + 1) * IMG)
         to_im = slice((2 * line + 1) * IMG, (2 * line + 2) * IMG)
         base = (line_base + line) * TY
-        cols = pl.ds(pl.multiple_of(step[0] * chunk + line * IMG, IMG), IMG)
+        cols = slice(step[0] * chunk + line * IMG, step[0] * chunk + (line + 1) * IMG)
         ref_re = refs[0, :, cols].astype(F32)
         ref_im = refs[1, :, cols].astype(F32)
 
@@ -262,7 +262,7 @@
     shards, rest = rest[:count], rest[count:]
     images, rest = by_group(sizes, rest)
     before, rest = rest[: groups * sums], rest[groups * sums :]
-    outs, (right, refs, left) = rest[:groups], rest[groups:]
+    outs, (right, refs, *lefts) = rest[:groups], rest[groups:]
     chunk = shards[0].shape[3]
     per_class = shards[0].shape[2]
     for place, shard in enumerate(shards):
@@ -273,14 +273,12 @@
     for g, out in enumerate(outs):
         out[...] = before[g][...] if sums else jnp.zeros_like(out)
 
-    def add_shard(place, carry):
+    for place in range(count):
         step = 2 * place + steps[0]
+        left = lefts[place % 2]
         shift_references(refs, right, (place, step), ids, orients, table_y)
         shift_images(images, left, ids[1] ^ step, ids, table_x)
         add_products(outs, left[...], right[place])
-        return carry
-
-    lax.fori_loop(0, count, add_shard, 0)
 
 
 def far_kernel(sizes, counts, table_x, *rest):
@@ -288,17 +286,16 @@
     groups = len(sizes)
     rights, rest = rest[: len(counts)], rest[len(counts) :]
     images, rest = by_group(sizes, rest)
-    outs, left = rest[:groups], rest[groups]
+    outs, lefts = rest[:groups], rest[groups:]
     for out in outs:
         out[...] = jnp.zeros_like(out)
+    turn = 0
     for first, (right, count) in enumerate(zip(rights, counts)):
-
-        def add_shard(place, carry, first=first, right=right):
+        for place in range(count):
+            left = lefts[turn % 2]
             shift_images(images, left, ids[1] ^ (2 * place + first), ids, table_x)
             add_products(outs, left[...], right[place])
-            return carry
-
-        lax.fori_loop(0, count, add_shard, 0)
+            turn += 1
 
 
 def logits_cost(micros):
@@ -325,6 +322,7 @@
         scratch_shapes=[
             pltpu.VMEM((parts, names, count * chunk), BF),
             pltpu.VMEM((groups * TX * rows, 2 * chunk), BF),
+            pltpu.VMEM((groups * TX * rows, 2 * chunk), BF),
         ],
         compiler_params=pltpu.CompilerParams(vmem_limit_bytes=VMEM_BYTES),
         cost_estimate=logits_cost(micros),
@@ -344,7 +342,7 @@
         out_shape=[pltpu.VMEM(out_shape, F32)] * groups,
         in_specs=specs,
         out_specs=[VMEM_SPEC] * groups,
-        scratch_shapes=[pltpu.VMEM((groups * TX * rows, chunk), BF)],
+        scratch_shapes=[pltpu.VMEM((groups * TX * rows, chunk), BF)] * 2,
         compiler_params=pltpu.CompilerParams(vmem_limit_bytes=VMEM_BYTES),
         cost_estimate=logits_cost(micros),
         name="far_logits",
@@ -593,7 +591,7 @@
         crossed_over = swap_dom(near[1], 3)
     far = list(far_logits(table_x, [right, right_late], groups[2:], 6))
     if one_phase:
-        far[1], crossed, crossed_over = lax.optimization_barrier((far[1], crossed, crossed_over))
+        far[1], crossed = lax.optimization_barrier((far[1], crossed))
         terms = [
             [near[0], swapped, swap_dom(far[0], 2), swap_dom(far[1], 3)],
             [far[0], swap_dom(far[1], 1), crossed, crossed_over],
@@ -609,6 +607,8 @@
             if step < dom:
                 here = {s: here[s] + there[s] for s in here}
         terms = [[here[s], there[s]] for s in sorted(here)]
+    if one_phase:
+        groups[2][0][0], terms[1][3] = lax.optimization_barrier((groups[2][0][0], terms[1][3]))
     aligned_far = aligned_rows(table_x, table_y, groups[2:], width)
     terms[0][-1], aligned_far = lax.optimization_barrier((terms[0][-1], aligned_far))
     stats = logit_stats(terms, classes, orients)

time: 53.1 us -> 52.4 us (0.987)
  waiting for transfers between devices: 13.4 us -> 14.9 us
  Pallas kernels: 16.5 us -> 15.2 us
  starting transfers between devices: 21.5 us -> 20.8 us
    ppermute x10, waiting for transfers between devices: 4.49 us -> 5.41 us  [swap_dom(): return lax.ppermute(array, 'dom', xor_pairs(dom, step))]
    pallas_call x1, Pallas kernels: 3.32 us -> 2.45 us  [far_logits(): pl.pallas_call(functools.partial(far_kernel, sizes_of(picked), [right.sha...]
  transfers between devices with their start and end apart: 18 -> 18, of which waited for: 9 -> 10; matrix products, arithmetic and copies ran while one was open for 1% -> 1% of each run, Pallas kernels for 24% -> 22%
where the time goes in v9:
time: 52.4 us; the launch traced here: 52.3 us
  starting transfers between devices  20.8 us (40%)
  Pallas kernels  15.2 us (29%)
  waiting for transfers between devices  14.9 us (28%)
  between operations  0.76 us (1%)
  local copies, waits for them, and re-layouts  0.66 us (1%)
    ppermute x6, starting transfers between devices, swap_orient(): return lax.ppermute(array, 'orient', xor_pairs(orient, step))  9.64 us
    ppermute x10, starting transfers between devices, swap_dom(): return lax.ppermute(array, 'dom', xor_pairs(dom, step))  7.7 us
    ppermute x6, waiting for transfers between devices, swap_orient(): return lax.ppermute(array, 'orient', xor_pairs(orient, step))  7.5 us
    ppermute x10, waiting for transfers between devices, swap_dom(): return lax.ppermute(array, 'dom', xor_pairs(dom, step))  5.41 us
    pallas_call x2, Pallas kernels, near_logits(): pl.pallas_call(functools.partial(near_kernel, sizes_of(picked), len(shard...  4.32 us
    pallas_call x2, Pallas kernels, aligned_rows(): pl.pallas_call(functools.partial(rows_kernel, sizes_of(picked)), out_shap...  3.79 us
    pallas_call x1, Pallas kernels, far_logits(): pl.pallas_call(functools.partial(far_kernel, sizes_of(picked), [right.sha...  2.45 us
    ppermute x1, waiting for transfers between devices, local(): stats_all = [stats, lax.ppermute(stats, 'cls', xor_pairs(cls, 1))]  1.95 us
  transfers between devices with their start and end apart: 18, of which 10 were waited for; matrix products, arithmetic and copies ran while one was open for 1% of the time, Pallas kernels for 22%

profile of v9, /device:TPU:0, one launch (start us, length us, event | category | flops | bytes accessed | tf_op | source)
XLA Modules:
  0.0 52.3 jit_solution(3479689174874164229)
XLA Ops:
  0.6 0.0 copy-start
  0.6 0.0 copy-start.1
  0.7 1.5 %image_bands.1 = (bf16[2,16,8320]{2,1,0:T(8,128)(2,1)S(1)}, bf16[2,16,4224]{2,1,0:T(8,128)(2,1)S(1)}, bf16[2,16,8320]{2,1,0:T(8,128)(2,1)S(1)}, bf16[2,16,128]{2...) custom-call(bf16[2,16,32768]{2,1,0:T(8,128)(2,1)} %images.3, bf16[2,4,4,2048]{3,2,1,0:T(4,128)(2,1)} %references.1, ...), custom_call_target="tpu_custom_call" | custom-call | bytes 3145728 | tf_op jit(solution)/shard_map/image_bands/pallas_call | solution.py:109
  2.2 0.5 collective-permute-start.1
  2.7 2.6 %collective-permute-start.5 = (bf16[2,16,4224]{2,1,0:T(8,128)(2,1)S(1)}, bf16[2,16,4224]{2,1,0:T(8,128)(2,1)S(1)}, u32[]{:S(2)}, u32[]{:S(2)}) collective-permute-start(bf16[2,16,4224]{2,1,0:T(8,128)(2,1)S(1)} %get-tuple-element.46), channel_id=1, source_target_pairs={{0,8},{4,12},{8,0},{12,4},{1,9},{5,13},{9,1},{13,5},{2,10},{6,14},... | collective-permute-start | bytes 811016 | tf_op jit(solution)/shard_map/ppermute | solution.py:560
  5.2 2.6 %collective-permute-start.3 = (bf16[2,4,4,2048]{3,2,1,0:T(4,128)(2,1)S(1)}, bf16[2,4,4,2048]{3,2,1,0:T(4,128)(2,1)S(1)}, u32[]{:S(2)}, u32[]{:S(2)}) collective-permute-start(bf16[2,4,4,2048]{3,2,1,0:T(4,128)(2,1)S(1)} %get-tuple-element.34.rest_0_), channel_id=1, source_target_pairs={{0,2},{1,3},{2,0},{3,1},{4,6},{5,7},{6,4},{7,5},{8,10},{9,11},{10,... | collective-permute-start | bytes 393224 | tf_op jit(solution)/shard_map/ppermute | solution.py:563
  7.8 1.6 %collective-permute-start = (bf16[2,4,4,2048]{3,2,1,0:T(4,128)(2,1)S(1)}, bf16[2,4,4,2048]{3,2,1,0:T(4,128)(2,1)S(1)}, u32[]{:S(2)}, u32[]{:S(2)}) collective-permute-start(bf16[2,4,4,2048]{3,2,1,0:T(4,128)(2,1)S(1)} %get-tuple-element.34.rest_0_), channel_id=1, source_target_pairs={{0,1},{1,0},{2,3},{3,2},{4,5},{5,4},{6,7},{7,6},{8,9},{9,8},{10,11... | collective-permute-start | bytes 393224 | tf_op jit(solution)/shard_map/ppermute | solution.py:563
  9.4 0.0 collective-permute-done.1.rest_1_.rest_3_
  9.4 0.2 collective-permute-start.2
  9.6 0.5 collective-permute-start.7
  10.1 1.0 %own_band.1.rest_2_ = bf16[2,16,8192]{2,1,0:T(8,128)(2,1)S(1)} custom-call(bf16[2,16,32768]{2,1,0:T(8,128)(2,1)} %images.3), custom_call_target="tpu_custom_call" | custom-call | tf_op jit(solution)/shard_map/own_band/pallas_call | solution.py:155
  11.2 1.1 %collective-permute-done.5.rest_2_.rest_0_.rest_4_ = bf16[2,16,4224]{2,1,0:T(8,128)(2,1)S(1)} collective-permute-done((bf16[2,16,4224]{2,1,0:T(8,128)(2,1)S(1)}, bf16[2,16,4224]{2,1,0:T(8,128)(2,1)S(1)}, u32[]{:S(2)}, u32[]{:S(2)}) %collective-permute-start.5) | collective-permute-done | bytes 270368 | tf_op jit(solution)/shard_map/ppermute | solution.py:560
  12.3 1.8 %collective-permute-start.6 = (bf16[2,16,4224]{2,1,0:T(8,128)(2,1)S(1)}, bf16[2,16,4224]{2,1,0:T(8,128)(2,1)S(1)}, u32[]{:S(2)}, u32[]{:S(2)}) collective-permute-start(bf16[2,16,4224]{2,1,0:T(8,128)(2,1)S(1)} %collective-permute-done.5.rest_2_.rest_0_.rest_4_), channel_id=1, source_target_pairs={{0,16},{16,0},{1,17},{17,1},{2,18},{18,2},{3,19},{19,3},{4,20},{20... | collective-permute-start | bytes 811016 | tf_op jit(solution)/shard_map/ppermute | solution.py:576
  14.1 0.0 copy-done
  14.1 0.0 copy-done.1
  14.1 1.7 %aligned_rows.2.rest_6_ = bf16[2,32,8192]{2,1,0:T(8,128)(2,1)S(1)} custom-call(f32[1024]{0:T(1024)S(1)} %copy-done.1, f32[8,256]{1,0:T(8,128)S(1)} %copy-done, bf16[2,16,128]{2,1,0:T(8,128)(2,1)S(1)} %get-tuple-element.36.rest_0_.rest_2_, bf16[2,16,8320]{2,1,0:T(8,128)(2,1)S(1)} %collective-permute-done.1.rest_1_.rest_3_, ...), custom_call_target="tpu_custom_call" | custom-call | tf_op jit(solution)/shard_map/aligned_rows/pallas_call | solution.py:442
  15.8 0.0 collective-permute-done.3.rest_1_
  15.8 2.2 %near_logits.2 = (f32[128,128]{1,0:T(8,128)S(1)}, f32[128,128]{1,0:T(8,128)S(1)}, bf16[2,128,4096]{2,1,0:T(8,128)(2,1)S(1)}) custom-call(f32[1024]{0:T(1024)S(1)} %copy-done.1, f32[8,256]{1,0:T(8,128)S(1)} %copy-done, bf16[2,4,4,2048]{3,2,1,0:T(4,128)(2,1)S(1)} %get-tuple-element.34.rest_0_, bf16[2,4,4,2048]{3,2,1,0:T(4,128)(2,1)S(1)} %collective-permute-done.3.rest_1_, ...), custom_call_target="tpu_custom_call" | custom-call | tf_op jit(solution)/shard_map/near_logits/pallas_call | solution.py:314
  18.0 0.0 collective-permute-done.rest_0_
  18.0 0.5 collective-permute-done.2.rest_1_
  18.5 2.2 %near_logits.3 = (f32[128,128]{1,0:T(8,128)S(1)}, f32[128,128]{1,0:T(8,128)S(1)}, bf16[2,128,4096]{2,1,0:T(8,128)(2,1)S(1)}) custom-call(f32[1024]{0:T(1024)S(1)} %copy-done.1, f32[8,256]{1,0:T(8,128)S(1)} %copy-done, bf16[2,4,4,2048]{3,2,1,0:T(4,128)(2,1)S(1)} %collective-permute-done.rest_0_, bf16[2,4,4,2048]{3,2,1,0:T(4,128)(2,1)S(1)} %collective-permute-done.2.rest_1_, ...), custom_call_target="tpu_custom_call" | custom-call | flops 20000000000 | tf_op jit(solution)/shard_map/near_logits/pallas_call | solution.py:314
  20.6 0.1 collective-permute-start.4
  20.7 1.5 %collective-permute-start.11 = (f32[128,128]{1,0:T(8,128)S(1)}, f32[128,128]{1,0:T(8,128)S(1)}, u32[]{:S(2)}, u32[]{:S(2)}) collective-permute-start(f32[128,128]{1,0:T(8,128)S(1)} %get-tuple-element.42), channel_id=1, source_target_pairs={{0,12},{4,8},{8,4},{12,0},{1,13},{5,9},{9,5},{13,1},{2,14},{6,10},... | collective-permute-start | bytes 196616 | tf_op jit(solution)/shard_map/ppermute | solution.py:560
  22.2 0.6 %collective-permute-start.9 = (f32[128,128]{1,0:T(8,128)S(1)}, f32[128,128]{1,0:T(8,128)S(1)}, u32[]{:S(2)}, u32[]{:S(2)}) collective-permute-start(f32[128,128]{1,0:T(8,128)S(1)} %get-tuple-element.40.refs_0_), channel_id=1, source_target_pairs={{0,8},{4,12},{8,0},{12,4},{1,9},{5,13},{9,1},{13,5},{2,10},{6,14},... | collective-permute-start | bytes 196616 | tf_op jit(solution)/shard_map/ppermute | solution.py:560
  22.9 0.0 collective-permute-done.4.refs_1_
  22.9 0.9 %collective-permute-done.7.rest_4_.rest_1_.rest_5_ = bf16[2,16,8320]{2,1,0:T(8,128)(2,1)S(1)} collective-permute-done((bf16[2,16,8320]{2,1,0:T(8,128)(2,1)S(1)}, bf16[2,16,8320]{2,1,0:T(8,128)(2,1)S(1)}, u32[]{:S(2)}, u32[]{:S(2)}) %collective-permute-start.7) | collective-permute-done | bytes 532512 | tf_op jit(solution)/shard_map/ppermute | solution.py:560
  23.7 0.0 collective-permute-done.6.rest_3_
  23.7 2.5 %far_logits.1 = (f32[128,128]{1,0:T(8,128)S(1)}, f32[128,128]{1,0:T(8,128)S(1)}) custom-call(f32[8,256]{1,0:T(8,128)S(1)} %copy-done, bf16[2,128,4096]{2,1,0:T(8,128)(2,1)S(1)} %get-tuple-element.44.rest_0_, bf16[2,128,4096]{2,1,0:T(8,128)(2,1)S(1)} %get-tuple-element.45.rest_1_, bf16[2,16,4224]{2,1,0:T(8,128)(2,1)S(1)} %collective-permute-done.5.rest_2_.rest_0_.rest_4_, ...), custom_call_target="tpu_custom_call" | custom-call | flops 6000000000 | tf_op jit(solution)/shard_map/far_logits/pallas_call | solution.py:340
  26.2 0.4 collective-permute-done.9.refs_6_
  26.6 1.4 %collective-permute-start.10 = (f32[128,128]{1,0:T(8,128)S(1)}, f32[128,128]{1,0:T(8,128)S(1)}, u32[]{:S(2)}, u32[]{:S(2)}) collective-permute-start(f32[128,128]{1,0:T(8,128)S(1)} %get-tuple-element.50), channel_id=1, source_target_pairs={{0,12},{4,8},{8,4},{12,0},{1,13},{5,9},{9,5},{13,1},{2,14},{6,10},... | collective-permute-start | bytes 196616 | tf_op jit(solution)/shard_map/ppermute | solution.py:560
  28.0 0.3 collective-permute-start.8
  28.3 0.1 collective-permute-start.12
  28.5 0.0 collective-permute-done.11.refs_7_
  28.5 2.1 %aligned_rows.3.rest_7_ = bf16[2,32,8192]{2,1,0:T(8,128)(2,1)S(1)} custom-call(f32[1024]{0:T(1024)S(1)} %copy-done.1, f32[8,256]{1,0:T(8,128)S(1)} %copy-done, bf16[2,16,4224]{2,1,0:T(8,128)(2,1)S(1)} %collective-permute-done.5.rest_2_.rest_0_.rest_4_, bf16[2,16,8320]{2,1,0:T(8,128)(2,1)S(1)} %collective-permute-done.7.rest_4_.rest_1_.rest_5_, ...), custom_call_target="tpu_custom_call" | custom-call | tf_op jit(solution)/shard_map/aligned_rows/pallas_call | solution.py:442
  30.5 0.2 collective-permute-done.10.refs_3_
  30.7 1.7 %collective-permute-done.8.refs_2_ = f32[128,128]{1,0:T(8,128)S(1)} collective-permute-done((f32[128,128]{1,0:T(8,128)S(1)}, f32[128,128]{1,0:T(8,128)S(1)}, u32[]{:S(2)}, u32[]{:S(2)}) %collective-permute-start.8) | collective-permute-done | bytes 65568 | tf_op jit(solution)/shard_map/ppermute | solution.py:560
  32.4 0.0 collective-permute-done.12.refs_5_
  32.4 0.3 logit_stats.1
  32.7 0.0 collective-permute-start.13
  32.7 1.2 %collective-permute-done.13 = f32[8,128]{1,0:T(8,128)S(1)} collective-permute-done((f32[8,128]{1,0:T(8,128)S(1)}, f32[8,128]{1,0:T(8,128)S(1)}, u32[]{:S(2)}, u32[]{:S(2)}) %collective-permute-start.13) | collective-permute-done | bytes 4128 | tf_op jit(solution)/shard_map/ppermute | solution.py:560
  33.9 1.7 %collective-permute-start.14 = (f32[16,128]{1,0:T(8,128)S(1)}, f32[16,128]{1,0:T(8,128)S(1)}, u32[]{:S(2)}, u32[]{:S(2)}) collective-permute-start(f32[16,128]{1,0:T(8,128)S(1)} %pad_maximum_fusion.rest_0_), channel_id=1, source_target_pairs={{0,16},{16,0},{1,17},{17,1},{2,18},{18,2},{3,19},{19,3},{4,20},{20... | collective-permute-start | bytes 24584 | tf_op jit(solution)/shard_map/ppermute | solution.py:617
  35.6 2.0 %collective-permute-done.14.rest_1_ = f32[16,128]{1,0:T(8,128)S(1)} collective-permute-done((f32[16,128]{1,0:T(8,128)S(1)}, f32[16,128]{1,0:T(8,128)S(1)}, u32[]{:S(2)}, u32[]{:S(2)}) %collective-permute-start.14) | collective-permute-done | bytes 8224 | tf_op jit(solution)/shard_map/ppermute | solution.py:617
  37.5 1.0 %volume_terms.1 = (f32[16,128]{1,0:T(8,128)S(1)}, f32[2,4,8192]{2,1,0:T(4,128)S(1)}, bf16[2,4,8192]{2,1,0:T(4,128)(2,1)S(1)}, bf16[2,4,8192]{2,1,0:T(4,128)(2,1)S(1)}, bf16[2,4,8192]{2,1,0:T(4,128)(2,1)S(1)}) custom-call(f32[16,128]{1,0:T(8,128)S(1)} %pad_maximum_fusion.rest_0_, f32[16,128]{1,0:T(8,128)S(1)} %collective-permute-done.14.rest_1_, ...), custom_call_target="tpu_custom_call" | custom-call | flops 33554432 | bytes 2621440 | tf_op jit(solution)/shard_map/volume_terms/pallas_call | solution.py:517
  38.5 3.7 %collective-permute-start.15 = (bf16[2,4,8192]{2,1,0:T(4,128)(2,1)S(1)}, bf16[2,4,8192]{2,1,0:T(4,128)(2,1)S(1)}, u32[]{:S(2)}, u32[]{:S(2)}) collective-permute-start(bf16[2,4,8192]{2,1,0:T(4,128)(2,1)S(1)} %get-tuple-element.59), channel_id=1, source_target_pairs={{0,2},{1,3},{2,0},{3,1},{4,6},{5,7},{6,4},{7,5},{8,10},{9,11},{10,... | collective-permute-start | bytes 393224 | tf_op jit(solution)/shard_map/ppermute | solution.py:563
  42.3 0.7 %collective-permute-start.16 = (bf16[2,4,8192]{2,1,0:T(4,128)(2,1)S(1)}, bf16[2,4,8192]{2,1,0:T(4,128)(2,1)S(1)}, u32[]{:S(2)}, u32[]{:S(2)}) collective-permute-start(bf16[2,4,8192]{2,1,0:T(4,128)(2,1)S(1)} %get-tuple-element.60), channel_id=1, source_target_pairs={{0,1},{1,0},{2,3},{3,2},{4,5},{5,4},{6,7},{7,6},{8,9},{9,8},{10,11... | collective-permute-start | bytes 393224 | tf_op jit(solution)/shard_map/ppermute | solution.py:563
  43.0 0.8 %collective-permute-start.17 = (bf16[2,4,8192]{2,1,0:T(4,128)(2,1)S(1)}, bf16[2,4,8192]{2,1,0:T(4,128)(2,1)S(1)}, u32[]{:S(2)}, u32[]{:S(2)}) collective-permute-start(bf16[2,4,8192]{2,1,0:T(4,128)(2,1)S(1)} %get-tuple-element.61), channel_id=1, source_target_pairs={{0,3},{1,2},{2,1},{3,0},{4,7},{5,6},{6,5},{7,4},{8,11},{9,10},{10,... | collective-permute-start | bytes 393224 | tf_op jit(solution)/shard_map/ppermute | solution.py:563
  43.8 0.7 %copy.9 = f32[16,4]{0,1:T(4,128)} copy(f32[16,4]{1,0:T(8,128)S(1)} %bitcast.4) | data formatting | bytes 512
  44.4 5.3 %collective-permute-done.15.rest_0_ = bf16[2,4,8192]{2,1,0:T(4,128)(2,1)S(1)} collective-permute-done((bf16[2,4,8192]{2,1,0:T(4,128)(2,1)S(1)}, bf16[2,4,8192]{2,1,0:T(4,128)(2,1)S(1)}, u32[]{:S(2)}, u32[]{:S(2)}) %collective-permute-start.15) | collective-permute-done | bytes 131104 | tf_op jit(solution)/shard_map/ppermute | solution.py:563
  49.7 1.7 %collective-permute-done.16.rest_1_ = bf16[2,4,8192]{2,1,0:T(4,128)(2,1)S(1)} collective-permute-done((bf16[2,4,8192]{2,1,0:T(4,128)(2,1)S(1)}, bf16[2,4,8192]{2,1,0:T(4,128)(2,1)S(1)}, u32[]{:S(2)}, u32[]{:S(2)}) %collective-permute-start.16) | collective-permute-done | bytes 131104 | tf_op jit(solution)/shard_map/ppermute | solution.py:563
  51.5 0.0 collective-permute-done.17.rest_2_
  51.5 0.8 %total_volume.1 = f32[2,4,1,8192]{3,2,1,0:T(1,128)} custom-call(f32[2,4,8192]{2,1,0:T(4,128)S(1)} %get-tuple-element.58.first, bf16[2,4,8192]{2,1,0:T(4,128)(2,1)S(1)} %collective-permute-done.15.rest_0_, bf16[2,4,8192]{2,1,0:T(4,128)(2,1)S(1)} %collective-permute-done.16.rest_1_, bf16[2,4,8192]{2,1,0:T(4,128)(2,1)S(1)} %collective-permute-done.17.rest_2_), custom_call_target="tpu_custom_call" | custom-call | tf_op jit(solution)/shard_map/total_volume/pallas_call | solution.py:546
  (1 shorter events, 0.0 us)
Async XLA Ops:
  0.6 13.5 %copy-start = (f32[8,256]{1,0:T(8,128)S(1)}, f32[8,256]{1,0:T(8,128)}, u32[]{:S(2)}) copy-start(f32[8,256]{1,0:T(8,128)} %constant.4.clone.table_x) | copy-start | bytes 24580
  0.6 13.5 %copy-start.1 = (f32[1024]{0:T(1024)S(1)}, f32[1024]{0:T(1024)}, u32[]{:S(2)}) copy-start(f32[1024]{0:T(1024)} %constant.5.clone.table_y) | copy-start | bytes 12292
  2.2 7.3 %collective-permute-start.1 = (bf16[2,16,8320]{2,1,0:T(8,128)(2,1)S(1)}, bf16[2,16,8320]{2,1,0:T(8,128)(2,1)S(1)}, u32[]{:S(2)}, u32[]{:S(2)}) collective-permute-start(bf16[2,16,8320]{2,1,0:T(8,128)(2,1)S(1)} %get-tuple-element.33), channel_id=1, source_target_pairs={{0,4},{4,0},{8,12},{12,8},{1,5},{5,1},{9,13},{13,9},{2,6},{6,2},{1... | collective-permute-start | bytes 1597448 | tf_op jit(solution)/shard_map/ppermute | solution.py:560
  2.7 9.6 %collective-permute-start.5 = (bf16[2,16,4224]{2,1,0:T(8,128)(2,1)S(1)}, bf16[2,16,4224]{2,1,0:T(8,128)(2,1)S(1)}, u32[]{:S(2)}, u32[]{:S(2)}) collective-permute-start(bf16[2,16,4224]{2,1,0:T(8,128)(2,1)S(1)} %get-tuple-element.46), channel_id=1, source_target_pairs={{0,8},{4,12},{8,0},{12,4},{1,9},{5,13},{9,1},{13,5},{2,10},{6,14},... | collective-permute-start | bytes 811016 | tf_op jit(solution)/shard_map/ppermute | solution.py:560
  5.2 10.6 %collective-permute-start.3 = (bf16[2,4,4,2048]{3,2,1,0:T(4,128)(2,1)S(1)}, bf16[2,4,4,2048]{3,2,1,0:T(4,128)(2,1)S(1)}, u32[]{:S(2)}, u32[]{:S(2)}) collective-permute-start(bf16[2,4,4,2048]{3,2,1,0:T(4,128)(2,1)S(1)} %get-tuple-element.34.rest_0_), channel_id=1, source_target_pairs={{0,2},{1,3},{2,0},{3,1},{4,6},{5,7},{6,4},{7,5},{8,10},{9,11},{10,... | collective-permute-start | bytes 393224 | tf_op jit(solution)/shard_map/ppermute | solution.py:563
  7.8 10.2 %collective-permute-start = (bf16[2,4,4,2048]{3,2,1,0:T(4,128)(2,1)S(1)}, bf16[2,4,4,2048]{3,2,1,0:T(4,128)(2,1)S(1)}, u32[]{:S(2)}, u32[]{:S(2)}) collective-permute-start(bf16[2,4,4,2048]{3,2,1,0:T(4,128)(2,1)S(1)} %get-tuple-element.34.rest_0_), channel_id=1, source_target_pairs={{0,1},{1,0},{2,3},{3,2},{4,5},{5,4},{6,7},{7,6},{8,9},{9,8},{10,11... | collective-permute-start | bytes 393224 | tf_op jit(solution)/shard_map/ppermute | solution.py:563
  9.4 9.1 %collective-permute-start.2 = (bf16[2,4,4,2048]{3,2,1,0:T(4,128)(2,1)S(1)}, bf16[2,4,4,2048]{3,2,1,0:T(4,128)(2,1)S(1)}, u32[]{:S(2)}, u32[]{:S(2)}) collective-permute-start(bf16[2,4,4,2048]{3,2,1,0:T(4,128)(2,1)S(1)} %get-tuple-element.34.rest_0_), channel_id=1, source_target_pairs={{0,3},{1,2},{2,1},{3,0},{4,7},{5,6},{6,5},{7,4},{8,11},{9,10},{10,... | collective-permute-start | bytes 393224 | tf_op jit(solution)/shard_map/ppermute | solution.py:563
  9.6 14.1 %collective-permute-start.7 = (bf16[2,16,8320]{2,1,0:T(8,128)(2,1)S(1)}, bf16[2,16,8320]{2,1,0:T(8,128)(2,1)S(1)}, u32[]{:S(2)}, u32[]{:S(2)}) collective-permute-start(bf16[2,16,8320]{2,1,0:T(8,128)(2,1)S(1)} %get-tuple-element.47), channel_id=1, source_target_pairs={{0,12},{4,8},{8,4},{12,0},{1,13},{5,9},{9,5},{13,1},{2,14},{6,10},... | collective-permute-start | bytes 1597448 | tf_op jit(solution)/shard_map/ppermute | solution.py:560
  12.3 11.4 %collective-permute-start.6 = (bf16[2,16,4224]{2,1,0:T(8,128)(2,1)S(1)}, bf16[2,16,4224]{2,1,0:T(8,128)(2,1)S(1)}, u32[]{:S(2)}, u32[]{:S(2)}) collective-permute-start(bf16[2,16,4224]{2,1,0:T(8,128)(2,1)S(1)} %collective-permute-done.5.rest_2_.rest_0_.rest_4_), channel_id=1, source_target_pairs={{0,16},{16,0},{1,17},{17,1},{2,18},{18,2},{3,19},{19,3},{4,20},{20... | collective-permute-start | bytes 811016 | tf_op jit(solution)/shard_map/ppermute | solution.py:576
  20.6 2.2 %collective-permute-start.4 = (f32[128,128]{1,0:T(8,128)S(1)}, f32[128,128]{1,0:T(8,128)S(1)}, u32[]{:S(2)}, u32[]{:S(2)}) collective-permute-start(f32[128,128]{1,0:T(8,128)S(1)} %get-tuple-element.42), channel_id=1, source_target_pairs={{0,4},{4,0},{8,12},{12,8},{1,5},{5,1},{9,13},{13,9},{2,6},{6,2},{1... | collective-permute-start | bytes 196616 | tf_op jit(solution)/shard_map/ppermute | solution.py:560
  20.7 7.7 %collective-permute-start.11 = (f32[128,128]{1,0:T(8,128)S(1)}, f32[128,128]{1,0:T(8,128)S(1)}, u32[]{:S(2)}, u32[]{:S(2)}) collective-permute-start(f32[128,128]{1,0:T(8,128)S(1)} %get-tuple-element.42), channel_id=1, source_target_pairs={{0,12},{4,8},{8,4},{12,0},{1,13},{5,9},{9,5},{13,1},{2,14},{6,10},... | collective-permute-start | bytes 196616 | tf_op jit(solution)/shard_map/ppermute | solution.py:560
  22.2 4.4 %collective-permute-start.9 = (f32[128,128]{1,0:T(8,128)S(1)}, f32[128,128]{1,0:T(8,128)S(1)}, u32[]{:S(2)}, u32[]{:S(2)}) collective-permute-start(f32[128,128]{1,0:T(8,128)S(1)} %get-tuple-element.40.refs_0_), channel_id=1, source_target_pairs={{0,8},{4,12},{8,0},{12,4},{1,9},{5,13},{9,1},{13,5},{2,10},{6,14},... | collective-permute-start | bytes 196616 | tf_op jit(solution)/shard_map/ppermute | solution.py:560
  26.6 4.1 %collective-permute-start.10 = (f32[128,128]{1,0:T(8,128)S(1)}, f32[128,128]{1,0:T(8,128)S(1)}, u32[]{:S(2)}, u32[]{:S(2)}) collective-permute-start(f32[128,128]{1,0:T(8,128)S(1)} %get-tuple-element.50), channel_id=1, source_target_pairs={{0,12},{4,8},{8,4},{12,0},{1,13},{5,9},{9,5},{13,1},{2,14},{6,10},... | collective-permute-start | bytes 196616 | tf_op jit(solution)/shard_map/ppermute | solution.py:560
  28.0 4.4 %collective-permute-start.8 = (f32[128,128]{1,0:T(8,128)S(1)}, f32[128,128]{1,0:T(8,128)S(1)}, u32[]{:S(2)}, u32[]{:S(2)}) collective-permute-start(f32[128,128]{1,0:T(8,128)S(1)} %get-tuple-element.48.refs_4_), channel_id=1, source_target_pairs={{0,8},{4,12},{8,0},{12,4},{1,9},{5,13},{9,1},{13,5},{2,10},{6,14},... | collective-permute-start | bytes 196616 | tf_op jit(solution)/shard_map/ppermute | solution.py:560
  28.3 4.1 %collective-permute-start.12 = (f32[128,128]{1,0:T(8,128)S(1)}, f32[128,128]{1,0:T(8,128)S(1)}, u32[]{:S(2)}, u32[]{:S(2)}) collective-permute-start(f32[128,128]{1,0:T(8,128)S(1)} %get-tuple-element.50), channel_id=1, source_target_pairs={{0,4},{4,0},{8,12},{12,8},{1,5},{5,1},{9,13},{13,9},{2,6},{6,2},{1... | collective-permute-start | bytes 196616 | tf_op jit(solution)/shard_map/ppermute | solution.py:560
  32.7 1.2 %collective-permute-start.13 = (f32[8,128]{1,0:T(8,128)S(1)}, f32[8,128]{1,0:T(8,128)S(1)}, u32[]{:S(2)}, u32[]{:S(2)}) collective-permute-start(f32[8,128]{1,0:T(8,128)S(1)} %logit_stats.1), channel_id=1, source_target_pairs={{0,4},{4,0},{8,12},{12,8},{1,5},{5,1},{9,13},{13,9},{2,6},{6,2},{1... | collective-permute-start | bytes 12296 | tf_op jit(solution)/shard_map/ppermute | solution.py:560
  33.9 3.7 %collective-permute-start.14 = (f32[16,128]{1,0:T(8,128)S(1)}, f32[16,128]{1,0:T(8,128)S(1)}, u32[]{:S(2)}, u32[]{:S(2)}) collective-permute-start(f32[16,128]{1,0:T(8,128)S(1)} %pad_maximum_fusion.rest_0_), channel_id=1, source_target_pairs={{0,16},{16,0},{1,17},{17,1},{2,18},{18,2},{3,19},{19,3},{4,20},{20... | collective-permute-start | bytes 24584 | tf_op jit(solution)/shard_map/ppermute | solution.py:617
  38.5 11.2 %collective-permute-start.15 = (bf16[2,4,8192]{2,1,0:T(4,128)(2,1)S(1)}, bf16[2,4,8192]{2,1,0:T(4,128)(2,1)S(1)}, u32[]{:S(2)}, u32[]{:S(2)}) collective-permute-start(bf16[2,4,8192]{2,1,0:T(4,128)(2,1)S(1)} %get-tuple-element.59), channel_id=1, source_target_pairs={{0,2},{1,3},{2,0},{3,1},{4,6},{5,7},{6,4},{7,5},{8,10},{9,11},{10,... | collective-permute-start | bytes 393224 | tf_op jit(solution)/shard_map/ppermute | solution.py:563
  42.3 9.2 %collective-permute-start.16 = (bf16[2,4,8192]{2,1,0:T(4,128)(2,1)S(1)}, bf16[2,4,8192]{2,1,0:T(4,128)(2,1)S(1)}, u32[]{:S(2)}, u32[]{:S(2)}) collective-permute-start(bf16[2,4,8192]{2,1,0:T(4,128)(2,1)S(1)} %get-tuple-element.60), channel_id=1, source_target_pairs={{0,1},{1,0},{2,3},{3,2},{4,5},{5,4},{6,7},{7,6},{8,9},{9,8},{10,11... | collective-permute-start | bytes 393224 | tf_op jit(solution)/shard_map/ppermute | solution.py:563
  43.0 8.5 %collective-permute-start.17 = (bf16[2,4,8192]{2,1,0:T(4,128)(2,1)S(1)}, bf16[2,4,8192]{2,1,0:T(4,128)(2,1)S(1)}, u32[]{:S(2)}, u32[]{:S(2)}) collective-permute-start(bf16[2,4,8192]{2,1,0:T(4,128)(2,1)S(1)} %get-tuple-element.61), channel_id=1, source_target_pairs={{0,3},{1,2},{2,1},{3,0},{4,7},{5,6},{6,5},{7,4},{8,11},{9,10},{10,... | collective-permute-start | bytes 393224 | tf_op jit(solution)/shard_map/ppermute | solution.py:563

commit v10 on v9

--- a/solution.py
+++ b/solution.py
@@ -591,7 +591,6 @@
         crossed_over = swap_dom(near[1], 3)
     far = list(far_logits(table_x, [right, right_late], groups[2:], 6))
     if one_phase:
-        far[1], crossed = lax.optimization_barrier((far[1], crossed))
         terms = [
             [near[0], swapped, swap_dom(far[0], 2), swap_dom(far[1], 3)],
             [far[0], swap_dom(far[1], 1), crossed, crossed_over],
@@ -608,7 +607,9 @@
                 here = {s: here[s] + there[s] for s in here}
         terms = [[here[s], there[s]] for s in sorted(here)]
     if one_phase:
-        groups[2][0][0], terms[1][3] = lax.optimization_barrier((groups[2][0][0], terms[1][3]))
+        groups[2][0][0], *terms[1][2:] = lax.optimization_barrier(
+            (groups[2][0][0], *terms[1][2:])
+        )
     aligned_far = aligned_rows(table_x, table_y, groups[2:], width)
     terms[0][-1], aligned_far = lax.optimization_barrier((terms[0][-1], aligned_far))
     stats = logit_stats(terms, classes, orients)

time: 52.4 us -> 52.1 us (level)
  transfers between devices with their start and end apart: 18 -> 18, of which waited for: 10 -> 9; matrix products, arithmetic and copies ran while one was open for 1% -> 1% of each run, Pallas kernels for 22% -> 23%
where the time goes in v10:
time: 52.1 us; the launch traced here: 51.5 us
  starting transfers between devices  20.3 us (39%)
  Pallas kernels  15.2 us (29%)
  waiting for transfers between devices  14.6 us (28%)
  between operations  0.76 us (1%)
  local copies, waits for them, and re-layouts  0.66 us (1%)
    ppermute x6, starting transfers between devices, swap_orient(): return lax.ppermute(array, 'orient', xor_pairs(orient, step))  9.12 us
    ppermute x10, starting transfers between devices, swap_dom(): return lax.ppermute(array, 'dom', xor_pairs(dom, step))  7.81 us
    ppermute x6, waiting for transfers between devices, swap_orient(): return lax.ppermute(array, 'orient', xor_pairs(orient, step))  7.41 us
    ppermute x10, waiting for transfers between devices, swap_dom(): return lax.ppermute(array, 'dom', xor_pairs(dom, step))  5.12 us
    pallas_call x2, Pallas kernels, near_logits(): pl.pallas_call(functools.partial(near_kernel, sizes_of(picked), len(shard...  4.32 us
    pallas_call x2, Pallas kernels, aligned_rows(): pl.pallas_call(functools.partial(rows_kernel, sizes_of(picked)), out_shap...  3.8 us
    pallas_call x1, Pallas kernels, far_logits(): pl.pallas_call(functools.partial(far_kernel, sizes_of(picked), [right.sha...  2.45 us
    ppermute x1, waiting for transfers between devices, local(): stats_all = [stats, lax.ppermute(stats, 'cls', xor_pairs(cls, 1))]  2.05 us
  transfers between devices with their start and end apart: 18, of which 9 were waited for; matrix products, arithmetic and copies ran while one was open for 1% of the time, Pallas kernels for 23%

profile of v10, /device:TPU:0, one launch (start us, length us, event | category | flops | bytes accessed | tf_op | source)
XLA Modules:
  0.0 51.5 jit_solution(9689353911234557624)
XLA Ops:
  0.6 0.0 copy-start
  0.6 0.0 copy-start.1
  0.7 1.5 %image_bands.1 = (bf16[2,16,8320]{2,1,0:T(8,128)(2,1)S(1)}, bf16[2,16,4224]{2,1,0:T(8,128)(2,1)S(1)}, bf16[2,16,8320]{2,1,0:T(8,128)(2,1)S(1)}, bf16[2,16,128]{2...) custom-call(bf16[2,16,32768]{2,1,0:T(8,128)(2,1)} %images.3, bf16[2,4,4,2048]{3,2,1,0:T(4,128)(2,1)} %references.1, ...), custom_call_target="tpu_custom_call" | custom-call | bytes 3145728 | tf_op jit(solution)/shard_map/image_bands/pallas_call | solution.py:109
  2.2 0.5 %collective-permute-start.1 = (bf16[2,16,8320]{2,1,0:T(8,128)(2,1)S(1)}, bf16[2,16,8320]{2,1,0:T(8,128)(2,1)S(1)}, u32[]{:S(2)}, u32[]{:S(2)}) collective-permute-start(bf16[2,16,8320]{2,1,0:T(8,128)(2,1)S(1)} %get-tuple-element.32), channel_id=1, source_target_pairs={{0,4},{4,0},{8,12},{12,8},{1,5},{5,1},{9,13},{13,9},{2,6},{6,2},{1... | collective-permute-start | bytes 1597448 | tf_op jit(solution)/shard_map/ppermute | solution.py:560
  2.7 2.6 %collective-permute-start.5 = (bf16[2,16,4224]{2,1,0:T(8,128)(2,1)S(1)}, bf16[2,16,4224]{2,1,0:T(8,128)(2,1)S(1)}, u32[]{:S(2)}, u32[]{:S(2)}) collective-permute-start(bf16[2,16,4224]{2,1,0:T(8,128)(2,1)S(1)} %get-tuple-element.45), channel_id=1, source_target_pairs={{0,8},{4,12},{8,0},{12,4},{1,9},{5,13},{9,1},{13,5},{2,10},{6,14},... | collective-permute-start | bytes 811016 | tf_op jit(solution)/shard_map/ppermute | solution.py:560
  5.2 2.6 %collective-permute-start.3 = (bf16[2,4,4,2048]{3,2,1,0:T(4,128)(2,1)S(1)}, bf16[2,4,4,2048]{3,2,1,0:T(4,128)(2,1)S(1)}, u32[]{:S(2)}, u32[]{:S(2)}) collective-permute-start(bf16[2,4,4,2048]{3,2,1,0:T(4,128)(2,1)S(1)} %get-tuple-element.33.rest_0_), channel_id=1, source_target_pairs={{0,2},{1,3},{2,0},{3,1},{4,6},{5,7},{6,4},{7,5},{8,10},{9,11},{10,... | collective-permute-start | bytes 393224 | tf_op jit(solution)/shard_map/ppermute | solution.py:563
  7.8 1.6 %collective-permute-start = (bf16[2,4,4,2048]{3,2,1,0:T(4,128)(2,1)S(1)}, bf16[2,4,4,2048]{3,2,1,0:T(4,128)(2,1)S(1)}, u32[]{:S(2)}, u32[]{:S(2)}) collective-permute-start(bf16[2,4,4,2048]{3,2,1,0:T(4,128)(2,1)S(1)} %get-tuple-element.33.rest_0_), channel_id=1, source_target_pairs={{0,1},{1,0},{2,3},{3,2},{4,5},{5,4},{6,7},{7,6},{8,9},{9,8},{10,11... | collective-permute-start | bytes 393224 | tf_op jit(solution)/shard_map/ppermute | solution.py:563
  9.4 0.0 collective-permute-done.1.rest_1_.rest_3_
  9.4 0.2 collective-permute-start.2
  9.6 0.5 collective-permute-start.7
  10.1 1.0 %own_band.1.rest_2_ = bf16[2,16,8192]{2,1,0:T(8,128)(2,1)S(1)} custom-call(bf16[2,16,32768]{2,1,0:T(8,128)(2,1)} %images.3), custom_call_target="tpu_custom_call" | custom-call | tf_op jit(solution)/shard_map/own_band/pallas_call | solution.py:155
  11.2 1.1 %collective-permute-done.5.rest_2_.rest_0_.rest_4_ = bf16[2,16,4224]{2,1,0:T(8,128)(2,1)S(1)} collective-permute-done((bf16[2,16,4224]{2,1,0:T(8,128)(2,1)S(1)}, bf16[2,16,4224]{2,1,0:T(8,128)(2,1)S(1)}, u32[]{:S(2)}, u32[]{:S(2)}) %collective-permute-start.5) | collective-permute-done | bytes 270368 | tf_op jit(solution)/shard_map/ppermute | solution.py:560
  12.3 1.8 %collective-permute-start.6 = (bf16[2,16,4224]{2,1,0:T(8,128)(2,1)S(1)}, bf16[2,16,4224]{2,1,0:T(8,128)(2,1)S(1)}, u32[]{:S(2)}, u32[]{:S(2)}) collective-permute-start(bf16[2,16,4224]{2,1,0:T(8,128)(2,1)S(1)} %collective-permute-done.5.rest_2_.rest_0_.rest_4_), channel_id=1, source_target_pairs={{0,16},{16,0},{1,17},{17,1},{2,18},{18,2},{3,19},{19,3},{4,20},{20... | collective-permute-start | bytes 811016 | tf_op jit(solution)/shard_map/ppermute | solution.py:576
  14.1 0.0 copy-done
  14.1 0.0 copy-done.1
  14.1 1.7 %aligned_rows.2.rest_6_ = bf16[2,32,8192]{2,1,0:T(8,128)(2,1)S(1)} custom-call(f32[1024]{0:T(1024)S(1)} %copy-done.1, f32[8,256]{1,0:T(8,128)S(1)} %copy-done, bf16[2,16,128]{2,1,0:T(8,128)(2,1)S(1)} %get-tuple-element.35.rest_0_.rest_2_, bf16[2,16,8320]{2,1,0:T(8,128)(2,1)S(1)} %collective-permute-done.1.rest_1_.rest_3_, ...), custom_call_target="tpu_custom_call" | custom-call | tf_op jit(solution)/shard_map/aligned_rows/pallas_call | solution.py:442
  15.8 0.0 collective-permute-done.3.rest_1_
  15.8 2.2 %near_logits.2 = (f32[128,128]{1,0:T(8,128)S(1)}, f32[128,128]{1,0:T(8,128)S(1)}, bf16[2,128,4096]{2,1,0:T(8,128)(2,1)S(1)}) custom-call(f32[1024]{0:T(1024)S(1)} %copy-done.1, f32[8,256]{1,0:T(8,128)S(1)} %copy-done, bf16[2,4,4,2048]{3,2,1,0:T(4,128)(2,1)S(1)} %get-tuple-element.33.rest_0_, bf16[2,4,4,2048]{3,2,1,0:T(4,128)(2,1)S(1)} %collective-permute-done.3.rest_1_, ...), custom_call_target="tpu_custom_call" | custom-call | tf_op jit(solution)/shard_map/near_logits/pallas_call | solution.py:314
  18.0 0.0 collective-permute-done.rest_0_
  18.0 0.5 collective-permute-done.2.rest_1_
  18.5 2.2 %near_logits.3 = (f32[128,128]{1,0:T(8,128)S(1)}, f32[128,128]{1,0:T(8,128)S(1)}, bf16[2,128,4096]{2,1,0:T(8,128)(2,1)S(1)}) custom-call(f32[1024]{0:T(1024)S(1)} %copy-done.1, f32[8,256]{1,0:T(8,128)S(1)} %copy-done, bf16[2,4,4,2048]{3,2,1,0:T(4,128)(2,1)S(1)} %collective-permute-done.rest_0_, bf16[2,4,4,2048]{3,2,1,0:T(4,128)(2,1)S(1)} %collective-permute-done.2.rest_1_, ...), custom_call_target="tpu_custom_call" | custom-call | flops 20000000000 | tf_op jit(solution)/shard_map/near_logits/pallas_call | solution.py:314
  20.6 0.1 collective-permute-start.4
  20.7 1.5 %collective-permute-start.11 = (f32[128,128]{1,0:T(8,128)S(1)}, f32[128,128]{1,0:T(8,128)S(1)}, u32[]{:S(2)}, u32[]{:S(2)}) collective-permute-start(f32[128,128]{1,0:T(8,128)S(1)} %get-tuple-element.41), channel_id=1, source_target_pairs={{0,12},{4,8},{8,4},{12,0},{1,13},{5,9},{9,5},{13,1},{2,14},{6,10},... | collective-permute-start | bytes 196616 | tf_op jit(solution)/shard_map/ppermute | solution.py:560
  22.2 0.6 %collective-permute-start.10 = (f32[128,128]{1,0:T(8,128)S(1)}, f32[128,128]{1,0:T(8,128)S(1)}, u32[]{:S(2)}, u32[]{:S(2)}) collective-permute-start(f32[128,128]{1,0:T(8,128)S(1)} %get-tuple-element.39.refs_0_), channel_id=1, source_target_pairs={{0,8},{4,12},{8,0},{12,4},{1,9},{5,13},{9,1},{13,5},{2,10},{6,14},... | collective-permute-start | bytes 196616 | tf_op jit(solution)/shard_map/ppermute | solution.py:560
  22.9 0.0 collective-permute-done.4.refs_1_
  22.9 0.9 %collective-permute-done.7.rest_4_.rest_1_.rest_5_ = bf16[2,16,8320]{2,1,0:T(8,128)(2,1)S(1)} collective-permute-done((bf16[2,16,8320]{2,1,0:T(8,128)(2,1)S(1)}, bf16[2,16,8320]{2,1,0:T(8,128)(2,1)S(1)}, u32[]{:S(2)}, u32[]{:S(2)}) %collective-permute-start.7) | collective-permute-done | bytes 532512 | tf_op jit(solution)/shard_map/ppermute | solution.py:560
  23.7 0.0 collective-permute-done.6.rest_3_
  23.7 2.5 %far_logits.1 = (f32[128,128]{1,0:T(8,128)S(1)}, f32[128,128]{1,0:T(8,128)S(1)}) custom-call(f32[8,256]{1,0:T(8,128)S(1)} %copy-done, bf16[2,128,4096]{2,1,0:T(8,128)(2,1)S(1)} %get-tuple-element.43.rest_0_, bf16[2,128,4096]{2,1,0:T(8,128)(2,1)S(1)} %get-tuple-element.44.rest_1_, bf16[2,16,4224]{2,1,0:T(8,128)(2,1)S(1)} %collective-permute-done.5.rest_2_.rest_0_.rest_4_, ...), custom_call_target="tpu_custom_call" | custom-call | flops 6000000000 | tf_op jit(solution)/shard_map/far_logits/pallas_call | solution.py:340
  26.2 1.8 %collective-permute-start.9 = (f32[128,128]{1,0:T(8,128)S(1)}, f32[128,128]{1,0:T(8,128)S(1)}, u32[]{:S(2)}, u32[]{:S(2)}) collective-permute-start(f32[128,128]{1,0:T(8,128)S(1)} %get-tuple-element.48), channel_id=1, source_target_pairs={{0,12},{4,8},{8,4},{12,0},{1,13},{5,9},{9,5},{13,1},{2,14},{6,10},... | collective-permute-start | bytes 196616 | tf_op jit(solution)/shard_map/ppermute | solution.py:560
  28.0 0.0 collective-permute-start.8
  28.0 0.2 collective-permute-start.12
  28.2 0.0 collective-permute-done.10.refs_6_
  28.2 0.0 collective-permute-done.11.refs_7_
  28.2 2.1 %aligned_rows.3.rest_7_ = bf16[2,32,8192]{2,1,0:T(8,128)(2,1)S(1)} custom-call(f32[1024]{0:T(1024)S(1)} %copy-done.1, f32[8,256]{1,0:T(8,128)S(1)} %copy-done, bf16[2,16,4224]{2,1,0:T(8,128)(2,1)S(1)} %collective-permute-done.5.rest_2_.rest_0_.rest_4_, bf16[2,16,8320]{2,1,0:T(8,128)(2,1)S(1)} %collective-permute-done.7.rest_4_.rest_1_.rest_5_, ...), custom_call_target="tpu_custom_call" | custom-call | tf_op jit(solution)/shard_map/aligned_rows/pallas_call | solution.py:442
  30.2 0.4 collective-permute-done.9.refs_3_
  30.6 1.6 %collective-permute-done.8.refs_2_ = f32[128,128]{1,0:T(8,128)S(1)} collective-permute-done((f32[128,128]{1,0:T(8,128)S(1)}, f32[128,128]{1,0:T(8,128)S(1)}, u32[]{:S(2)}, u32[]{:S(2)}) %collective-permute-start.8) | collective-permute-done | bytes 65568 | tf_op jit(solution)/shard_map/ppermute | solution.py:560
  32.2 0.0 collective-permute-done.12.refs_5_
  32.2 0.3 logit_stats.1
  32.5 0.0 collective-permute-start.13
  32.5 1.2 %collective-permute-done.13 = f32[8,128]{1,0:T(8,128)S(1)} collective-permute-done((f32[8,128]{1,0:T(8,128)S(1)}, f32[8,128]{1,0:T(8,128)S(1)}, u32[]{:S(2)}, u32[]{:S(2)}) %collective-permute-start.13) | collective-permute-done | bytes 4128 | tf_op jit(solution)/shard_map/ppermute | solution.py:560
  33.7 1.6 %collective-permute-start.14 = (f32[16,128]{1,0:T(8,128)S(1)}, f32[16,128]{1,0:T(8,128)S(1)}, u32[]{:S(2)}, u32[]{:S(2)}) collective-permute-start(f32[16,128]{1,0:T(8,128)S(1)} %pad_maximum_fusion.rest_0_), channel_id=1, source_target_pairs={{0,16},{16,0},{1,17},{17,1},{2,18},{18,2},{3,19},{19,3},{4,20},{20... | collective-permute-start | bytes 24584 | tf_op jit(solution)/shard_map/ppermute | solution.py:618
  35.3 2.1 %collective-permute-done.14.rest_1_ = f32[16,128]{1,0:T(8,128)S(1)} collective-permute-done((f32[16,128]{1,0:T(8,128)S(1)}, f32[16,128]{1,0:T(8,128)S(1)}, u32[]{:S(2)}, u32[]{:S(2)}) %collective-permute-start.14) | collective-permute-done | bytes 8224 | tf_op jit(solution)/shard_map/ppermute | solution.py:618
  37.3 1.0 %volume_terms.1 = (f32[16,128]{1,0:T(8,128)S(1)}, f32[2,4,8192]{2,1,0:T(4,128)S(1)}, bf16[2,4,8192]{2,1,0:T(4,128)(2,1)S(1)}, bf16[2,4,8192]{2,1,0:T(4,128)(2,1)S(1)}, bf16[2,4,8192]{2,1,0:T(4,128)(2,1)S(1)}) custom-call(f32[16,128]{1,0:T(8,128)S(1)} %pad_maximum_fusion.rest_0_, f32[16,128]{1,0:T(8,128)S(1)} %collective-permute-done.14.rest_1_, ...), custom_call_target="tpu_custom_call" | custom-call | flops 33554432 | bytes 2621440 | tf_op jit(solution)/shard_map/volume_terms/pallas_call | solution.py:517
  38.4 3.2 %collective-permute-start.15 = (bf16[2,4,8192]{2,1,0:T(4,128)(2,1)S(1)}, bf16[2,4,8192]{2,1,0:T(4,128)(2,1)S(1)}, u32[]{:S(2)}, u32[]{:S(2)}) collective-permute-start(bf16[2,4,8192]{2,1,0:T(4,128)(2,1)S(1)} %get-tuple-element.57), channel_id=1, source_target_pairs={{0,2},{1,3},{2,0},{3,1},{4,6},{5,7},{6,4},{7,5},{8,10},{9,11},{10,... | collective-permute-start | bytes 393224 | tf_op jit(solution)/shard_map/ppermute | solution.py:563
  41.6 1.1 %collective-permute-start.16 = (bf16[2,4,8192]{2,1,0:T(4,128)(2,1)S(1)}, bf16[2,4,8192]{2,1,0:T(4,128)(2,1)S(1)}, u32[]{:S(2)}, u32[]{:S(2)}) collective-permute-start(bf16[2,4,8192]{2,1,0:T(4,128)(2,1)S(1)} %get-tuple-element.58), channel_id=1, source_target_pairs={{0,1},{1,0},{2,3},{3,2},{4,5},{5,4},{6,7},{7,6},{8,9},{9,8},{10,11... | collective-permute-start | bytes 393224 | tf_op jit(solution)/shard_map/ppermute | solution.py:563
  42.7 0.4 collective-permute-start.17
  43.1 0.7 %copy.9 = f32[16,4]{0,1:T(4,128)} copy(f32[16,4]{1,0:T(8,128)S(1)} %bitcast.4) | data formatting | bytes 512
  43.7 6.8 %collective-permute-done.15.rest_0_ = bf16[2,4,8192]{2,1,0:T(4,128)(2,1)S(1)} collective-permute-done((bf16[2,4,8192]{2,1,0:T(4,128)(2,1)S(1)}, bf16[2,4,8192]{2,1,0:T(4,128)(2,1)S(1)}, u32[]{:S(2)}, u32[]{:S(2)}) %collective-permute-start.15) | collective-permute-done | bytes 131104 | tf_op jit(solution)/shard_map/ppermute | solution.py:563
  50.6 0.1 collective-permute-done.16.rest_1_
  50.7 0.0 collective-permute-done.17.rest_2_
  50.7 0.8 %total_volume.1 = f32[2,4,1,8192]{3,2,1,0:T(1,128)} custom-call(f32[2,4,8192]{2,1,0:T(4,128)S(1)} %get-tuple-element.56.first, bf16[2,4,8192]{2,1,0:T(4,128)(2,1)S(1)} %collective-permute-done.15.rest_0_, bf16[2,4,8192]{2,1,0:T(4,128)(2,1)S(1)} %collective-permute-done.16.rest_1_, bf16[2,4,8192]{2,1,0:T(4,128)(2,1)S(1)} %collective-permute-done.17.rest_2_), custom_call_target="tpu_custom_call" | custom-call | tf_op jit(solution)/shard_map/total_volume/pallas_call | solution.py:546
  (1 shorter events, 0.0 us)
Async XLA Ops:
  0.6 13.5 %copy-start = (f32[8,256]{1,0:T(8,128)S(1)}, f32[8,256]{1,0:T(8,128)}, u32[]{:S(2)}) copy-start(f32[8,256]{1,0:T(8,128)} %constant.4.clone.table_x) | copy-start | bytes 24580
  0.6 13.5 %copy-start.1 = (f32[1024]{0:T(1024)S(1)}, f32[1024]{0:T(1024)}, u32[]{:S(2)}) copy-start(f32[1024]{0:T(1024)} %constant.5.clone.table_y) | copy-start | bytes 12292
  2.2 7.3 %collective-permute-start.1 = (bf16[2,16,8320]{2,1,0:T(8,128)(2,1)S(1)}, bf16[2,16,8320]{2,1,0:T(8,128)(2,1)S(1)}, u32[]{:S(2)}, u32[]{:S(2)}) collective-permute-start(bf16[2,16,8320]{2,1,0:T(8,128)(2,1)S(1)} %get-tuple-element.32), channel_id=1, source_target_pairs={{0,4},{4,0},{8,12},{12,8},{1,5},{5,1},{9,13},{13,9},{2,6},{6,2},{1... | collective-permute-start | bytes 1597448 | tf_op jit(solution)/shard_map/ppermute | solution.py:560
  2.7 9.6 %collective-permute-start.5 = (bf16[2,16,4224]{2,1,0:T(8,128)(2,1)S(1)}, bf16[2,16,4224]{2,1,0:T(8,128)(2,1)S(1)}, u32[]{:S(2)}, u32[]{:S(2)}) collective-permute-start(bf16[2,16,4224]{2,1,0:T(8,128)(2,1)S(1)} %get-tuple-element.45), channel_id=1, source_target_pairs={{0,8},{4,12},{8,0},{12,4},{1,9},{5,13},{9,1},{13,5},{2,10},{6,14},... | collective-permute-start | bytes 811016 | tf_op jit(solution)/shard_map/ppermute | solution.py:560
  5.2 10.6 %collective-permute-start.3 = (bf16[2,4,4,2048]{3,2,1,0:T(4,128)(2,1)S(1)}, bf16[2,4,4,2048]{3,2,1,0:T(4,128)(2,1)S(1)}, u32[]{:S(2)}, u32[]{:S(2)}) collective-permute-start(bf16[2,4,4,2048]{3,2,1,0:T(4,128)(2,1)S(1)} %get-tuple-element.33.rest_0_), channel_id=1, source_target_pairs={{0,2},{1,3},{2,0},{3,1},{4,6},{5,7},{6,4},{7,5},{8,10},{9,11},{10,... | collective-permute-start | bytes 393224 | tf_op jit(solution)/shard_map/ppermute | solution.py:563
  7.8 10.2 %collective-permute-start = (bf16[2,4,4,2048]{3,2,1,0:T(4,128)(2,1)S(1)}, bf16[2,4,4,2048]{3,2,1,0:T(4,128)(2,1)S(1)}, u32[]{:S(2)}, u32[]{:S(2)}) collective-permute-start(bf16[2,4,4,2048]{3,2,1,0:T(4,128)(2,1)S(1)} %get-tuple-element.33.rest_0_), channel_id=1, source_target_pairs={{0,1},{1,0},{2,3},{3,2},{4,5},{5,4},{6,7},{7,6},{8,9},{9,8},{10,11... | collective-permute-start | bytes 393224 | tf_op jit(solution)/shard_map/ppermute | solution.py:563
  9.4 9.1 %collective-permute-start.2 = (bf16[2,4,4,2048]{3,2,1,0:T(4,128)(2,1)S(1)}, bf16[2,4,4,2048]{3,2,1,0:T(4,128)(2,1)S(1)}, u32[]{:S(2)}, u32[]{:S(2)}) collective-permute-start(bf16[2,4,4,2048]{3,2,1,0:T(4,128)(2,1)S(1)} %get-tuple-element.33.rest_0_), channel_id=1, source_target_pairs={{0,3},{1,2},{2,1},{3,0},{4,7},{5,6},{6,5},{7,4},{8,11},{9,10},{10,... | collective-permute-start | bytes 393224 | tf_op jit(solution)/shard_map/ppermute | solution.py:563
  9.6 14.1 %collective-permute-start.7 = (bf16[2,16,8320]{2,1,0:T(8,128)(2,1)S(1)}, bf16[2,16,8320]{2,1,0:T(8,128)(2,1)S(1)}, u32[]{:S(2)}, u32[]{:S(2)}) collective-permute-start(bf16[2,16,8320]{2,1,0:T(8,128)(2,1)S(1)} %get-tuple-element.46), channel_id=1, source_target_pairs={{0,12},{4,8},{8,4},{12,0},{1,13},{5,9},{9,5},{13,1},{2,14},{6,10},... | collective-permute-start | bytes 1597448 | tf_op jit(solution)/shard_map/ppermute | solution.py:560
  12.3 11.4 %collective-permute-start.6 = (bf16[2,16,4224]{2,1,0:T(8,128)(2,1)S(1)}, bf16[2,16,4224]{2,1,0:T(8,128)(2,1)S(1)}, u32[]{:S(2)}, u32[]{:S(2)}) collective-permute-start(bf16[2,16,4224]{2,1,0:T(8,128)(2,1)S(1)} %collective-permute-done.5.rest_2_.rest_0_.rest_4_), channel_id=1, source_target_pairs={{0,16},{16,0},{1,17},{17,1},{2,18},{18,2},{3,19},{19,3},{4,20},{20... | collective-permute-start | bytes 811016 | tf_op jit(solution)/shard_map/ppermute | solution.py:576
  20.6 2.2 %collective-permute-start.4 = (f32[128,128]{1,0:T(8,128)S(1)}, f32[128,128]{1,0:T(8,128)S(1)}, u32[]{:S(2)}, u32[]{:S(2)}) collective-permute-start(f32[128,128]{1,0:T(8,128)S(1)} %get-tuple-element.41), channel_id=1, source_target_pairs={{0,4},{4,0},{8,12},{12,8},{1,5},{5,1},{9,13},{13,9},{2,6},{6,2},{1... | collective-permute-start | bytes 196616 | tf_op jit(solution)/shard_map/ppermute | solution.py:560
  20.7 7.5 %collective-permute-start.11 = (f32[128,128]{1,0:T(8,128)S(1)}, f32[128,128]{1,0:T(8,128)S(1)}, u32[]{:S(2)}, u32[]{:S(2)}) collective-permute-start(f32[128,128]{1,0:T(8,128)S(1)} %get-tuple-element.41), channel_id=1, source_target_pairs={{0,12},{4,8},{8,4},{12,0},{1,13},{5,9},{9,5},{13,1},{2,14},{6,10},... | collective-permute-start | bytes 196616 | tf_op jit(solution)/shard_map/ppermute | solution.py:560
  22.2 5.9 %collective-permute-start.10 = (f32[128,128]{1,0:T(8,128)S(1)}, f32[128,128]{1,0:T(8,128)S(1)}, u32[]{:S(2)}, u32[]{:S(2)}) collective-permute-start(f32[128,128]{1,0:T(8,128)S(1)} %get-tuple-element.39.refs_0_), channel_id=1, source_target_pairs={{0,8},{4,12},{8,0},{12,4},{1,9},{5,13},{9,1},{13,5},{2,10},{6,14},... | collective-permute-start | bytes 196616 | tf_op jit(solution)/shard_map/ppermute | solution.py:560
  26.2 4.4 %collective-permute-start.9 = (f32[128,128]{1,0:T(8,128)S(1)}, f32[128,128]{1,0:T(8,128)S(1)}, u32[]{:S(2)}, u32[]{:S(2)}) collective-permute-start(f32[128,128]{1,0:T(8,128)S(1)} %get-tuple-element.48), channel_id=1, source_target_pairs={{0,12},{4,8},{8,4},{12,0},{1,13},{5,9},{9,5},{13,1},{2,14},{6,10},... | collective-permute-start | bytes 196616 | tf_op jit(solution)/shard_map/ppermute | solution.py:560
  28.0 4.3 %collective-permute-start.8 = (f32[128,128]{1,0:T(8,128)S(1)}, f32[128,128]{1,0:T(8,128)S(1)}, u32[]{:S(2)}, u32[]{:S(2)}) collective-permute-start(f32[128,128]{1,0:T(8,128)S(1)} %get-tuple-element.47.refs_4_), channel_id=1, source_target_pairs={{0,8},{4,12},{8,0},{12,4},{1,9},{5,13},{9,1},{13,5},{2,10},{6,14},... | collective-permute-start | bytes 196616 | tf_op jit(solution)/shard_map/ppermute | solution.py:560
  28.0 4.3 %collective-permute-start.12 = (f32[128,128]{1,0:T(8,128)S(1)}, f32[128,128]{1,0:T(8,128)S(1)}, u32[]{:S(2)}, u32[]{:S(2)}) collective-permute-start(f32[128,128]{1,0:T(8,128)S(1)} %get-tuple-element.48), channel_id=1, source_target_pairs={{0,4},{4,0},{8,12},{12,8},{1,5},{5,1},{9,13},{13,9},{2,6},{6,2},{1... | collective-permute-start | bytes 196616 | tf_op jit(solution)/shard_map/ppermute | solution.py:560
  32.5 1.2 %collective-permute-start.13 = (f32[8,128]{1,0:T(8,128)S(1)}, f32[8,128]{1,0:T(8,128)S(1)}, u32[]{:S(2)}, u32[]{:S(2)}) collective-permute-start(f32[8,128]{1,0:T(8,128)S(1)} %logit_stats.1), channel_id=1, source_target_pairs={{0,4},{4,0},{8,12},{12,8},{1,5},{5,1},{9,13},{13,9},{2,6},{6,2},{1... | collective-permute-start | bytes 12296 | tf_op jit(solution)/shard_map/ppermute | solution.py:560
  33.7 3.7 %collective-permute-start.14 = (f32[16,128]{1,0:T(8,128)S(1)}, f32[16,128]{1,0:T(8,128)S(1)}, u32[]{:S(2)}, u32[]{:S(2)}) collective-permute-start(f32[16,128]{1,0:T(8,128)S(1)} %pad_maximum_fusion.rest_0_), channel_id=1, source_target_pairs={{0,16},{16,0},{1,17},{17,1},{2,18},{18,2},{3,19},{19,3},{4,20},{20... | collective-permute-start | bytes 24584 | tf_op jit(solution)/shard_map/ppermute | solution.py:618
  38.4 12.2 %collective-permute-start.15 = (bf16[2,4,8192]{2,1,0:T(4,128)(2,1)S(1)}, bf16[2,4,8192]{2,1,0:T(4,128)(2,1)S(1)}, u32[]{:S(2)}, u32[]{:S(2)}) collective-permute-start(bf16[2,4,8192]{2,1,0:T(4,128)(2,1)S(1)} %get-tuple-element.57), channel_id=1, source_target_pairs={{0,2},{1,3},{2,0},{3,1},{4,6},{5,7},{6,4},{7,5},{8,10},{9,11},{10,... | collective-permute-start | bytes 393224 | tf_op jit(solution)/shard_map/ppermute | solution.py:563
  41.6 9.1 %collective-permute-start.16 = (bf16[2,4,8192]{2,1,0:T(4,128)(2,1)S(1)}, bf16[2,4,8192]{2,1,0:T(4,128)(2,1)S(1)}, u32[]{:S(2)}, u32[]{:S(2)}) collective-permute-start(bf16[2,4,8192]{2,1,0:T(4,128)(2,1)S(1)} %get-tuple-element.58), channel_id=1, source_target_pairs={{0,1},{1,0},{2,3},{3,2},{4,5},{5,4},{6,7},{7,6},{8,9},{9,8},{10,11... | collective-permute-start | bytes 393224 | tf_op jit(solution)/shard_map/ppermute | solution.py:563
  42.7 8.0 %collective-permute-start.17 = (bf16[2,4,8192]{2,1,0:T(4,128)(2,1)S(1)}, bf16[2,4,8192]{2,1,0:T(4,128)(2,1)S(1)}, u32[]{:S(2)}, u32[]{:S(2)}) collective-permute-start(bf16[2,4,8192]{2,1,0:T(4,128)(2,1)S(1)} %get-tuple-element.59), channel_id=1, source_target_pairs={{0,3},{1,2},{2,1},{3,0},{4,7},{5,6},{6,5},{7,4},{8,11},{9,10},{10,... | collective-permute-start | bytes 393224 | tf_op jit(solution)/shard_map/ppermute | solution.py:563

commit v11 on v10

--- a/solution.py
+++ b/solution.py
@@ -531,13 +531,18 @@
 
 
 def total_kernel(first, *rest):
-    out = rest[-1]
-    total = first[...]
-    for term in rest[:-1]:
-        total = total + term[...].astype(F32)
-    for part in range(out.shape[0]):
-        for k in range(out.shape[1]):
-            out[part, k] = total[part, k : k + 1]
+    terms, (out, held, sems) = rest[:-3], rest[-3:]
+    copies = []
+    for part in range(held.shape[0]):
+        total = first[part]
+        for term in terms:
+            total = total + term[part].astype(F32)
+        for k in range(held.shape[1]):
+            held[part, k] = total[k : k + 1]
+        copies.append(pltpu.make_async_copy(held.at[part], out.at[part], sems.at[part]))
+        copies[-1].start()
+    for copy in copies:
+        copy.wait()
 
 
 def total_volume(terms):
@@ -547,6 +552,11 @@
         total_kernel,
         out_shape=jax.ShapeDtypeStruct((parts, classes, 1, width), F32),
         in_specs=specs,
+        out_specs=pl.BlockSpec(memory_space=pl.ANY),
+        scratch_shapes=[
+            pltpu.VMEM((parts, classes, 1, width), F32),
+            pltpu.SemaphoreType.DMA((parts,)),
+        ],
         compiler_params=pltpu.CompilerParams(vmem_limit_bytes=VMEM_BYTES),
         name="total_volume",
     )(*arrays)

time: 52.1 us -> 52 us (level)
  no operation moved by 1% of the time
where the time goes in v11:
time: 52 us; the launch traced here: 51.5 us
  starting transfers between devices  20.3 us (39%)
  Pallas kernels  15.1 us (29%)
  waiting for transfers between devices  14.6 us (28%)
  between operations  0.76 us (1%)
  local copies, waits for them, and re-layouts  0.66 us (1%)
    ppermute x6, starting transfers between devices, swap_orient(): return lax.ppermute(array, 'orient', xor_pairs(orient, step))  9.12 us
    ppermute x10, starting transfers between devices, swap_dom(): return lax.ppermute(array, 'dom', xor_pairs(dom, step))  7.81 us
    ppermute x6, waiting for transfers between devices, swap_orient(): return lax.ppermute(array, 'orient', xor_pairs(orient, step))  7.41 us
    ppermute x10, waiting for transfers between devices, swap_dom(): return lax.ppermute(array, 'dom', xor_pairs(dom, step))  5.12 us
    pallas_call x2, Pallas kernels, near_logits(): pl.pallas_call(functools.partial(near_kernel, sizes_of(picked), len(shard...  4.32 us
    pallas_call x2, Pallas kernels, aligned_rows(): pl.pallas_call(functools.partial(rows_kernel, sizes_of(picked)), out_shap...  3.8 us
    pallas_call x1, Pallas kernels, far_logits(): pl.pallas_call(functools.partial(far_kernel, sizes_of(picked), [right.sha...  2.45 us
    ppermute x1, waiting for transfers between devices, local(): stats_all = [stats, lax.ppermute(stats, 'cls', xor_pairs(cls, 1))]  2.05 us
  transfers between devices with their start and end apart: 18, of which 9 were waited for; matrix products, arithmetic and copies ran while one was open for 1% of the time, Pallas kernels for 23%

profile of v11, /device:TPU:0, one launch (start us, length us, event | category | flops | bytes accessed | tf_op | source)
XLA Modules:
  0.0 51.5 jit_solution(6480256117205076073)
XLA Ops:
  0.6 0.0 copy-start
  0.6 0.0 copy-start.1
  0.7 1.5 %image_bands.1 = (bf16[2,16,8320]{2,1,0:T(8,128)(2,1)S(1)}, bf16[2,16,4224]{2,1,0:T(8,128)(2,1)S(1)}, bf16[2,16,8320]{2,1,0:T(8,128)(2,1)S(1)}, bf16[2,16,128]{2...) custom-call(bf16[2,16,32768]{2,1,0:T(8,128)(2,1)} %images.3, bf16[2,4,4,2048]{3,2,1,0:T(4,128)(2,1)} %references.1, ...), custom_call_target="tpu_custom_call" | custom-call | bytes 3145728 | tf_op jit(solution)/shard_map/image_bands/pallas_call | solution.py:109
  2.2 0.5 %collective-permute-start.1 = (bf16[2,16,8320]{2,1,0:T(8,128)(2,1)S(1)}, bf16[2,16,8320]{2,1,0:T(8,128)(2,1)S(1)}, u32[]{:S(2)}, u32[]{:S(2)}) collective-permute-start(bf16[2,16,8320]{2,1,0:T(8,128)(2,1)S(1)} %get-tuple-element.32), channel_id=1, source_target_pairs={{0,4},{4,0},{8,12},{12,8},{1,5},{5,1},{9,13},{13,9},{2,6},{6,2},{1... | collective-permute-start | bytes 1597448 | tf_op jit(solution)/shard_map/ppermute | solution.py:570
  2.7 2.6 %collective-permute-start.5 = (bf16[2,16,4224]{2,1,0:T(8,128)(2,1)S(1)}, bf16[2,16,4224]{2,1,0:T(8,128)(2,1)S(1)}, u32[]{:S(2)}, u32[]{:S(2)}) collective-permute-start(bf16[2,16,4224]{2,1,0:T(8,128)(2,1)S(1)} %get-tuple-element.45), channel_id=1, source_target_pairs={{0,8},{4,12},{8,0},{12,4},{1,9},{5,13},{9,1},{13,5},{2,10},{6,14},... | collective-permute-start | bytes 811016 | tf_op jit(solution)/shard_map/ppermute | solution.py:570
  5.2 2.6 %collective-permute-start.3 = (bf16[2,4,4,2048]{3,2,1,0:T(4,128)(2,1)S(1)}, bf16[2,4,4,2048]{3,2,1,0:T(4,128)(2,1)S(1)}, u32[]{:S(2)}, u32[]{:S(2)}) collective-permute-start(bf16[2,4,4,2048]{3,2,1,0:T(4,128)(2,1)S(1)} %get-tuple-element.33.rest_0_), channel_id=1, source_target_pairs={{0,2},{1,3},{2,0},{3,1},{4,6},{5,7},{6,4},{7,5},{8,10},{9,11},{10,... | collective-permute-start | bytes 393224 | tf_op jit(solution)/shard_map/ppermute | solution.py:573
  7.8 1.6 %collective-permute-start = (bf16[2,4,4,2048]{3,2,1,0:T(4,128)(2,1)S(1)}, bf16[2,4,4,2048]{3,2,1,0:T(4,128)(2,1)S(1)}, u32[]{:S(2)}, u32[]{:S(2)}) collective-permute-start(bf16[2,4,4,2048]{3,2,1,0:T(4,128)(2,1)S(1)} %get-tuple-element.33.rest_0_), channel_id=1, source_target_pairs={{0,1},{1,0},{2,3},{3,2},{4,5},{5,4},{6,7},{7,6},{8,9},{9,8},{10,11... | collective-permute-start | bytes 393224 | tf_op jit(solution)/shard_map/ppermute | solution.py:573
  9.4 0.0 collective-permute-done.1.rest_1_.rest_3_
  9.4 0.2 collective-permute-start.2
  9.6 0.5 %collective-permute-start.7 = (bf16[2,16,8320]{2,1,0:T(8,128)(2,1)S(1)}, bf16[2,16,8320]{2,1,0:T(8,128)(2,1)S(1)}, u32[]{:S(2)}, u32[]{:S(2)}) collective-permute-start(bf16[2,16,8320]{2,1,0:T(8,128)(2,1)S(1)} %get-tuple-element.46), channel_id=1, source_target_pairs={{0,12},{4,8},{8,4},{12,0},{1,13},{5,9},{9,5},{13,1},{2,14},{6,10},... | collective-permute-start | bytes 1597448 | tf_op jit(solution)/shard_map/ppermute | solution.py:570
  10.1 1.0 %own_band.1.rest_2_ = bf16[2,16,8192]{2,1,0:T(8,128)(2,1)S(1)} custom-call(bf16[2,16,32768]{2,1,0:T(8,128)(2,1)} %images.3), custom_call_target="tpu_custom_call" | custom-call | tf_op jit(solution)/shard_map/own_band/pallas_call | solution.py:155
  11.2 1.1 %collective-permute-done.5.rest_2_.rest_0_.rest_4_ = bf16[2,16,4224]{2,1,0:T(8,128)(2,1)S(1)} collective-permute-done((bf16[2,16,4224]{2,1,0:T(8,128)(2,1)S(1)}, bf16[2,16,4224]{2,1,0:T(8,128)(2,1)S(1)}, u32[]{:S(2)}, u32[]{:S(2)}) %collective-permute-start.5) | collective-permute-done | bytes 270368 | tf_op jit(solution)/shard_map/ppermute | solution.py:570
  12.3 1.8 %collective-permute-start.6 = (bf16[2,16,4224]{2,1,0:T(8,128)(2,1)S(1)}, bf16[2,16,4224]{2,1,0:T(8,128)(2,1)S(1)}, u32[]{:S(2)}, u32[]{:S(2)}) collective-permute-start(bf16[2,16,4224]{2,1,0:T(8,128)(2,1)S(1)} %collective-permute-done.5.rest_2_.rest_0_.rest_4_), channel_id=1, source_target_pairs={{0,16},{16,0},{1,17},{17,1},{2,18},{18,2},{3,19},{19,3},{4,20},{20... | collective-permute-start | bytes 811016 | tf_op jit(solution)/shard_map/ppermute | solution.py:586
  14.1 0.0 copy-done
  14.1 0.0 copy-done.1
  14.1 1.7 %aligned_rows.2.rest_6_ = bf16[2,32,8192]{2,1,0:T(8,128)(2,1)S(1)} custom-call(f32[1024]{0:T(1024)S(1)} %copy-done.1, f32[8,256]{1,0:T(8,128)S(1)} %copy-done, bf16[2,16,128]{2,1,0:T(8,128)(2,1)S(1)} %get-tuple-element.35.rest_0_.rest_2_, bf16[2,16,8320]{2,1,0:T(8,128)(2,1)S(1)} %collective-permute-done.1.rest_1_.rest_3_, ...), custom_call_target="tpu_custom_call" | custom-call | tf_op jit(solution)/shard_map/aligned_rows/pallas_call | solution.py:442
  15.8 0.0 collective-permute-done.3.rest_1_
  15.8 2.2 %near_logits.2 = (f32[128,128]{1,0:T(8,128)S(1)}, f32[128,128]{1,0:T(8,128)S(1)}, bf16[2,128,4096]{2,1,0:T(8,128)(2,1)S(1)}) custom-call(f32[1024]{0:T(1024)S(1)} %copy-done.1, f32[8,256]{1,0:T(8,128)S(1)} %copy-done, bf16[2,4,4,2048]{3,2,1,0:T(4,128)(2,1)S(1)} %get-tuple-element.33.rest_0_, bf16[2,4,4,2048]{3,2,1,0:T(4,128)(2,1)S(1)} %collective-permute-done.3.rest_1_, ...), custom_call_target="tpu_custom_call" | custom-call | tf_op jit(solution)/shard_map/near_logits/pallas_call | solution.py:314
  18.0 0.0 collective-permute-done.rest_0_
  18.0 0.5 collective-permute-done.2.rest_1_
  18.5 2.2 %near_logits.3 = (f32[128,128]{1,0:T(8,128)S(1)}, f32[128,128]{1,0:T(8,128)S(1)}, bf16[2,128,4096]{2,1,0:T(8,128)(2,1)S(1)}) custom-call(f32[1024]{0:T(1024)S(1)} %copy-done.1, f32[8,256]{1,0:T(8,128)S(1)} %copy-done, bf16[2,4,4,2048]{3,2,1,0:T(4,128)(2,1)S(1)} %collective-permute-done.rest_0_, bf16[2,4,4,2048]{3,2,1,0:T(4,128)(2,1)S(1)} %collective-permute-done.2.rest_1_, ...), custom_call_target="tpu_custom_call" | custom-call | flops 20000000000 | tf_op jit(solution)/shard_map/near_logits/pallas_call | solution.py:314
  20.6 0.1 collective-permute-start.4
  20.7 1.5 %collective-permute-start.11 = (f32[128,128]{1,0:T(8,128)S(1)}, f32[128,128]{1,0:T(8,128)S(1)}, u32[]{:S(2)}, u32[]{:S(2)}) collective-permute-start(f32[128,128]{1,0:T(8,128)S(1)} %get-tuple-element.41), channel_id=1, source_target_pairs={{0,12},{4,8},{8,4},{12,0},{1,13},{5,9},{9,5},{13,1},{2,14},{6,10},... | collective-permute-start | bytes 196616 | tf_op jit(solution)/shard_map/ppermute | solution.py:570
  22.2 0.6 %collective-permute-start.10 = (f32[128,128]{1,0:T(8,128)S(1)}, f32[128,128]{1,0:T(8,128)S(1)}, u32[]{:S(2)}, u32[]{:S(2)}) collective-permute-start(f32[128,128]{1,0:T(8,128)S(1)} %get-tuple-element.39.refs_0_), channel_id=1, source_target_pairs={{0,8},{4,12},{8,0},{12,4},{1,9},{5,13},{9,1},{13,5},{2,10},{6,14},... | collective-permute-start | bytes 196616 | tf_op jit(solution)/shard_map/ppermute | solution.py:570
  22.9 0.0 collective-permute-done.4.refs_1_
  22.9 0.9 %collective-permute-done.7.rest_4_.rest_1_.rest_5_ = bf16[2,16,8320]{2,1,0:T(8,128)(2,1)S(1)} collective-permute-done((bf16[2,16,8320]{2,1,0:T(8,128)(2,1)S(1)}, bf16[2,16,8320]{2,1,0:T(8,128)(2,1)S(1)}, u32[]{:S(2)}, u32[]{:S(2)}) %collective-permute-start.7) | collective-permute-done | bytes 532512 | tf_op jit(solution)/shard_map/ppermute | solution.py:570
  23.7 0.0 collective-permute-done.6.rest_3_
  23.7 2.5 %far_logits.1 = (f32[128,128]{1,0:T(8,128)S(1)}, f32[128,128]{1,0:T(8,128)S(1)}) custom-call(f32[8,256]{1,0:T(8,128)S(1)} %copy-done, bf16[2,128,4096]{2,1,0:T(8,128)(2,1)S(1)} %get-tuple-element.43.rest_0_, bf16[2,128,4096]{2,1,0:T(8,128)(2,1)S(1)} %get-tuple-element.44.rest_1_, bf16[2,16,4224]{2,1,0:T(8,128)(2,1)S(1)} %collective-permute-done.5.rest_2_.rest_0_.rest_4_, ...), custom_call_target="tpu_custom_call" | custom-call | flops 6000000000 | tf_op jit(solution)/shard_map/far_logits/pallas_call | solution.py:340
  26.2 1.8 %collective-permute-start.9 = (f32[128,128]{1,0:T(8,128)S(1)}, f32[128,128]{1,0:T(8,128)S(1)}, u32[]{:S(2)}, u32[]{:S(2)}) collective-permute-start(f32[128,128]{1,0:T(8,128)S(1)} %get-tuple-element.48), channel_id=1, source_target_pairs={{0,12},{4,8},{8,4},{12,0},{1,13},{5,9},{9,5},{13,1},{2,14},{6,10},... | collective-permute-start | bytes 196616 | tf_op jit(solution)/shard_map/ppermute | solution.py:570
  28.0 0.0 collective-permute-start.8
  28.0 0.2 collective-permute-start.12
  28.2 0.0 collective-permute-done.10.refs_6_
  28.2 0.0 collective-permute-done.11.refs_7_
  28.2 2.1 %aligned_rows.3.rest_7_ = bf16[2,32,8192]{2,1,0:T(8,128)(2,1)S(1)} custom-call(f32[1024]{0:T(1024)S(1)} %copy-done.1, f32[8,256]{1,0:T(8,128)S(1)} %copy-done, bf16[2,16,4224]{2,1,0:T(8,128)(2,1)S(1)} %collective-permute-done.5.rest_2_.rest_0_.rest_4_, bf16[2,16,8320]{2,1,0:T(8,128)(2,1)S(1)} %collective-permute-done.7.rest_4_.rest_1_.rest_5_, ...), custom_call_target="tpu_custom_call" | custom-call | tf_op jit(solution)/shard_map/aligned_rows/pallas_call | solution.py:442
  30.2 0.4 collective-permute-done.9.refs_3_
  30.6 1.6 %collective-permute-done.8.refs_2_ = f32[128,128]{1,0:T(8,128)S(1)} collective-permute-done((f32[128,128]{1,0:T(8,128)S(1)}, f32[128,128]{1,0:T(8,128)S(1)}, u32[]{:S(2)}, u32[]{:S(2)}) %collective-permute-start.8) | collective-permute-done | bytes 65568 | tf_op jit(solution)/shard_map/ppermute | solution.py:570
  32.2 0.0 collective-permute-done.12.refs_5_
  32.2 0.3 logit_stats.1
  32.5 0.0 collective-permute-start.13
  32.5 1.2 %collective-permute-done.13 = f32[8,128]{1,0:T(8,128)S(1)} collective-permute-done((f32[8,128]{1,0:T(8,128)S(1)}, f32[8,128]{1,0:T(8,128)S(1)}, u32[]{:S(2)}, u32[]{:S(2)}) %collective-permute-start.13) | collective-permute-done | bytes 4128 | tf_op jit(solution)/shard_map/ppermute | solution.py:570
  33.7 1.6 %collective-permute-start.14 = (f32[16,128]{1,0:T(8,128)S(1)}, f32[16,128]{1,0:T(8,128)S(1)}, u32[]{:S(2)}, u32[]{:S(2)}) collective-permute-start(f32[16,128]{1,0:T(8,128)S(1)} %pad_maximum_fusion.rest_0_), channel_id=1, source_target_pairs={{0,16},{16,0},{1,17},{17,1},{2,18},{18,2},{3,19},{19,3},{4,20},{20... | collective-permute-start | bytes 24584 | tf_op jit(solution)/shard_map/ppermute | solution.py:628
  35.3 2.1 %collective-permute-done.14.rest_1_ = f32[16,128]{1,0:T(8,128)S(1)} collective-permute-done((f32[16,128]{1,0:T(8,128)S(1)}, f32[16,128]{1,0:T(8,128)S(1)}, u32[]{:S(2)}, u32[]{:S(2)}) %collective-permute-start.14) | collective-permute-done | bytes 8224 | tf_op jit(solution)/shard_map/ppermute | solution.py:628
  37.3 1.0 %volume_terms.1 = (f32[16,128]{1,0:T(8,128)S(1)}, f32[2,4,8192]{2,1,0:T(4,128)S(1)}, bf16[2,4,8192]{2,1,0:T(4,128)(2,1)S(1)}, bf16[2,4,8192]{2,1,0:T(4,128)(2,1)S(1)}, bf16[2,4,8192]{2,1,0:T(4,128)(2,1)S(1)}) custom-call(f32[16,128]{1,0:T(8,128)S(1)} %pad_maximum_fusion.rest_0_, f32[16,128]{1,0:T(8,128)S(1)} %collective-permute-done.14.rest_1_, ...), custom_call_target="tpu_custom_call" | custom-call | flops 33554432 | bytes 2621440 | tf_op jit(solution)/shard_map/volume_terms/pallas_call | solution.py:517
  38.4 3.2 %collective-permute-start.15 = (bf16[2,4,8192]{2,1,0:T(4,128)(2,1)S(1)}, bf16[2,4,8192]{2,1,0:T(4,128)(2,1)S(1)}, u32[]{:S(2)}, u32[]{:S(2)}) collective-permute-start(bf16[2,4,8192]{2,1,0:T(4,128)(2,1)S(1)} %get-tuple-element.57), channel_id=1, source_target_pairs={{0,2},{1,3},{2,0},{3,1},{4,6},{5,7},{6,4},{7,5},{8,10},{9,11},{10,... | collective-permute-start | bytes 393224 | tf_op jit(solution)/shard_map/ppermute | solution.py:573
  41.6 1.1 %collective-permute-start.16 = (bf16[2,4,8192]{2,1,0:T(4,128)(2,1)S(1)}, bf16[2,4,8192]{2,1,0:T(4,128)(2,1)S(1)}, u32[]{:S(2)}, u32[]{:S(2)}) collective-permute-start(bf16[2,4,8192]{2,1,0:T(4,128)(2,1)S(1)} %get-tuple-element.58), channel_id=1, source_target_pairs={{0,1},{1,0},{2,3},{3,2},{4,5},{5,4},{6,7},{7,6},{8,9},{9,8},{10,11... | collective-permute-start | bytes 393224 | tf_op jit(solution)/shard_map/ppermute | solution.py:573
  42.7 0.4 collective-permute-start.17
  43.1 0.7 %copy.9 = f32[16,4]{0,1:T(4,128)} copy(f32[16,4]{1,0:T(8,128)S(1)} %bitcast.4) | data formatting | bytes 512
  43.7 6.8 %collective-permute-done.15.rest_0_ = bf16[2,4,8192]{2,1,0:T(4,128)(2,1)S(1)} collective-permute-done((bf16[2,4,8192]{2,1,0:T(4,128)(2,1)S(1)}, bf16[2,4,8192]{2,1,0:T(4,128)(2,1)S(1)}, u32[]{:S(2)}, u32[]{:S(2)}) %collective-permute-start.15) | collective-permute-done | bytes 131104 | tf_op jit(solution)/shard_map/ppermute | solution.py:573
  50.6 0.1 collective-permute-done.16.rest_1_
  50.7 0.0 collective-permute-done.17.rest_2_
  50.7 0.8 %total_volume.1 = f32[2,4,1,8192]{3,2,1,0:T(1,128)} custom-call(f32[2,4,8192]{2,1,0:T(4,128)S(1)} %get-tuple-element.56.first, bf16[2,4,8192]{2,1,0:T(4,128)(2,1)S(1)} %collective-permute-done.15.rest_0_, bf16[2,4,8192]{2,1,0:T(4,128)(2,1)S(1)} %collective-permute-done.16.rest_1_, bf16[2,4,8192]{2,1,0:T(4,128)(2,1)S(1)} %collective-permute-done.17.rest_2_), custom_call_target="tpu_custom_call" | custom-call | tf_op jit(solution)/shard_map/total_volume/pallas_call | solution.py:551
  (1 shorter events, 0.0 us)
Async XLA Ops:
  0.6 13.5 %copy-start = (f32[8,256]{1,0:T(8,128)S(1)}, f32[8,256]{1,0:T(8,128)}, u32[]{:S(2)}) copy-start(f32[8,256]{1,0:T(8,128)} %constant.4.clone.table_x) | copy-start | bytes 24580
  0.6 13.5 %copy-start.1 = (f32[1024]{0:T(1024)S(1)}, f32[1024]{0:T(1024)}, u32[]{:S(2)}) copy-start(f32[1024]{0:T(1024)} %constant.5.clone.table_y) | copy-start | bytes 12292
  2.2 7.3 %collective-permute-start.1 = (bf16[2,16,8320]{2,1,0:T(8,128)(2,1)S(1)}, bf16[2,16,8320]{2,1,0:T(8,128)(2,1)S(1)}, u32[]{:S(2)}, u32[]{:S(2)}) collective-permute-start(bf16[2,16,8320]{2,1,0:T(8,128)(2,1)S(1)} %get-tuple-element.32), channel_id=1, source_target_pairs={{0,4},{4,0},{8,12},{12,8},{1,5},{5,1},{9,13},{13,9},{2,6},{6,2},{1... | collective-permute-start | bytes 1597448 | tf_op jit(solution)/shard_map/ppermute | solution.py:570
  2.7 9.6 %collective-permute-start.5 = (bf16[2,16,4224]{2,1,0:T(8,128)(2,1)S(1)}, bf16[2,16,4224]{2,1,0:T(8,128)(2,1)S(1)}, u32[]{:S(2)}, u32[]{:S(2)}) collective-permute-start(bf16[2,16,4224]{2,1,0:T(8,128)(2,1)S(1)} %get-tuple-element.45), channel_id=1, source_target_pairs={{0,8},{4,12},{8,0},{12,4},{1,9},{5,13},{9,1},{13,5},{2,10},{6,14},... | collective-permute-start | bytes 811016 | tf_op jit(solution)/shard_map/ppermute | solution.py:570
  5.2 10.6 %collective-permute-start.3 = (bf16[2,4,4,2048]{3,2,1,0:T(4,128)(2,1)S(1)}, bf16[2,4,4,2048]{3,2,1,0:T(4,128)(2,1)S(1)}, u32[]{:S(2)}, u32[]{:S(2)}) collective-permute-start(bf16[2,4,4,2048]{3,2,1,0:T(4,128)(2,1)S(1)} %get-tuple-element.33.rest_0_), channel_id=1, source_target_pairs={{0,2},{1,3},{2,0},{3,1},{4,6},{5,7},{6,4},{7,5},{8,10},{9,11},{10,... | collective-permute-start | bytes 393224 | tf_op jit(solution)/shard_map/ppermute | solution.py:573
  7.8 10.2 %collective-permute-start = (bf16[2,4,4,2048]{3,2,1,0:T(4,128)(2,1)S(1)}, bf16[2,4,4,2048]{3,2,1,0:T(4,128)(2,1)S(1)}, u32[]{:S(2)}, u32[]{:S(2)}) collective-permute-start(bf16[2,4,4,2048]{3,2,1,0:T(4,128)(2,1)S(1)} %get-tuple-element.33.rest_0_), channel_id=1, source_target_pairs={{0,1},{1,0},{2,3},{3,2},{4,5},{5,4},{6,7},{7,6},{8,9},{9,8},{10,11... | collective-permute-start | bytes 393224 | tf_op jit(solution)/shard_map/ppermute | solution.py:573
  9.4 9.1 %collective-permute-start.2 = (bf16[2,4,4,2048]{3,2,1,0:T(4,128)(2,1)S(1)}, bf16[2,4,4,2048]{3,2,1,0:T(4,128)(2,1)S(1)}, u32[]{:S(2)}, u32[]{:S(2)}) collective-permute-start(bf16[2,4,4,2048]{3,2,1,0:T(4,128)(2,1)S(1)} %get-tuple-element.33.rest_0_), channel_id=1, source_target_pairs={{0,3},{1,2},{2,1},{3,0},{4,7},{5,6},{6,5},{7,4},{8,11},{9,10},{10,... | collective-permute-start | bytes 393224 | tf_op jit(solution)/shard_map/ppermute | solution.py:573
  9.6 14.1 %collective-permute-start.7 = (bf16[2,16,8320]{2,1,0:T(8,128)(2,1)S(1)}, bf16[2,16,8320]{2,1,0:T(8,128)(2,1)S(1)}, u32[]{:S(2)}, u32[]{:S(2)}) collective-permute-start(bf16[2,16,8320]{2,1,0:T(8,128)(2,1)S(1)} %get-tuple-element.46), channel_id=1, source_target_pairs={{0,12},{4,8},{8,4},{12,0},{1,13},{5,9},{9,5},{13,1},{2,14},{6,10},... | collective-permute-start | bytes 1597448 | tf_op jit(solution)/shard_map/ppermute | solution.py:570
  12.3 11.4 %collective-permute-start.6 = (bf16[2,16,4224]{2,1,0:T(8,128)(2,1)S(1)}, bf16[2,16,4224]{2,1,0:T(8,128)(2,1)S(1)}, u32[]{:S(2)}, u32[]{:S(2)}) collective-permute-start(bf16[2,16,4224]{2,1,0:T(8,128)(2,1)S(1)} %collective-permute-done.5.rest_2_.rest_0_.rest_4_), channel_id=1, source_target_pairs={{0,16},{16,0},{1,17},{17,1},{2,18},{18,2},{3,19},{19,3},{4,20},{20... | collective-permute-start | bytes 811016 | tf_op jit(solution)/shard_map/ppermute | solution.py:586
  20.6 2.2 %collective-permute-start.4 = (f32[128,128]{1,0:T(8,128)S(1)}, f32[128,128]{1,0:T(8,128)S(1)}, u32[]{:S(2)}, u32[]{:S(2)}) collective-permute-start(f32[128,128]{1,0:T(8,128)S(1)} %get-tuple-element.41), channel_id=1, source_target_pairs={{0,4},{4,0},{8,12},{12,8},{1,5},{5,1},{9,13},{13,9},{2,6},{6,2},{1... | collective-permute-start | bytes 196616 | tf_op jit(solution)/shard_map/ppermute | solution.py:570
  20.7 7.5 %collective-permute-start.11 = (f32[128,128]{1,0:T(8,128)S(1)}, f32[128,128]{1,0:T(8,128)S(1)}, u32[]{:S(2)}, u32[]{:S(2)}) collective-permute-start(f32[128,128]{1,0:T(8,128)S(1)} %get-tuple-element.41), channel_id=1, source_target_pairs={{0,12},{4,8},{8,4},{12,0},{1,13},{5,9},{9,5},{13,1},{2,14},{6,10},... | collective-permute-start | bytes 196616 | tf_op jit(solution)/shard_map/ppermute | solution.py:570
  22.2 5.9 %collective-permute-start.10 = (f32[128,128]{1,0:T(8,128)S(1)}, f32[128,128]{1,0:T(8,128)S(1)}, u32[]{:S(2)}, u32[]{:S(2)}) collective-permute-start(f32[128,128]{1,0:T(8,128)S(1)} %get-tuple-element.39.refs_0_), channel_id=1, source_target_pairs={{0,8},{4,12},{8,0},{12,4},{1,9},{5,13},{9,1},{13,5},{2,10},{6,14},... | collective-permute-start | bytes 196616 | tf_op jit(solution)/shard_map/ppermute | solution.py:570
  26.2 4.4 %collective-permute-start.9 = (f32[128,128]{1,0:T(8,128)S(1)}, f32[128,128]{1,0:T(8,128)S(1)}, u32[]{:S(2)}, u32[]{:S(2)}) collective-permute-start(f32[128,128]{1,0:T(8,128)S(1)} %get-tuple-element.48), channel_id=1, source_target_pairs={{0,12},{4,8},{8,4},{12,0},{1,13},{5,9},{9,5},{13,1},{2,14},{6,10},... | collective-permute-start | bytes 196616 | tf_op jit(solution)/shard_map/ppermute | solution.py:570
  28.0 4.3 %collective-permute-start.8 = (f32[128,128]{1,0:T(8,128)S(1)}, f32[128,128]{1,0:T(8,128)S(1)}, u32[]{:S(2)}, u32[]{:S(2)}) collective-permute-start(f32[128,128]{1,0:T(8,128)S(1)} %get-tuple-element.47.refs_4_), channel_id=1, source_target_pairs={{0,8},{4,12},{8,0},{12,4},{1,9},{5,13},{9,1},{13,5},{2,10},{6,14},... | collective-permute-start | bytes 196616 | tf_op jit(solution)/shard_map/ppermute | solution.py:570
  28.0 4.3 %collective-permute-start.12 = (f32[128,128]{1,0:T(8,128)S(1)}, f32[128,128]{1,0:T(8,128)S(1)}, u32[]{:S(2)}, u32[]{:S(2)}) collective-permute-start(f32[128,128]{1,0:T(8,128)S(1)} %get-tuple-element.48), channel_id=1, source_target_pairs={{0,4},{4,0},{8,12},{12,8},{1,5},{5,1},{9,13},{13,9},{2,6},{6,2},{1... | collective-permute-start | bytes 196616 | tf_op jit(solution)/shard_map/ppermute | solution.py:570
  32.5 1.2 %collective-permute-start.13 = (f32[8,128]{1,0:T(8,128)S(1)}, f32[8,128]{1,0:T(8,128)S(1)}, u32[]{:S(2)}, u32[]{:S(2)}) collective-permute-start(f32[8,128]{1,0:T(8,128)S(1)} %logit_stats.1), channel_id=1, source_target_pairs={{0,4},{4,0},{8,12},{12,8},{1,5},{5,1},{9,13},{13,9},{2,6},{6,2},{1... | collective-permute-start | bytes 12296 | tf_op jit(solution)/shard_map/ppermute | solution.py:570
  33.7 3.7 %collective-permute-start.14 = (f32[16,128]{1,0:T(8,128)S(1)}, f32[16,128]{1,0:T(8,128)S(1)}, u32[]{:S(2)}, u32[]{:S(2)}) collective-permute-start(f32[16,128]{1,0:T(8,128)S(1)} %pad_maximum_fusion.rest_0_), channel_id=1, source_target_pairs={{0,16},{16,0},{1,17},{17,1},{2,18},{18,2},{3,19},{19,3},{4,20},{20... | collective-permute-start | bytes 24584 | tf_op jit(solution)/shard_map/ppermute | solution.py:628
  38.4 12.2 %collective-permute-start.15 = (bf16[2,4,8192]{2,1,0:T(4,128)(2,1)S(1)}, bf16[2,4,8192]{2,1,0:T(4,128)(2,1)S(1)}, u32[]{:S(2)}, u32[]{:S(2)}) collective-permute-start(bf16[2,4,8192]{2,1,0:T(4,128)(2,1)S(1)} %get-tuple-element.57), channel_id=1, source_target_pairs={{0,2},{1,3},{2,0},{3,1},{4,6},{5,7},{6,4},{7,5},{8,10},{9,11},{10,... | collective-permute-start | bytes 393224 | tf_op jit(solution)/shard_map/ppermute | solution.py:573
  41.6 9.1 %collective-permute-start.16 = (bf16[2,4,8192]{2,1,0:T(4,128)(2,1)S(1)}, bf16[2,4,8192]{2,1,0:T(4,128)(2,1)S(1)}, u32[]{:S(2)}, u32[]{:S(2)}) collective-permute-start(bf16[2,4,8192]{2,1,0:T(4,128)(2,1)S(1)} %get-tuple-element.58), channel_id=1, source_target_pairs={{0,1},{1,0},{2,3},{3,2},{4,5},{5,4},{6,7},{7,6},{8,9},{9,8},{10,11... | collective-permute-start | bytes 393224 | tf_op jit(solution)/shard_map/ppermute | solution.py:573
  42.7 8.0 %collective-permute-start.17 = (bf16[2,4,8192]{2,1,0:T(4,128)(2,1)S(1)}, bf16[2,4,8192]{2,1,0:T(4,128)(2,1)S(1)}, u32[]{:S(2)}, u32[]{:S(2)}) collective-permute-start(bf16[2,4,8192]{2,1,0:T(4,128)(2,1)S(1)} %get-tuple-element.59), channel_id=1, source_target_pairs={{0,3},{1,2},{2,1},{3,0},{4,7},{5,6},{6,5},{7,4},{8,11},{9,10},{10,... | collective-permute-start | bytes 393224 | tf_op jit(solution)/shard_map/ppermute | solution.py:573

commit v12 on v10

--- a/solution.py
+++ b/solution.py
@@ -432,7 +432,7 @@
                 out[1, own, cols] = (re * sine + im * cosine).astype(BF)
             return carry
 
-        lax.fori_loop(0, lines, add_line, 0, unroll=min(lines, 4))
+        lax.fori_loop(0, lines, add_line, 0, unroll=min(lines, 8))
 
 
 def aligned_rows(table_x, table_y, picked, width):
@@ -468,7 +468,7 @@
     prob, outs = rest[4 + groups], rest[5 + groups :]
     rows = metas[0].shape[1]
     width = near.shape[2]
-    chunk = min(width, 8 * IMG)
+    chunk = min(width, 4 * IMG)
     lane = lax.broadcasted_iota(jnp.int32, (rows, LANES), 1)
     pieces = []
     for g in range(groups):

time: 52.1 us -> 52 us (level)
  transfers between devices with their start and end apart: 18 -> 18, of which waited for: 9 -> 8; matrix products, arithmetic and copies ran while one was open for 1% -> 1% of each run, Pallas kernels for 23% -> 22%
where the time goes in v12:
time: 52 us; the launch traced here: 51.4 us
  starting transfers between devices  20.2 us (39%)
  Pallas kernels  15.1 us (29%)
  waiting for transfers between devices  14.7 us (28%)
  between operations  0.76 us (1%)
  local copies, waits for them, and re-layouts  0.66 us (1%)
    ppermute x6, starting transfers between devices, swap_orient(): return lax.ppermute(array, 'orient', xor_pairs(orient, step))  9 us
    ppermute x10, starting transfers between devices, swap_dom(): return lax.ppermute(array, 'dom', xor_pairs(dom, step))  7.89 us
    ppermute x6, waiting for transfers between devices, swap_orient(): return lax.ppermute(array, 'orient', xor_pairs(orient, step))  7.39 us
    ppermute x10, waiting for transfers between devices, swap_dom(): return lax.ppermute(array, 'dom', xor_pairs(dom, step))  5.13 us
    pallas_call x2, Pallas kernels, near_logits(): pl.pallas_call(functools.partial(near_kernel, sizes_of(picked), len(shard...  4.32 us
    pallas_call x2, Pallas kernels, aligned_rows(): pl.pallas_call(functools.partial(rows_kernel, sizes_of(picked)), out_shap...  3.72 us
    pallas_call x1, Pallas kernels, far_logits(): pl.pallas_call(functools.partial(far_kernel, sizes_of(picked), [right.sha...  2.45 us
    ppermute x1, waiting for transfers between devices, local(): stats_all = [stats, lax.ppermute(stats, 'cls', xor_pairs(cls, 1))]  2.13 us
  transfers between devices with their start and end apart: 18, of which 8 were waited for; matrix products, arithmetic and copies ran while one was open for 1% of the time, Pallas kernels for 22%

profile of v12, /device:TPU:0, one launch (start us, length us, event | category | flops | bytes accessed | tf_op | source)
XLA Modules:
  0.0 51.4 jit_solution(12145101920312859072)
XLA Ops:
  0.6 0.0 copy-start
  0.6 0.0 copy-start.1
  0.7 1.5 %image_bands.1 = (bf16[2,16,8320]{2,1,0:T(8,128)(2,1)S(1)}, bf16[2,16,4224]{2,1,0:T(8,128)(2,1)S(1)}, bf16[2,16,8320]{2,1,0:T(8,128)(2,1)S(1)}, bf16[2,16,128]{2...) custom-call(bf16[2,16,32768]{2,1,0:T(8,128)(2,1)} %images.3, bf16[2,4,4,2048]{3,2,1,0:T(4,128)(2,1)} %references.1, ...), custom_call_target="tpu_custom_call" | custom-call | bytes 3145728 | tf_op jit(solution)/shard_map/image_bands/pallas_call | solution.py:109
  2.2 0.5 %collective-permute-start.1 = (bf16[2,16,8320]{2,1,0:T(8,128)(2,1)S(1)}, bf16[2,16,8320]{2,1,0:T(8,128)(2,1)S(1)}, u32[]{:S(2)}, u32[]{:S(2)}) collective-permute-start(bf16[2,16,8320]{2,1,0:T(8,128)(2,1)S(1)} %get-tuple-element.32), channel_id=1, source_target_pairs={{0,4},{4,0},{8,12},{12,8},{1,5},{5,1},{9,13},{13,9},{2,6},{6,2},{1... | collective-permute-start | bytes 1597448 | tf_op jit(solution)/shard_map/ppermute | solution.py:560
  2.7 2.6 %collective-permute-start.5 = (bf16[2,16,4224]{2,1,0:T(8,128)(2,1)S(1)}, bf16[2,16,4224]{2,1,0:T(8,128)(2,1)S(1)}, u32[]{:S(2)}, u32[]{:S(2)}) collective-permute-start(bf16[2,16,4224]{2,1,0:T(8,128)(2,1)S(1)} %get-tuple-element.45), channel_id=1, source_target_pairs={{0,8},{4,12},{8,0},{12,4},{1,9},{5,13},{9,1},{13,5},{2,10},{6,14},... | collective-permute-start | bytes 811016 | tf_op jit(solution)/shard_map/ppermute | solution.py:560
  5.2 2.6 %collective-permute-start.3 = (bf16[2,4,4,2048]{3,2,1,0:T(4,128)(2,1)S(1)}, bf16[2,4,4,2048]{3,2,1,0:T(4,128)(2,1)S(1)}, u32[]{:S(2)}, u32[]{:S(2)}) collective-permute-start(bf16[2,4,4,2048]{3,2,1,0:T(4,128)(2,1)S(1)} %get-tuple-element.33.rest_0_), channel_id=1, source_target_pairs={{0,2},{1,3},{2,0},{3,1},{4,6},{5,7},{6,4},{7,5},{8,10},{9,11},{10,... | collective-permute-start | bytes 393224 | tf_op jit(solution)/shard_map/ppermute | solution.py:563
  7.8 1.6 %collective-permute-start = (bf16[2,4,4,2048]{3,2,1,0:T(4,128)(2,1)S(1)}, bf16[2,4,4,2048]{3,2,1,0:T(4,128)(2,1)S(1)}, u32[]{:S(2)}, u32[]{:S(2)}) collective-permute-start(bf16[2,4,4,2048]{3,2,1,0:T(4,128)(2,1)S(1)} %get-tuple-element.33.rest_0_), channel_id=1, source_target_pairs={{0,1},{1,0},{2,3},{3,2},{4,5},{5,4},{6,7},{7,6},{8,9},{9,8},{10,11... | collective-permute-start | bytes 393224 | tf_op jit(solution)/shard_map/ppermute | solution.py:563
  9.4 0.0 collective-permute-done.1.rest_1_.rest_3_
  9.4 0.2 collective-permute-start.2
  9.6 0.5 %collective-permute-start.7 = (bf16[2,16,8320]{2,1,0:T(8,128)(2,1)S(1)}, bf16[2,16,8320]{2,1,0:T(8,128)(2,1)S(1)}, u32[]{:S(2)}, u32[]{:S(2)}) collective-permute-start(bf16[2,16,8320]{2,1,0:T(8,128)(2,1)S(1)} %get-tuple-element.46), channel_id=1, source_target_pairs={{0,12},{4,8},{8,4},{12,0},{1,13},{5,9},{9,5},{13,1},{2,14},{6,10},... | collective-permute-start | bytes 1597448 | tf_op jit(solution)/shard_map/ppermute | solution.py:560
  10.1 1.0 %own_band.1.rest_2_ = bf16[2,16,8192]{2,1,0:T(8,128)(2,1)S(1)} custom-call(bf16[2,16,32768]{2,1,0:T(8,128)(2,1)} %images.3), custom_call_target="tpu_custom_call" | custom-call | tf_op jit(solution)/shard_map/own_band/pallas_call | solution.py:155
  11.2 1.1 %collective-permute-done.5.rest_2_.rest_0_.rest_4_ = bf16[2,16,4224]{2,1,0:T(8,128)(2,1)S(1)} collective-permute-done((bf16[2,16,4224]{2,1,0:T(8,128)(2,1)S(1)}, bf16[2,16,4224]{2,1,0:T(8,128)(2,1)S(1)}, u32[]{:S(2)}, u32[]{:S(2)}) %collective-permute-start.5) | collective-permute-done | bytes 270368 | tf_op jit(solution)/shard_map/ppermute | solution.py:560
  12.3 1.8 %collective-permute-start.6 = (bf16[2,16,4224]{2,1,0:T(8,128)(2,1)S(1)}, bf16[2,16,4224]{2,1,0:T(8,128)(2,1)S(1)}, u32[]{:S(2)}, u32[]{:S(2)}) collective-permute-start(bf16[2,16,4224]{2,1,0:T(8,128)(2,1)S(1)} %collective-permute-done.5.rest_2_.rest_0_.rest_4_), channel_id=1, source_target_pairs={{0,16},{16,0},{1,17},{17,1},{2,18},{18,2},{3,19},{19,3},{4,20},{20... | collective-permute-start | bytes 811016 | tf_op jit(solution)/shard_map/ppermute | solution.py:576
  14.1 0.0 copy-done
  14.1 0.0 copy-done.1
  14.1 1.7 %aligned_rows.2.rest_6_ = bf16[2,32,8192]{2,1,0:T(8,128)(2,1)S(1)} custom-call(f32[1024]{0:T(1024)S(1)} %copy-done.1, f32[8,256]{1,0:T(8,128)S(1)} %copy-done, bf16[2,16,128]{2,1,0:T(8,128)(2,1)S(1)} %get-tuple-element.35.rest_0_.rest_2_, bf16[2,16,8320]{2,1,0:T(8,128)(2,1)S(1)} %collective-permute-done.1.rest_1_.rest_3_, ...), custom_call_target="tpu_custom_call" | custom-call | tf_op jit(solution)/shard_map/aligned_rows/pallas_call | solution.py:442
  15.8 0.0 collective-permute-done.3.rest_1_
  15.8 2.2 %near_logits.2 = (f32[128,128]{1,0:T(8,128)S(1)}, f32[128,128]{1,0:T(8,128)S(1)}, bf16[2,128,4096]{2,1,0:T(8,128)(2,1)S(1)}) custom-call(f32[1024]{0:T(1024)S(1)} %copy-done.1, f32[8,256]{1,0:T(8,128)S(1)} %copy-done, bf16[2,4,4,2048]{3,2,1,0:T(4,128)(2,1)S(1)} %get-tuple-element.33.rest_0_, bf16[2,4,4,2048]{3,2,1,0:T(4,128)(2,1)S(1)} %collective-permute-done.3.rest_1_, ...), custom_call_target="tpu_custom_call" | custom-call | tf_op jit(solution)/shard_map/near_logits/pallas_call | solution.py:314
  18.0 0.0 collective-permute-done.rest_0_
  18.0 0.5 %collective-permute-done.2.rest_1_ = bf16[2,4,4,2048]{3,2,1,0:T(4,128)(2,1)S(1)} collective-permute-done((bf16[2,4,4,2048]{3,2,1,0:T(4,128)(2,1)S(1)}, bf16[2,4,4,2048]{3,2,1,0:T(4,128)(2,1)S(1)}, u32[]{:S(2)}, u32[]{:S(2)}) %collective-permute-start.2) | collective-permute-done | bytes 131104 | tf_op jit(solution)/shard_map/ppermute | solution.py:563
  18.5 2.2 %near_logits.3 = (f32[128,128]{1,0:T(8,128)S(1)}, f32[128,128]{1,0:T(8,128)S(1)}, bf16[2,128,4096]{2,1,0:T(8,128)(2,1)S(1)}) custom-call(f32[1024]{0:T(1024)S(1)} %copy-done.1, f32[8,256]{1,0:T(8,128)S(1)} %copy-done, bf16[2,4,4,2048]{3,2,1,0:T(4,128)(2,1)S(1)} %collective-permute-done.rest_0_, bf16[2,4,4,2048]{3,2,1,0:T(4,128)(2,1)S(1)} %collective-permute-done.2.rest_1_, ...), custom_call_target="tpu_custom_call" | custom-call | flops 20000000000 | tf_op jit(solution)/shard_map/near_logits/pallas_call | solution.py:314
  20.6 0.1 collective-permute-start.4
  20.7 1.4 %collective-permute-start.11 = (f32[128,128]{1,0:T(8,128)S(1)}, f32[128,128]{1,0:T(8,128)S(1)}, u32[]{:S(2)}, u32[]{:S(2)}) collective-permute-start(f32[128,128]{1,0:T(8,128)S(1)} %get-tuple-element.41), channel_id=1, source_target_pairs={{0,12},{4,8},{8,4},{12,0},{1,13},{5,9},{9,5},{13,1},{2,14},{6,10},... | collective-permute-start | bytes 196616 | tf_op jit(solution)/shard_map/ppermute | solution.py:560
  22.2 0.7 %collective-permute-start.10 = (f32[128,128]{1,0:T(8,128)S(1)}, f32[128,128]{1,0:T(8,128)S(1)}, u32[]{:S(2)}, u32[]{:S(2)}) collective-permute-start(f32[128,128]{1,0:T(8,128)S(1)} %get-tuple-element.39.refs_0_), channel_id=1, source_target_pairs={{0,8},{4,12},{8,0},{12,4},{1,9},{5,13},{9,1},{13,5},{2,10},{6,14},... | collective-permute-start | bytes 196616 | tf_op jit(solution)/shard_map/ppermute | solution.py:560
  22.9 0.0 collective-permute-done.4.refs_1_
  22.9 0.9 %collective-permute-done.7.rest_4_.rest_1_.rest_5_ = bf16[2,16,8320]{2,1,0:T(8,128)(2,1)S(1)} collective-permute-done((bf16[2,16,8320]{2,1,0:T(8,128)(2,1)S(1)}, bf16[2,16,8320]{2,1,0:T(8,128)(2,1)S(1)}, u32[]{:S(2)}, u32[]{:S(2)}) %collective-permute-start.7) | collective-permute-done | bytes 532512 | tf_op jit(solution)/shard_map/ppermute | solution.py:560
  23.7 0.0 collective-permute-done.6.rest_3_
  23.7 2.5 %far_logits.1 = (f32[128,128]{1,0:T(8,128)S(1)}, f32[128,128]{1,0:T(8,128)S(1)}) custom-call(f32[8,256]{1,0:T(8,128)S(1)} %copy-done, bf16[2,128,4096]{2,1,0:T(8,128)(2,1)S(1)} %get-tuple-element.43.rest_0_, bf16[2,128,4096]{2,1,0:T(8,128)(2,1)S(1)} %get-tuple-element.44.rest_1_, bf16[2,16,4224]{2,1,0:T(8,128)(2,1)S(1)} %collective-permute-done.5.rest_2_.rest_0_.rest_4_, ...), custom_call_target="tpu_custom_call" | custom-call | flops 6000000000 | tf_op jit(solution)/shard_map/far_logits/pallas_call | solution.py:340
  26.2 1.9 %collective-permute-start.9 = (f32[128,128]{1,0:T(8,128)S(1)}, f32[128,128]{1,0:T(8,128)S(1)}, u32[]{:S(2)}, u32[]{:S(2)}) collective-permute-start(f32[128,128]{1,0:T(8,128)S(1)} %get-tuple-element.48), channel_id=1, source_target_pairs={{0,12},{4,8},{8,4},{12,0},{1,13},{5,9},{9,5},{13,1},{2,14},{6,10},... | collective-permute-start | bytes 196616 | tf_op jit(solution)/shard_map/ppermute | solution.py:560
  28.1 0.0 collective-permute-start.8
  28.1 0.2 collective-permute-start.12
  28.2 0.0 collective-permute-done.10.refs_6_
  28.3 0.0 collective-permute-done.11.refs_7_
  28.3 2.1 %aligned_rows.3.rest_7_ = bf16[2,32,8192]{2,1,0:T(8,128)(2,1)S(1)} custom-call(f32[1024]{0:T(1024)S(1)} %copy-done.1, f32[8,256]{1,0:T(8,128)S(1)} %copy-done, bf16[2,16,4224]{2,1,0:T(8,128)(2,1)S(1)} %collective-permute-done.5.rest_2_.rest_0_.rest_4_, bf16[2,16,8320]{2,1,0:T(8,128)(2,1)S(1)} %collective-permute-done.7.rest_4_.rest_1_.rest_5_, ...), custom_call_target="tpu_custom_call" | custom-call | tf_op jit(solution)/shard_map/aligned_rows/pallas_call | solution.py:442
  30.3 0.3 collective-permute-done.9.refs_3_
  30.6 1.7 %collective-permute-done.8.refs_2_ = f32[128,128]{1,0:T(8,128)S(1)} collective-permute-done((f32[128,128]{1,0:T(8,128)S(1)}, f32[128,128]{1,0:T(8,128)S(1)}, u32[]{:S(2)}, u32[]{:S(2)}) %collective-permute-start.8) | collective-permute-done | bytes 65568 | tf_op jit(solution)/shard_map/ppermute | solution.py:560
  32.3 0.0 collective-permute-done.12.refs_5_
  32.3 0.3 logit_stats.1
  32.6 0.0 collective-permute-start.13
  32.6 1.2 %collective-permute-done.13 = f32[8,128]{1,0:T(8,128)S(1)} collective-permute-done((f32[8,128]{1,0:T(8,128)S(1)}, f32[8,128]{1,0:T(8,128)S(1)}, u32[]{:S(2)}, u32[]{:S(2)}) %collective-permute-start.13) | collective-permute-done | bytes 4128 | tf_op jit(solution)/shard_map/ppermute | solution.py:560
  33.8 1.5 %collective-permute-start.14 = (f32[16,128]{1,0:T(8,128)S(1)}, f32[16,128]{1,0:T(8,128)S(1)}, u32[]{:S(2)}, u32[]{:S(2)}) collective-permute-start(f32[16,128]{1,0:T(8,128)S(1)} %pad_maximum_fusion.rest_0_), channel_id=1, source_target_pairs={{0,16},{16,0},{1,17},{17,1},{2,18},{18,2},{3,19},{19,3},{4,20},{20... | collective-permute-start | bytes 24584 | tf_op jit(solution)/shard_map/ppermute | solution.py:618
  35.3 2.1 %collective-permute-done.14.rest_1_ = f32[16,128]{1,0:T(8,128)S(1)} collective-permute-done((f32[16,128]{1,0:T(8,128)S(1)}, f32[16,128]{1,0:T(8,128)S(1)}, u32[]{:S(2)}, u32[]{:S(2)}) %collective-permute-start.14) | collective-permute-done | bytes 8224 | tf_op jit(solution)/shard_map/ppermute | solution.py:618
  37.4 1.0 %volume_terms.1 = (f32[16,128]{1,0:T(8,128)S(1)}, f32[2,4,8192]{2,1,0:T(4,128)S(1)}, bf16[2,4,8192]{2,1,0:T(4,128)(2,1)S(1)}, bf16[2,4,8192]{2,1,0:T(4,128)(2,1)S(1)}, bf16[2,4,8192]{2,1,0:T(4,128)(2,1)S(1)}) custom-call(f32[16,128]{1,0:T(8,128)S(1)} %pad_maximum_fusion.rest_0_, f32[16,128]{1,0:T(8,128)S(1)} %collective-permute-done.14.rest_1_, ...), custom_call_target="tpu_custom_call" | custom-call | flops 33554432 | bytes 2621440 | tf_op jit(solution)/shard_map/volume_terms/pallas_call | solution.py:517
  38.5 3.1 %collective-permute-start.15 = (bf16[2,4,8192]{2,1,0:T(4,128)(2,1)S(1)}, bf16[2,4,8192]{2,1,0:T(4,128)(2,1)S(1)}, u32[]{:S(2)}, u32[]{:S(2)}) collective-permute-start(bf16[2,4,8192]{2,1,0:T(4,128)(2,1)S(1)} %get-tuple-element.57), channel_id=1, source_target_pairs={{0,2},{1,3},{2,0},{3,1},{4,6},{5,7},{6,4},{7,5},{8,10},{9,11},{10,... | collective-permute-start | bytes 393224 | tf_op jit(solution)/shard_map/ppermute | solution.py:563
  41.6 1.1 %collective-permute-start.16 = (bf16[2,4,8192]{2,1,0:T(4,128)(2,1)S(1)}, bf16[2,4,8192]{2,1,0:T(4,128)(2,1)S(1)}, u32[]{:S(2)}, u32[]{:S(2)}) collective-permute-start(bf16[2,4,8192]{2,1,0:T(4,128)(2,1)S(1)} %get-tuple-element.58), channel_id=1, source_target_pairs={{0,1},{1,0},{2,3},{3,2},{4,5},{5,4},{6,7},{7,6},{8,9},{9,8},{10,11... | collective-permute-start | bytes 393224 | tf_op jit(solution)/shard_map/ppermute | solution.py:563
  42.7 0.4 collective-permute-start.17
  43.1 0.7 %copy.9 = f32[16,4]{0,1:T(4,128)} copy(f32[16,4]{1,0:T(8,128)S(1)} %bitcast.4) | data formatting | bytes 512
  43.7 6.9 %collective-permute-done.15.rest_0_ = bf16[2,4,8192]{2,1,0:T(4,128)(2,1)S(1)} collective-permute-done((bf16[2,4,8192]{2,1,0:T(4,128)(2,1)S(1)}, bf16[2,4,8192]{2,1,0:T(4,128)(2,1)S(1)}, u32[]{:S(2)}, u32[]{:S(2)}) %collective-permute-start.15) | collective-permute-done | bytes 131104 | tf_op jit(solution)/shard_map/ppermute | solution.py:563
  50.6 0.0 collective-permute-done.16.rest_1_
  50.6 0.0 collective-permute-done.17.rest_2_
  50.6 0.8 %total_volume.1 = f32[2,4,1,8192]{3,2,1,0:T(1,128)} custom-call(f32[2,4,8192]{2,1,0:T(4,128)S(1)} %get-tuple-element.56.first, bf16[2,4,8192]{2,1,0:T(4,128)(2,1)S(1)} %collective-permute-done.15.rest_0_, bf16[2,4,8192]{2,1,0:T(4,128)(2,1)S(1)} %collective-permute-done.16.rest_1_, bf16[2,4,8192]{2,1,0:T(4,128)(2,1)S(1)} %collective-permute-done.17.rest_2_), custom_call_target="tpu_custom_call" | custom-call | tf_op jit(solution)/shard_map/total_volume/pallas_call | solution.py:546
  (1 shorter events, 0.0 us)
Async XLA Ops:
  0.6 13.5 %copy-start = (f32[8,256]{1,0:T(8,128)S(1)}, f32[8,256]{1,0:T(8,128)}, u32[]{:S(2)}) copy-start(f32[8,256]{1,0:T(8,128)} %constant.4.clone.table_x) | copy-start | bytes 24580
  0.6 13.5 %copy-start.1 = (f32[1024]{0:T(1024)S(1)}, f32[1024]{0:T(1024)}, u32[]{:S(2)}) copy-start(f32[1024]{0:T(1024)} %constant.5.clone.table_y) | copy-start | bytes 12292
  2.2 7.3 %collective-permute-start.1 = (bf16[2,16,8320]{2,1,0:T(8,128)(2,1)S(1)}, bf16[2,16,8320]{2,1,0:T(8,128)(2,1)S(1)}, u32[]{:S(2)}, u32[]{:S(2)}) collective-permute-start(bf16[2,16,8320]{2,1,0:T(8,128)(2,1)S(1)} %get-tuple-element.32), channel_id=1, source_target_pairs={{0,4},{4,0},{8,12},{12,8},{1,5},{5,1},{9,13},{13,9},{2,6},{6,2},{1... | collective-permute-start | bytes 1597448 | tf_op jit(solution)/shard_map/ppermute | solution.py:560
  2.7 9.6 %collective-permute-start.5 = (bf16[2,16,4224]{2,1,0:T(8,128)(2,1)S(1)}, bf16[2,16,4224]{2,1,0:T(8,128)(2,1)S(1)}, u32[]{:S(2)}, u32[]{:S(2)}) collective-permute-start(bf16[2,16,4224]{2,1,0:T(8,128)(2,1)S(1)} %get-tuple-element.45), channel_id=1, source_target_pairs={{0,8},{4,12},{8,0},{12,4},{1,9},{5,13},{9,1},{13,5},{2,10},{6,14},... | collective-permute-start | bytes 811016 | tf_op jit(solution)/shard_map/ppermute | solution.py:560
  5.2 10.5 %collective-permute-start.3 = (bf16[2,4,4,2048]{3,2,1,0:T(4,128)(2,1)S(1)}, bf16[2,4,4,2048]{3,2,1,0:T(4,128)(2,1)S(1)}, u32[]{:S(2)}, u32[]{:S(2)}) collective-permute-start(bf16[2,4,4,2048]{3,2,1,0:T(4,128)(2,1)S(1)} %get-tuple-element.33.rest_0_), channel_id=1, source_target_pairs={{0,2},{1,3},{2,0},{3,1},{4,6},{5,7},{6,4},{7,5},{8,10},{9,11},{10,... | collective-permute-start | bytes 393224 | tf_op jit(solution)/shard_map/ppermute | solution.py:563
  7.8 10.1 %collective-permute-start = (bf16[2,4,4,2048]{3,2,1,0:T(4,128)(2,1)S(1)}, bf16[2,4,4,2048]{3,2,1,0:T(4,128)(2,1)S(1)}, u32[]{:S(2)}, u32[]{:S(2)}) collective-permute-start(bf16[2,4,4,2048]{3,2,1,0:T(4,128)(2,1)S(1)} %get-tuple-element.33.rest_0_), channel_id=1, source_target_pairs={{0,1},{1,0},{2,3},{3,2},{4,5},{5,4},{6,7},{7,6},{8,9},{9,8},{10,11... | collective-permute-start | bytes 393224 | tf_op jit(solution)/shard_map/ppermute | solution.py:563
  9.4 9.1 %collective-permute-start.2 = (bf16[2,4,4,2048]{3,2,1,0:T(4,128)(2,1)S(1)}, bf16[2,4,4,2048]{3,2,1,0:T(4,128)(2,1)S(1)}, u32[]{:S(2)}, u32[]{:S(2)}) collective-permute-start(bf16[2,4,4,2048]{3,2,1,0:T(4,128)(2,1)S(1)} %get-tuple-element.33.rest_0_), channel_id=1, source_target_pairs={{0,3},{1,2},{2,1},{3,0},{4,7},{5,6},{6,5},{7,4},{8,11},{9,10},{10,... | collective-permute-start | bytes 393224 | tf_op jit(solution)/shard_map/ppermute | solution.py:563
  9.6 14.1 %collective-permute-start.7 = (bf16[2,16,8320]{2,1,0:T(8,128)(2,1)S(1)}, bf16[2,16,8320]{2,1,0:T(8,128)(2,1)S(1)}, u32[]{:S(2)}, u32[]{:S(2)}) collective-permute-start(bf16[2,16,8320]{2,1,0:T(8,128)(2,1)S(1)} %get-tuple-element.46), channel_id=1, source_target_pairs={{0,12},{4,8},{8,4},{12,0},{1,13},{5,9},{9,5},{13,1},{2,14},{6,10},... | collective-permute-start | bytes 1597448 | tf_op jit(solution)/shard_map/ppermute | solution.py:560
  12.3 11.4 %collective-permute-start.6 = (bf16[2,16,4224]{2,1,0:T(8,128)(2,1)S(1)}, bf16[2,16,4224]{2,1,0:T(8,128)(2,1)S(1)}, u32[]{:S(2)}, u32[]{:S(2)}) collective-permute-start(bf16[2,16,4224]{2,1,0:T(8,128)(2,1)S(1)} %collective-permute-done.5.rest_2_.rest_0_.rest_4_), channel_id=1, source_target_pairs={{0,16},{16,0},{1,17},{17,1},{2,18},{18,2},{3,19},{19,3},{4,20},{20... | collective-permute-start | bytes 811016 | tf_op jit(solution)/shard_map/ppermute | solution.py:576
  20.6 2.2 %collective-permute-start.4 = (f32[128,128]{1,0:T(8,128)S(1)}, f32[128,128]{1,0:T(8,128)S(1)}, u32[]{:S(2)}, u32[]{:S(2)}) collective-permute-start(f32[128,128]{1,0:T(8,128)S(1)} %get-tuple-element.41), channel_id=1, source_target_pairs={{0,4},{4,0},{8,12},{12,8},{1,5},{5,1},{9,13},{13,9},{2,6},{6,2},{1... | collective-permute-start | bytes 196616 | tf_op jit(solution)/shard_map/ppermute | solution.py:560
  20.7 7.5 %collective-permute-start.11 = (f32[128,128]{1,0:T(8,128)S(1)}, f32[128,128]{1,0:T(8,128)S(1)}, u32[]{:S(2)}, u32[]{:S(2)}) collective-permute-start(f32[128,128]{1,0:T(8,128)S(1)} %get-tuple-element.41), channel_id=1, source_target_pairs={{0,12},{4,8},{8,4},{12,0},{1,13},{5,9},{9,5},{13,1},{2,14},{6,10},... | collective-permute-start | bytes 196616 | tf_op jit(solution)/shard_map/ppermute | solution.py:560
  22.2 6.1 %collective-permute-start.10 = (f32[128,128]{1,0:T(8,128)S(1)}, f32[128,128]{1,0:T(8,128)S(1)}, u32[]{:S(2)}, u32[]{:S(2)}) collective-permute-start(f32[128,128]{1,0:T(8,128)S(1)} %get-tuple-element.39.refs_0_), channel_id=1, source_target_pairs={{0,8},{4,12},{8,0},{12,4},{1,9},{5,13},{9,1},{13,5},{2,10},{6,14},... | collective-permute-start | bytes 196616 | tf_op jit(solution)/shard_map/ppermute | solution.py:560
  26.2 4.4 %collective-permute-start.9 = (f32[128,128]{1,0:T(8,128)S(1)}, f32[128,128]{1,0:T(8,128)S(1)}, u32[]{:S(2)}, u32[]{:S(2)}) collective-permute-start(f32[128,128]{1,0:T(8,128)S(1)} %get-tuple-element.48), channel_id=1, source_target_pairs={{0,12},{4,8},{8,4},{12,0},{1,13},{5,9},{9,5},{13,1},{2,14},{6,10},... | collective-permute-start | bytes 196616 | tf_op jit(solution)/shard_map/ppermute | solution.py:560
  28.1 4.3 %collective-permute-start.8 = (f32[128,128]{1,0:T(8,128)S(1)}, f32[128,128]{1,0:T(8,128)S(1)}, u32[]{:S(2)}, u32[]{:S(2)}) collective-permute-start(f32[128,128]{1,0:T(8,128)S(1)} %get-tuple-element.47.refs_4_), channel_id=1, source_target_pairs={{0,8},{4,12},{8,0},{12,4},{1,9},{5,13},{9,1},{13,5},{2,10},{6,14},... | collective-permute-start | bytes 196616 | tf_op jit(solution)/shard_map/ppermute | solution.py:560
  28.1 4.3 %collective-permute-start.12 = (f32[128,128]{1,0:T(8,128)S(1)}, f32[128,128]{1,0:T(8,128)S(1)}, u32[]{:S(2)}, u32[]{:S(2)}) collective-permute-start(f32[128,128]{1,0:T(8,128)S(1)} %get-tuple-element.48), channel_id=1, source_target_pairs={{0,4},{4,0},{8,12},{12,8},{1,5},{5,1},{9,13},{13,9},{2,6},{6,2},{1... | collective-permute-start | bytes 196616 | tf_op jit(solution)/shard_map/ppermute | solution.py:560
  32.6 1.2 %collective-permute-start.13 = (f32[8,128]{1,0:T(8,128)S(1)}, f32[8,128]{1,0:T(8,128)S(1)}, u32[]{:S(2)}, u32[]{:S(2)}) collective-permute-start(f32[8,128]{1,0:T(8,128)S(1)} %logit_stats.1), channel_id=1, source_target_pairs={{0,4},{4,0},{8,12},{12,8},{1,5},{5,1},{9,13},{13,9},{2,6},{6,2},{1... | collective-permute-start | bytes 12296 | tf_op jit(solution)/shard_map/ppermute | solution.py:560
  33.8 3.7 %collective-permute-start.14 = (f32[16,128]{1,0:T(8,128)S(1)}, f32[16,128]{1,0:T(8,128)S(1)}, u32[]{:S(2)}, u32[]{:S(2)}) collective-permute-start(f32[16,128]{1,0:T(8,128)S(1)} %pad_maximum_fusion.rest_0_), channel_id=1, source_target_pairs={{0,16},{16,0},{1,17},{17,1},{2,18},{18,2},{3,19},{19,3},{4,20},{20... | collective-permute-start | bytes 24584 | tf_op jit(solution)/shard_map/ppermute | solution.py:618
  38.5 12.1 %collective-permute-start.15 = (bf16[2,4,8192]{2,1,0:T(4,128)(2,1)S(1)}, bf16[2,4,8192]{2,1,0:T(4,128)(2,1)S(1)}, u32[]{:S(2)}, u32[]{:S(2)}) collective-permute-start(bf16[2,4,8192]{2,1,0:T(4,128)(2,1)S(1)} %get-tuple-element.57), channel_id=1, source_target_pairs={{0,2},{1,3},{2,0},{3,1},{4,6},{5,7},{6,4},{7,5},{8,10},{9,11},{10,... | collective-permute-start | bytes 393224 | tf_op jit(solution)/shard_map/ppermute | solution.py:563
  41.6 9.1 %collective-permute-start.16 = (bf16[2,4,8192]{2,1,0:T(4,128)(2,1)S(1)}, bf16[2,4,8192]{2,1,0:T(4,128)(2,1)S(1)}, u32[]{:S(2)}, u32[]{:S(2)}) collective-permute-start(bf16[2,4,8192]{2,1,0:T(4,128)(2,1)S(1)} %get-tuple-element.58), channel_id=1, source_target_pairs={{0,1},{1,0},{2,3},{3,2},{4,5},{5,4},{6,7},{7,6},{8,9},{9,8},{10,11... | collective-permute-start | bytes 393224 | tf_op jit(solution)/shard_map/ppermute | solution.py:563
  42.7 7.9 %collective-permute-start.17 = (bf16[2,4,8192]{2,1,0:T(4,128)(2,1)S(1)}, bf16[2,4,8192]{2,1,0:T(4,128)(2,1)S(1)}, u32[]{:S(2)}, u32[]{:S(2)}) collective-permute-start(bf16[2,4,8192]{2,1,0:T(4,128)(2,1)S(1)} %get-tuple-element.59), channel_id=1, source_target_pairs={{0,3},{1,2},{2,1},{3,0},{4,7},{5,6},{6,5},{7,4},{8,11},{9,10},{10,... | collective-permute-start | bytes 393224 | tf_op jit(solution)/shard_map/ppermute | solution.py:563
